TPU v7x, 32 devices: a whole 2x2x4 slice. The times are simulated.
32 devices in a mesh: pipe: 8 (over z, y), dp: 2 (over x), mp: 2 (over core).
Axes of the slice: x: 2, y: 2, z: 4, core: 2. Of those that a mesh axis runs over, the one named last changes fastest.
Arguments:
- activations: bfloat16 [2, 128, 7168], P('dp', 'pipe', 'mp'), may hold values from -6 to 6
- cotangent: bfloat16 [2, 128, 7168], P('dp', 'pipe', 'mp'), may hold values from -6 to 6
- squeeze_old: bfloat16 [8, 7168, 64], P('pipe', 'mp'), may hold values from -5 to 5
- expand_old: bfloat16 [8, 64, 7168], P('pipe', None, 'mp'), may hold values from -5 to 5
- squeeze_late: bfloat16 [2, 8, 7168, 64], P('dp', 'pipe', 'mp'), may hold values from -6 to 6
- expand_late: bfloat16 [2, 8, 64, 7168], P('dp', 'pipe', None, 'mp'), may hold values from -6 to 6
- stash_inputs: bfloat16 [2, 8, 8, 16, 7168], P('dp', 'pipe', None, None, 'mp'), may hold values from -6 to 6
- forward_in: bfloat16 [2, 8, 16, 7168], P('dp', 'pipe', None, 'mp'), may hold values from -6 to 6
- backward_in: bfloat16 [2, 8, 16, 7168], P('dp', 'pipe', None, 'mp'), may hold values from -6 to 6
Outputs:
- squeeze_new: bfloat16 [8, 7168, 64], P('pipe', 'mp')
- expand_new: bfloat16 [8, 64, 7168], P('pipe', None, 'mp')
- squeeze_grad: bfloat16 [2, 8, 7168, 64], P('dp', 'pipe', 'mp')
- expand_grad: bfloat16 [2, 8, 64, 7168], P('dp', 'pipe', None, 'mp')
- forward_carry: bfloat16 [2, 8, 16, 7168], P('dp', 'pipe', None, 'mp')
- backward_carry: bfloat16 [2, 8, 16, 7168], P('dp', 'pipe', None, 'mp')
All inputs are finite; a program needn't handle non-finite values.
Results may differ from a plain program's by a relative error of at most 0.009.
Values may be sent and summed in bfloat16 or wider, within the bound.
No kernel may reach another device: no remote copies, remote signals or barrier semaphores. Data moves between devices by JAX's collectives and lax.ppermute only.
A program may use at most 64 MiB of HBM per device.

v0:
```python
import math

import jax
import jax.numpy as jnp
from jax import lax
from jax.sharding import PartitionSpec as P

D = 7168
RANK = 64


BRANCH_SCALE = 0.25
STEP_RATE = 0.5


def passed_along(block, axis, distance):
    devices = range(lax.axis_size(axis))
    route = [(i - distance, i) for i in devices if i - distance in devices]
    return lax.ppermute(block, axis, route)


def activate(values):
    return jax.nn.gelu(values, approximate=True)


def shards(
    activations,
    cotangent,
    squeeze_old,
    expand_old,
    squeeze_late,
    expand_late,
    stash_inputs,
    forward_in,
    backward_in,
):
    sections = lax.axis_size("pipe")
    section_index = lax.axis_index("pipe")
    replicas = lax.axis_size("dp")
    squeeze = squeeze_old[0]
    expand = expand_old[0]
    ticks = stash_inputs.shape[2]
    rows = stash_inputs.shape[3]
    inv_width = 1.0 / math.sqrt(D)
    inv_rank = BRANCH_SCALE / math.sqrt(RANK)
    total_squeeze, total_expand = (
        lax.psum(squeeze_late[0, 0].astype(jnp.float32).astype(jnp.bfloat16), "dp").astype(
            jnp.float32
        ),
        lax.psum(expand_late[0, 0].astype(jnp.float32).astype(jnp.bfloat16), "dp").astype(
            jnp.float32
        ),
    )
    squeeze_new = (squeeze.astype(jnp.float32) - STEP_RATE * total_squeeze / replicas).astype(
        jnp.bfloat16
    )
    expand_new = (expand.astype(jnp.float32) - STEP_RATE * total_expand / replicas).astype(
        jnp.bfloat16
    )
    feed_all, target_all = (
        lax.all_gather(activations, "pipe", axis=1, tiled=True),
        lax.all_gather(cotangent, "pipe", axis=1, tiled=True),
    )
    feed_rows = feed_all[0]
    target_rows = target_all[0]
    stash = stash_inputs[0, 0]
    is_first = section_index == 0
    is_last = section_index == sections - 1
    lag = 2 * sections - 1 - 2 * section_index
    incoming_fwd = forward_in[0, 0]
    incoming_bwd = backward_in[0, 0]
    squeeze_sum = jnp.zeros(squeeze.shape, jnp.float32)
    expand_sum = jnp.zeros(expand.shape, jnp.float32)
    history = []
    layer_out = incoming_fwd
    downstream = incoming_bwd
    for tick in range(ticks):
        fed = feed_rows[tick * rows : (tick + 1) * rows]
        target = target_rows[tick * rows : (tick + 1) * rows]
        layer_in = jnp.where(is_first, fed, incoming_fwd)
        upstream = jnp.where(is_last, target, incoming_bwd)
        history.append(layer_in)
        stacked = jnp.stack(history)
        back = tick - lag
        picked = lax.dynamic_index_in_dim(stacked, jnp.clip(back, 0, tick), 0, keepdims=False)
        saved = jnp.where(back >= 0, picked, stash[tick])
        forward_partial = jnp.dot(layer_in, squeeze, preferred_element_type=jnp.float32)
        again_partial = jnp.dot(saved, squeeze, preferred_element_type=jnp.float32)
        grad_partial = lax.dot_general(
            upstream, expand, (((1,), (1,)), ((), ())), preferred_element_type=jnp.float32
        )
        hidden_total = lax.psum(forward_partial, "mp")
        again_total, grad_total = lax.psum((again_partial, grad_partial), "mp")
        hidden = hidden_total * inv_width
        gated = activate(hidden).astype(jnp.bfloat16)
        layer_out = (
            layer_in.astype(jnp.float32)
            + jnp.dot(gated, expand, preferred_element_type=jnp.float32) * inv_rank
        ).astype(jnp.bfloat16)
        again = again_total * inv_width
        gate_grad = grad_total * inv_rank
        regated, pullback = jax.vjp(activate, again)
        hidden_grad = pullback(gate_grad)[0].astype(jnp.bfloat16)
        regated = regated.astype(jnp.bfloat16)
        downstream = (
            upstream.astype(jnp.float32)
            + lax.dot_general(
                hidden_grad, squeeze, (((1,), (1,)), ((), ())), preferred_element_type=jnp.float32
            )
            * inv_width
        ).astype(jnp.bfloat16)
        squeeze_sum = (
            squeeze_sum
            + lax.dot_general(
                saved, hidden_grad, (((0,), (0,)), ((), ())), preferred_element_type=jnp.float32
            )
            * inv_width
        )
        expand_sum = (
            expand_sum
            + lax.dot_general(
                regated, upstream, (((0,), (0,)), ((), ())), preferred_element_type=jnp.float32
            )
            * inv_rank
        )
        if tick + 1 < ticks:
            incoming_fwd = passed_along(layer_out, "pipe", 1)
            incoming_bwd = passed_along(downstream, "pipe", -1)
    return (
        squeeze_new[None],
        expand_new[None],
        squeeze_sum.astype(jnp.bfloat16)[None, None],
        expand_sum.astype(jnp.bfloat16)[None, None],
        layer_out[None, None],
        downstream[None, None],
    )


def solution(mesh):
    placed = (
        P("dp", "pipe", "mp"),
        P("dp", "pipe", "mp"),
        P("pipe", "mp", None),
        P("pipe", None, "mp"),
        P("dp", "pipe", "mp", None),
        P("dp", "pipe", None, "mp"),
        P("dp", "pipe", None, None, "mp"),
        P("dp", "pipe", None, "mp"),
        P("dp", "pipe", None, "mp"),
    )
    return jax.shard_map(
        shards,
        mesh=mesh,
        in_specs=placed,
        out_specs=(
            P("pipe", "mp", None),
            P("pipe", None, "mp"),
            P("dp", "pipe", "mp", None),
            P("dp", "pipe", None, "mp"),
            P("dp", "pipe", None, "mp"),
            P("dp", "pipe", None, "mp"),
        ),
        check_vma=False,
    )
```

profile of v0, /device:TPU:25, one launch (start us, length us, event | category | flops | bytes accessed | tf_op | source)
XLA Modules:
  0.0 239.8 jit_solution(3805880507688496803)
XLA Ops:
  7.2 24.8 %all_gather.6 = bf16[1,128,3584]{2,1,0:T(8,128)(2,1)S(1)} all-gather(bf16[1,16,3584]{2,1,0:T(8,128)(2,1)} %param.9), channel_id=1, replica_groups=mesh['pipe'=8,'dp'=2,'mp'=2] {'pipe'}, dimensions={1}, use_global_device_ids=true | all-gather | bytes 1032192 | tf_op jit(solution)/shard_map/all_gather | solution.py:61
  32.1 28.5 %all_gather.7 = bf16[1,128,3584]{2,1,0:T(8,128)(2,1)S(1)} all-gather(bf16[1,16,3584]{2,1,0:T(8,128)(2,1)S(1)} %copy-done.17), channel_id=1, replica_groups=mesh['pipe'=8,'dp'=2,'mp'=2] {'pipe'}, dimensions={1}, use_global_device_ids=true | all-gather | bytes 1032192 | tf_op jit(solution)/shard_map/all_gather | solution.py:62
  61.9 1.2 fusion.79
  63.3 13.2 %all-reduce.7 = (f32[16,64]{1,0:T(8,128)S(1)}, f32[16,64]{1,0:T(8,128)S(1)}, f32[16,64]{1,0:T(8,128)S(1)}) all-reduce(f32[16,64]{1,0:T(8,128)S(1)} %fusion.39, f32[16,64]{1,0:T(8,128)S(1)} %fusion.79, f32[16,64]{1,0:T(8,128)S(1)} %fusion.77), channel_id=1, replica_groups=mesh['pipe'=8,'dp'=2,'mp'=2] {'mp'}, use_global_device_ids=true, to_apply=%region_2.3 | all-reduce | flops 3072 | bytes 24576 | tf_op jit(solution)/shard_map/psum | solution.py:93
  76.8 6.1 %collective-permute-start = (bf16[16,3584]{1,0:T(8,128)(2,1)S(1)}, bf16[16,3584]{1,0:T(8,128)(2,1)S(1)}, u32[]{:S(2)}, u32[]{:S(2)}) collective-permute-start(bf16[16,3584]{1,0:T(8,128)(2,1)S(1)} %fusion.13), channel_id=1, source_target_pairs={{0,4},{4,8},{8,12},{12,16},{16,20},{20,24},{24,28},{1,5},{5,9},{9,... | collective-permute-start | bytes 344072 | tf_op jit(solution)/shard_map/ppermute | solution.py:19
  83.1 1.9 collective-permute-start.1
  85.1 2.2 fusion.123
  87.3 1.3 fusion.196
  91.6 4.6 %all-reduce.6 = (f32[16,64]{1,0:T(8,128)S(1)}, f32[16,64]{1,0:T(8,128)S(1)}, f32[16,64]{1,0:T(8,128)S(1)}) all-reduce(f32[16,64]{1,0:T(8,128)S(1)} %fusion.36, f32[16,64]{1,0:T(8,128)S(1)} %fusion.74, f32[16,64]{1,0:T(8,128)S(1)} %fusion.72), channel_id=1, replica_groups=mesh['pipe'=8,'dp'=2,'mp'=2] {'mp'}, use_global_device_ids=true, to_apply=%region_5.6 | all-reduce | flops 3072 | bytes 24576 | tf_op jit(solution)/shard_map/psum | solution.py:93
  96.4 2.6 %convolution_add_fusion.8 = f32[3584,64]{0,1:T(8,128)} fusion(f32[3584,64]{0,1:T(8,128)} %fusion.123, pred[]{:T(512)S(6)} %ge.25, bf16[1,1,8,16,3584]{4,3,2,1,0:T(8,128)(2,1)} %param.15, s32[]{:T(128)S(6)} %min.23, bf16[1,16,3584]{2,1,0:T(8,128)(2,1)S(1)} %get-tuple-element.47, bf16[1,16,3584]{2,1,0:T(8,128)(2,1)S(1)} %bitcast.408, ...), kind=kOutput, calls=%fused_computation.10 | convolution fusion | flops 7706624 | bytes 2187269 | tf_op jit(solution)/shard_map/dot_general | solution.py:114
  99.2 2.1 collective-permute-start.2
  101.2 4.1 %collective-permute-start.3 = (bf16[16,3584]{1,0:T(8,128)(2,1)S(1)}, bf16[16,3584]{1,0:T(8,128)(2,1)S(1)}, u32[]{:S(2)}, u32[]{:S(2)}) collective-permute-start(bf16[16,3584]{1,0:T(8,128)(2,1)S(1)} %add_convert_fusion.12), channel_id=1, source_target_pairs={{4,0},{8,4},{12,8},{16,12},{20,16},{24,20},{28,24},{5,1},{9,5},{13... | collective-permute-start | bytes 344072 | tf_op jit(solution)/shard_map/ppermute | solution.py:19
  105.4 1.3 convolution_add_fusion.1
  106.6 2.9 %collective-permute-done.3 = bf16[16,3584]{1,0:T(8,128)(2,1)S(1)} collective-permute-done((bf16[16,3584]{1,0:T(8,128)(2,1)S(1)}, bf16[16,3584]{1,0:T(8,128)(2,1)S(1)}, u32[]{:S(2)}, u32[]{:S(2)}) %collective-permute-start.3) | collective-permute-done | bytes 114720 | tf_op jit(solution)/shard_map/ppermute | solution.py:19
  111.8 3.8 %all-reduce.5 = (f32[16,64]{1,0:T(8,128)S(1)}, f32[16,64]{1,0:T(8,128)S(1)}, f32[16,64]{1,0:T(8,128)S(1)}) all-reduce(f32[16,64]{1,0:T(8,128)S(1)} %fusion.33, f32[16,64]{1,0:T(8,128)S(1)} %fusion.69, f32[16,64]{1,0:T(8,128)S(1)} %fusion.67), channel_id=1, replica_groups=mesh['pipe'=8,'dp'=2,'mp'=2] {'mp'}, use_global_device_ids=true, to_apply=%region_8.9 | all-reduce | flops 3072 | bytes 24576 | tf_op jit(solution)/shard_map/psum | solution.py:93
  116.2 2.5 %convolution_add_fusion.7 = f32[3584,64]{0,1:T(8,128)} fusion(f32[3584,64]{0,1:T(8,128)} %convolution_add_fusion.8, bf16[1,16,3584]{2,1,0:T(8,128)(2,1)S(1)} %fusion.85, pred[]{:T(512)S(6)} %ge.26, bf16[1,1,8,16,3584]{4,3,2,1,0:T(8,128)(2,1)} %param.15, f32[16,64]{1,0:T(8,128)S(1)} %get-tuple-element.21, f32[16,64]{1,0:T(8,128)S(1)} %get-tuple-element.22), kind=kOutput, calls=%fused_computation.9 | convolution fusion | flops 7649280 | bytes 2072577 | tf_op jit(solution)/shard_map/dot_general | solution.py:114
  118.7 3.7 %collective-permute-start.5 = (bf16[16,3584]{1,0:T(8,128)(2,1)S(1)}, bf16[16,3584]{1,0:T(8,128)(2,1)S(1)}, u32[]{:S(2)}, u32[]{:S(2)}) collective-permute-start(bf16[16,3584]{1,0:T(8,128)(2,1)S(1)} %add_convert_fusion.10), channel_id=1, source_target_pairs={{4,0},{8,4},{12,8},{16,12},{20,16},{24,20},{28,24},{5,1},{9,5},{13... | collective-permute-start | bytes 344072 | tf_op jit(solution)/shard_map/ppermute | solution.py:19
  122.7 1.9 collective-permute-start.4
  126.1 3.6 %collective-permute-done.4 = bf16[16,3584]{1,0:T(8,128)(2,1)S(1)} collective-permute-done((bf16[16,3584]{1,0:T(8,128)(2,1)S(1)}, bf16[16,3584]{1,0:T(8,128)(2,1)S(1)}, u32[]{:S(2)}, u32[]{:S(2)}) %collective-permute-start.4) | collective-permute-done | bytes 114720 | tf_op jit(solution)/shard_map/ppermute | solution.py:19
  133.1 4.6 %all-reduce.4 = (f32[16,64]{1,0:T(8,128)S(1)}, f32[16,64]{1,0:T(8,128)S(1)}, f32[16,64]{1,0:T(8,128)S(1)}) all-reduce(f32[16,64]{1,0:T(8,128)S(1)} %copy-done.23, f32[16,64]{1,0:T(8,128)S(1)} %fusion.64, f32[16,64]{1,0:T(8,128)S(1)} %copy-done.24), channel_id=1, replica_groups=mesh['pipe'=8,'dp'=2,'mp'=2] {'mp'}, use_global_device_ids=true, to_apply=%region_11.12 | all-reduce | flops 3072 | bytes 24576 | tf_op jit(solution)/shard_map/psum | solution.py:93
  137.7 1.2 fusion.317
  139.1 2.2 convolution_add_fusion.6
  141.5 1.9 collective-permute-start.6
  143.4 4.3 %collective-permute-start.7 = (bf16[16,3584]{1,0:T(8,128)(2,1)S(1)}, bf16[16,3584]{1,0:T(8,128)(2,1)S(1)}, u32[]{:S(2)}, u32[]{:S(2)}) collective-permute-start(bf16[16,3584]{1,0:T(8,128)(2,1)S(1)} %add_convert_fusion.8), channel_id=1, source_target_pairs={{4,0},{8,4},{12,8},{16,12},{20,16},{24,20},{28,24},{5,1},{9,5},{13... | collective-permute-start | bytes 344072 | tf_op jit(solution)/shard_map/ppermute | solution.py:19
  149.9 2.0 collective-permute-done.7
  155.7 3.7 %all-reduce.3 = (f32[16,64]{1,0:T(8,128)S(1)}, f32[16,64]{1,0:T(8,128)S(1)}, f32[16,64]{1,0:T(8,128)S(1)}) all-reduce(f32[16,64]{1,0:T(8,128)S(1)} %fusion.27, f32[16,64]{1,0:T(8,128)S(1)} %fusion.59, f32[16,64]{1,0:T(8,128)S(1)} %fusion.57), channel_id=1, replica_groups=mesh['pipe'=8,'dp'=2,'mp'=2] {'mp'}, use_global_device_ids=true, to_apply=%region_14.15 | all-reduce | flops 3072 | bytes 24576 | tf_op jit(solution)/shard_map/psum | solution.py:93
  159.5 1.2 fusion.318
  160.9 2.2 convolution_add_fusion.5
  163.2 3.7 %collective-permute-start.9 = (bf16[16,3584]{1,0:T(8,128)(2,1)S(1)}, bf16[16,3584]{1,0:T(8,128)(2,1)S(1)}, u32[]{:S(2)}, u32[]{:S(2)}) collective-permute-start(bf16[16,3584]{1,0:T(8,128)(2,1)S(1)} %add_convert_fusion.6), channel_id=1, source_target_pairs={{4,0},{8,4},{12,8},{16,12},{20,16},{24,20},{28,24},{5,1},{9,5},{13... | collective-permute-start | bytes 344072 | tf_op jit(solution)/shard_map/ppermute | solution.py:19
  167.1 1.9 collective-permute-start.8
  169.9 4.3 %collective-permute-done.8 = bf16[16,3584]{1,0:T(8,128)(2,1)S(1)} collective-permute-done((bf16[16,3584]{1,0:T(8,128)(2,1)S(1)}, bf16[16,3584]{1,0:T(8,128)(2,1)S(1)}, u32[]{:S(2)}, u32[]{:S(2)}) %collective-permute-start.8) | collective-permute-done | bytes 114720 | tf_op jit(solution)/shard_map/ppermute | solution.py:19
  176.9 4.6 %all-reduce.2 = (f32[16,64]{1,0:T(8,128)S(1)}, f32[16,64]{1,0:T(8,128)S(1)}, f32[16,64]{1,0:T(8,128)S(1)}) all-reduce(f32[16,64]{1,0:T(8,128)S(1)} %fusion.24, f32[16,64]{1,0:T(8,128)S(1)} %fusion.54, f32[16,64]{1,0:T(8,128)S(1)} %fusion.52), channel_id=1, replica_groups=mesh['pipe'=8,'dp'=2,'mp'=2] {'mp'}, use_global_device_ids=true, to_apply=%region_17.18 | all-reduce | flops 3072 | bytes 24576 | tf_op jit(solution)/shard_map/psum | solution.py:93
  181.7 2.1 collective-permute-start.10
  183.8 1.3 fusion.319
  185.0 2.2 convolution_add_fusion.4
  187.5 4.3 %collective-permute-start.11 = (bf16[16,3584]{1,0:T(8,128)(2,1)S(1)}, bf16[16,3584]{1,0:T(8,128)(2,1)S(1)}, u32[]{:S(2)}, u32[]{:S(2)}) collective-permute-start(bf16[16,3584]{1,0:T(8,128)(2,1)S(1)} %add_convert_fusion.4), channel_id=1, source_target_pairs={{4,0},{8,4},{12,8},{16,12},{20,16},{24,20},{28,24},{5,1},{9,5},{13... | collective-permute-start | bytes 344072 | tf_op jit(solution)/shard_map/ppermute | solution.py:19
  194.2 1.2 fusion.49
  195.4 4.4 %all-reduce.1 = (f32[16,64]{1,0:T(8,128)S(1)}, f32[16,64]{1,0:T(8,128)S(1)}, f32[16,64]{1,0:T(8,128)S(1)}) all-reduce(f32[16,64]{1,0:T(8,128)S(1)} %fusion.21, f32[16,64]{1,0:T(8,128)S(1)} %fusion.49, f32[16,64]{1,0:T(8,128)S(1)} %fusion.47), channel_id=1, replica_groups=mesh['pipe'=8,'dp'=2,'mp'=2] {'mp'}, use_global_device_ids=true, to_apply=%region_20.21 | all-reduce | flops 3072 | bytes 24576 | tf_op jit(solution)/shard_map/psum | solution.py:93
  199.8 1.2 fusion.320
  201.3 2.2 convolution_add_fusion.3
  203.5 5.0 %collective-permute-start.13 = (bf16[16,3584]{1,0:T(8,128)(2,1)S(1)}, bf16[16,3584]{1,0:T(8,128)(2,1)S(1)}, u32[]{:S(2)}, u32[]{:S(2)}) collective-permute-start(bf16[16,3584]{1,0:T(8,128)(2,1)S(1)} %add_convert_fusion.2), channel_id=1, source_target_pairs={{4,0},{8,4},{12,8},{16,12},{20,16},{24,20},{28,24},{5,1},{9,5},{13... | collective-permute-start | bytes 344072 | tf_op jit(solution)/shard_map/ppermute | solution.py:19
  208.7 1.9 collective-permute-start.12
  211.1 4.7 %collective-permute-done.12 = bf16[16,3584]{1,0:T(8,128)(2,1)S(1)} collective-permute-done((bf16[16,3584]{1,0:T(8,128)(2,1)S(1)}, bf16[16,3584]{1,0:T(8,128)(2,1)S(1)}, u32[]{:S(2)}, u32[]{:S(2)}) %collective-permute-start.12) | collective-permute-done | bytes 114720 | tf_op jit(solution)/shard_map/ppermute | solution.py:19
  216.7 1.3 fusion.44
  217.9 4.6 %all-reduce = (f32[16,64]{1,0:T(8,128)S(1)}, f32[16,64]{1,0:T(8,128)S(1)}, f32[16,64]{1,0:T(8,128)S(1)}) all-reduce(f32[16,64]{1,0:T(8,128)S(1)} %fusion.18, f32[16,64]{1,0:T(8,128)S(1)} %fusion.44, f32[16,64]{1,0:T(8,128)S(1)} %fusion.42), channel_id=1, replica_groups=mesh['pipe'=8,'dp'=2,'mp'=2] {'mp'}, use_global_device_ids=true, to_apply=%region_23.24 | all-reduce | flops 3072 | bytes 24576 | tf_op jit(solution)/shard_map/psum | solution.py:93
  224.2 2.1 fusion.10
  227.5 2.5 %fusion.9 = bf16[1,1,64,3584]{3,2,1,0:T(8,128)(2,1)} fusion(f32[64,3584]{1,0:T(8,128)S(1)} %fusion.321, f32[64,3584]{1,0:T(8,128)} %fusion.320, f32[64,3584]{1,0:T(8,128)S(1)} %copy-done.11, f32[64,3584]{1,0:T(8,128)S(1)} %copy-done.10, f32[64,3584]{1,0:T(8,128)S(1)} %copy-done.9, f32[64,3584]{1,0:T(8,128)S(1)} %copy-done.8, ...), kind=kOutput, calls=%fused_computation.18 | convolution fusion | flops 9185280 | bytes 6082560 | tf_op jit(solution)/shard_map/dot_general | solution.py:121
  230.0 2.0 fusion.15
  (124 shorter events, 32.1 us)
Async XLA Ops:
  7.2 222.9 %all-reduce.11.cloned.1.call-start = ((), (), s32[]{:S(2)}) async-start(), calls=%async_computation | async-start | bytes 1835008 | tf_op jit(solution)/shard_map/psum | solution.py:47
  7.2 24.8 %copy-start.17 = (bf16[1,16,3584]{2,1,0:T(8,128)(2,1)S(1)}, bf16[1,16,3584]{2,1,0:T(8,128)(2,1)}, u32[]{:S(2)}) copy-start(bf16[1,16,3584]{2,1,0:T(8,128)(2,1)} %param.10) | copy-start | bytes 344068
  32.1 28.5 %copy-start.12 = (bf16[1,1,16,3584]{3,2,1,0:T(8,128)(2,1)S(1)}, bf16[1,1,16,3584]{3,2,1,0:T(8,128)(2,1)}, u32[]{:S(2)}) copy-start(bf16[1,1,16,3584]{3,2,1,0:T(8,128)(2,1)} %param.16) | copy-start | bytes 344068
  60.6 1.1 copy-start
  61.9 1.2 copy-start.1
  61.9 1.2 copy-start.13
  76.6 6.4 %copy-start.20 = (f32[16,64]{1,0:T(8,128)}, f32[16,64]{1,0:T(8,128)S(1)}, u32[]{:S(2)}) copy-start(f32[16,64]{1,0:T(8,128)S(1)} %get-tuple-element.28) | copy-start | bytes 12292
  76.6 6.4 %copy-start.22 = (f32[16,64]{1,0:T(8,128)}, f32[16,64]{1,0:T(8,128)S(1)}, u32[]{:S(2)}) copy-start(f32[16,64]{1,0:T(8,128)S(1)} %get-tuple-element.27) | copy-start | bytes 12292
  76.8 12.8 %collective-permute-start = (bf16[16,3584]{1,0:T(8,128)(2,1)S(1)}, bf16[16,3584]{1,0:T(8,128)(2,1)S(1)}, u32[]{:S(2)}, u32[]{:S(2)}) collective-permute-start(bf16[16,3584]{1,0:T(8,128)(2,1)S(1)} %fusion.13), channel_id=1, source_target_pairs={{0,4},{4,8},{8,12},{12,16},{16,20},{20,24},{24,28},{1,5},{5,9},{9,... | collective-permute-start | bytes 344072 | tf_op jit(solution)/shard_map/ppermute | solution.py:19
  83.1 6.2 %collective-permute-start.1 = (bf16[16,3584]{1,0:T(8,128)(2,1)S(1)}, bf16[16,3584]{1,0:T(8,128)(2,1)S(1)}, u32[]{:S(2)}, u32[]{:S(2)}) collective-permute-start(bf16[16,3584]{1,0:T(8,128)(2,1)S(1)} %fusion.14), channel_id=1, source_target_pairs={{4,0},{8,4},{12,8},{16,12},{20,16},{24,20},{28,24},{5,1},{9,5},{13... | collective-permute-start | bytes 344072 | tf_op jit(solution)/shard_map/ppermute | solution.py:19
  85.1 2.2 copy-start.21
  96.3 9.0 %copy-start.4 = (f32[64,3584]{1,0:T(8,128)S(1)}, f32[64,3584]{1,0:T(8,128)}, u32[]{:S(2)}) copy-start(f32[64,3584]{1,0:T(8,128)} %fusion.196) | copy-start | bytes 2752516
  99.2 10.6 %collective-permute-start.2 = (bf16[16,3584]{1,0:T(8,128)(2,1)S(1)}, bf16[16,3584]{1,0:T(8,128)(2,1)S(1)}, u32[]{:S(2)}, u32[]{:S(2)}) collective-permute-start(bf16[16,3584]{1,0:T(8,128)(2,1)S(1)} %add_convert_fusion.13), channel_id=1, source_target_pairs={{0,4},{4,8},{8,12},{12,16},{16,20},{20,24},{24,28},{1,5},{5,9},{9,... | collective-permute-start | bytes 344072 | tf_op jit(solution)/shard_map/ppermute | solution.py:19
  101.2 8.3 %collective-permute-start.3 = (bf16[16,3584]{1,0:T(8,128)(2,1)S(1)}, bf16[16,3584]{1,0:T(8,128)(2,1)S(1)}, u32[]{:S(2)}, u32[]{:S(2)}) collective-permute-start(bf16[16,3584]{1,0:T(8,128)(2,1)S(1)} %add_convert_fusion.12), channel_id=1, source_target_pairs={{4,0},{8,4},{12,8},{16,12},{20,16},{24,20},{28,24},{5,1},{9,5},{13... | collective-permute-start | bytes 344072 | tf_op jit(solution)/shard_map/ppermute | solution.py:19
  115.6 0.6 copy-start.18
  118.7 6.5 %collective-permute-start.5 = (bf16[16,3584]{1,0:T(8,128)(2,1)S(1)}, bf16[16,3584]{1,0:T(8,128)(2,1)S(1)}, u32[]{:S(2)}, u32[]{:S(2)}) collective-permute-start(bf16[16,3584]{1,0:T(8,128)(2,1)S(1)} %add_convert_fusion.10), channel_id=1, source_target_pairs={{4,0},{8,4},{12,8},{16,12},{20,16},{24,20},{28,24},{5,1},{9,5},{13... | collective-permute-start | bytes 344072 | tf_op jit(solution)/shard_map/ppermute | solution.py:19
  122.7 7.1 %collective-permute-start.4 = (bf16[16,3584]{1,0:T(8,128)(2,1)S(1)}, bf16[16,3584]{1,0:T(8,128)(2,1)S(1)}, u32[]{:S(2)}, u32[]{:S(2)}) collective-permute-start(bf16[16,3584]{1,0:T(8,128)(2,1)S(1)} %add_convert_fusion.11), channel_id=1, source_target_pairs={{0,4},{4,8},{8,12},{12,16},{16,20},{20,24},{24,28},{1,5},{5,9},{9,... | collective-permute-start | bytes 344072 | tf_op jit(solution)/shard_map/ppermute | solution.py:19
  132.0 1.1 copy-start.23
  132.0 1.1 copy-start.24
  137.7 1.5 copy-start.2
  141.3 6.4 %copy-start.15 = (bf16[5,16,3584]{2,1,0:T(8,128)(2,1)S(1)}, bf16[5,16,3584]{2,1,0:T(8,128)(2,1)}, u32[]{:S(2)}) copy-start(bf16[5,16,3584]{2,1,0:T(8,128)(2,1)} %get-tuple-element.64) | copy-start | bytes 1720324
  141.5 10.6 %collective-permute-start.6 = (bf16[16,3584]{1,0:T(8,128)(2,1)S(1)}, bf16[16,3584]{1,0:T(8,128)(2,1)S(1)}, u32[]{:S(2)}, u32[]{:S(2)}) collective-permute-start(bf16[16,3584]{1,0:T(8,128)(2,1)S(1)} %add_convert_fusion.9), channel_id=1, source_target_pairs={{0,4},{4,8},{8,12},{12,16},{16,20},{20,24},{24,28},{1,5},{5,9},{9,... | collective-permute-start | bytes 344072 | tf_op jit(solution)/shard_map/ppermute | solution.py:19
  143.4 8.4 %collective-permute-start.7 = (bf16[16,3584]{1,0:T(8,128)(2,1)S(1)}, bf16[16,3584]{1,0:T(8,128)(2,1)S(1)}, u32[]{:S(2)}, u32[]{:S(2)}) collective-permute-start(bf16[16,3584]{1,0:T(8,128)(2,1)S(1)} %add_convert_fusion.8), channel_id=1, source_target_pairs={{4,0},{8,4},{12,8},{16,12},{20,16},{24,20},{28,24},{5,1},{9,5},{13... | collective-permute-start | bytes 344072 | tf_op jit(solution)/shard_map/ppermute | solution.py:19
  153.8 0.8 copy-start.16
  159.5 1.5 copy-start.3
  163.2 6.5 %collective-permute-start.9 = (bf16[16,3584]{1,0:T(8,128)(2,1)S(1)}, bf16[16,3584]{1,0:T(8,128)(2,1)S(1)}, u32[]{:S(2)}, u32[]{:S(2)}) collective-permute-start(bf16[16,3584]{1,0:T(8,128)(2,1)S(1)} %add_convert_fusion.6), channel_id=1, source_target_pairs={{4,0},{8,4},{12,8},{16,12},{20,16},{24,20},{28,24},{5,1},{9,5},{13... | collective-permute-start | bytes 344072 | tf_op jit(solution)/shard_map/ppermute | solution.py:19
  167.1 7.1 %collective-permute-start.8 = (bf16[16,3584]{1,0:T(8,128)(2,1)S(1)}, bf16[16,3584]{1,0:T(8,128)(2,1)S(1)}, u32[]{:S(2)}, u32[]{:S(2)}) collective-permute-start(bf16[16,3584]{1,0:T(8,128)(2,1)S(1)} %add_convert_fusion.7), channel_id=1, source_target_pairs={{0,4},{4,8},{8,12},{12,16},{16,20},{20,24},{24,28},{1,5},{5,9},{9,... | collective-permute-start | bytes 344072 | tf_op jit(solution)/shard_map/ppermute | solution.py:19
  181.5 3.5 %copy-start.5 = (f32[3584,64]{0,1:T(8,128)S(1)}, f32[3584,64]{0,1:T(8,128)}, u32[]{:S(2)}) copy-start(f32[3584,64]{0,1:T(8,128)} %convolution_add_fusion.5) | copy-start | bytes 2752516
  181.7 10.0 %collective-permute-start.10 = (bf16[16,3584]{1,0:T(8,128)(2,1)S(1)}, bf16[16,3584]{1,0:T(8,128)(2,1)S(1)}, u32[]{:S(2)}, u32[]{:S(2)}) collective-permute-start(bf16[16,3584]{1,0:T(8,128)(2,1)S(1)} %add_convert_fusion.5), channel_id=1, source_target_pairs={{0,4},{4,8},{8,12},{12,16},{16,20},{20,24},{24,28},{1,5},{5,9},{9,... | collective-permute-start | bytes 344072 | tf_op jit(solution)/shard_map/ppermute | solution.py:19
  187.5 6.5 %collective-permute-start.11 = (bf16[16,3584]{1,0:T(8,128)(2,1)S(1)}, bf16[16,3584]{1,0:T(8,128)(2,1)S(1)}, u32[]{:S(2)}, u32[]{:S(2)}) collective-permute-start(bf16[16,3584]{1,0:T(8,128)(2,1)S(1)} %add_convert_fusion.4), channel_id=1, source_target_pairs={{4,0},{8,4},{12,8},{16,12},{20,16},{24,20},{28,24},{5,1},{9,5},{13... | collective-permute-start | bytes 344072 | tf_op jit(solution)/shard_map/ppermute | solution.py:19
  199.8 1.5 copy-start.7
  203.5 7.4 %collective-permute-start.13 = (bf16[16,3584]{1,0:T(8,128)(2,1)S(1)}, bf16[16,3584]{1,0:T(8,128)(2,1)S(1)}, u32[]{:S(2)}, u32[]{:S(2)}) collective-permute-start(bf16[16,3584]{1,0:T(8,128)(2,1)S(1)} %add_convert_fusion.2), channel_id=1, source_target_pairs={{4,0},{8,4},{12,8},{16,12},{20,16},{24,20},{28,24},{5,1},{9,5},{13... | collective-permute-start | bytes 344072 | tf_op jit(solution)/shard_map/ppermute | solution.py:19
  208.7 7.1 %collective-permute-start.12 = (bf16[16,3584]{1,0:T(8,128)(2,1)S(1)}, bf16[16,3584]{1,0:T(8,128)(2,1)S(1)}, u32[]{:S(2)}, u32[]{:S(2)}) collective-permute-start(bf16[16,3584]{1,0:T(8,128)(2,1)S(1)} %add_convert_fusion.3), channel_id=1, source_target_pairs={{0,4},{4,8},{8,12},{12,16},{16,20},{20,24},{24,28},{1,5},{5,9},{9,... | collective-permute-start | bytes 344072 | tf_op jit(solution)/shard_map/ppermute | solution.py:19
  216.7 7.5 %copy-start.6 = (f32[3584,64]{0,1:T(8,128)S(1)}, f32[3584,64]{0,1:T(8,128)}, u32[]{:S(2)}) copy-start(f32[3584,64]{0,1:T(8,128)} %convolution_add_fusion.3) | copy-start | bytes 2752516
  222.5 4.2 %copy-start.11 = (f32[64,3584]{1,0:T(8,128)S(1)}, f32[64,3584]{1,0:T(8,128)}, u32[]{:S(2)}) copy-start(f32[64,3584]{1,0:T(8,128)} %fusion.319) | copy-start | bytes 2752516
  223.3 3.3 %copy-start.10 = (f32[64,3584]{1,0:T(8,128)S(1)}, f32[64,3584]{1,0:T(8,128)}, u32[]{:S(2)}) copy-start(f32[64,3584]{1,0:T(8,128)} %fusion.318) | copy-start | bytes 2752516
  224.2 2.5 %copy-start.9 = (f32[64,3584]{1,0:T(8,128)S(1)}, f32[64,3584]{1,0:T(8,128)}, u32[]{:S(2)}) copy-start(f32[64,3584]{1,0:T(8,128)} %fusion.317) | copy-start | bytes 2752516
  226.3 1.2 copy-start.8
  226.3 1.2 copy-start.19
  230.0 2.0 copy-start.14
Sparse Core Ops, SparseCore 0:
  85.2 38.6 all-reduce.10
where the time goes:
time: 241 us; the launch traced here: 240 us
  blocking collectives  96.7 us (40%)
  matrix products  47.1 us (20%)
  starting transfers between devices  45 us (19%)
  waiting for transfers between devices  20.4 us (8%)
  between operations  14.5 us (6%)
  other arithmetic  9.29 us (4%)
  local copies, waits for them, and re-layouts  6.82 us (3%)
    ppermute x14, starting transfers between devices, passed_along(): return lax.ppermute(block, axis, route)  44.9 us
    psum x8, blocking collectives, shards(): again_total, grad_total = lax.psum((again_partial, grad_partial), 'mp')  43.3 us
    all_gather x1, blocking collectives, shards(): lax.all_gather(cotangent, 'pipe', axis=1, tiled=True)  28.5 us
    all_gather x1, blocking collectives, shards(): lax.all_gather(activations, 'pipe', axis=1, tiled=True)  24.8 us
    ppermute x14, waiting for transfers between devices, passed_along(): return lax.ppermute(block, axis, route)  20.4 us
    dot_general x8, matrix products, shards(): lax.dot_general(saved, hidden_grad, (((0,), (0,)), ((), ())), preferred_e...  18.4 us
    dot_general x8, matrix products, shards(): lax.dot_general(regated, upstream, (((0,), (0,)), ((), ())), preferred_el...  10.3 us
    dot_general x8, matrix products, shards(): again_partial = jnp.dot(saved, squeeze, preferred_element_type=jnp.float32)  9.33 us
  transfers between devices with their start and end apart: 15, of which 10 were waited for; matrix products, arithmetic and copies ran while one was open for 23% of the time, Pallas kernels for 0%

commit v1 on v0

v1 whole, which is shorter than its diff:
```python
import functools
import math

import jax
import jax.numpy as jnp
from jax import lax
from jax.experimental import pallas as pl
from jax.experimental.pallas import tpu as pltpu
from jax.sharding import PartitionSpec as P

BRANCH_SCALE = 0.25
STEP_RATE = 0.5
CHUNK = 512

VMEM = pl.BlockSpec(memory_space=pltpu.VMEM)
SMEM = pl.BlockSpec(memory_space=pltpu.SMEM)
ANY = pl.BlockSpec(memory_space=pl.ANY)
NT = (((1,), (1,)), ((), ()))
TN = (((0,), (0,)), ((), ()))


def dot(a, b, dims=(((1,), (0,)), ((), ()))):
    return lax.dot_general(a, b, dims, preferred_element_type=jnp.float32)


def gelu_and_slope(x):
    c = math.sqrt(2.0 / math.pi)
    t = jnp.tanh(c * (x + 0.044715 * (x * x * x)))
    half = 0.5 * (1.0 + t)
    slope = half + 0.5 * x * (1.0 - t * t) * (c * (1.0 + 3 * 0.044715 * (x * x)))
    return x * half, slope


def split_words(x):
    hi = x.astype(jnp.bfloat16)
    lo = (x - hi.astype(jnp.float32)).astype(jnp.bfloat16)
    return jnp.concatenate([hi, lo], axis=1)


def join_words(words):
    rank = words.shape[1] // 2
    return words[:, :rank].astype(jnp.float32) + words[:, rank:].astype(jnp.float32)


def start_kernel(scale, where, stash, squeeze, fwd, bwd, message, partial):
    ticks, rows, half = stash.shape
    rank = squeeze.shape[0]
    forward = where[1] == 0
    message[:, :half] = jnp.where(forward, bwd[...], fwd[...])
    whole = dot(stash[...].reshape(ticks * rows, half), squeeze[...], NT) * scale
    for t in range(ticks):
        own = whole[t * rows : (t + 1) * rows]
        partial[t] = own
        message[:, half + t * 2 * rank : half + (t + 1) * 2 * rank] = split_words(own)


def tick_kernel(tick, ticks, slots, in_scale, out_scale, where, x_in, feed, again_stash, own, other, *rest):
    mine_in, other_in, out, hist_mine, hist_other, keep_mine, keep_other, sems = rest
    del mine_in, other_in
    rows, half = x_in.shape[0], own.shape[2]
    rank = own.shape[1]
    section, role, sections = where[0], where[1], where[2]
    forward = role == 0
    back = sections - 1 - section
    at_end = jnp.where(forward, section, back) == 0
    x0 = jnp.where(at_end, feed[:, :half], x_in[:, :half])
    x1 = jnp.where(at_end, feed[:, half:], x_in[:, half : 2 * half])
    keep_mine[...] = x0
    keep_other[0, :, :half] = x1
    first = pltpu.make_async_copy(keep_mine, hist_mine.at[tick], sems.at[0])
    first.start()
    h = (dot(x0, own[role], NT) + dot(x1, other[role], NT)) * jnp.where(forward, in_scale, out_scale)
    again = again_stash[tick]
    for j in range(slots):
        if 2 * j + 1 <= tick:
            words = x_in[:, 2 * half + j * 2 * rank : 2 * half + (j + 1) * 2 * rank]
            again = jnp.where(back == j, join_words(words), again)
    value, slope = gelu_and_slope(jnp.where(forward, h, again))
    z = jnp.where(forward, value, h * slope).astype(jnp.bfloat16)
    keep_other[0, :, half:] = jnp.concatenate([value.astype(jnp.bfloat16), z], axis=1)
    scale = jnp.where(forward, out_scale, in_scale)
    y0 = (x0.astype(jnp.float32) + dot(z, own[1 - role]) * scale).astype(jnp.bfloat16)
    y1 = (x1.astype(jnp.float32) + dot(z, other[1 - role]) * scale).astype(jnp.bfloat16)
    out[:, :half] = y0
    if tick + 1 < ticks:
        out[:, half : 2 * half] = y1
        words = split_words(h)
        for j in range(slots):
            place = slice(2 * half + j * 2 * rank, 2 * half + (j + 1) * 2 * rank)
            out[:, place] = jnp.where(jnp.logical_and(forward, back == j), words, x_in[:, place])
        second = pltpu.make_async_copy(keep_other, hist_other.at[pl.ds(tick, 1)], sems.at[1])
    else:
        keep_other[1, :, :half] = y1
        keep_other[1, :, half:] = jnp.zeros((rows, 2 * rank), jnp.bfloat16)
        second = pltpu.make_async_copy(keep_other, hist_other.at[pl.ds(tick, 2)], sems.at[1])
    second.start()
    first.wait()
    second.wait()


def end_kernel(in_scale, out_scale, where, mine, sent, got, stash, carry, squeeze_grad, expand_grad, fwd, bwd):
    ticks, rows, half = mine.shape
    rank = squeeze_grad.shape[0]
    section, role, sections = where[0], where[1], where[2]
    forward = role == 0
    lag = 2 * (sections - 1 - section) + 1
    ranks = jnp.concatenate(
        [jnp.where(forward, got[t, :, half:], sent[t, :, half:]) for t in range(ticks)], axis=0
    )
    regated, hidden_grad = ranks[:, :rank], ranks[:, rank:]
    for lo in range(0, half, CHUNK):
        cols = slice(lo, min(lo + CHUNK, half))
        u, g = [], []
        for t in range(ticks):
            g.append(jnp.where(forward, got[t, :, cols], mine[t, :, cols]))
            back = jnp.maximum(t - lag, 0)
            a = jnp.where(forward, mine[back, :, cols], got[back, :, cols])
            u.append(jnp.where(t >= lag, a, stash[t, :, cols]))
        u, g = jnp.concatenate(u, axis=0), jnp.concatenate(g, axis=0)
        squeeze_grad[:, cols] = (dot(hidden_grad, u, TN) * in_scale).astype(jnp.bfloat16)
        expand_grad[:, cols] = (dot(regated, g, TN) * out_scale).astype(jnp.bfloat16)
    fwd[...] = jnp.where(forward, carry[...], got[ticks, :, :half])
    bwd[...] = jnp.where(forward, got[ticks, :, :half], carry[...])


def params(**more):
    return pltpu.CompilerParams(vmem_limit_bytes=24 * 1024 * 1024, **more)


def cost(flops, nbytes):
    return pl.CostEstimate(flops=flops, bytes_accessed=nbytes, transcendentals=0)


def shards(
    activations,
    cotangent,
    squeeze_old,
    expand_old,
    squeeze_late,
    expand_late,
    stash_inputs,
    forward_in,
    backward_in,
):
    sections = lax.axis_size("pipe")
    replicas = lax.axis_size("dp")
    section = lax.axis_index("pipe")
    role = lax.axis_index("mp")
    half = squeeze_old.shape[1]
    rank = squeeze_old.shape[2]
    ticks, rows = stash_inputs.shape[2], stash_inputs.shape[3]
    width = half * lax.axis_size("mp")
    in_scale = 1.0 / math.sqrt(width)
    out_scale = BRANCH_SCALE / math.sqrt(rank)
    slots = ticks // 2
    bf16, f32 = jnp.bfloat16, jnp.float32

    def send(x, pairs):
        return lax.ppermute(x, ("pipe", "mp"), [(a * 2 + b, c * 2 + d) for (a, b), (c, d) in pairs])

    def swap(x):
        return lax.ppermute(x, "mp", [(0, 1), (1, 0)])

    def shape(*dims, dtype=bf16):
        return jax.ShapeDtypeStruct(dims, dtype)

    where = jnp.stack([section, role, jnp.int32(sections)]).astype(jnp.int32)
    forward = role == 0
    squeeze = squeeze_old[0].T
    expand = expand_old[0]
    stash = stash_inputs[0, 0]
    fwd_in, bwd_in = forward_in[0, 0], backward_in[0, 0]
    acts, cots = activations[0], cotangent[0]

    own = jnp.stack([squeeze, expand])
    other = swap(own)
    entering = jnp.where(forward, acts, cots)
    entering_full = jnp.concatenate([entering, swap(jnp.where(forward, cots, acts))], axis=1)

    message, partial = pl.pallas_call(
        functools.partial(start_kernel, in_scale),
        out_shape=(shape(rows, half + ticks * 2 * rank), shape(ticks, rows, rank, dtype=f32)),
        in_specs=[SMEM, VMEM, VMEM, VMEM, VMEM],
        out_specs=(VMEM, VMEM),
        compiler_params=params(),
        cost_estimate=cost(2 * ticks * rows * half * rank, ticks * rows * half * 2),
        name="start",
    )(where, stash, squeeze, fwd_in, bwd_in)
    got = swap(message)
    words = got[:, half:].reshape(rows, ticks, 2 * rank).transpose(1, 0, 2)
    again_stash = partial + words[..., :rank].astype(f32) + words[..., rank:].astype(f32)

    block = acts.shape[0]
    per_tick = rows // block
    last = sections - 1

    def piece(i, tied):
        pairs = [((i, 0), (0, 0))] * (i != 0) + [((i, 1), (last, 1))] * (i != last)
        came = send(tied, pairs)
        return jnp.where(section == i, entering_full, came) if i in (0, last) else came

    def fed(t, after):
        tied = entering_full if after is None else lax.optimization_barrier((entering_full, after))[0]
        return jnp.concatenate([piece(i, tied) for i in range(t * per_tick, (t + 1) * per_tick)], axis=0)

    first_cots = jnp.concatenate(
        [
            jnp.concatenate([send(cots, [((i, 1), (last, 1))]), send(cots, [((i, 0), (last, 1))])], axis=1)
            for i in range(per_tick)
        ],
        axis=0,
    )
    first_acts = [entering_full] + [send(entering_full, [((i, 0), (0, 0))]) for i in range(1, per_tick)]
    first_feed = jnp.where(forward, jnp.concatenate(first_acts, axis=0), first_cots)
    x = jnp.concatenate(
        [jnp.where(forward, fwd_in, bwd_in), got[:, :half], jnp.zeros((rows, slots * 2 * rank), bf16)], axis=1
    )

    ring = (
        [((s, 0), (s + 1, 0)) for s in range(last)]
        + [((last, 0), (last, 1))]
        + [((s, 1), (s - 1, 1)) for s in range(1, sections)]
    )
    hist_mine = jnp.zeros((ticks, rows, half), bf16)
    hist_other = jnp.zeros((ticks + 1, rows, half + 2 * rank), bf16)
    feeds = [first_feed, fed(1, None)]
    for tick in range(ticks):
        final = tick + 1 == ticks
        columns = half if final else x.shape[1]
        out, hist_mine, hist_other = pl.pallas_call(
            functools.partial(tick_kernel, tick, ticks, slots, in_scale, out_scale),
            out_shape=(
                shape(rows, columns),
                shape(*hist_mine.shape),
                shape(*hist_other.shape),
            ),
            in_specs=[SMEM, VMEM, VMEM, VMEM, VMEM, VMEM, ANY, ANY],
            out_specs=(VMEM, ANY, ANY),
            scratch_shapes=[
                pltpu.VMEM((rows, half), bf16),
                pltpu.VMEM((2 if final else 1, rows, half + 2 * rank), bf16),
                pltpu.SemaphoreType.DMA((2,)),
            ],
            input_output_aliases={6: 1, 7: 2},
            compiler_params=params(),
            cost_estimate=cost(4 * rows * width * rank, 4 * width * rank),
            name=f"tick{tick}",
        )(where, x, feeds[tick], again_stash, own, other, hist_mine, hist_other)
        if not final:
            x = send(out, ring)
            if tick + 2 < ticks:
                feeds.append(fed(tick + 2, out))
    came = swap(hist_other)
    squeeze_grad, expand_grad, fwd_carry, bwd_carry = pl.pallas_call(
        functools.partial(end_kernel, in_scale, out_scale),
        out_shape=(shape(rank, half), shape(rank, half), shape(rows, half), shape(rows, half)),
        in_specs=[SMEM, VMEM, VMEM, VMEM, VMEM, VMEM],
        out_specs=(VMEM, VMEM, VMEM, VMEM),
        compiler_params=params(),
        cost_estimate=cost(4 * ticks * rows * half * rank, 4 * ticks * rows * half * 2),
        name="finish",
    )(where, hist_mine, hist_other, came, stash, out)

    def averaged(old, late):
        if replicas == 2:
            total = late.astype(f32) + lax.ppermute(late, "dp", [(0, 1), (1, 0)]).astype(f32)
        else:
            total = lax.psum(late, "dp").astype(f32)
        return (old.astype(f32) - STEP_RATE * total / replicas).astype(bf16)

    squeeze_new = averaged(squeeze, squeeze_late[0, 0].T)
    expand_new = averaged(expand, expand_late[0, 0])
    return (
        squeeze_new.T[None],
        expand_new[None],
        squeeze_grad.T[None, None],
        expand_grad[None, None],
        fwd_carry[None, None],
        bwd_carry[None, None],
    )


def solution(mesh):
    placed = (
        P("dp", "pipe", "mp"),
        P("dp", "pipe", "mp"),
        P("pipe", "mp", None),
        P("pipe", None, "mp"),
        P("dp", "pipe", "mp", None),
        P("dp", "pipe", None, "mp"),
        P("dp", "pipe", None, None, "mp"),
        P("dp", "pipe", None, "mp"),
        P("dp", "pipe", None, "mp"),
    )
    return jax.shard_map(
        shards,
        mesh=mesh,
        in_specs=placed,
        out_specs=(
            P("pipe", "mp", None),
            P("pipe", None, "mp"),
            P("dp", "pipe", "mp", None),
            P("dp", "pipe", None, "mp"),
            P("dp", "pipe", None, "mp"),
            P("dp", "pipe", None, "mp"),
        ),
        check_vma=False,
    )
```

time: 241 us -> 110 us (0.46)
  blocking collectives: 96.7 us -> 0 us
  matrix products: 47.1 us -> 0 us
  waiting for transfers between devices: 20.4 us -> 42.1 us
  Pallas kernels: 0 us -> 18.3 us
  between operations: 14.5 us -> 0.98 us
  starting transfers between devices: 45 us -> 35.6 us
  other arithmetic: 9.29 us -> 6.4 us
    all_gather x2 -> x0, blocking collectives: 53.4 us -> none  [the longest x1 28.5 us: shards(): lax.all_gather(cotangent, 'pipe', axis=1, tiled=True)]
    dot_general x56 -> x0, matrix products: 47.1 us -> none  [the longest x8 18.4 us: shards(): lax.dot_general(saved, hidden_grad, (((0,), (0,)), ((), ())), preferred_e...]
    psum x8 -> x0, blocking collectives: 43.3 us -> none  [shards(): again_total, grad_total = lax.psum((again_partial, grad_partial), 'mp')]
    ppermute x14 -> x22, waiting for transfers between devices: 20.4 us -> 42.1 us  [the longest x16 41.1 us: send(): lax.ppermute(x, ('pipe', 'mp'), [(a * 2 + b, c * 2 + d) for (a, b), (c, d...]
    pallas_call x0 -> x10, Pallas kernels: none -> 18.3 us  [the longest x8 15.3 us: shards(): pl.pallas_call(functools.partial(tick_kernel, tick, ticks, slots, in_scal...]
    ppermute x14 -> x22, starting transfers between devices: 44.9 us -> 35.6 us  [the longest x16 26.7 us: send(): lax.ppermute(x, ('pipe', 'mp'), [(a * 2 + b, c * 2 + d) for (a, b), (c, d...]
    unnamed x8 -> x0, other arithmetic: 5.53 us -> none
    unnamed x55 -> x32, local copies, waits for them, and re-layouts: 6.18 us -> 5.39 us
  transfers between devices with their start and end apart: 15 -> 22, of which waited for: 10 -> 9; matrix products, arithmetic and copies ran while one was open for 23% -> 6% of each run, Pallas kernels for 0% -> 5%
where the time goes in v1:
time: 110 us; the launch traced here: 109 us
  waiting for transfers between devices  42.1 us (38%)
  starting transfers between devices  35.6 us (32%)
  Pallas kernels  18.3 us (17%)
  other arithmetic  6.4 us (6%)
  local copies, waits for them, and re-layouts  5.55 us (5%)
    ppermute x16, waiting for transfers between devices, send(): lax.ppermute(x, ('pipe', 'mp'), [(a * 2 + b, c * 2 + d) for (a, b), (c, d...  41.1 us
    ppermute x16, starting transfers between devices, send(): lax.ppermute(x, ('pipe', 'mp'), [(a * 2 + b, c * 2 + d) for (a, b), (c, d...  26.7 us
    pallas_call x8, Pallas kernels, shards(): pl.pallas_call(functools.partial(tick_kernel, tick, ticks, slots, in_scal...  15.3 us
    ppermute x4, starting transfers between devices, swap(): return lax.ppermute(x, 'mp', [(0, 1), (1, 0)])  7.46 us
    unnamed x32, local copies, waits for them, and re-layouts  5.39 us
    broadcast_in_dim x1, other arithmetic, shards(): expand_new[None]  2.2 us
  transfers between devices with their start and end apart: 22, of which 9 were waited for; matrix products, arithmetic and copies ran while one was open for 6% of the time, Pallas kernels for 5%

profile of v1, /device:TPU:25, one launch (start us, length us, event | category | flops | bytes accessed | tf_op | source)
XLA Modules:
  0.0 109.0 jit_solution(15062523388453557653)
XLA Ops:
  0.6 0.7 collective-permute-start.4
  1.3 0.7 collective-permute-start.5
  2.1 1.0 copy-done.2
  3.1 1.2 %copy-done.4 = bf16[1,1,8,16,3584]{4,3,2,1,0:T(8,128)(2,1)S(1)} copy-done((bf16[1,1,8,16,3584]{4,3,2,1,0:T(8,128)(2,1)S(1)}, bf16[1,1,8,16,3584]{4,3,2,1,0:T(8,128)(2,1)}, u32[]{:S(2)}) %copy-start.4) | copy-done | bytes 917528
  4.3 0.9 copy-done.6
  5.2 0.9 copy-done.8
  6.1 1.0 start.1
  7.1 0.7 collective-permute-start.2
  8.1 0.5 collective-permute-start.6
  8.8 0.4 collective-permute-done.3
  9.3 0.7 pad_maximum_fusion.1
  10.2 0.5 collective-permute-done.6.other
  10.9 1.7 %tick0.1 = (bf16[16,7680]{1,0:T(8,128)(2,1)S(1)}, bf16[8,16,3584]{2,1,0:T(8,128)(2,1)S(1)}, bf16[9,16,3712]{2,1,0:T(8,128)(2,1)S(1)}) custom-call(s32[3]{0:T(128)S(1)} %pad_add_fusion.where, bf16[16,7680]{1,0:T(8,128)(2,1)S(1)} %maximum_maximum_fusion.x_in, ...), custom_call_target="tpu_custom_call", output_to_operand_aliasing={{1}: (6, {}), {2}: (7, {})} | custom-call | flops 29360128 | bytes 1835008 | tf_op jit(solution)/shard_map/tick0/pallas_call | solution.py:230
  12.6 3.0 %collective-permute-start.7 = (bf16[16,7680]{1,0:T(8,128)(2,1)S(1)}, bf16[16,7680]{1,0:T(8,128)(2,1)S(1)}, u32[]{:S(2)}, u32[]{:S(2)}) collective-permute-start(bf16[16,7680]{1,0:T(8,128)(2,1)S(1)} %get-tuple-element.44), channel_id=1, source_target_pairs={{0,4},{4,8},{8,12},{12,16},{16,20},{20,24},{24,28},{28,29},{5,1},{... | collective-permute-start | bytes 737288 | tf_op jit(solution)/shard_map/ppermute | solution.py:159
  15.6 0.7 collective-permute-start.8
  16.3 6.8 %collective-permute-done.7.x_in = bf16[16,7680]{1,0:T(8,128)(2,1)S(1)} collective-permute-done((bf16[16,7680]{1,0:T(8,128)(2,1)S(1)}, bf16[16,7680]{1,0:T(8,128)(2,1)S(1)}, u32[]{:S(2)}, u32[]{:S(2)}) %collective-permute-start.7) | collective-permute-done | bytes 245792 | tf_op jit(solution)/shard_map/ppermute | solution.py:159
  23.1 1.7 %tick1.1 = (bf16[16,7680]{1,0:T(8,128)(2,1)S(1)}, bf16[8,16,3584]{2,1,0:T(8,128)(2,1)S(1)}, bf16[9,16,3712]{2,1,0:T(8,128)(2,1)S(1)}) custom-call(s32[3]{0:T(128)S(1)} %pad_add_fusion.where, bf16[16,7680]{1,0:T(8,128)(2,1)S(1)} %collective-permute-done.7.x_in, ...), custom_call_target="tpu_custom_call", output_to_operand_aliasing={{1}: (6, {}), {2}: (7, {})} | custom-call | flops 29360128 | bytes 1835008 | tf_op jit(solution)/shard_map/tick1/pallas_call | solution.py:230
  24.9 1.9 %collective-permute-start.9 = (bf16[16,7680]{1,0:T(8,128)(2,1)S(1)}, bf16[16,7680]{1,0:T(8,128)(2,1)S(1)}, u32[]{:S(2)}, u32[]{:S(2)}) collective-permute-start(bf16[16,7680]{1,0:T(8,128)(2,1)S(1)} %get-tuple-element.47), channel_id=1, source_target_pairs={{0,4},{4,8},{8,12},{12,16},{16,20},{20,24},{24,28},{28,29},{5,1},{... | collective-permute-start | bytes 737288 | tf_op jit(solution)/shard_map/ppermute | solution.py:159
  26.8 0.7 collective-permute-start.10
  27.5 7.4 %collective-permute-done.9.x_in = bf16[16,7680]{1,0:T(8,128)(2,1)S(1)} collective-permute-done((bf16[16,7680]{1,0:T(8,128)(2,1)S(1)}, bf16[16,7680]{1,0:T(8,128)(2,1)S(1)}, u32[]{:S(2)}, u32[]{:S(2)}) %collective-permute-start.9) | collective-permute-done | bytes 245792 | tf_op jit(solution)/shard_map/ppermute | solution.py:159
  34.9 1.7 %tick2.1 = (bf16[16,7680]{1,0:T(8,128)(2,1)S(1)}, bf16[8,16,3584]{2,1,0:T(8,128)(2,1)S(1)}, bf16[9,16,3712]{2,1,0:T(8,128)(2,1)S(1)}) custom-call(s32[3]{0:T(128)S(1)} %pad_add_fusion.where, bf16[16,7680]{1,0:T(8,128)(2,1)S(1)} %collective-permute-done.9.x_in, ...), custom_call_target="tpu_custom_call", output_to_operand_aliasing={{1}: (6, {}), {2}: (7, {})} | custom-call | flops 29360128 | bytes 1835008 | tf_op jit(solution)/shard_map/tick2/pallas_call | solution.py:230
  36.6 1.9 %collective-permute-start.11 = (bf16[16,7680]{1,0:T(8,128)(2,1)S(1)}, bf16[16,7680]{1,0:T(8,128)(2,1)S(1)}, u32[]{:S(2)}, u32[]{:S(2)}) collective-permute-start(bf16[16,7680]{1,0:T(8,128)(2,1)S(1)} %get-tuple-element.51), channel_id=1, source_target_pairs={{0,4},{4,8},{8,12},{12,16},{16,20},{20,24},{24,28},{28,29},{5,1},{... | collective-permute-start | bytes 737288 | tf_op jit(solution)/shard_map/ppermute | solution.py:159
  38.5 0.7 collective-permute-start.12
  39.2 7.1 %collective-permute-done.11.x_in = bf16[16,7680]{1,0:T(8,128)(2,1)S(1)} collective-permute-done((bf16[16,7680]{1,0:T(8,128)(2,1)S(1)}, bf16[16,7680]{1,0:T(8,128)(2,1)S(1)}, u32[]{:S(2)}, u32[]{:S(2)}) %collective-permute-start.11) | collective-permute-done | bytes 245792 | tf_op jit(solution)/shard_map/ppermute | solution.py:159
  46.4 1.7 %tick3.1 = (bf16[16,7680]{1,0:T(8,128)(2,1)S(1)}, bf16[8,16,3584]{2,1,0:T(8,128)(2,1)S(1)}, bf16[9,16,3712]{2,1,0:T(8,128)(2,1)S(1)}) custom-call(s32[3]{0:T(128)S(1)} %pad_add_fusion.where, bf16[16,7680]{1,0:T(8,128)(2,1)S(1)} %collective-permute-done.11.x_in, ...), custom_call_target="tpu_custom_call", output_to_operand_aliasing={{1}: (6, {}), {2}: (7, {})} | custom-call | flops 29360128 | bytes 1835008 | tf_op jit(solution)/shard_map/tick3/pallas_call | solution.py:230
  48.1 1.9 %collective-permute-start.13 = (bf16[16,7680]{1,0:T(8,128)(2,1)S(1)}, bf16[16,7680]{1,0:T(8,128)(2,1)S(1)}, u32[]{:S(2)}, u32[]{:S(2)}) collective-permute-start(bf16[16,7680]{1,0:T(8,128)(2,1)S(1)} %get-tuple-element.55), channel_id=1, source_target_pairs={{0,4},{4,8},{8,12},{12,16},{16,20},{20,24},{24,28},{28,29},{5,1},{... | collective-permute-start | bytes 737288 | tf_op jit(solution)/shard_map/ppermute | solution.py:159
  50.0 0.7 collective-permute-start.14
  50.7 7.2 %collective-permute-done.13.x_in = bf16[16,7680]{1,0:T(8,128)(2,1)S(1)} collective-permute-done((bf16[16,7680]{1,0:T(8,128)(2,1)S(1)}, bf16[16,7680]{1,0:T(8,128)(2,1)S(1)}, u32[]{:S(2)}, u32[]{:S(2)}) %collective-permute-start.13) | collective-permute-done | bytes 245792 | tf_op jit(solution)/shard_map/ppermute | solution.py:159
  57.9 1.7 %tick4.1 = (bf16[16,7680]{1,0:T(8,128)(2,1)S(1)}, bf16[8,16,3584]{2,1,0:T(8,128)(2,1)S(1)}, bf16[9,16,3712]{2,1,0:T(8,128)(2,1)S(1)}) custom-call(s32[3]{0:T(128)S(1)} %pad_add_fusion.where, bf16[16,7680]{1,0:T(8,128)(2,1)S(1)} %collective-permute-done.13.x_in, ...), custom_call_target="tpu_custom_call", output_to_operand_aliasing={{1}: (6, {}), {2}: (7, {})} | custom-call | flops 29360128 | bytes 1835008 | tf_op jit(solution)/shard_map/tick4/pallas_call | solution.py:230
  59.7 1.9 %collective-permute-start.15 = (bf16[16,7680]{1,0:T(8,128)(2,1)S(1)}, bf16[16,7680]{1,0:T(8,128)(2,1)S(1)}, u32[]{:S(2)}, u32[]{:S(2)}) collective-permute-start(bf16[16,7680]{1,0:T(8,128)(2,1)S(1)} %get-tuple-element.59), channel_id=1, source_target_pairs={{0,4},{4,8},{8,12},{12,16},{16,20},{20,24},{24,28},{28,29},{5,1},{... | collective-permute-start | bytes 737288 | tf_op jit(solution)/shard_map/ppermute | solution.py:159
  61.6 0.7 collective-permute-start.16
  62.3 7.2 %collective-permute-done.15.x_in = bf16[16,7680]{1,0:T(8,128)(2,1)S(1)} collective-permute-done((bf16[16,7680]{1,0:T(8,128)(2,1)S(1)}, bf16[16,7680]{1,0:T(8,128)(2,1)S(1)}, u32[]{:S(2)}, u32[]{:S(2)}) %collective-permute-start.15) | collective-permute-done | bytes 245792 | tf_op jit(solution)/shard_map/ppermute | solution.py:159
  69.5 2.4 %tick5.1 = (bf16[16,7680]{1,0:T(8,128)(2,1)}, bf16[8,16,3584]{2,1,0:T(8,128)(2,1)S(1)}, bf16[9,16,3712]{2,1,0:T(8,128)(2,1)S(1)}) custom-call(s32[3]{0:T(128)S(1)} %pad_add_fusion.where, bf16[16,7680]{1,0:T(8,128)(2,1)S(1)} %collective-permute-done.15.x_in, ...), custom_call_target="tpu_custom_call", output_to_operand_aliasing={{1}: (6, {}), {2}: (7, {})} | custom-call | flops 29360128 | bytes 1835008 | tf_op jit(solution)/shard_map/tick5/pallas_call | solution.py:230
  71.9 4.7 %collective-permute-start.17 = (bf16[16,7680]{1,0:T(8,128)(2,1)}, bf16[16,7680]{1,0:T(8,128)(2,1)}, u32[]{:S(2)}, u32[]{:S(2)}) collective-permute-start(bf16[16,7680]{1,0:T(8,128)(2,1)} %get-tuple-element.63), channel_id=1, source_target_pairs={{0,4},{4,8},{8,12},{12,16},{16,20},{20,24},{24,28},{28,29},{5,1},{... | collective-permute-start | bytes 737288 | tf_op jit(solution)/shard_map/ppermute | solution.py:159
  76.6 3.2 %collective-permute-start.18 = (bf16[16,7168]{1,0:T(8,128)(2,1)}, bf16[16,7168]{1,0:T(8,128)(2,1)}, u32[]{:S(2)}, u32[]{:S(2)}) collective-permute-start(bf16[16,7168]{1,0:T(8,128)(2,1)} %get-tuple-element.68), channel_id=1, source_target_pairs={{24,0},{25,29},{26,2},{27,31}} | collective-permute-start | bytes 688136 | tf_op jit(solution)/shard_map/ppermute | solution.py:159
  79.9 1.4 %collective-permute-start.20 = (bf16[16,7168]{1,0:T(8,128)(2,1)}, bf16[16,7168]{1,0:T(8,128)(2,1)}, u32[]{:S(2)}, u32[]{:S(2)}) collective-permute-start(bf16[16,7168]{1,0:T(8,128)(2,1)} %get-tuple-element.68), channel_id=1, source_target_pairs={{28,0},{30,2}} | collective-permute-start | bytes 688136 | tf_op jit(solution)/shard_map/ppermute | solution.py:159
  81.2 1.2 %collective-permute-start = (bf16[64,3584]{1,0:T(8,128)(2,1)}, bf16[64,3584]{1,0:T(8,128)(2,1)}, u32[]{:S(2)}, u32[]{:S(2)}) collective-permute-start(bf16[64,3584]{1,0:T(8,128)(2,1)} %bitcast.3), channel_id=1, source_target_pairs={{0,2},{2,0},{1,3},{3,1},{4,6},{6,4},{5,7},{7,5},{8,10},{10,8},{9,1... | collective-permute-start | bytes 1376264 | tf_op jit(solution)/shard_map/ppermute | solution.py:266
  82.7 1.1 collective-permute-done.17.x_in
  83.8 1.2 %copy-done.1 = bf16[2,64,3584]{2,1,0:T(8,128)(2,1)S(1)} copy-done((bf16[2,64,3584]{2,1,0:T(8,128)(2,1)S(1)}, bf16[2,64,3584]{2,1,0:T(8,128)(2,1)}, u32[]{:S(2)}) %copy-start.1) | copy-done | bytes 917528
  84.9 2.3 %tick6.1 = (bf16[16,7680]{1,0:T(8,128)(2,1)S(1)}, bf16[8,16,3584]{2,1,0:T(8,128)(2,1)S(1)}, bf16[9,16,3712]{2,1,0:T(8,128)(2,1)S(1)}) custom-call(s32[3]{0:T(128)S(1)} %pad_add_fusion.where, bf16[16,7680]{1,0:T(8,128)(2,1)} %collective-permute-done.17.x_in, ...), custom_call_target="tpu_custom_call", output_to_operand_aliasing={{1}: (6, {}), {2}: (7, {})} | custom-call | flops 29360128 | bytes 1835008 | tf_op jit(solution)/shard_map/tick6/pallas_call | solution.py:230
  87.2 1.9 %collective-permute-start.19 = (bf16[16,7680]{1,0:T(8,128)(2,1)S(1)}, bf16[16,7680]{1,0:T(8,128)(2,1)S(1)}, u32[]{:S(2)}, u32[]{:S(2)}) collective-permute-start(bf16[16,7680]{1,0:T(8,128)(2,1)S(1)} %get-tuple-element.67), channel_id=1, source_target_pairs={{0,4},{4,8},{8,12},{12,16},{16,20},{20,24},{24,28},{28,29},{5,1},{... | collective-permute-start | bytes 737288 | tf_op jit(solution)/shard_map/ppermute | solution.py:159
  89.2 1.0 broadcast_select_fusion.feed
  90.2 4.4 %collective-permute-done.19.x_in = bf16[16,7680]{1,0:T(8,128)(2,1)S(1)} collective-permute-done((bf16[16,7680]{1,0:T(8,128)(2,1)S(1)}, bf16[16,7680]{1,0:T(8,128)(2,1)S(1)}, u32[]{:S(2)}, u32[]{:S(2)}) %collective-permute-start.19) | collective-permute-done | bytes 245792 | tf_op jit(solution)/shard_map/ppermute | solution.py:159
  94.6 1.9 %tick7.1 = (bf16[16,3584]{1,0:T(8,128)(2,1)S(1)}, bf16[8,16,3584]{2,1,0:T(8,128)(2,1)S(1)}, bf16[9,16,3712]{2,1,0:T(8,128)(2,1)S(1)}) custom-call(s32[3]{0:T(128)S(1)} %pad_add_fusion.where, bf16[16,7680]{1,0:T(8,128)(2,1)S(1)} %collective-permute-done.19.x_in, ...), custom_call_target="tpu_custom_call", output_to_operand_aliasing={{1}: (6, {}), {2}: (7, {})} | custom-call | flops 29360128 | bytes 1835008 | tf_op jit(solution)/shard_map/tick7/pallas_call | solution.py:230
  96.5 6.1 %collective-permute-start.21 = (bf16[9,16,3712]{2,1,0:T(8,128)(2,1)S(1)}, bf16[9,16,3712]{2,1,0:T(8,128)(2,1)S(1)}, u32[]{:S(2)}, u32[]{:S(2)}) collective-permute-start(bf16[9,16,3712]{2,1,0:T(8,128)(2,1)S(1)} %get-tuple-element.72.sent), channel_id=1, source_target_pairs={{0,1},{1,0},{2,3},{3,2},{4,5},{5,4},{6,7},{7,6},{8,9},{9,8},{10,11... | collective-permute-start | bytes 3207176 | tf_op jit(solution)/shard_map/ppermute | solution.py:162
  102.6 2.1 %fusion.1 = bf16[1,3584,64]{1,2,0:T(8,128)(2,1)} fusion(bf16[64,3584]{1,0:T(8,128)(2,1)} %collective-permute-done, bf16[1,3584,64]{1,2,0:T(8,128)(2,1)S(1)} %copy-done.3, bf16[1,1,3584,64]{2,3,1,0:T(8,128)(2,1)} %param.13), kind=kLoop, calls=%fused_computation.4 | loop fusion | flops 1605632 | bytes 1835008 | tf_op jit(solution)/shard_map/broadcast_in_dim | solution.py:274
  104.7 2.2 %fusion.2 = bf16[1,64,3584]{2,1,0:T(8,128)(2,1)} fusion(bf16[64,3584]{1,0:T(8,128)(2,1)} %collective-permute-done.1, bf16[1,64,3584]{2,1,0:T(8,128)(2,1)S(1)} %copy-done.11, bf16[1,1,64,3584]{3,2,1,0:T(8,128)(2,1)} %param.14), kind=kLoop, calls=%fused_computation.5 | loop fusion | flops 1605632 | bytes 1835008 | tf_op jit(solution)/shard_map/broadcast_in_dim | solution.py:275
  106.9 2.0 %finish.1 = (bf16[64,3584]{1,0:T(8,128)(2,1)}, bf16[64,3584]{1,0:T(8,128)(2,1)}, bf16[16,3584]{1,0:T(8,128)(2,1)}, bf16[16,3584]{1,0:T(8,128)(2,1)}) custom-call(s32[3]{0:T(128)S(1)} %pad_add_fusion.where, bf16[8,16,3584]{2,1,0:T(8,128)(2,1)S(1)} %get-tuple-element.71.mine, bf16[9,16,3712]{2,1,0:T(8,128)(2,1)S(1)} %get-tuple-element.72.sent, ...), custom_call_target="tpu_custom_call" | custom-call | flops 117440512 | bytes 3670016 | tf_op jit(solution)/shard_map/finish/pallas_call | solution.py:254
  (54 shorter events, 1.1 us)
Async XLA Ops:
  0.6 8.6 %collective-permute-start.4 = (bf16[16,3584]{1,0:T(8,128)(2,1)}, bf16[16,3584]{1,0:T(8,128)(2,1)S(1)}, u32[]{:S(2)}, u32[]{:S(2)}) collective-permute-start(bf16[16,3584]{1,0:T(8,128)(2,1)} %bitcast.53), channel_id=1, source_target_pairs={{1,29},{3,31}} | collective-permute-start | bytes 344072 | tf_op jit(solution)/shard_map/ppermute | solution.py:159
  1.3 8.0 %collective-permute-start.5 = (bf16[16,3584]{1,0:T(8,128)(2,1)}, bf16[16,3584]{1,0:T(8,128)(2,1)S(1)}, u32[]{:S(2)}, u32[]{:S(2)}) collective-permute-start(bf16[16,3584]{1,0:T(8,128)(2,1)} %bitcast.54), channel_id=1, source_target_pairs={{0,29},{2,31}} | collective-permute-start | bytes 344072 | tf_op jit(solution)/shard_map/ppermute | solution.py:159
  2.1 1.0 copy-start.2
  3.1 1.2 %copy-start.4 = (bf16[1,1,8,16,3584]{4,3,2,1,0:T(8,128)(2,1)S(1)}, bf16[1,1,8,16,3584]{4,3,2,1,0:T(8,128)(2,1)}, u32[]{:S(2)}) copy-start(bf16[1,1,8,16,3584]{4,3,2,1,0:T(8,128)(2,1)} %param.15) | copy-start | bytes 2752516
  4.3 0.9 copy-start.6
  5.2 0.9 copy-start.8
  6.1 1.8 %copy-start.14 = (bf16[1,16,3584]{2,1,0:T(8,128)(2,1)S(1)}, bf16[1,16,3584]{2,1,0:T(8,128)(2,1)}, u32[]{:S(2)}) copy-start(bf16[1,16,3584]{2,1,0:T(8,128)(2,1)} %param.9) | copy-start | bytes 344068
  6.1 1.8 %copy-start.15 = (bf16[1,16,3584]{2,1,0:T(8,128)(2,1)S(1)}, bf16[1,16,3584]{2,1,0:T(8,128)(2,1)}, u32[]{:S(2)}) copy-start(bf16[1,16,3584]{2,1,0:T(8,128)(2,1)} %param.10) | copy-start | bytes 344068
  6.1 1.9 %copy-start.3 = (bf16[1,3584,64]{1,2,0:T(8,128)(2,1)S(1)}, bf16[1,3584,64]{1,2,0:T(8,128)(2,1)}, u32[]{:S(2)}) copy-start(bf16[1,3584,64]{1,2,0:T(8,128)(2,1)} %param.11) | copy-start | bytes 1376260
  6.1 1.9 %copy-start.10 = (bf16[1,64,3584]{2,1,0:T(8,128)(2,1)S(1)}, bf16[1,64,3584]{2,1,0:T(8,128)(2,1)}, u32[]{:S(2)}) copy-start(bf16[1,64,3584]{2,1,0:T(8,128)(2,1)} %param.12) | copy-start | bytes 1376260
  7.1 2.9 %collective-permute-start.2 = (bf16[16,4608]{1,0:T(8,128)(2,1)S(1)}, bf16[16,4608]{1,0:T(8,128)(2,1)S(1)}, u32[]{:S(2)}, u32[]{:S(2)}) collective-permute-start(bf16[16,4608]{1,0:T(8,128)(2,1)S(1)} %get-tuple-element.42), channel_id=1, source_target_pairs={{0,1},{1,0},{2,3},{3,2},{4,5},{5,4},{6,7},{7,6},{8,9},{9,8},{10,11... | collective-permute-start | bytes 442376 | tf_op jit(solution)/shard_map/ppermute | solution.py:162
  7.8 0.9 copy-start.7
  7.8 1.0 copy-start.9
  7.9 1.4 %collective-permute-start.3 = (bf16[16,3584]{1,0:T(8,128)(2,1)S(1)}, bf16[16,3584]{1,0:T(8,128)(2,1)S(1)}, u32[]{:S(2)}, u32[]{:S(2)}) collective-permute-start(bf16[16,3584]{1,0:T(8,128)(2,1)S(1)} %get-tuple-element.81), channel_id=1, source_target_pairs={{0,1},{1,0},{2,3},{3,2},{4,5},{5,4},{6,7},{7,6},{8,9},{9,8},{10,11... | collective-permute-start | bytes 344072 | tf_op jit(solution)/shard_map/ppermute | solution.py:162
  8.1 2.6 %collective-permute-start.6 = (bf16[2,64,3584]{2,1,0:T(8,128)(2,1)S(1)}, bf16[2,64,3584]{2,1,0:T(8,128)(2,1)S(1)}, u32[]{:S(2)}, u32[]{:S(2)}) collective-permute-start(bf16[2,64,3584]{2,1,0:T(8,128)(2,1)S(1)} %pad_maximum_fusion.own), channel_id=1, source_target_pairs={{0,1},{1,0},{2,3},{3,2},{4,5},{5,4},{6,7},{7,6},{8,9},{9,8},{10,11... | collective-permute-start | bytes 2752520 | tf_op jit(solution)/shard_map/ppermute | solution.py:162
  9.3 1.4 %copy-start.12 = (bf16[16,3584]{1,0:T(8,128)(2,1)}, bf16[16,3584]{1,0:T(8,128)(2,1)S(1)}, u32[]{:S(2)}) copy-start(bf16[16,3584]{1,0:T(8,128)(2,1)S(1)} %collective-permute-done.3) | copy-start | bytes 344068
  10.7 58.8 %copy-start = (bf16[2,64,3584]{2,1,0:T(8,128)(2,1)}, bf16[2,64,3584]{2,1,0:T(8,128)(2,1)S(1)}, u32[]{:S(2)}) copy-start(bf16[2,64,3584]{2,1,0:T(8,128)(2,1)S(1)} %collective-permute-done.6.other) | copy-start | bytes 2752516
  12.6 10.5 %collective-permute-start.7 = (bf16[16,7680]{1,0:T(8,128)(2,1)S(1)}, bf16[16,7680]{1,0:T(8,128)(2,1)S(1)}, u32[]{:S(2)}, u32[]{:S(2)}) collective-permute-start(bf16[16,7680]{1,0:T(8,128)(2,1)S(1)} %get-tuple-element.44), channel_id=1, source_target_pairs={{0,4},{4,8},{8,12},{12,16},{16,20},{20,24},{24,28},{28,29},{5,1},{... | collective-permute-start | bytes 737288 | tf_op jit(solution)/shard_map/ppermute | solution.py:159
  15.6 0.7 collective-permute-start.8
  24.9 10.0 %collective-permute-start.9 = (bf16[16,7680]{1,0:T(8,128)(2,1)S(1)}, bf16[16,7680]{1,0:T(8,128)(2,1)S(1)}, u32[]{:S(2)}, u32[]{:S(2)}) collective-permute-start(bf16[16,7680]{1,0:T(8,128)(2,1)S(1)} %get-tuple-element.47), channel_id=1, source_target_pairs={{0,4},{4,8},{8,12},{12,16},{16,20},{20,24},{24,28},{28,29},{5,1},{... | collective-permute-start | bytes 737288 | tf_op jit(solution)/shard_map/ppermute | solution.py:159
  26.8 0.7 collective-permute-start.10
  36.6 9.8 %collective-permute-start.11 = (bf16[16,7680]{1,0:T(8,128)(2,1)S(1)}, bf16[16,7680]{1,0:T(8,128)(2,1)S(1)}, u32[]{:S(2)}, u32[]{:S(2)}) collective-permute-start(bf16[16,7680]{1,0:T(8,128)(2,1)S(1)} %get-tuple-element.51), channel_id=1, source_target_pairs={{0,4},{4,8},{8,12},{12,16},{16,20},{20,24},{24,28},{28,29},{5,1},{... | collective-permute-start | bytes 737288 | tf_op jit(solution)/shard_map/ppermute | solution.py:159
  38.5 0.7 collective-permute-start.12
  48.1 9.8 %collective-permute-start.13 = (bf16[16,7680]{1,0:T(8,128)(2,1)S(1)}, bf16[16,7680]{1,0:T(8,128)(2,1)S(1)}, u32[]{:S(2)}, u32[]{:S(2)}) collective-permute-start(bf16[16,7680]{1,0:T(8,128)(2,1)S(1)} %get-tuple-element.55), channel_id=1, source_target_pairs={{0,4},{4,8},{8,12},{12,16},{16,20},{20,24},{24,28},{28,29},{5,1},{... | collective-permute-start | bytes 737288 | tf_op jit(solution)/shard_map/ppermute | solution.py:159
  50.0 0.7 collective-permute-start.14
  59.7 9.8 %collective-permute-start.15 = (bf16[16,7680]{1,0:T(8,128)(2,1)S(1)}, bf16[16,7680]{1,0:T(8,128)(2,1)S(1)}, u32[]{:S(2)}, u32[]{:S(2)}) collective-permute-start(bf16[16,7680]{1,0:T(8,128)(2,1)S(1)} %get-tuple-element.59), channel_id=1, source_target_pairs={{0,4},{4,8},{8,12},{12,16},{16,20},{20,24},{24,28},{28,29},{5,1},{... | collective-permute-start | bytes 737288 | tf_op jit(solution)/shard_map/ppermute | solution.py:159
  61.6 0.7 collective-permute-start.16
  71.9 11.9 %collective-permute-start.17 = (bf16[16,7680]{1,0:T(8,128)(2,1)}, bf16[16,7680]{1,0:T(8,128)(2,1)}, u32[]{:S(2)}, u32[]{:S(2)}) collective-permute-start(bf16[16,7680]{1,0:T(8,128)(2,1)} %get-tuple-element.63), channel_id=1, source_target_pairs={{0,4},{4,8},{8,12},{12,16},{16,20},{20,24},{24,28},{28,29},{5,1},{... | collective-permute-start | bytes 737288 | tf_op jit(solution)/shard_map/ppermute | solution.py:159
  76.6 6.1 %collective-permute-start.18 = (bf16[16,7168]{1,0:T(8,128)(2,1)}, bf16[16,7168]{1,0:T(8,128)(2,1)}, u32[]{:S(2)}, u32[]{:S(2)}) collective-permute-start(bf16[16,7168]{1,0:T(8,128)(2,1)} %get-tuple-element.68), channel_id=1, source_target_pairs={{24,0},{25,29},{26,2},{27,31}} | collective-permute-start | bytes 688136 | tf_op jit(solution)/shard_map/ppermute | solution.py:159
  79.9 9.3 %collective-permute-start.20 = (bf16[16,7168]{1,0:T(8,128)(2,1)}, bf16[16,7168]{1,0:T(8,128)(2,1)}, u32[]{:S(2)}, u32[]{:S(2)}) collective-permute-start(bf16[16,7168]{1,0:T(8,128)(2,1)} %get-tuple-element.68), channel_id=1, source_target_pairs={{28,0},{30,2}} | collective-permute-start | bytes 688136 | tf_op jit(solution)/shard_map/ppermute | solution.py:159
  81.2 21.4 %collective-permute-start = (bf16[64,3584]{1,0:T(8,128)(2,1)}, bf16[64,3584]{1,0:T(8,128)(2,1)}, u32[]{:S(2)}, u32[]{:S(2)}) collective-permute-start(bf16[64,3584]{1,0:T(8,128)(2,1)} %bitcast.3), channel_id=1, source_target_pairs={{0,2},{2,0},{1,3},{3,1},{4,6},{6,4},{5,7},{7,5},{8,10},{10,8},{9,1... | collective-permute-start | bytes 1376264 | tf_op jit(solution)/shard_map/ppermute | solution.py:266
  82.4 22.3 %collective-permute-start.1 = (bf16[64,3584]{1,0:T(8,128)(2,1)}, bf16[64,3584]{1,0:T(8,128)(2,1)}, u32[]{:S(2)}, u32[]{:S(2)}) collective-permute-start(bf16[64,3584]{1,0:T(8,128)(2,1)} %bitcast.8), channel_id=1, source_target_pairs={{0,2},{2,0},{1,3},{3,1},{4,6},{6,4},{5,7},{7,5},{8,10},{10,8},{9,1... | collective-permute-start | bytes 1376264 | tf_op jit(solution)/shard_map/ppermute | solution.py:266
  83.8 1.2 %copy-start.1 = (bf16[2,64,3584]{2,1,0:T(8,128)(2,1)S(1)}, bf16[2,64,3584]{2,1,0:T(8,128)(2,1)}, u32[]{:S(2)}) copy-start(bf16[2,64,3584]{2,1,0:T(8,128)(2,1)} %copy-done) | copy-start | bytes 2752516
  84.9 4.2 %copy-start.13 = (bf16[16,3584]{1,0:T(8,128)(2,1)S(1)}, bf16[16,3584]{1,0:T(8,128)(2,1)}, u32[]{:S(2)}) copy-start(bf16[16,3584]{1,0:T(8,128)(2,1)} %copy-done.12) | copy-start | bytes 344068
  87.2 7.3 %collective-permute-start.19 = (bf16[16,7680]{1,0:T(8,128)(2,1)S(1)}, bf16[16,7680]{1,0:T(8,128)(2,1)S(1)}, u32[]{:S(2)}, u32[]{:S(2)}) collective-permute-start(bf16[16,7680]{1,0:T(8,128)(2,1)S(1)} %get-tuple-element.67), channel_id=1, source_target_pairs={{0,4},{4,8},{8,12},{12,16},{16,20},{20,24},{24,28},{28,29},{5,1},{... | collective-permute-start | bytes 737288 | tf_op jit(solution)/shard_map/ppermute | solution.py:159
  96.5 8.2 %copy-start.11 = (bf16[1,64,3584]{2,1,0:T(8,128)(2,1)S(1)}, bf16[1,64,3584]{2,1,0:T(8,128)(2,1)}, u32[]{:S(2)}) copy-start(bf16[1,64,3584]{2,1,0:T(8,128)(2,1)} %param.12) | copy-start | bytes 1376260
  96.5 10.4 %collective-permute-start.21 = (bf16[9,16,3712]{2,1,0:T(8,128)(2,1)S(1)}, bf16[9,16,3712]{2,1,0:T(8,128)(2,1)S(1)}, u32[]{:S(2)}, u32[]{:S(2)}) collective-permute-start(bf16[9,16,3712]{2,1,0:T(8,128)(2,1)S(1)} %get-tuple-element.72.sent), channel_id=1, source_target_pairs={{0,1},{1,0},{2,3},{3,2},{4,5},{5,4},{6,7},{7,6},{8,9},{9,8},{10,11... | collective-permute-start | bytes 3207176 | tf_op jit(solution)/shard_map/ppermute | solution.py:162
  104.7 2.2 %copy-start.5 = (bf16[1,1,8,16,3584]{4,3,2,1,0:T(8,128)(2,1)S(1)}, bf16[1,1,8,16,3584]{4,3,2,1,0:T(8,128)(2,1)}, u32[]{:S(2)}) copy-start(bf16[1,1,8,16,3584]{4,3,2,1,0:T(8,128)(2,1)} %param.15) | copy-start | bytes 2752516

commit v2 on v0

v2 whole, which is shorter than its diff:
```python
import functools
import math

import jax
import jax.numpy as jnp
from jax import lax
from jax.experimental import pallas as pl
from jax.experimental.pallas import tpu as pltpu
from jax.sharding import PartitionSpec as P

BRANCH_SCALE = 0.25
STEP_RATE = 0.5
CHUNK = 512

VMEM = pl.BlockSpec(memory_space=pltpu.VMEM)
SMEM = pl.BlockSpec(memory_space=pltpu.SMEM)
ANY = pl.BlockSpec(memory_space=pl.ANY)
NT = (((1,), (1,)), ((), ()))
TN = (((0,), (0,)), ((), ()))


def dot(a, b, dims=(((1,), (0,)), ((), ()))):
    return lax.dot_general(a, b, dims, preferred_element_type=jnp.float32)


def gelu_and_slope(x):
    c = math.sqrt(2.0 / math.pi)
    t = jnp.tanh(c * (x + 0.044715 * (x * x * x)))
    half = 0.5 * (1.0 + t)
    slope = half + 0.5 * x * (1.0 - t * t) * (c * (1.0 + 3 * 0.044715 * (x * x)))
    return x * half, slope


def split_words(x):
    hi = x.astype(jnp.bfloat16)
    lo = (x - hi.astype(jnp.float32)).astype(jnp.bfloat16)
    return jnp.concatenate([hi, lo], axis=1)


def join_words(words):
    rank = words.shape[1] // 2
    return words[:, :rank].astype(jnp.float32) + words[:, rank:].astype(jnp.float32)


class Place:
    def __init__(self, where):
        self.section, self.role, self.sections = where[0], where[1], where[2]
        self.side = where[3]
        self.forward = self.role == 0
        self.aligned = self.side == self.role
        self.peer = self.section + 1 - 2 * self.side
        pair = jnp.where(self.forward, self.section, self.sections - 1 - self.section)
        self.at_end = pair < 2


class Sizes:
    def __init__(self, ticks, rows, rank, half):
        self.ticks, self.rows, self.rank, self.half = ticks, rows, rank, half
        self.steps = ticks // 2
        self.slots = ticks // 2
        self.width = 2 * half
        self.message = 2 * half + self.slots * 2 * rank
        self.kept = half + 2 * rank
        self.in_scale = 1.0 / math.sqrt(2 * half)
        self.out_scale = BRANCH_SCALE / math.sqrt(rank)


def section_step(size, place, section, tick, x0, x1, again, payload, mine, other, at):
    forward = place.forward
    back = place.sections - 1 - section
    first, second = at + place.role, at + 1 - place.role
    h = (dot(x0, mine[first], NT) + dot(x1, other[first], NT)) * jnp.where(
        forward, size.in_scale, size.out_scale
    )
    for j in range(size.slots):
        ready = jnp.logical_and(back == j, tick >= 2 * j + 1)
        again = jnp.where(ready, join_words(payload[j]), again)
    value, slope = gelu_and_slope(jnp.where(forward, h, again))
    z = jnp.where(forward, value, h * slope).astype(jnp.bfloat16)
    ranks = jnp.concatenate([value.astype(jnp.bfloat16), z], axis=1)
    scale = jnp.where(forward, size.out_scale, size.in_scale)
    y0 = (x0.astype(jnp.float32) + dot(z, mine[second]) * scale).astype(jnp.bfloat16)
    y1 = (x1.astype(jnp.float32) + dot(z, other[second]) * scale).astype(jnp.bfloat16)
    words = split_words(h)
    payload = [jnp.where(jnp.logical_and(forward, back == j), words, payload[j]) for j in range(size.slots)]
    return y0, y1, ranks, payload


def read(size, ref):
    half, span = size.half, 2 * size.rank
    payload = [ref[:, 2 * half + j * span : 2 * half + (j + 1) * span] for j in range(size.slots)]
    return ref[:, :half], ref[:, half : 2 * half], payload


def write(size, ref, y0, y1, payload):
    half, span = size.half, 2 * size.rank
    ref[:, :half] = y0
    ref[:, half : 2 * half] = y1
    for j in range(size.slots):
        ref[:, 2 * half + j * span : 2 * half + (j + 1) * span] = payload[j]


def stash_kernel(size, stash, squeeze, partial):
    ticks, rows, half = stash.shape
    whole = dot(stash[...].reshape(ticks * rows, half), squeeze[...], NT) * size.in_scale
    for t in range(ticks):
        partial[t] = whole[t * rows : (t + 1) * rows]


def keep(size, keep_mine, keep_other, slot, x0, x1, ranks):
    keep_mine[slot] = x0
    keep_other[slot, :, : size.half] = x1
    keep_other[slot, :, size.half :] = ranks


def first_kernel(size, where, x_in, again_own, mine, other, out, hist_mine, hist_other, keep_mine, keep_other, sems):
    place = Place(where)
    x0, x1, payload = read(size, x_in)
    y0, y1, ranks, payload = section_step(
        size, place, place.section, 0, x0, x1, again_own[0], payload, mine, other, 0
    )
    keep(size, keep_mine, keep_other, 0, x0, x1, ranks)
    copies = [
        pltpu.make_async_copy(keep_mine, hist_mine.at[pl.ds(0, 1)], sems.at[0]),
        pltpu.make_async_copy(keep_other, hist_other.at[pl.ds(0, 1)], sems.at[1]),
    ]
    for copy in copies:
        copy.start()
    write(size, out, y0, y1, payload)
    for copy in copies:
        copy.wait()


def second_kernel(size, where, x_in, again_peer, mine, other, out, passed):
    place = Place(where)
    x0, x1, payload = read(size, x_in)
    y0, y1, ranks, sent = section_step(
        size, place, place.peer, 1, x0, x1, again_peer[0], payload, mine, other, 2
    )
    passed[0, :, : size.half] = x0
    passed[1, :, : size.half] = x1
    passed[0, :, size.half :] = ranks
    passed[1, :, size.half :] = ranks
    aligned = place.aligned
    sent = [jnp.where(aligned, sent[j], payload[j]) for j in range(size.slots)]
    write(size, out, jnp.where(aligned, y0, x0), jnp.where(aligned, y1, x1), sent)


def pair_kernel(size, step, where, x_in, feed, again_own, again_peer, mine, other, came, *rest):
    _, _, out, passed, hist_mine, hist_other, keep_mine, keep_other, sems = rest
    half, kept = size.half, size.kept
    place = Place(where)
    aligned = place.aligned
    x0, x1, payload = read(size, x_in)
    x0 = jnp.where(place.at_end, feed[:, :half], x0)
    x1 = jnp.where(place.at_end, feed[:, half:], x1)
    tick = jnp.where(aligned, 2 * step, 2 * step - 1)
    again_peer = again_peer[jnp.where(aligned, step, step - 1)]
    own = again_own[2 * step]
    at_peer = jnp.where(aligned, 0, 2)
    y0, y1, ranks, payload = section_step(
        size, place, jnp.where(aligned, place.section, place.peer), tick, x0, x1,
        jnp.where(aligned, own, again_peer), payload, mine, other, at_peer,
    )
    z0, z1, ranks_b, payload = section_step(
        size, place, jnp.where(aligned, place.peer, place.section), tick + 1, y0, y1,
        jnp.where(aligned, again_peer, own), payload, mine, other, 2 - at_peer,
    )
    keep(
        size, keep_mine, keep_other, 0,
        jnp.where(aligned, x0, y0), jnp.where(aligned, x1, y1), jnp.where(aligned, ranks, ranks_b),
    )
    keep_mine[1] = came[0, :, :half]
    keep_other[1] = came[1, :, :kept]
    odd = jnp.where(aligned, 2 * step - 3 if step > 1 else size.ticks, 2 * step - 1)
    copies = [
        pltpu.make_async_copy(keep_mine.at[pl.ds(0, 1)], hist_mine.at[pl.ds(2 * step, 1)], sems.at[0]),
        pltpu.make_async_copy(keep_other.at[pl.ds(0, 1)], hist_other.at[pl.ds(2 * step, 1)], sems.at[1]),
        pltpu.make_async_copy(keep_mine.at[pl.ds(1, 1)], hist_mine.at[pl.ds(odd, 1)], sems.at[2]),
        pltpu.make_async_copy(keep_other.at[pl.ds(1, 1)], hist_other.at[pl.ds(odd, 1)], sems.at[3]),
    ]
    for copy in copies:
        copy.start()
    ranks_peer = jnp.where(aligned, ranks_b, ranks)
    passed[0, :, :half] = jnp.where(aligned, y0, x0)
    passed[1, :, :half] = jnp.where(aligned, y1, x1)
    passed[0, :, half:kept] = ranks_peer
    passed[1, :, half:kept] = ranks_peer
    if step + 1 == size.steps:
        passed[0, :, kept:] = z0
        passed[1, :, kept:] = z1
    write(size, out, z0, z1, payload)
    for copy in copies:
        copy.wait()


def last_kernel(size, where, x_in, feed, again_peer, mine, other, passed):
    half, kept = size.half, size.kept
    place = Place(where)
    x0, x1, payload = read(size, x_in)
    x0 = jnp.where(place.at_end, feed[:, :half], x0)
    x1 = jnp.where(place.at_end, feed[:, half:], x1)
    y0, y1, ranks, _ = section_step(
        size, place, place.peer, size.ticks - 1, x0, x1, again_peer[size.steps - 1], payload, mine, other, 2
    )
    passed[0, :, :half] = x0
    passed[1, :, :half] = x1
    passed[0, :, half:kept] = ranks
    passed[1, :, half:kept] = ranks
    passed[0, :, kept:] = y0
    passed[1, :, kept:] = y1


def end_kernel(size, where, mine, sent, got, late, late_got, last, last_got, stash, squeeze_grad, expand_grad, fwd, bwd):
    ticks, half, kept, rank = size.ticks, size.half, size.kept, size.rank
    place = Place(where)
    forward = place.forward

    def block(role, t, cols, part=0):
        aligned = place.side == role
        here = place.role == role

        def pick(own, other):
            return jnp.where(here, own, other)

        def hist():
            own = mine[t, :, cols] if part == 0 else sent[t, :, cols]
            return pick(own, got[t, :, cols])

        if t == ticks - 3:
            return jnp.where(aligned, pick(late[part, :, cols], late_got[:, cols]), hist())
        if t == ticks - 1:
            return jnp.where(
                aligned,
                pick(last[part, :, cols], last_got[:, cols]),
                pick(late[part, :, cols], late_got[:, cols]),
            )
        return hist()

    lag = 2 * (place.sections - 1 - place.section) + 1
    ranks = jnp.concatenate([block(1, t, slice(half, kept), 1) for t in range(ticks)], axis=0)
    regated, hidden_grad = ranks[:, :rank], ranks[:, rank:]
    for lo in range(0, half, CHUNK):
        cols = slice(lo, min(lo + CHUNK, half))
        a = [block(0, t, cols) for t in range(ticks - 1)]
        u = []
        for t in range(ticks):
            at = stash[t, :, cols]
            for j in range((t + 1) // 2):
                at = jnp.where(lag == 2 * j + 1, a[t - 2 * j - 1], at)
            u.append(at)
        u = jnp.concatenate(u, axis=0)
        g = jnp.concatenate([block(1, t, cols) for t in range(ticks)], axis=0)
        squeeze_grad[:, cols] = (dot(hidden_grad, u, TN) * size.in_scale).astype(jnp.bfloat16)
        expand_grad[:, cols] = (dot(regated, g, TN) * size.out_scale).astype(jnp.bfloat16)

    def carry(role):
        here = place.role == role
        early = jnp.where(here, late[0, :, kept:], late_got[:, kept:])
        final = jnp.where(here, last[0, :, kept:], last_got[:, kept:])
        return jnp.where(place.side == role, final, early)

    fwd[...] = carry(0)
    bwd[...] = carry(1)


def params():
    return pltpu.CompilerParams(vmem_limit_bytes=24 * 1024 * 1024)


def shape(*dims, dtype=jnp.bfloat16):
    return jax.ShapeDtypeStruct(dims, dtype)


def shards(
    activations,
    cotangent,
    squeeze_old,
    expand_old,
    squeeze_late,
    expand_late,
    stash_inputs,
    forward_in,
    backward_in,
):
    sections = lax.axis_size("pipe")
    replicas = lax.axis_size("dp")
    section = lax.axis_index("pipe")
    role = lax.axis_index("mp")
    half, rank = squeeze_old.shape[1], squeeze_old.shape[2]
    ticks, rows = stash_inputs.shape[2], stash_inputs.shape[3]
    size = Sizes(ticks, rows, rank, half)
    bf16, f32 = jnp.bfloat16, jnp.float32
    everyone = range(sections)

    def send(x, pairs):
        return lax.ppermute(x, ("pipe", "mp"), [(a * 2 + b, c * 2 + d) for (a, b), (c, d) in pairs])

    def swap(x):
        return lax.ppermute(x, "mp", [(0, 1), (1, 0)])

    def to_peer(x, senders):
        return send(x, [((s, c), (s ^ 1, c)) for s, c in senders])

    def tied(x, *others):
        return lax.optimization_barrier((x, *others))[0]

    def call(body, name, outs, in_specs, out_specs, scratch=(), aliases=None):
        return pl.pallas_call(
            functools.partial(body, size),
            out_shape=outs,
            in_specs=in_specs,
            out_specs=out_specs,
            scratch_shapes=list(scratch),
            input_output_aliases=aliases or {},
            compiler_params=params(),
            cost_estimate=pl.CostEstimate(
                flops=8 * rows * size.width * rank, bytes_accessed=8 * size.width * rank, transcendentals=0
            ),
            name=name,
        )

    side = section % 2
    where = jnp.stack([section, role, jnp.int32(sections), side]).astype(jnp.int32)
    forward = role == 0
    squeeze, expand = squeeze_old[0].T, expand_old[0]
    stash = stash_inputs[0, 0]
    fwd_in, bwd_in = forward_in[0, 0], backward_in[0, 0]
    acts, cots = activations[0], cotangent[0]
    both = [(s, c) for s in everyone for c in (0, 1)]

    squeeze_peer, expand_peer = to_peer(squeeze, both), to_peer(expand, both)
    own = jnp.stack([squeeze, expand])
    other = swap(own)
    mine_all = jnp.concatenate([own, squeeze_peer[None], expand_peer[None]], axis=0)
    other_all = jnp.concatenate([other, swap(squeeze_peer)[None], swap(expand_peer)[None]], axis=0)

    partial = call(
        stash_kernel, "stashed", shape(ticks, rows, rank, dtype=f32), [VMEM, VMEM], VMEM
    )(stash, squeeze)
    again_own = partial + swap(partial)
    again_peer = to_peer(again_own[1::2], [(s, 1) for s in everyone])

    entering_full = jnp.concatenate(
        [jnp.where(forward, acts, cots), swap(jnp.where(forward, cots, acts))], axis=1
    )
    per_tick = rows // acts.shape[0]

    def fed(step):
        pieces = []
        for m in range(per_tick):
            blocks = [b for b in (2 * step, 2 * step - 1) if 0 <= b < ticks]
            moves = [((b * per_tick + m, 0), (b % 2, 0)) for b in blocks]
            moves += [((b * per_tick + m, 1), (sections - 1 - b % 2, 1)) for b in blocks]
            came = send(entering_full, [(a, b) for a, b in moves if a != b])
            for a, b in moves:
                if a == b:
                    here = jnp.logical_and(section == a[0], role == a[1])
                    came = jnp.where(here, entering_full, came)
            pieces.append(came)
        return jnp.concatenate(pieces, axis=0)

    first_cots, first_acts = [], []
    for i in range(per_tick):
        halves = [send(cots, [((i, c), (sections - 1, 1))]) for c in (1, 0)]
        first_cots.append(jnp.concatenate(halves, axis=1))
        first_acts.append(entering_full if i == 0 else send(entering_full, [((i, 0), (0, 0))]))
    first_feed = jnp.where(forward, jnp.concatenate(first_acts, axis=0), jnp.concatenate(first_cots, axis=0))
    first_end = section == jnp.where(forward, 0, sections - 1)
    x = jnp.concatenate([jnp.where(forward, fwd_in, bwd_in), swap(jnp.where(forward, bwd_in, fwd_in))], axis=1)
    x = jnp.concatenate([jnp.where(first_end, first_feed, x), jnp.zeros((rows, size.message - size.width), bf16)], axis=1)
    feeds = {1: fed(1), 2: fed(2)}

    hist_shapes = (shape(ticks + 1, rows, half), shape(ticks + 1, rows, size.kept))

    def scratch(n):
        return (
            pltpu.VMEM((n, rows, half), bf16),
            pltpu.VMEM((n, rows, size.kept), bf16),
            pltpu.SemaphoreType.DMA((2 * n,)),
        )

    def averaged(old, late):
        if replicas == 2:
            total = late.astype(f32) + lax.ppermute(late, "dp", [(0, 1), (1, 0)]).astype(f32)
        else:
            total = lax.psum(late, "dp").astype(f32)
        return (old.astype(f32) - STEP_RATE * total / replicas).astype(bf16)

    squeeze_new = averaged(squeeze, squeeze_late[0, 0].T)
    expand_new = averaged(expand, expand_late[0, 0])

    ring = (
        [((s, 0), (s + 2, 0)) for s in range(sections - 2)]
        + [((sections - 2, 0), (sections - 1, 1)), ((sections - 1, 0), (sections - 2, 1))]
        + [((s, 1), (s - 2, 1)) for s in range(2, sections)]
    )
    aligned = [(s, s % 2) for s in everyone]
    late_ones = [(s, 1 - s % 2) for s in everyone]

    x, hist_mine, hist_other = call(
        first_kernel, "first", (shape(rows, size.message), *hist_shapes),
        [SMEM, VMEM, VMEM, VMEM, VMEM], (VMEM, ANY, ANY), scratch(1),
    )(where, x, again_own, own, other)
    x, passed = call(
        second_kernel, "second", (shape(rows, size.message), shape(2, rows, size.kept)),
        [SMEM, VMEM, VMEM, VMEM, VMEM], (VMEM, VMEM),
    )(where, tied(x, feeds[1], feeds[2]), again_peer, mine_all, other_all)
    came = to_peer(passed, aligned)
    x = send(x, ring)
    for step in range(1, size.steps):
        final = step + 1 == size.steps
        if step == 2:
            x = tied(x, squeeze_new)
        if step == 3:
            x = tied(x, expand_new)
        x, passed, hist_mine, hist_other = call(
            lambda size, *refs, step=step: pair_kernel(size, step, *refs), f"pair{step}",
            (
                shape(rows, size.message),
                shape(2, rows, size.kept + (half if final else 0)),
                *hist_shapes,
            ),
            [SMEM, VMEM, VMEM, VMEM, VMEM, VMEM, VMEM, VMEM, ANY, ANY], (VMEM, VMEM, ANY, ANY),
            scratch(2), {8: 2, 9: 3},
        )(where, x, feeds[step], again_own, again_peer, mine_all, other_all, came, hist_mine, hist_other)
        if step + 2 not in feeds and step + 2 <= size.steps:
            feeds[step + 2] = fed(step + 2)
        x = send(x, ring)
        came = to_peer(passed, both)
    hist_got = swap(hist_other)
    late, late_got = came, swap(came[1])
    passed = call(
        last_kernel, "last", shape(2, rows, size.kept + half),
        [SMEM, VMEM, VMEM, VMEM, VMEM, VMEM], VMEM,
    )(where, x, feeds[size.steps], again_peer, mine_all, other_all)
    last = to_peer(passed, late_ones)
    last_got = swap(last[1])
    squeeze_grad, expand_grad, fwd_carry, bwd_carry = call(
        end_kernel, "finish",
        (shape(rank, half), shape(rank, half), shape(rows, half), shape(rows, half)),
        [SMEM] + [VMEM] * 8, (VMEM,) * 4,
    )(where, hist_mine, hist_other, hist_got, late, late_got, last, last_got, stash)
    return (
        squeeze_new.T[None],
        expand_new[None],
        squeeze_grad.T[None, None],
        expand_grad[None, None],
        fwd_carry[None, None],
        bwd_carry[None, None],
    )


def solution(mesh):
    placed = (
        P("dp", "pipe", "mp"),
        P("dp", "pipe", "mp"),
        P("pipe", "mp", None),
        P("pipe", None, "mp"),
        P("dp", "pipe", "mp", None),
        P("dp", "pipe", None, "mp"),
        P("dp", "pipe", None, None, "mp"),
        P("dp", "pipe", None, "mp"),
        P("dp", "pipe", None, "mp"),
    )
    return jax.shard_map(
        shards,
        mesh=mesh,
        in_specs=placed,
        out_specs=(
            P("pipe", "mp", None),
            P("pipe", None, "mp"),
            P("dp", "pipe", "mp", None),
            P("dp", "pipe", None, "mp"),
            P("dp", "pipe", None, "mp"),
            P("dp", "pipe", None, "mp"),
        ),
        check_vma=False,
    )
```

time: 241 us -> 118 us (0.49)
  blocking collectives: 96.7 us -> 0 us
  matrix products: 47.1 us -> 0 us
  waiting for transfers between devices: 20.4 us -> 57.4 us
  Pallas kernels: 0 us -> 16.1 us
  between operations: 14.5 us -> 1 us
  starting transfers between devices: 45 us -> 35 us
  local copies, waits for them, and re-layouts: 6.82 us -> 2.27 us
  other arithmetic: 9.29 us -> 6.12 us
    all_gather x2 -> x0, blocking collectives: 53.4 us -> none  [the longest x1 28.5 us: shards(): lax.all_gather(cotangent, 'pipe', axis=1, tiled=True)]
    dot_general x56 -> x0, matrix products: 47.1 us -> none  [the longest x8 18.4 us: shards(): lax.dot_general(saved, hidden_grad, (((0,), (0,)), ((), ())), preferred_e...]
    psum x8 -> x0, blocking collectives: 43.3 us -> none  [shards(): again_total, grad_total = lax.psum((again_partial, grad_partial), 'mp')]
    ppermute x14 -> x29, waiting for transfers between devices: 20.4 us -> 57.4 us  [the longest x18 56.2 us: send(): lax.ppermute(x, ('pipe', 'mp'), [(a * 2 + b, c * 2 + d) for (a, b), (c, d...]
    pallas_call x0 -> x8, Pallas kernels: none -> 16.1 us  [the longest x3 9.06 us: shards(): call(lambda size, *refs, step=step: pair_kernel(size, step, *refs), f'pai...]
    ppermute x14 -> x29, starting transfers between devices: 44.9 us -> 35 us  [the longest x18 25.5 us: send(): lax.ppermute(x, ('pipe', 'mp'), [(a * 2 + b, c * 2 + d) for (a, b), (c, d...]
    unnamed x8 -> x0, other arithmetic: 5.53 us -> none
    unnamed x55 -> x14, local copies, waits for them, and re-layouts: 6.18 us -> 2.22 us
  transfers between devices with their start and end apart: 15 -> 29, of which waited for: 10 -> 11; matrix products, arithmetic and copies ran while one was open for 23% -> 5% of each run, Pallas kernels for 0% -> 9%
where the time goes in v2:
time: 118 us
  waiting for transfers between devices  57.4 us (49%)
  starting transfers between devices  35 us (30%)
  Pallas kernels  16.1 us (14%)
  other arithmetic  6.12 us (5%)
  local copies, waits for them, and re-layouts  2.27 us (2%)
    ppermute x18, waiting for transfers between devices, send(): lax.ppermute(x, ('pipe', 'mp'), [(a * 2 + b, c * 2 + d) for (a, b), (c, d...  56.2 us
    ppermute x18, starting transfers between devices, send(): lax.ppermute(x, ('pipe', 'mp'), [(a * 2 + b, c * 2 + d) for (a, b), (c, d...  25.5 us
    pallas_call x3, Pallas kernels, shards(): call(lambda size, *refs, step=step: pair_kernel(size, step, *refs), f'pai...  9.06 us
    ppermute x9, starting transfers between devices, swap(): return lax.ppermute(x, 'mp', [(0, 1), (1, 0)])  6.94 us
    ppermute x2, starting transfers between devices, averaged(): lax.ppermute(late, 'dp', [(0, 1), (1, 0)]).astype(f32)  2.56 us
  transfers between devices with their start and end apart: 29, of which 11 were waited for; matrix products, arithmetic and copies ran while one was open for 5% of the time, Pallas kernels for 9%

profile of v2, /device:TPU:25, one launch (start us, length us, event | category | flops | bytes accessed | tf_op | source)
XLA Modules:
  0.0 117.9 jit_solution(1665132184774215312)
XLA Ops:
  0.6 0.8 collective-permute-start.3
  1.4 0.7 collective-permute-start.4
  2.1 1.0 bitcast_select_fusion.1
  3.1 0.7 collective-permute-start.2
  3.9 1.6 %select_bitcast_fusion.1 = (bf16[16,3584]{1,0:T(8,128)(2,1)S(1)}, bf16[16,3584]{1,0:T(8,128)(2,1)}) fusion(bf16[1,1,16,3584]{3,2,1,0:T(8,128)(2,1)} %param.16, bf16[1,1,16,3584]{3,2,1,0:T(8,128)(2,1)} %param.17, pred[]{:T(512)S(6)} %eq.12), kind=kLoop, calls=%fused_computation.14 | loop fusion | flops 114688 | bytes 458753 | tf_op jit(solution)/shard_map/jit(_where)/select_n | solution.py:370
  5.5 1.0 copy-done
  6.5 1.2 copy-done.2
  8.1 0.5 collective-permute-start.6
  8.6 1.3 %collective-permute-start.8 = (bf16[16,7168]{1,0:T(8,128)(2,1)S(1)}, bf16[16,7168]{1,0:T(8,128)(2,1)S(1)}, u32[]{:S(2)}, u32[]{:S(2)}) collective-permute-start(bf16[16,7168]{1,0:T(8,128)(2,1)S(1)} %pad_maximum_fusion.3), channel_id=1, source_target_pairs={{8,0},{9,29},{5,25},{10,2},{11,31},{7,27}} | collective-permute-start | bytes 688136 | tf_op jit(solution)/shard_map/ppermute | solution.py:297
  10.1 1.9 %collective-permute-start.11 = (bf16[64,3584]{1,0:T(8,128)(2,1)S(1)}, bf16[64,3584]{1,0:T(8,128)(2,1)S(1)}, u32[]{:S(2)}, u32[]{:S(2)}) collective-permute-start(bf16[64,3584]{1,0:T(8,128)(2,1)S(1)} %bitcast.48), channel_id=1, source_target_pairs={{0,4},{1,5},{4,0},{5,1},{8,12},{9,13},{12,8},{13,9},{16,20},{17,21... | collective-permute-start | bytes 1376264 | tf_op jit(solution)/shard_map/ppermute | solution.py:297
  12.0 0.8 add.18.again_own.refs_3_
  13.2 1.3 %collective-permute-start = (bf16[64,3584]{1,0:T(8,128)(2,1)S(1)}, bf16[64,3584]{1,0:T(8,128)(2,1)S(1)}, u32[]{:S(2)}, u32[]{:S(2)}) collective-permute-start(bf16[64,3584]{1,0:T(8,128)(2,1)S(1)} %bitcast.53), channel_id=1, source_target_pairs={{0,2},{2,0},{1,3},{3,1},{4,6},{6,4},{5,7},{7,5},{8,10},{10,8},{9,1... | collective-permute-start | bytes 1376264 | tf_op jit(solution)/shard_map/ppermute | solution.py:385
  14.5 3.7 %collective-permute-done.8 = bf16[16,7168]{1,0:T(8,128)(2,1)S(1)} collective-permute-done((bf16[16,7168]{1,0:T(8,128)(2,1)S(1)}, bf16[16,7168]{1,0:T(8,128)(2,1)S(1)}, u32[]{:S(2)}, u32[]{:S(2)}) %collective-permute-start.8) | collective-permute-done | bytes 229408 | tf_op jit(solution)/shard_map/ppermute | solution.py:297
  18.2 2.8 %collective-permute-start.10 = (f32[4,16,64]{2,1,0:T(8,128)S(1)}, f32[4,16,64]{2,1,0:T(8,128)S(1)}, u32[]{:S(2)}, u32[]{:S(2)}) collective-permute-start(f32[4,16,64]{2,1,0:T(8,128)S(1)} %slice.9), channel_id=1, source_target_pairs={{1,5},{5,1},{9,13},{13,9},{17,21},{21,17},{25,29},{29,25},{3,7},{7... | collective-permute-start | bytes 49160 | tf_op jit(solution)/shard_map/ppermute | solution.py:297
  21.2 4.2 %collective-permute-done.11 = bf16[64,3584]{1,0:T(8,128)(2,1)S(1)} collective-permute-done((bf16[64,3584]{1,0:T(8,128)(2,1)S(1)}, bf16[64,3584]{1,0:T(8,128)(2,1)S(1)}, u32[]{:S(2)}, u32[]{:S(2)}) %collective-permute-start.11) | collective-permute-done | bytes 458784 | tf_op jit(solution)/shard_map/ppermute | solution.py:297
  25.5 0.6 collective-permute-start.13
  26.1 9.2 %collective-permute-done.12 = bf16[64,3584]{1,0:T(8,128)(2,1)S(1)} collective-permute-done((bf16[64,3584]{1,0:T(8,128)(2,1)S(1)}, bf16[64,3584]{1,0:T(8,128)(2,1)S(1)}, u32[]{:S(2)}, u32[]{:S(2)}) %collective-permute-start.12) | collective-permute-done | bytes 458784 | tf_op jit(solution)/shard_map/ppermute | solution.py:297
  35.3 0.6 collective-permute-start.14
  36.2 1.3 %collective-permute-start.9 = (bf16[16,7168]{1,0:T(8,128)(2,1)S(1)}, bf16[16,7168]{1,0:T(8,128)(2,1)S(1)}, u32[]{:S(2)}, u32[]{:S(2)}) collective-permute-start(bf16[16,7168]{1,0:T(8,128)(2,1)S(1)} %pad_maximum_fusion.3), channel_id=1, source_target_pairs={{16,0},{12,4},{17,29},{13,25},{18,2},{14,6},{19,31},{15,27}} | collective-permute-start | bytes 688136 | tf_op jit(solution)/shard_map/ppermute | solution.py:297
  37.7 1.7 %first.1 = (bf16[16,7680]{1,0:T(8,128)(2,1)S(1)}, bf16[9,16,3584]{2,1,0:T(8,128)(2,1)S(1)}, bf16[9,16,3712]{2,1,0:T(8,128)(2,1)S(1)}) custom-call(s32[4]{0:T(128)S(1)} %pad_add_fusion.where.refs_0_, bf16[16,7680]{1,0:T(8,128)(2,1)S(1)} %concatenate.22.x_in, f32[8,16,64]{2,1,0:T(8,128)S(1)} %add.18.again_own.refs_3_, ...), custom_call_target="tpu_custom_call" | custom-call | flops 58720256 | bytes 3670016 | tf_op jit(solution)/shard_map/first/pallas_call | solution.py:401
  39.4 5.3 %collective-permute-done.9.refs_2_ = bf16[16,7168]{1,0:T(8,128)(2,1)S(1)} collective-permute-done((bf16[16,7168]{1,0:T(8,128)(2,1)S(1)}, bf16[16,7168]{1,0:T(8,128)(2,1)S(1)}, u32[]{:S(2)}, u32[]{:S(2)}) %collective-permute-start.9) | collective-permute-done | bytes 229408 | tf_op jit(solution)/shard_map/ppermute | solution.py:297
  44.7 1.4 %second.1 = (bf16[16,7680]{1,0:T(8,128)(2,1)S(1)}, bf16[2,16,3712]{2,1,0:T(8,128)(2,1)S(1)}) custom-call(s32[4]{0:T(128)S(1)} %pad_add_fusion.where.refs_0_, bf16[16,7680]{1,0:T(8,128)(2,1)S(1)} %get-tuple-element.31.x_in, f32[4,16,64]{2,1,0:T(8,128)S(1)} %collective-permute-done.10.again_peer.refs_4_, ...), custom_call_target="tpu_custom_call" | custom-call | flops 58720256 | bytes 3670016 | tf_op jit(solution)/shard_map/second/pallas_call | solution.py:405
  46.1 1.9 %collective-permute-start.15 = (bf16[16,7680]{1,0:T(8,128)(2,1)S(1)}, bf16[16,7680]{1,0:T(8,128)(2,1)S(1)}, u32[]{:S(2)}, u32[]{:S(2)}) collective-permute-start(bf16[16,7680]{1,0:T(8,128)(2,1)S(1)} %get-tuple-element.32), channel_id=1, source_target_pairs={{0,8},{4,12},{8,16},{12,20},{16,24},{20,28},{24,29},{28,25},{9,1},... | collective-permute-start | bytes 737288 | tf_op jit(solution)/shard_map/ppermute | solution.py:297
  48.1 1.3 %collective-permute-start.16 = (bf16[2,16,3712]{2,1,0:T(8,128)(2,1)S(1)}, bf16[2,16,3712]{2,1,0:T(8,128)(2,1)S(1)}, u32[]{:S(2)}, u32[]{:S(2)}) collective-permute-start(bf16[2,16,3712]{2,1,0:T(8,128)(2,1)S(1)} %get-tuple-element.33), channel_id=1, source_target_pairs={{0,4},{5,1},{8,12},{13,9},{16,20},{21,17},{24,28},{29,25},{2,6},{7... | collective-permute-start | bytes 712712 | tf_op jit(solution)/shard_map/ppermute | solution.py:297
  49.4 1.3 %collective-permute-start.1 = (bf16[64,3584]{1,0:T(8,128)(2,1)S(1)}, bf16[64,3584]{1,0:T(8,128)(2,1)S(1)}, u32[]{:S(2)}, u32[]{:S(2)}) collective-permute-start(bf16[64,3584]{1,0:T(8,128)(2,1)S(1)} %bitcast.54), channel_id=1, source_target_pairs={{0,2},{2,0},{1,3},{3,1},{4,6},{6,4},{5,7},{7,5},{8,10},{10,8},{9,1... | collective-permute-start | bytes 1376264 | tf_op jit(solution)/shard_map/ppermute | solution.py:385
  50.6 4.0 %collective-permute-start.20 = (bf16[16,7168]{1,0:T(8,128)(2,1)S(1)}, bf16[16,7168]{1,0:T(8,128)(2,1)S(1)}, u32[]{:S(2)}, u32[]{:S(2)}) collective-permute-start(bf16[16,7168]{1,0:T(8,128)(2,1)S(1)} %pad_maximum_fusion.3), channel_id=1, source_target_pairs={{24,0},{20,4},{25,29},{21,25},{26,2},{22,6},{27,31},{23,27}} | collective-permute-start | bytes 688136 | tf_op jit(solution)/shard_map/ppermute | solution.py:297
  54.6 4.3 %collective-permute-done.16.refs_7_ = bf16[2,16,3712]{2,1,0:T(8,128)(2,1)S(1)} collective-permute-done((bf16[2,16,3712]{2,1,0:T(8,128)(2,1)S(1)}, bf16[2,16,3712]{2,1,0:T(8,128)(2,1)S(1)}, u32[]{:S(2)}, u32[]{:S(2)}) %collective-permute-start.16) | collective-permute-done | bytes 237600 | tf_op jit(solution)/shard_map/ppermute | solution.py:297
  58.9 3.0 %pair1.1 = (bf16[16,7680]{1,0:T(8,128)(2,1)S(1)}, bf16[2,16,3712]{2,1,0:T(8,128)(2,1)S(1)}, bf16[9,16,3584]{2,1,0:T(8,128)(2,1)S(1)}, bf16[9,16,3712]{2,1,0:T(8,128)(2,1)S(1)}) custom-call(s32[4]{0:T(128)S(1)} %pad_add_fusion.where.refs_0_, bf16[16,7680]{1,0:T(8,128)(2,1)S(1)} %collective-permute-done.15.refs_1_, ...), custom_call_target="tpu_custom_call", output_to_operand_aliasing={{2}: (8, {}), {3}: (9, {})} | custom-call | flops 58720256 | bytes 3670016 | tf_op jit(solution)/shard_map/pair1/pallas_call | solution.py:417
  62.0 1.9 %collective-permute-start.17 = (bf16[16,7680]{1,0:T(8,128)(2,1)S(1)}, bf16[16,7680]{1,0:T(8,128)(2,1)S(1)}, u32[]{:S(2)}, u32[]{:S(2)}) collective-permute-start(bf16[16,7680]{1,0:T(8,128)(2,1)S(1)} %get-tuple-element.36), channel_id=1, source_target_pairs={{0,8},{4,12},{8,16},{12,20},{16,24},{20,28},{24,29},{28,25},{9,1},... | collective-permute-start | bytes 737288 | tf_op jit(solution)/shard_map/ppermute | solution.py:297
  64.0 1.0 subtract_convert_fusion.1
  65.0 6.6 %collective-permute-done.17.refs_1_ = bf16[16,7680]{1,0:T(8,128)(2,1)S(1)} collective-permute-done((bf16[16,7680]{1,0:T(8,128)(2,1)S(1)}, bf16[16,7680]{1,0:T(8,128)(2,1)S(1)}, u32[]{:S(2)}, u32[]{:S(2)}) %collective-permute-start.17) | collective-permute-done | bytes 245792 | tf_op jit(solution)/shard_map/ppermute | solution.py:297
  71.6 3.0 %pair2.1 = (bf16[16,7680]{1,0:T(8,128)(2,1)S(1)}, bf16[2,16,3712]{2,1,0:T(8,128)(2,1)S(1)}, bf16[9,16,3584]{2,1,0:T(8,128)(2,1)S(1)}, bf16[9,16,3712]{2,1,0:T(8,128)(2,1)S(1)}) custom-call(s32[4]{0:T(128)S(1)} %pad_add_fusion.where.refs_0_, bf16[16,7680]{1,0:T(8,128)(2,1)S(1)} %collective-permute-done.17.refs_1_, ...), custom_call_target="tpu_custom_call", output_to_operand_aliasing={{2}: (8, {}), {3}: (9, {})} | custom-call | flops 58720256 | bytes 3670016 | tf_op jit(solution)/shard_map/pair2/pallas_call | solution.py:417
  74.6 1.9 %collective-permute-start.19 = (bf16[16,7680]{1,0:T(8,128)(2,1)S(1)}, bf16[16,7680]{1,0:T(8,128)(2,1)S(1)}, u32[]{:S(2)}, u32[]{:S(2)}) collective-permute-start(bf16[16,7680]{1,0:T(8,128)(2,1)S(1)} %get-tuple-element.41), channel_id=1, source_target_pairs={{0,8},{4,12},{8,16},{12,20},{16,24},{20,28},{24,29},{28,25},{9,1},... | collective-permute-start | bytes 737288 | tf_op jit(solution)/shard_map/ppermute | solution.py:297
  76.8 1.0 subtract_convert_fusion
  77.8 6.7 %collective-permute-done.19.refs_1_ = bf16[16,7680]{1,0:T(8,128)(2,1)S(1)} collective-permute-done((bf16[16,7680]{1,0:T(8,128)(2,1)S(1)}, bf16[16,7680]{1,0:T(8,128)(2,1)S(1)}, u32[]{:S(2)}, u32[]{:S(2)}) %collective-permute-start.19) | collective-permute-done | bytes 245792 | tf_op jit(solution)/shard_map/ppermute | solution.py:297
  84.5 3.0 %pair3.1 = (bf16[16,7680]{1,0:T(8,128)(2,1)S(1)}, bf16[2,16,7296]{2,1,0:T(8,128)(2,1)S(1)}, bf16[9,16,3584]{2,1,0:T(8,128)(2,1)S(1)}, bf16[9,16,3712]{2,1,0:T(8,128)(2,1)S(1)}) custom-call(s32[4]{0:T(128)S(1)} %pad_add_fusion.where.refs_0_, bf16[16,7680]{1,0:T(8,128)(2,1)S(1)} %collective-permute-done.19.refs_1_, ...), custom_call_target="tpu_custom_call", output_to_operand_aliasing={{2}: (8, {}), {3}: (9, {})} | custom-call | flops 58720256 | bytes 3670016 | tf_op jit(solution)/shard_map/pair3/pallas_call | solution.py:417
  87.5 0.8 collective-permute-start.23
  88.4 1.9 %collective-permute-start.25 = (bf16[16,7680]{1,0:T(8,128)(2,1)S(1)}, bf16[16,7680]{1,0:T(8,128)(2,1)S(1)}, u32[]{:S(2)}, u32[]{:S(2)}) collective-permute-start(bf16[16,7680]{1,0:T(8,128)(2,1)S(1)} %get-tuple-element.49), channel_id=1, source_target_pairs={{0,8},{4,12},{8,16},{12,20},{16,24},{20,28},{24,29},{28,25},{9,1},... | collective-permute-start | bytes 737288 | tf_op jit(solution)/shard_map/ppermute | solution.py:297
  90.3 1.3 %collective-permute-start.26 = (bf16[16,7168]{1,0:T(8,128)(2,1)S(1)}, bf16[16,7168]{1,0:T(8,128)(2,1)S(1)}, u32[]{:S(2)}, u32[]{:S(2)}) collective-permute-start(bf16[16,7168]{1,0:T(8,128)(2,1)S(1)} %pad_maximum_fusion.3), channel_id=1, source_target_pairs={{28,4},{29,25},{30,6},{31,27}} | collective-permute-start | bytes 688136 | tf_op jit(solution)/shard_map/ppermute | solution.py:297
  91.6 2.7 %collective-permute-start.22 = (bf16[9,16,3712]{2,1,0:T(8,128)(2,1)S(1)}, bf16[9,16,3712]{2,1,0:T(8,128)(2,1)S(1)}, u32[]{:S(2)}, u32[]{:S(2)}) collective-permute-start(bf16[9,16,3712]{2,1,0:T(8,128)(2,1)S(1)} %get-tuple-element.47.sent), channel_id=1, source_target_pairs={{0,1},{1,0},{2,3},{3,2},{4,5},{5,4},{6,7},{7,6},{8,9},{9,8},{10,11... | collective-permute-start | bytes 3207176 | tf_op jit(solution)/shard_map/ppermute | solution.py:300
  94.2 7.5 %collective-permute-done.26.feed = bf16[16,7168]{1,0:T(8,128)(2,1)S(1)} collective-permute-done((bf16[16,7168]{1,0:T(8,128)(2,1)S(1)}, bf16[16,7168]{1,0:T(8,128)(2,1)S(1)}, u32[]{:S(2)}, u32[]{:S(2)}) %collective-permute-start.26) | collective-permute-done | bytes 229408 | tf_op jit(solution)/shard_map/ppermute | solution.py:297
  101.7 3.3 %collective-permute-done.25.x_in = bf16[16,7680]{1,0:T(8,128)(2,1)S(1)} collective-permute-done((bf16[16,7680]{1,0:T(8,128)(2,1)S(1)}, bf16[16,7680]{1,0:T(8,128)(2,1)S(1)}, u32[]{:S(2)}, u32[]{:S(2)}) %collective-permute-start.25) | collective-permute-done | bytes 245792 | tf_op jit(solution)/shard_map/ppermute | solution.py:297
  105.1 1.4 %last.1 = bf16[2,16,7296]{2,1,0:T(8,128)(2,1)S(1)} custom-call(s32[4]{0:T(128)S(1)} %pad_add_fusion.where.refs_0_, bf16[16,7680]{1,0:T(8,128)(2,1)S(1)} %collective-permute-done.25.x_in, bf16[16,7168]{1,0:T(8,128)(2,1)S(1)} %collective-permute-done.26.feed, f32[4,16,64]{2,1,0:T(8,128)S(1)} %collective-permute-done.10.again_peer.refs_4_, ...), custom_call_target="tpu_custom_call" | custom-call | flops 58720256 | bytes 3670016 | tf_op jit(solution)/shard_map/last/pallas_call | solution.py:433
  106.5 1.3 %collective-permute-start.27 = (bf16[2,16,7296]{2,1,0:T(8,128)(2,1)S(1)}, bf16[2,16,7296]{2,1,0:T(8,128)(2,1)S(1)}, u32[]{:S(2)}, u32[]{:S(2)}) collective-permute-start(bf16[2,16,7296]{2,1,0:T(8,128)(2,1)S(1)} %last.1), channel_id=1, source_target_pairs={{1,5},{4,0},{9,13},{12,8},{17,21},{20,16},{25,29},{28,24},{3,7},{6... | collective-permute-start | bytes 1400840 | tf_op jit(solution)/shard_map/ppermute | solution.py:297
  107.9 5.3 %collective-permute-done.27.last = bf16[2,16,7296]{2,1,0:T(8,128)(2,1)S(1)} collective-permute-done((bf16[2,16,7296]{2,1,0:T(8,128)(2,1)S(1)}, bf16[2,16,7296]{2,1,0:T(8,128)(2,1)S(1)}, u32[]{:S(2)}, u32[]{:S(2)}) %collective-permute-start.27) | collective-permute-done | bytes 466976 | tf_op jit(solution)/shard_map/ppermute | solution.py:297
  113.3 1.3 %collective-permute-start.28 = (bf16[16,7296]{1,0:T(8,128)(2,1)S(1)}, bf16[16,7296]{1,0:T(8,128)(2,1)S(1)}, u32[]{:S(2)}, u32[]{:S(2)}) collective-permute-start(bf16[16,7296]{1,0:T(8,128)(2,1)S(1)} %slice_bitcast_fusion), channel_id=1, source_target_pairs={{0,1},{1,0},{2,3},{3,2},{4,5},{5,4},{6,7},{7,6},{8,9},{9,8},{10,11... | collective-permute-start | bytes 700424 | tf_op jit(solution)/shard_map/ppermute | solution.py:300
  114.6 1.1 collective-permute-done.28.last_got
  115.7 2.2 %finish.1 = (bf16[64,3584]{1,0:T(8,128)(2,1)}, bf16[64,3584]{1,0:T(8,128)(2,1)}, bf16[16,3584]{1,0:T(8,128)(2,1)}, bf16[16,3584]{1,0:T(8,128)(2,1)}) custom-call(s32[4]{0:T(128)S(1)} %pad_add_fusion.where.refs_0_, bf16[9,16,3584]{2,1,0:T(8,128)(2,1)S(1)} %get-tuple-element.46.mine, bf16[9,16,3712]{2,1,0:T(8,128)(2,1)S(1)} %get-tuple-element.47.sent, ...), custom_call_target="tpu_custom_call" | custom-call | flops 58720256 | bytes 3670016 | tf_op jit(solution)/shard_map/finish/pallas_call | solution.py:439
  (47 shorter events, 2.0 us)
Async XLA Ops:
  0.6 9.3 %copy-start.4 = (bf16[1,64,3584]{2,1,0:T(8,128)(2,1)S(1)}, bf16[1,64,3584]{2,1,0:T(8,128)(2,1)}, u32[]{:S(2)}) copy-start(bf16[1,64,3584]{2,1,0:T(8,128)(2,1)} %param.12) | copy-start | bytes 1376260
  0.6 12.6 %collective-permute-start.3 = (bf16[16,3584]{1,0:T(8,128)(2,1)}, bf16[16,3584]{1,0:T(8,128)(2,1)S(1)}, u32[]{:S(2)}, u32[]{:S(2)}) collective-permute-start(bf16[16,3584]{1,0:T(8,128)(2,1)} %bitcast.61), channel_id=1, source_target_pairs={{1,29},{3,31}} | collective-permute-start | bytes 344072 | tf_op jit(solution)/shard_map/ppermute | solution.py:297
  1.4 11.8 %collective-permute-start.4 = (bf16[16,3584]{1,0:T(8,128)(2,1)}, bf16[16,3584]{1,0:T(8,128)(2,1)S(1)}, u32[]{:S(2)}, u32[]{:S(2)}) collective-permute-start(bf16[16,3584]{1,0:T(8,128)(2,1)} %bitcast.62), channel_id=1, source_target_pairs={{0,29},{2,31}} | collective-permute-start | bytes 344072 | tf_op jit(solution)/shard_map/ppermute | solution.py:297
  3.1 5.5 %collective-permute-start.2 = (bf16[16,3584]{1,0:T(8,128)(2,1)S(1)}, bf16[16,3584]{1,0:T(8,128)(2,1)S(1)}, u32[]{:S(2)}, u32[]{:S(2)}) collective-permute-start(bf16[16,3584]{1,0:T(8,128)(2,1)S(1)} %get-tuple-element.57), channel_id=1, source_target_pairs={{0,1},{1,0},{2,3},{3,2},{4,5},{5,4},{6,7},{7,6},{8,9},{9,8},{10,11... | collective-permute-start | bytes 344072 | tf_op jit(solution)/shard_map/ppermute | solution.py:300
  5.5 7.4 %collective-permute-start.5 = (bf16[16,3584]{1,0:T(8,128)(2,1)}, bf16[16,3584]{1,0:T(8,128)(2,1)S(1)}, u32[]{:S(2)}, u32[]{:S(2)}) collective-permute-start(bf16[16,3584]{1,0:T(8,128)(2,1)} %get-tuple-element.59), channel_id=1, source_target_pairs={{0,1},{1,0},{2,3},{3,2},{4,5},{5,4},{6,7},{7,6},{8,9},{9,8},{10,11... | collective-permute-start | bytes 344072 | tf_op jit(solution)/shard_map/ppermute | solution.py:300
  5.5 1.0 copy-start
  6.5 1.2 copy-start.2
  7.7 2.5 %copy-start.1 = (bf16[1,3584,64]{1,2,0:T(8,128)(2,1)S(1)}, bf16[1,3584,64]{1,2,0:T(8,128)(2,1)}, u32[]{:S(2)}) copy-start(bf16[1,3584,64]{1,2,0:T(8,128)(2,1)} %param.11) | copy-start | bytes 1376260
  7.7 5.5 %copy-start.5 = (bf16[1,1,3584,64]{2,3,1,0:T(8,128)(2,1)S(1)}, bf16[1,1,3584,64]{2,3,1,0:T(8,128)(2,1)}, u32[]{:S(2)}) copy-start(bf16[1,1,3584,64]{2,3,1,0:T(8,128)(2,1)} %param.13) | copy-start | bytes 1376260
  8.1 2.1 %collective-permute-start.6 = (f32[8,16,64]{2,1,0:T(8,128)S(1)}, f32[8,16,64]{2,1,0:T(8,128)}, u32[]{:S(2)}, u32[]{:S(2)}) collective-permute-start(f32[8,16,64]{2,1,0:T(8,128)S(1)} %stashed.1), channel_id=1, source_target_pairs={{0,1},{1,0},{2,3},{3,2},{4,5},{5,4},{6,7},{7,6},{8,9},{9,8},{10,11... | collective-permute-start | bytes 98312 | tf_op jit(solution)/shard_map/ppermute | solution.py:300
  8.6 9.6 %collective-permute-start.8 = (bf16[16,7168]{1,0:T(8,128)(2,1)S(1)}, bf16[16,7168]{1,0:T(8,128)(2,1)S(1)}, u32[]{:S(2)}, u32[]{:S(2)}) collective-permute-start(bf16[16,7168]{1,0:T(8,128)(2,1)S(1)} %pad_maximum_fusion.3), channel_id=1, source_target_pairs={{8,0},{9,29},{5,25},{10,2},{11,31},{7,27}} | collective-permute-start | bytes 688136 | tf_op jit(solution)/shard_map/ppermute | solution.py:297
  10.1 15.3 %collective-permute-start.11 = (bf16[64,3584]{1,0:T(8,128)(2,1)S(1)}, bf16[64,3584]{1,0:T(8,128)(2,1)S(1)}, u32[]{:S(2)}, u32[]{:S(2)}) collective-permute-start(bf16[64,3584]{1,0:T(8,128)(2,1)S(1)} %bitcast.48), channel_id=1, source_target_pairs={{0,4},{1,5},{4,0},{5,1},{8,12},{9,13},{12,8},{13,9},{16,20},{17,21... | collective-permute-start | bytes 1376264 | tf_op jit(solution)/shard_map/ppermute | solution.py:297
  12.9 23.2 %collective-permute-start.7 = (bf16[2,64,3584]{2,1,0:T(8,128)(2,1)S(1)}, bf16[2,64,3584]{2,1,0:T(8,128)(2,1)S(1)}, u32[]{:S(2)}, u32[]{:S(2)}) collective-permute-start(bf16[2,64,3584]{2,1,0:T(8,128)(2,1)S(1)} %pad_maximum_fusion.2.mine), channel_id=1, source_target_pairs={{0,1},{1,0},{2,3},{3,2},{4,5},{5,4},{6,7},{7,6},{8,9},{9,8},{10,11... | collective-permute-start | bytes 2752520 | tf_op jit(solution)/shard_map/ppermute | solution.py:300
  13.2 22.1 %collective-permute-start.12 = (bf16[64,3584]{1,0:T(8,128)(2,1)S(1)}, bf16[64,3584]{1,0:T(8,128)(2,1)S(1)}, u32[]{:S(2)}, u32[]{:S(2)}) collective-permute-start(bf16[64,3584]{1,0:T(8,128)(2,1)S(1)} %bitcast.52), channel_id=1, source_target_pairs={{0,4},{1,5},{4,0},{5,1},{8,12},{9,13},{12,8},{13,9},{16,20},{17,21... | collective-permute-start | bytes 1376264 | tf_op jit(solution)/shard_map/ppermute | solution.py:297
  13.2 50.7 %collective-permute-start = (bf16[64,3584]{1,0:T(8,128)(2,1)S(1)}, bf16[64,3584]{1,0:T(8,128)(2,1)S(1)}, u32[]{:S(2)}, u32[]{:S(2)}) collective-permute-start(bf16[64,3584]{1,0:T(8,128)(2,1)S(1)} %bitcast.53), channel_id=1, source_target_pairs={{0,2},{2,0},{1,3},{3,1},{4,6},{6,4},{5,7},{7,5},{8,10},{10,8},{9,1... | collective-permute-start | bytes 1376264 | tf_op jit(solution)/shard_map/ppermute | solution.py:385
  18.2 26.5 %collective-permute-start.10 = (f32[4,16,64]{2,1,0:T(8,128)S(1)}, f32[4,16,64]{2,1,0:T(8,128)S(1)}, u32[]{:S(2)}, u32[]{:S(2)}) collective-permute-start(f32[4,16,64]{2,1,0:T(8,128)S(1)} %slice.9), channel_id=1, source_target_pairs={{1,5},{5,1},{9,13},{13,9},{17,21},{21,17},{25,29},{29,25},{3,7},{7... | collective-permute-start | bytes 49160 | tf_op jit(solution)/shard_map/ppermute | solution.py:297
  25.5 12.0 %collective-permute-start.13 = (bf16[64,3584]{1,0:T(8,128)(2,1)S(1)}, bf16[64,3584]{1,0:T(8,128)(2,1)S(1)}, u32[]{:S(2)}, u32[]{:S(2)}) collective-permute-start(bf16[64,3584]{1,0:T(8,128)(2,1)S(1)} %collective-permute-done.11), channel_id=1, source_target_pairs={{0,1},{1,0},{2,3},{3,2},{4,5},{5,4},{6,7},{7,6},{8,9},{9,8},{10,11... | collective-permute-start | bytes 1376264 | tf_op jit(solution)/shard_map/ppermute | solution.py:300
  35.3 2.2 %collective-permute-start.14 = (bf16[64,3584]{1,0:T(8,128)(2,1)S(1)}, bf16[64,3584]{1,0:T(8,128)(2,1)S(1)}, u32[]{:S(2)}, u32[]{:S(2)}) collective-permute-start(bf16[64,3584]{1,0:T(8,128)(2,1)S(1)} %collective-permute-done.12), channel_id=1, source_target_pairs={{0,1},{1,0},{2,3},{3,2},{4,5},{5,4},{6,7},{7,6},{8,9},{9,8},{10,11... | collective-permute-start | bytes 1376264 | tf_op jit(solution)/shard_map/ppermute | solution.py:300
  36.2 8.6 %collective-permute-start.9 = (bf16[16,7168]{1,0:T(8,128)(2,1)S(1)}, bf16[16,7168]{1,0:T(8,128)(2,1)S(1)}, u32[]{:S(2)}, u32[]{:S(2)}) collective-permute-start(bf16[16,7168]{1,0:T(8,128)(2,1)S(1)} %pad_maximum_fusion.3), channel_id=1, source_target_pairs={{16,0},{12,4},{17,29},{13,25},{18,2},{14,6},{19,31},{15,27}} | collective-permute-start | bytes 688136 | tf_op jit(solution)/shard_map/ppermute | solution.py:297
  44.7 4.6 %copy-start.6 = (bf16[1,1,64,3584]{3,2,1,0:T(8,128)(2,1)S(1)}, bf16[1,1,64,3584]{3,2,1,0:T(8,128)(2,1)}, u32[]{:S(2)}) copy-start(bf16[1,1,64,3584]{3,2,1,0:T(8,128)(2,1)} %param.14) | copy-start | bytes 1376260
  46.1 12.8 %collective-permute-start.15 = (bf16[16,7680]{1,0:T(8,128)(2,1)S(1)}, bf16[16,7680]{1,0:T(8,128)(2,1)S(1)}, u32[]{:S(2)}, u32[]{:S(2)}) collective-permute-start(bf16[16,7680]{1,0:T(8,128)(2,1)S(1)} %get-tuple-element.32), channel_id=1, source_target_pairs={{0,8},{4,12},{8,16},{12,20},{16,24},{20,28},{24,29},{28,25},{9,1},... | collective-permute-start | bytes 737288 | tf_op jit(solution)/shard_map/ppermute | solution.py:297
  48.1 10.9 %collective-permute-start.16 = (bf16[2,16,3712]{2,1,0:T(8,128)(2,1)S(1)}, bf16[2,16,3712]{2,1,0:T(8,128)(2,1)S(1)}, u32[]{:S(2)}, u32[]{:S(2)}) collective-permute-start(bf16[2,16,3712]{2,1,0:T(8,128)(2,1)S(1)} %get-tuple-element.33), channel_id=1, source_target_pairs={{0,4},{5,1},{8,12},{13,9},{16,20},{21,17},{24,28},{29,25},{2,6},{7... | collective-permute-start | bytes 712712 | tf_op jit(solution)/shard_map/ppermute | solution.py:297
  49.4 27.4 %collective-permute-start.1 = (bf16[64,3584]{1,0:T(8,128)(2,1)S(1)}, bf16[64,3584]{1,0:T(8,128)(2,1)S(1)}, u32[]{:S(2)}, u32[]{:S(2)}) collective-permute-start(bf16[64,3584]{1,0:T(8,128)(2,1)S(1)} %bitcast.54), channel_id=1, source_target_pairs={{0,2},{2,0},{1,3},{3,1},{4,6},{6,4},{5,7},{7,5},{8,10},{10,8},{9,1... | collective-permute-start | bytes 1376264 | tf_op jit(solution)/shard_map/ppermute | solution.py:385
  50.6 33.8 %collective-permute-start.20 = (bf16[16,7168]{1,0:T(8,128)(2,1)S(1)}, bf16[16,7168]{1,0:T(8,128)(2,1)S(1)}, u32[]{:S(2)}, u32[]{:S(2)}) collective-permute-start(bf16[16,7168]{1,0:T(8,128)(2,1)S(1)} %pad_maximum_fusion.3), channel_id=1, source_target_pairs={{24,0},{20,4},{25,29},{21,25},{26,2},{22,6},{27,31},{23,27}} | collective-permute-start | bytes 688136 | tf_op jit(solution)/shard_map/ppermute | solution.py:297
  62.0 9.6 %collective-permute-start.17 = (bf16[16,7680]{1,0:T(8,128)(2,1)S(1)}, bf16[16,7680]{1,0:T(8,128)(2,1)S(1)}, u32[]{:S(2)}, u32[]{:S(2)}) collective-permute-start(bf16[16,7680]{1,0:T(8,128)(2,1)S(1)} %get-tuple-element.36), channel_id=1, source_target_pairs={{0,8},{4,12},{8,16},{12,20},{16,24},{20,28},{24,29},{28,25},{9,1},... | collective-permute-start | bytes 737288 | tf_op jit(solution)/shard_map/ppermute | solution.py:297
  63.9 7.7 %collective-permute-start.18 = (bf16[2,16,3712]{2,1,0:T(8,128)(2,1)S(1)}, bf16[2,16,3712]{2,1,0:T(8,128)(2,1)S(1)}, u32[]{:S(2)}, u32[]{:S(2)}) collective-permute-start(bf16[2,16,3712]{2,1,0:T(8,128)(2,1)S(1)} %get-tuple-element.38), channel_id=1, source_target_pairs={{0,4},{1,5},{4,0},{5,1},{8,12},{9,13},{12,8},{13,9},{16,20},{17,21... | collective-permute-start | bytes 712712 | tf_op jit(solution)/shard_map/ppermute | solution.py:297
  74.6 9.9 %collective-permute-start.19 = (bf16[16,7680]{1,0:T(8,128)(2,1)S(1)}, bf16[16,7680]{1,0:T(8,128)(2,1)S(1)}, u32[]{:S(2)}, u32[]{:S(2)}) collective-permute-start(bf16[16,7680]{1,0:T(8,128)(2,1)S(1)} %get-tuple-element.41), channel_id=1, source_target_pairs={{0,8},{4,12},{8,16},{12,20},{16,24},{20,28},{24,29},{28,25},{9,1},... | collective-permute-start | bytes 737288 | tf_op jit(solution)/shard_map/ppermute | solution.py:297
  76.5 8.0 %collective-permute-start.21 = (bf16[2,16,3712]{2,1,0:T(8,128)(2,1)S(1)}, bf16[2,16,3712]{2,1,0:T(8,128)(2,1)S(1)}, u32[]{:S(2)}, u32[]{:S(2)}) collective-permute-start(bf16[2,16,3712]{2,1,0:T(8,128)(2,1)S(1)} %get-tuple-element.43), channel_id=1, source_target_pairs={{0,4},{1,5},{4,0},{5,1},{8,12},{9,13},{12,8},{13,9},{16,20},{17,21... | collective-permute-start | bytes 712712 | tf_op jit(solution)/shard_map/ppermute | solution.py:297
  87.5 20.3 %collective-permute-start.23 = (bf16[2,16,7296]{2,1,0:T(8,128)(2,1)S(1)}, bf16[2,16,7296]{2,1,0:T(8,128)(2,1)S(1)}, u32[]{:S(2)}, u32[]{:S(2)}) collective-permute-start(bf16[2,16,7296]{2,1,0:T(8,128)(2,1)S(1)} %get-tuple-element.48), channel_id=1, source_target_pairs={{0,4},{1,5},{4,0},{5,1},{8,12},{9,13},{12,8},{13,9},{16,20},{17,21... | collective-permute-start | bytes 1400840 | tf_op jit(solution)/shard_map/ppermute | solution.py:297
  88.4 16.7 %collective-permute-start.25 = (bf16[16,7680]{1,0:T(8,128)(2,1)S(1)}, bf16[16,7680]{1,0:T(8,128)(2,1)S(1)}, u32[]{:S(2)}, u32[]{:S(2)}) collective-permute-start(bf16[16,7680]{1,0:T(8,128)(2,1)S(1)} %get-tuple-element.49), channel_id=1, source_target_pairs={{0,8},{4,12},{8,16},{12,20},{16,24},{20,28},{24,29},{28,25},{9,1},... | collective-permute-start | bytes 737288 | tf_op jit(solution)/shard_map/ppermute | solution.py:297
  90.3 11.5 %collective-permute-start.26 = (bf16[16,7168]{1,0:T(8,128)(2,1)S(1)}, bf16[16,7168]{1,0:T(8,128)(2,1)S(1)}, u32[]{:S(2)}, u32[]{:S(2)}) collective-permute-start(bf16[16,7168]{1,0:T(8,128)(2,1)S(1)} %pad_maximum_fusion.3), channel_id=1, source_target_pairs={{28,4},{29,25},{30,6},{31,27}} | collective-permute-start | bytes 688136 | tf_op jit(solution)/shard_map/ppermute | solution.py:297
  91.6 24.2 %copy-start.3 = (bf16[1,1,8,16,3584]{4,3,2,1,0:T(8,128)(2,1)S(1)}, bf16[1,1,8,16,3584]{4,3,2,1,0:T(8,128)(2,1)}, u32[]{:S(2)}) copy-start(bf16[1,1,8,16,3584]{4,3,2,1,0:T(8,128)(2,1)} %param.15) | copy-start | bytes 2752516
  91.6 24.2 %collective-permute-start.22 = (bf16[9,16,3712]{2,1,0:T(8,128)(2,1)S(1)}, bf16[9,16,3712]{2,1,0:T(8,128)(2,1)S(1)}, u32[]{:S(2)}, u32[]{:S(2)}) collective-permute-start(bf16[9,16,3712]{2,1,0:T(8,128)(2,1)S(1)} %get-tuple-element.47.sent), channel_id=1, source_target_pairs={{0,1},{1,0},{2,3},{3,2},{4,5},{5,4},{6,7},{7,6},{8,9},{9,8},{10,11... | collective-permute-start | bytes 3207176 | tf_op jit(solution)/shard_map/ppermute | solution.py:300
  106.5 6.8 %collective-permute-start.27 = (bf16[2,16,7296]{2,1,0:T(8,128)(2,1)S(1)}, bf16[2,16,7296]{2,1,0:T(8,128)(2,1)S(1)}, u32[]{:S(2)}, u32[]{:S(2)}) collective-permute-start(bf16[2,16,7296]{2,1,0:T(8,128)(2,1)S(1)} %last.1), channel_id=1, source_target_pairs={{1,5},{4,0},{9,13},{12,8},{17,21},{20,16},{25,29},{28,24},{3,7},{6... | collective-permute-start | bytes 1400840 | tf_op jit(solution)/shard_map/ppermute | solution.py:297
  107.8 6.8 %collective-permute-start.24 = (bf16[16,7296]{1,0:T(8,128)(2,1)S(1)}, bf16[16,7296]{1,0:T(8,128)(2,1)S(1)}, u32[]{:S(2)}, u32[]{:S(2)}) collective-permute-start(bf16[16,7296]{1,0:T(8,128)(2,1)S(1)} %slice_bitcast_fusion.1), channel_id=1, source_target_pairs={{0,1},{1,0},{2,3},{3,2},{4,5},{5,4},{6,7},{7,6},{8,9},{9,8},{10,11... | collective-permute-start | bytes 700424 | tf_op jit(solution)/shard_map/ppermute | solution.py:300
  113.3 2.5 %collective-permute-start.28 = (bf16[16,7296]{1,0:T(8,128)(2,1)S(1)}, bf16[16,7296]{1,0:T(8,128)(2,1)S(1)}, u32[]{:S(2)}, u32[]{:S(2)}) collective-permute-start(bf16[16,7296]{1,0:T(8,128)(2,1)S(1)} %slice_bitcast_fusion), channel_id=1, source_target_pairs={{0,1},{1,0},{2,3},{3,2},{4,5},{5,4},{6,7},{7,6},{8,9},{9,8},{10,11... | collective-permute-start | bytes 700424 | tf_op jit(solution)/shard_map/ppermute | solution.py:300

commit v3 on v2

--- a/solution.py
+++ b/solution.py
@@ -194,24 +194,24 @@
         copy.wait()
 
 
-def last_kernel(size, where, x_in, feed, again_peer, mine, other, passed):
+def last_kernel(size, where, x_in, feed, again_own, mine, other, last_mine, last_other):
     half, kept = size.half, size.kept
     place = Place(where)
     x0, x1, payload = read(size, x_in)
     x0 = jnp.where(place.at_end, feed[:, :half], x0)
     x1 = jnp.where(place.at_end, feed[:, half:], x1)
+    tick = size.ticks - 1
     y0, y1, ranks, _ = section_step(
-        size, place, place.peer, size.ticks - 1, x0, x1, again_peer[size.steps - 1], payload, mine, other, 2
-    )
-    passed[0, :, :half] = x0
-    passed[1, :, :half] = x1
-    passed[0, :, half:kept] = ranks
-    passed[1, :, half:kept] = ranks
-    passed[0, :, kept:] = y0
-    passed[1, :, kept:] = y1
-
-
-def end_kernel(size, where, mine, sent, got, late, late_got, last, last_got, stash, squeeze_grad, expand_grad, fwd, bwd):
+        size, place, place.section, tick, x0, x1, again_own[tick], payload, mine, other, 0
+    )
+    for ref, x, y in ((last_mine, x0, y0), (last_other, x1, y1)):
+        ref[:, :half] = x
+        ref[:, half:kept] = ranks
+        ref[:, kept:] = y
+
+
+def end_kernel(size, where, mine, sent, got, late, late_got, last_mine, last_other, last_got, stash, *outs):
+    squeeze_grad, expand_grad, fwd, bwd = outs
     ticks, half, kept, rank = size.ticks, size.half, size.kept, size.rank
     place = Place(where)
     forward = place.forward
@@ -232,7 +232,7 @@
         if t == ticks - 1:
             return jnp.where(
                 aligned,
-                pick(last[part, :, cols], last_got[:, cols]),
+                pick((last_mine, last_other)[part][:, cols], last_got[:, cols]),
                 pick(late[part, :, cols], late_got[:, cols]),
             )
         return hist()
@@ -257,7 +257,7 @@
     def carry(role):
         here = place.role == role
         early = jnp.where(here, late[0, :, kept:], late_got[:, kept:])
-        final = jnp.where(here, last[0, :, kept:], last_got[:, kept:])
+        final = jnp.where(here, last_mine[:, kept:], last_got[:, kept:])
         return jnp.where(place.side == role, final, early)
 
     fwd[...] = carry(0)
@@ -329,11 +329,11 @@
     acts, cots = activations[0], cotangent[0]
     both = [(s, c) for s in everyone for c in (0, 1)]
 
-    squeeze_peer, expand_peer = to_peer(squeeze, both), to_peer(expand, both)
+    squeeze_peer = to_peer(squeeze, both)
+    expand_peer = to_peer(tied(expand, squeeze_peer), both)
     own = jnp.stack([squeeze, expand])
     other = swap(own)
-    mine_all = jnp.concatenate([own, squeeze_peer[None], expand_peer[None]], axis=0)
-    other_all = jnp.concatenate([other, swap(squeeze_peer)[None], swap(expand_peer)[None]], axis=0)
+    squeeze_peer_other = swap(squeeze_peer)
 
     partial = call(
         stash_kernel, "stashed", shape(ticks, rows, rank, dtype=f32), [VMEM, VMEM], VMEM
@@ -346,13 +346,16 @@
     )
     per_tick = rows // acts.shape[0]
 
-    def fed(step):
+    def fed(step, *after):
         pieces = []
+        entering_now = tied(entering_full, *after) if after else entering_full
         for m in range(per_tick):
-            blocks = [b for b in (2 * step, 2 * step - 1) if 0 <= b < ticks]
-            moves = [((b * per_tick + m, 0), (b % 2, 0)) for b in blocks]
-            moves += [((b * per_tick + m, 1), (sections - 1 - b % 2, 1)) for b in blocks]
-            came = send(entering_full, [(a, b) for a, b in moves if a != b])
+            moves = []
+            for b in (2 * step, 2 * step - 1):
+                if 0 <= b < ticks:
+                    to = b % 2 if step < size.steps else 0
+                    moves += [((b * per_tick + m, 0), (to, 0)), ((b * per_tick + m, 1), (sections - 1 - to, 1))]
+            came = send(entering_now, [(a, b) for a, b in moves if a != b])
             for a, b in moves:
                 if a == b:
                     here = jnp.logical_and(section == a[0], role == a[1])
@@ -360,16 +363,12 @@
             pieces.append(came)
         return jnp.concatenate(pieces, axis=0)
 
-    first_cots, first_acts = [], []
-    for i in range(per_tick):
-        halves = [send(cots, [((i, c), (sections - 1, 1))]) for c in (1, 0)]
-        first_cots.append(jnp.concatenate(halves, axis=1))
-        first_acts.append(entering_full if i == 0 else send(entering_full, [((i, 0), (0, 0))]))
-    first_feed = jnp.where(forward, jnp.concatenate(first_acts, axis=0), jnp.concatenate(first_cots, axis=0))
+    feeds = [fed(0)]
+    for step in range(1, size.steps + 1):
+        feeds.append(fed(step, *(feeds[:1] if step < 3 else feeds[step - 2 : step])))
     first_end = section == jnp.where(forward, 0, sections - 1)
     x = jnp.concatenate([jnp.where(forward, fwd_in, bwd_in), swap(jnp.where(forward, bwd_in, fwd_in))], axis=1)
-    x = jnp.concatenate([jnp.where(first_end, first_feed, x), jnp.zeros((rows, size.message - size.width), bf16)], axis=1)
-    feeds = {1: fed(1), 2: fed(2)}
+    x = jnp.concatenate([jnp.where(first_end, feeds[0], x), jnp.zeros((rows, size.message - size.width), bf16)], axis=1)
 
     hist_shapes = (shape(ticks + 1, rows, half), shape(ticks + 1, rows, size.kept))
 
@@ -382,13 +381,15 @@
 
     def averaged(old, late):
         if replicas == 2:
-            total = late.astype(f32) + lax.ppermute(late, "dp", [(0, 1), (1, 0)]).astype(f32)
+            came = lax.ppermute(late, "dp", [(0, 1), (1, 0)])
+            total = late.astype(f32) + came.astype(f32)
         else:
-            total = lax.psum(late, "dp").astype(f32)
-        return (old.astype(f32) - STEP_RATE * total / replicas).astype(bf16)
-
-    squeeze_new = averaged(squeeze, squeeze_late[0, 0].T)
-    expand_new = averaged(expand, expand_late[0, 0])
+            came = lax.psum(late, "dp")
+            total = came.astype(f32)
+        return (old.astype(f32) - STEP_RATE * total / replicas).astype(bf16), came
+
+    squeeze_new, came = averaged(squeeze, squeeze_late[0, 0].T)
+    expand_new, _ = averaged(expand, tied(expand_late[0, 0], came))
 
     ring = (
         [((s, 0), (s + 2, 0)) for s in range(sections - 2)]
@@ -396,23 +397,30 @@
         + [((s, 1), (s - 2, 1)) for s in range(2, sections)]
     )
     aligned = [(s, s % 2) for s in everyone]
-    late_ones = [(s, 1 - s % 2) for s in everyone]
+    ring_last = (
+        [((s, 0), (s + 1, 0)) for s in range(1, sections - 1, 2)]
+        + [((sections - 1, 0), (sections - 1, 1))]
+        + [((s, 1), (s - 1, 1)) for s in range(2, sections, 2)]
+    )
 
     x, hist_mine, hist_other = call(
         first_kernel, "first", (shape(rows, size.message), *hist_shapes),
         [SMEM, VMEM, VMEM, VMEM, VMEM], (VMEM, ANY, ANY), scratch(1),
     )(where, x, again_own, own, other)
+    expand_peer_other = swap(tied(expand_peer, x))
+    mine_all = jnp.concatenate([own, squeeze_peer[None], expand_peer[None]], axis=0)
+    other_all = jnp.concatenate([other, squeeze_peer_other[None], expand_peer_other[None]], axis=0)
     x, passed = call(
         second_kernel, "second", (shape(rows, size.message), shape(2, rows, size.kept)),
         [SMEM, VMEM, VMEM, VMEM, VMEM], (VMEM, VMEM),
-    )(where, tied(x, feeds[1], feeds[2]), again_peer, mine_all, other_all)
+    )(where, tied(x, *feeds[1:]), again_peer, mine_all, other_all)
     came = to_peer(passed, aligned)
     x = send(x, ring)
     for step in range(1, size.steps):
         final = step + 1 == size.steps
+        if step == 1:
+            x = tied(x, squeeze_new)
         if step == 2:
-            x = tied(x, squeeze_new)
-        if step == 3:
             x = tied(x, expand_new)
         x, passed, hist_mine, hist_other = call(
             lambda size, *refs, step=step: pair_kernel(size, step, *refs), f"pair{step}",
@@ -424,23 +432,20 @@
             [SMEM, VMEM, VMEM, VMEM, VMEM, VMEM, VMEM, VMEM, ANY, ANY], (VMEM, VMEM, ANY, ANY),
             scratch(2), {8: 2, 9: 3},
         )(where, x, feeds[step], again_own, again_peer, mine_all, other_all, came, hist_mine, hist_other)
-        if step + 2 not in feeds and step + 2 <= size.steps:
-            feeds[step + 2] = fed(step + 2)
-        x = send(x, ring)
+        x = send(x, ring_last if final else ring)
         came = to_peer(passed, both)
     hist_got = swap(hist_other)
     late, late_got = came, swap(came[1])
-    passed = call(
-        last_kernel, "last", shape(2, rows, size.kept + half),
-        [SMEM, VMEM, VMEM, VMEM, VMEM, VMEM], VMEM,
-    )(where, x, feeds[size.steps], again_peer, mine_all, other_all)
-    last = to_peer(passed, late_ones)
-    last_got = swap(last[1])
+    last_mine, last_other = call(
+        last_kernel, "last", (shape(rows, size.kept + half), shape(rows, size.kept + half)),
+        [SMEM, VMEM, VMEM, VMEM, VMEM, VMEM], (VMEM, VMEM),
+    )(where, x, feeds[size.steps], again_own, own, other)
+    last_got = swap(last_other)
     squeeze_grad, expand_grad, fwd_carry, bwd_carry = call(
         end_kernel, "finish",
         (shape(rank, half), shape(rank, half), shape(rows, half), shape(rows, half)),
-        [SMEM] + [VMEM] * 8, (VMEM,) * 4,
-    )(where, hist_mine, hist_other, hist_got, late, late_got, last, last_got, stash)
+        [SMEM] + [VMEM] * 9, (VMEM,) * 4,
+    )(where, hist_mine, hist_other, hist_got, late, late_got, last_mine, last_other, last_got, stash)
     return (
         squeeze_new.T[None],
         expand_new[None],

time: 118 us -> 108 us (0.915)
  waiting for transfers between devices: 57.4 us -> 33.8 us
  starting transfers between devices: 35 us -> 44.5 us
  other arithmetic: 6.12 us -> 10.3 us
    ppermute x18 -> x16, waiting for transfers between devices: 56.2 us -> 30.5 us  [send(): lax.ppermute(x, ('pipe', 'mp'), [(a * 2 + b, c * 2 + d) for (a, b), (c, d...]
    ppermute x9, starting transfers between devices: 6.94 us -> 16.3 us  [swap(): return lax.ppermute(x, 'mp', [(0, 1), (1, 0)])]
    ppermute x9, waiting for transfers between devices: 1.14 us -> 3.3 us  [swap(): return lax.ppermute(x, 'mp', [(0, 1), (1, 0)])]
    unnamed x14 -> x24, local copies, waits for them, and re-layouts: 2.22 us -> 0.75 us
    concatenate x1, other arithmetic: 0.23 us -> 1.43 us  [shards(): jnp.concatenate([own, squeeze_peer[None], expand_peer[None]], axis=0)]
    ppermute x18 -> x16, starting transfers between devices: 25.5 us -> 26.1 us  [send(): lax.ppermute(x, ('pipe', 'mp'), [(a * 2 + b, c * 2 + d) for (a, b), (c, d...]
  transfers between devices with their start and end apart: 29 -> 27, of which waited for: 11 -> 11; matrix products, arithmetic and copies ran while one was open for 5% -> 9% of each run, Pallas kernels for 9% -> 7%
where the time goes in v3:
time: 108 us
  starting transfers between devices  44.5 us (41%)
  waiting for transfers between devices  33.8 us (31%)
  Pallas kernels  16.5 us (15%)
  other arithmetic  10.3 us (10%)
  local copies, waits for them, and re-layouts  1.73 us (2%)
    ppermute x16, waiting for transfers between devices, send(): lax.ppermute(x, ('pipe', 'mp'), [(a * 2 + b, c * 2 + d) for (a, b), (c, d...  30.5 us
    ppermute x16, starting transfers between devices, send(): lax.ppermute(x, ('pipe', 'mp'), [(a * 2 + b, c * 2 + d) for (a, b), (c, d...  26.1 us
    ppermute x9, starting transfers between devices, swap(): return lax.ppermute(x, 'mp', [(0, 1), (1, 0)])  16.3 us
    pallas_call x3, Pallas kernels, shards(): call(lambda size, *refs, step=step: pair_kernel(size, step, *refs), f'pai...  9.47 us
    ppermute x9, waiting for transfers between devices, swap(): return lax.ppermute(x, 'mp', [(0, 1), (1, 0)])  3.3 us
    convert_element_type x2, other arithmetic, averaged(): return ((old.astype(f32) - STEP_RATE * total / replicas).astype(bf16), came)  2.96 us
  transfers between devices with their start and end apart: 27, of which 11 were waited for; matrix products, arithmetic and copies ran while one was open for 9% of the time, Pallas kernels for 7%

profile of v3, /device:TPU:25, one launch (start us, length us, event | category | flops | bytes accessed | tf_op | source)
XLA Modules:
  0.0 107.9 jit_solution(14267857535991979302)
XLA Ops:
  0.7 1.1 select_bitcast_fusion.3
  1.7 0.7 collective-permute-start.2
  2.5 1.0 collective-permute-done.2
  3.4 0.7 pad_maximum_fusion.3
  4.8 1.0 select_bitcast_fusion.1
  6.2 1.2 %collective-permute-start = (bf16[64,3584]{1,0:T(8,128)(2,1)}, bf16[64,3584]{1,0:T(8,128)(2,1)}, u32[]{:S(2)}, u32[]{:S(2)}) collective-permute-start(bf16[64,3584]{1,0:T(8,128)(2,1)} %bitcast.48), channel_id=1, source_target_pairs={{0,2},{2,0},{1,3},{3,1},{4,6},{6,4},{5,7},{7,5},{8,10},{10,8},{9,1... | collective-permute-start | bytes 1376264 | tf_op jit(solution)/shard_map/ppermute | solution.py:384
  7.5 1.6 %collective-permute-start.12 = (bf16[64,3584]{1,0:T(8,128)(2,1)}, bf16[64,3584]{1,0:T(8,128)(2,1)}, u32[]{:S(2)}, u32[]{:S(2)}) collective-permute-start(bf16[64,3584]{1,0:T(8,128)(2,1)} %bitcast.41), channel_id=1, source_target_pairs={{0,4},{1,5},{4,0},{5,1},{8,12},{9,13},{12,8},{13,9},{16,20},{17,21... | collective-permute-start | bytes 1376264 | tf_op jit(solution)/shard_map/ppermute | solution.py:297
  9.0 0.8 maximum_select_fusion
  9.8 1.3 %collective-permute-start.7 = (bf16[16,7168]{1,0:T(8,128)(2,1)}, bf16[16,7168]{1,0:T(8,128)(2,1)}, u32[]{:S(2)}, u32[]{:S(2)}) collective-permute-start(bf16[16,7168]{1,0:T(8,128)(2,1)} %pad_maximum_fusion.3), channel_id=1, source_target_pairs={{8,0},{9,29},{5,25},{10,2},{11,31},{7,27}} | collective-permute-start | bytes 688136 | tf_op jit(solution)/shard_map/ppermute | solution.py:297
  11.2 1.1 %collective-permute-start.6 = (bf16[2,64,3584]{2,1,0:T(8,128)(2,1)S(1)}, bf16[2,64,3584]{2,1,0:T(8,128)(2,1)S(1)}, u32[]{:S(2)}, u32[]{:S(2)}) collective-permute-start(bf16[2,64,3584]{2,1,0:T(8,128)(2,1)S(1)} %pad_maximum_fusion.2.mine), channel_id=1, source_target_pairs={{0,1},{1,0},{2,3},{3,2},{4,5},{5,4},{6,7},{7,6},{8,9},{9,8},{10,11... | collective-permute-start | bytes 2752520 | tf_op jit(solution)/shard_map/ppermute | solution.py:300
  12.3 1.3 %collective-permute-start.8 = (bf16[16,7168]{1,0:T(8,128)(2,1)}, bf16[16,7168]{1,0:T(8,128)(2,1)S(1)}, u32[]{:S(2)}, u32[]{:S(2)}) collective-permute-start(bf16[16,7168]{1,0:T(8,128)(2,1)} %pad_maximum_fusion.3), channel_id=1, source_target_pairs={{16,0},{17,29},{12,4},{13,25},{18,2},{19,31},{14,6},{15,27}} | collective-permute-start | bytes 688136 | tf_op jit(solution)/shard_map/ppermute | solution.py:297
  13.6 12.2 %collective-permute-done.12 = bf16[64,3584]{1,0:T(8,128)(2,1)} collective-permute-done((bf16[64,3584]{1,0:T(8,128)(2,1)}, bf16[64,3584]{1,0:T(8,128)(2,1)}, u32[]{:S(2)}, u32[]{:S(2)}) %collective-permute-start.12) | collective-permute-done | bytes 458784 | tf_op jit(solution)/shard_map/ppermute | solution.py:297
  25.9 2.3 %collective-permute-start.13 = (bf16[64,3584]{1,0:T(8,128)(2,1)}, bf16[64,3584]{1,0:T(8,128)(2,1)}, u32[]{:S(2)}, u32[]{:S(2)}) collective-permute-start(bf16[64,3584]{1,0:T(8,128)(2,1)} %bitcast.47), channel_id=1, source_target_pairs={{0,4},{1,5},{4,0},{5,1},{8,12},{9,13},{12,8},{13,9},{16,20},{17,21... | collective-permute-start | bytes 1376264 | tf_op jit(solution)/shard_map/ppermute | solution.py:297
  28.2 1.1 %broadcast_select_fusion.1.refs_2_ = bf16[16,7168]{1,0:T(8,128)(2,1)S(1)} fusion(bf16[16,7168]{1,0:T(8,128)(2,1)} %collective-permute-done.7, pred[]{:T(512)S(6)} %and.18, bf16[16,3584]{1,0:T(8,128)(2,1)} %copy-done.8, bf16[16,3584]{1,0:T(8,128)(2,1)} %copy-done.6), kind=kLoop, calls=%fused_computation.9 | loop fusion | flops 573440 | bytes 688129 | tf_op jit(solution)/shard_map/jit(_where)/select_n | solution.py:362
  29.4 0.7 copy-done.2
  30.0 1.9 %collective-permute-start.9 = (bf16[16,7168]{1,0:T(8,128)(2,1)}, bf16[16,7168]{1,0:T(8,128)(2,1)}, u32[]{:S(2)}, u32[]{:S(2)}) collective-permute-start(bf16[16,7168]{1,0:T(8,128)(2,1)} %pad_maximum_fusion.3), channel_id=1, source_target_pairs={{24,0},{25,29},{20,4},{21,25},{26,2},{27,31},{22,6},{23,27}} | collective-permute-start | bytes 688136 | tf_op jit(solution)/shard_map/ppermute | solution.py:297
  32.4 1.8 %collective-permute-start.5 = (f32[8,16,64]{2,1,0:T(8,128)S(1)}, f32[8,16,64]{2,1,0:T(8,128)}, u32[]{:S(2)}, u32[]{:S(2)}) collective-permute-start(f32[8,16,64]{2,1,0:T(8,128)S(1)} %stashed.1), channel_id=1, source_target_pairs={{0,1},{1,0},{2,3},{3,2},{4,5},{5,4},{6,7},{7,6},{8,9},{9,8},{10,11... | collective-permute-start | bytes 98312 | tf_op jit(solution)/shard_map/ppermute | solution.py:300
  34.3 1.0 collective-permute-done.5
  35.2 0.9 add.18.again_own.refs_3_
  36.1 1.9 %collective-permute-start.11 = (f32[4,16,64]{2,1,0:T(8,128)S(1)}, f32[4,16,64]{2,1,0:T(8,128)S(1)}, u32[]{:S(2)}, u32[]{:S(2)}) collective-permute-start(f32[4,16,64]{2,1,0:T(8,128)S(1)} %slice.6), channel_id=1, source_target_pairs={{1,5},{5,1},{9,13},{13,9},{17,21},{21,17},{25,29},{29,25},{3,7},{7... | collective-permute-start | bytes 49160 | tf_op jit(solution)/shard_map/ppermute | solution.py:297
  38.0 1.0 concatenate.18.x_in
  39.0 0.9 collective-permute-start.1
  39.9 1.4 %collective-permute-done.9.refs_2_ = bf16[16,7168]{1,0:T(8,128)(2,1)} collective-permute-done((bf16[16,7168]{1,0:T(8,128)(2,1)}, bf16[16,7168]{1,0:T(8,128)(2,1)}, u32[]{:S(2)}, u32[]{:S(2)}) %collective-permute-start.9) | collective-permute-done | bytes 229408 | tf_op jit(solution)/shard_map/ppermute | solution.py:297
  41.3 0.7 collective-permute-start.10
  42.0 1.7 %first.1 = (bf16[16,7680]{1,0:T(8,128)(2,1)S(1)}, bf16[9,16,3584]{2,1,0:T(8,128)(2,1)S(1)}, bf16[9,16,3712]{2,1,0:T(8,128)(2,1)S(1)}) custom-call(s32[4]{0:T(128)S(1)} %pad_add_fusion.where.refs_0_, bf16[16,7680]{1,0:T(8,128)(2,1)S(1)} %concatenate.18.x_in, f32[8,16,64]{2,1,0:T(8,128)S(1)} %add.18.again_own.refs_3_, ...), custom_call_target="tpu_custom_call" | custom-call | flops 58720256 | bytes 3670016 | tf_op jit(solution)/shard_map/first/pallas_call | solution.py:406
  44.3 1.4 %pad_maximum_fusion.mine.refs_5_ = bf16[4,64,3584]{2,1,0:T(8,128)(2,1)S(1)} fusion(bf16[1,64,3584]{2,1,0:T(8,128)(2,1)} %bitcast.22, bf16[1,64,3584]{2,1,0:T(8,128)(2,1)} %bitcast.21, bf16[1,64,3584]{2,1,0:T(8,128)(2,1)S(1)} %copy-done.5, bf16[1,64,3584]{2,1,0:T(8,128)(2,1)S(1)} %bitcast.44), kind=kLoop, calls=%fused_computation | loop fusion | flops 2752512 | bytes 3670016 | tf_op jit(solution)/shard_map/concatenate | solution.py:411
  46.2 1.4 %second.1 = (bf16[16,7680]{1,0:T(8,128)(2,1)S(1)}, bf16[2,16,3712]{2,1,0:T(8,128)(2,1)S(1)}) custom-call(s32[4]{0:T(128)S(1)} %pad_add_fusion.where.refs_0_, bf16[16,7680]{1,0:T(8,128)(2,1)S(1)} %get-tuple-element.43.x_in, f32[4,16,64]{2,1,0:T(8,128)S(1)} %collective-permute-done.11.again_peer.refs_4_, ...), custom_call_target="tpu_custom_call" | custom-call | flops 58720256 | bytes 3670016 | tf_op jit(solution)/shard_map/second/pallas_call | solution.py:413
  47.6 1.3 %collective-permute-start.17 = (bf16[2,16,3712]{2,1,0:T(8,128)(2,1)S(1)}, bf16[2,16,3712]{2,1,0:T(8,128)(2,1)S(1)}, u32[]{:S(2)}, u32[]{:S(2)}) collective-permute-start(bf16[2,16,3712]{2,1,0:T(8,128)(2,1)S(1)} %get-tuple-element.48), channel_id=1, source_target_pairs={{0,4},{5,1},{8,12},{13,9},{16,20},{21,17},{24,28},{29,25},{2,6},{7... | collective-permute-start | bytes 712712 | tf_op jit(solution)/shard_map/ppermute | solution.py:297
  48.9 1.9 %collective-permute-start.16 = (bf16[16,7680]{1,0:T(8,128)(2,1)S(1)}, bf16[16,7680]{1,0:T(8,128)(2,1)S(1)}, u32[]{:S(2)}, u32[]{:S(2)}) collective-permute-start(bf16[16,7680]{1,0:T(8,128)(2,1)S(1)} %get-tuple-element.46), channel_id=1, source_target_pairs={{0,8},{4,12},{8,16},{12,20},{16,24},{20,28},{24,29},{28,25},{9,1},... | collective-permute-start | bytes 737288 | tf_op jit(solution)/shard_map/ppermute | solution.py:297
  50.8 2.0 %subtract_convert_fusion.1 = bf16[64,3584]{1,0:T(8,128)(2,1)} fusion(bf16[64,3584]{1,0:T(8,128)(2,1)} %collective-permute-done, bf16[1,3584,64]{1,2,0:T(8,128)(2,1)S(1)} %copy-done, bf16[1,1,3584,64]{2,3,1,0:T(8,128)(2,1)S(1)} %copy-done.10), kind=kLoop, calls=%fused_computation.4 | loop fusion | flops 1605632 | bytes 1835008 | tf_op jit(solution)/shard_map/convert_element_type | solution.py:389
  52.8 4.9 %collective-permute-done.16.refs_1_ = bf16[16,7680]{1,0:T(8,128)(2,1)S(1)} collective-permute-done((bf16[16,7680]{1,0:T(8,128)(2,1)S(1)}, bf16[16,7680]{1,0:T(8,128)(2,1)S(1)}, u32[]{:S(2)}, u32[]{:S(2)}) %collective-permute-start.16) | collective-permute-done | bytes 245792 | tf_op jit(solution)/shard_map/ppermute | solution.py:297
  57.7 3.0 %pair1.1 = (bf16[16,7680]{1,0:T(8,128)(2,1)S(1)}, bf16[2,16,3712]{2,1,0:T(8,128)(2,1)S(1)}, bf16[9,16,3584]{2,1,0:T(8,128)(2,1)S(1)}, bf16[9,16,3712]{2,1,0:T(8,128)(2,1)S(1)}) custom-call(s32[4]{0:T(128)S(1)} %pad_add_fusion.where.refs_0_, bf16[16,7680]{1,0:T(8,128)(2,1)S(1)} %collective-permute-done.16.refs_1_, ...), custom_call_target="tpu_custom_call", output_to_operand_aliasing={{2}: (8, {}), {3}: (9, {})} | custom-call | flops 58720256 | bytes 3670016 | tf_op jit(solution)/shard_map/pair1/pallas_call | solution.py:425
  60.8 3.0 %collective-permute-start.19 = (bf16[2,16,3712]{2,1,0:T(8,128)(2,1)S(1)}, bf16[2,16,3712]{2,1,0:T(8,128)(2,1)S(1)}, u32[]{:S(2)}, u32[]{:S(2)}) collective-permute-start(bf16[2,16,3712]{2,1,0:T(8,128)(2,1)S(1)} %get-tuple-element.53), channel_id=1, source_target_pairs={{0,4},{1,5},{4,0},{5,1},{8,12},{9,13},{12,8},{13,9},{16,20},{17,21... | collective-permute-start | bytes 712712 | tf_op jit(solution)/shard_map/ppermute | solution.py:297
  63.8 1.9 %collective-permute-start.18 = (bf16[16,7680]{1,0:T(8,128)(2,1)S(1)}, bf16[16,7680]{1,0:T(8,128)(2,1)S(1)}, u32[]{:S(2)}, u32[]{:S(2)}) collective-permute-start(bf16[16,7680]{1,0:T(8,128)(2,1)S(1)} %get-tuple-element.51), channel_id=1, source_target_pairs={{0,8},{4,12},{8,16},{12,20},{16,24},{20,28},{24,29},{28,25},{9,1},... | collective-permute-start | bytes 737288 | tf_op jit(solution)/shard_map/ppermute | solution.py:297
  65.8 1.0 subtract_convert_fusion
  66.7 5.8 %collective-permute-done.18.refs_1_ = bf16[16,7680]{1,0:T(8,128)(2,1)S(1)} collective-permute-done((bf16[16,7680]{1,0:T(8,128)(2,1)S(1)}, bf16[16,7680]{1,0:T(8,128)(2,1)S(1)}, u32[]{:S(2)}, u32[]{:S(2)}) %collective-permute-start.18) | collective-permute-done | bytes 245792 | tf_op jit(solution)/shard_map/ppermute | solution.py:297
  72.5 3.0 %pair2.1 = (bf16[16,7680]{1,0:T(8,128)(2,1)S(1)}, bf16[2,16,3712]{2,1,0:T(8,128)(2,1)S(1)}, bf16[9,16,3584]{2,1,0:T(8,128)(2,1)S(1)}, bf16[9,16,3712]{2,1,0:T(8,128)(2,1)S(1)}) custom-call(s32[4]{0:T(128)S(1)} %pad_add_fusion.where.refs_0_, bf16[16,7680]{1,0:T(8,128)(2,1)S(1)} %collective-permute-done.18.refs_1_, ...), custom_call_target="tpu_custom_call", output_to_operand_aliasing={{2}: (8, {}), {3}: (9, {})} | custom-call | flops 58720256 | bytes 3670016 | tf_op jit(solution)/shard_map/pair2/pallas_call | solution.py:425
  75.5 1.9 %collective-permute-start.20 = (bf16[16,7680]{1,0:T(8,128)(2,1)S(1)}, bf16[16,7680]{1,0:T(8,128)(2,1)S(1)}, u32[]{:S(2)}, u32[]{:S(2)}) collective-permute-start(bf16[16,7680]{1,0:T(8,128)(2,1)S(1)} %get-tuple-element.56), channel_id=1, source_target_pairs={{0,8},{4,12},{8,16},{12,20},{16,24},{20,28},{24,29},{28,25},{9,1},... | collective-permute-start | bytes 737288 | tf_op jit(solution)/shard_map/ppermute | solution.py:297
  77.5 1.5 %collective-permute-start.21 = (bf16[2,16,3712]{2,1,0:T(8,128)(2,1)S(1)}, bf16[2,16,3712]{2,1,0:T(8,128)(2,1)S(1)}, u32[]{:S(2)}, u32[]{:S(2)}) collective-permute-start(bf16[2,16,3712]{2,1,0:T(8,128)(2,1)S(1)} %get-tuple-element.57), channel_id=1, source_target_pairs={{0,4},{1,5},{4,0},{5,1},{8,12},{9,13},{12,8},{13,9},{16,20},{17,21... | collective-permute-start | bytes 712712 | tf_op jit(solution)/shard_map/ppermute | solution.py:297
  79.0 5.6 %collective-permute-done.21.refs_7_ = bf16[2,16,3712]{2,1,0:T(8,128)(2,1)S(1)} collective-permute-done((bf16[2,16,3712]{2,1,0:T(8,128)(2,1)S(1)}, bf16[2,16,3712]{2,1,0:T(8,128)(2,1)S(1)}, u32[]{:S(2)}, u32[]{:S(2)}) %collective-permute-start.21) | collective-permute-done | bytes 237600 | tf_op jit(solution)/shard_map/ppermute | solution.py:297
  85.1 3.4 %pair3.1 = (bf16[16,7680]{1,0:T(8,128)(2,1)S(1)}, bf16[2,16,7296]{2,1,0:T(8,128)(2,1)S(1)}, bf16[9,16,3584]{2,1,0:T(8,128)(2,1)S(1)}, bf16[9,16,3712]{2,1,0:T(8,128)(2,1)S(1)}) custom-call(s32[4]{0:T(128)S(1)} %pad_add_fusion.where.refs_0_, bf16[16,7680]{1,0:T(8,128)(2,1)S(1)} %collective-permute-done.20.refs_1_, ...), custom_call_target="tpu_custom_call", output_to_operand_aliasing={{2}: (8, {}), {3}: (9, {})} | custom-call | flops 58720256 | bytes 3670016 | tf_op jit(solution)/shard_map/pair3/pallas_call | solution.py:425
  88.5 1.5 %collective-permute-start.23 = (bf16[2,16,7296]{2,1,0:T(8,128)(2,1)S(1)}, bf16[2,16,7296]{2,1,0:T(8,128)(2,1)S(1)}, u32[]{:S(2)}, u32[]{:S(2)}) collective-permute-start(bf16[2,16,7296]{2,1,0:T(8,128)(2,1)S(1)} %get-tuple-element.62), channel_id=1, source_target_pairs={{0,4},{1,5},{4,0},{5,1},{8,12},{9,13},{12,8},{13,9},{16,20},{17,21... | collective-permute-start | bytes 1400840 | tf_op jit(solution)/shard_map/ppermute | solution.py:297
  90.1 1.3 %collective-permute-start.25 = (bf16[16,7680]{1,0:T(8,128)(2,1)S(1)}, bf16[16,7680]{1,0:T(8,128)(2,1)S(1)}, u32[]{:S(2)}, u32[]{:S(2)}) collective-permute-start(bf16[16,7680]{1,0:T(8,128)(2,1)S(1)} %get-tuple-element.63), channel_id=1, source_target_pairs={{4,8},{12,16},{20,24},{28,29},{9,5},{17,13},{25,21},{6,10},{14,18}... | collective-permute-start | bytes 737288 | tf_op jit(solution)/shard_map/ppermute | solution.py:297
  91.4 3.6 %collective-permute-start.22 = (bf16[9,16,3712]{2,1,0:T(8,128)(2,1)S(1)}, bf16[9,16,3712]{2,1,0:T(8,128)(2,1)S(1)}, u32[]{:S(2)}, u32[]{:S(2)}) collective-permute-start(bf16[9,16,3712]{2,1,0:T(8,128)(2,1)S(1)} %get-tuple-element.61.sent), channel_id=1, source_target_pairs={{0,1},{1,0},{2,3},{3,2},{4,5},{5,4},{6,7},{7,6},{8,9},{9,8},{10,11... | collective-permute-start | bytes 3207176 | tf_op jit(solution)/shard_map/ppermute | solution.py:300
  95.0 1.4 %last.1 = (bf16[16,7296]{1,0:T(8,128)(2,1)S(1)}, bf16[16,7296]{1,0:T(8,128)(2,1)S(1)}) custom-call(s32[4]{0:T(128)S(1)} %pad_add_fusion.where.refs_0_, bf16[16,7680]{1,0:T(8,128)(2,1)S(1)} %collective-permute-done.25.x_in, bf16[16,7168]{1,0:T(8,128)(2,1)S(1)} %broadcast_select_fusion.feed, f32[8,16,64]{2,1,0:T(8,128)S(1)} %add.18.again_own.refs_3_, ...), custom_call_target="tpu_custom_call" | custom-call | flops 58720256 | bytes 3670016 | tf_op jit(solution)/shard_map/last/pallas_call | solution.py:439
  96.3 7.8 %collective-permute-start.26 = (bf16[16,7296]{1,0:T(8,128)(2,1)S(1)}, bf16[16,7296]{1,0:T(8,128)(2,1)S(1)}, u32[]{:S(2)}, u32[]{:S(2)}) collective-permute-start(bf16[16,7296]{1,0:T(8,128)(2,1)S(1)} %get-tuple-element.65.last_other), channel_id=1, source_target_pairs={{0,1},{1,0},{2,3},{3,2},{4,5},{5,4},{6,7},{7,6},{8,9},{9,8},{10,11... | collective-permute-start | bytes 700424 | tf_op jit(solution)/shard_map/ppermute | solution.py:300
  104.4 0.8 collective-permute-done.26.last_got
  105.7 2.1 %finish.1 = (bf16[64,3584]{1,0:T(8,128)(2,1)}, bf16[64,3584]{1,0:T(8,128)(2,1)}, bf16[16,3584]{1,0:T(8,128)(2,1)}, bf16[16,3584]{1,0:T(8,128)(2,1)}) custom-call(s32[4]{0:T(128)S(1)} %pad_add_fusion.where.refs_0_, bf16[9,16,3584]{2,1,0:T(8,128)(2,1)S(1)} %get-tuple-element.60.mine, bf16[9,16,3712]{2,1,0:T(8,128)(2,1)S(1)} %get-tuple-element.61.sent, ...), custom_call_target="tpu_custom_call" | custom-call | flops 58720256 | bytes 3670016 | tf_op jit(solution)/shard_map/finish/pallas_call | solution.py:444
  (54 shorter events, 3.9 us)
Async XLA Ops:
  0.6 10.5 %copy-start = (bf16[1,3584,64]{1,2,0:T(8,128)(2,1)S(1)}, bf16[1,3584,64]{1,2,0:T(8,128)(2,1)}, u32[]{:S(2)}) copy-start(bf16[1,3584,64]{1,2,0:T(8,128)(2,1)} %param.11) | copy-start | bytes 1376260
  0.6 10.5 %copy-start.4 = (bf16[1,64,3584]{2,1,0:T(8,128)(2,1)S(1)}, bf16[1,64,3584]{2,1,0:T(8,128)(2,1)}, u32[]{:S(2)}) copy-start(bf16[1,64,3584]{2,1,0:T(8,128)(2,1)} %param.12) | copy-start | bytes 1376260
  1.7 9.4 %copy-start.6 = (bf16[16,3584]{1,0:T(8,128)(2,1)}, bf16[16,3584]{1,0:T(8,128)(2,1)S(1)}, u32[]{:S(2)}) copy-start(bf16[16,3584]{1,0:T(8,128)(2,1)S(1)} %get-tuple-element.72) | copy-start | bytes 344068
  1.7 1.7 %collective-permute-start.2 = (bf16[16,3584]{1,0:T(8,128)(2,1)S(1)}, bf16[16,3584]{1,0:T(8,128)(2,1)S(1)}, u32[]{:S(2)}, u32[]{:S(2)}) collective-permute-start(bf16[16,3584]{1,0:T(8,128)(2,1)S(1)} %get-tuple-element.73), channel_id=1, source_target_pairs={{0,1},{1,0},{2,3},{3,2},{4,5},{5,4},{6,7},{7,6},{8,9},{9,8},{10,11... | collective-permute-start | bytes 344072 | tf_op jit(solution)/shard_map/ppermute | solution.py:300
  3.4 7.7 %copy-start.8 = (bf16[16,3584]{1,0:T(8,128)(2,1)}, bf16[16,3584]{1,0:T(8,128)(2,1)S(1)}, u32[]{:S(2)}) copy-start(bf16[16,3584]{1,0:T(8,128)(2,1)S(1)} %collective-permute-done.2) | copy-start | bytes 344068
  4.2 4.9 %collective-permute-start.3 = (bf16[16,7168]{1,0:T(8,128)(2,1)}, bf16[16,7168]{1,0:T(8,128)(2,1)S(1)}, u32[]{:S(2)}, u32[]{:S(2)}) collective-permute-start(bf16[16,7168]{1,0:T(8,128)(2,1)} %pad_maximum_fusion.3), channel_id=1, source_target_pairs={{1,29},{3,31}} | collective-permute-start | bytes 688136 | tf_op jit(solution)/shard_map/ppermute | solution.py:297
  5.8 26.2 %copy-start.1 = (bf16[1,1,8,16,3584]{4,3,2,1,0:T(8,128)(2,1)S(1)}, bf16[1,1,8,16,3584]{4,3,2,1,0:T(8,128)(2,1)}, u32[]{:S(2)}) copy-start(bf16[1,1,8,16,3584]{4,3,2,1,0:T(8,128)(2,1)} %param.15) | copy-start | bytes 2752516
  5.8 3.2 %collective-permute-start.4 = (bf16[16,3584]{1,0:T(8,128)(2,1)S(1)}, bf16[16,3584]{1,0:T(8,128)(2,1)S(1)}, u32[]{:S(2)}, u32[]{:S(2)}) collective-permute-start(bf16[16,3584]{1,0:T(8,128)(2,1)S(1)} %get-tuple-element.75), channel_id=1, source_target_pairs={{0,1},{1,0},{2,3},{3,2},{4,5},{5,4},{6,7},{7,6},{8,9},{9,8},{10,11... | collective-permute-start | bytes 344072 | tf_op jit(solution)/shard_map/ppermute | solution.py:300
  6.2 32.7 %collective-permute-start = (bf16[64,3584]{1,0:T(8,128)(2,1)}, bf16[64,3584]{1,0:T(8,128)(2,1)}, u32[]{:S(2)}, u32[]{:S(2)}) collective-permute-start(bf16[64,3584]{1,0:T(8,128)(2,1)} %bitcast.48), channel_id=1, source_target_pairs={{0,2},{2,0},{1,3},{3,1},{4,6},{6,4},{5,7},{7,5},{8,10},{10,8},{9,1... | collective-permute-start | bytes 1376264 | tf_op jit(solution)/shard_map/ppermute | solution.py:384
  7.5 18.4 %collective-permute-start.12 = (bf16[64,3584]{1,0:T(8,128)(2,1)}, bf16[64,3584]{1,0:T(8,128)(2,1)}, u32[]{:S(2)}, u32[]{:S(2)}) collective-permute-start(bf16[64,3584]{1,0:T(8,128)(2,1)} %bitcast.41), channel_id=1, source_target_pairs={{0,4},{1,5},{4,0},{5,1},{8,12},{9,13},{12,8},{13,9},{16,20},{17,21... | collective-permute-start | bytes 1376264 | tf_op jit(solution)/shard_map/ppermute | solution.py:297
  9.8 18.4 %collective-permute-start.7 = (bf16[16,7168]{1,0:T(8,128)(2,1)}, bf16[16,7168]{1,0:T(8,128)(2,1)}, u32[]{:S(2)}, u32[]{:S(2)}) collective-permute-start(bf16[16,7168]{1,0:T(8,128)(2,1)} %pad_maximum_fusion.3), channel_id=1, source_target_pairs={{8,0},{9,29},{5,25},{10,2},{11,31},{7,27}} | collective-permute-start | bytes 688136 | tf_op jit(solution)/shard_map/ppermute | solution.py:297
  11.2 30.1 %collective-permute-start.6 = (bf16[2,64,3584]{2,1,0:T(8,128)(2,1)S(1)}, bf16[2,64,3584]{2,1,0:T(8,128)(2,1)S(1)}, u32[]{:S(2)}, u32[]{:S(2)}) collective-permute-start(bf16[2,64,3584]{2,1,0:T(8,128)(2,1)S(1)} %pad_maximum_fusion.2.mine), channel_id=1, source_target_pairs={{0,1},{1,0},{2,3},{3,2},{4,5},{5,4},{6,7},{7,6},{8,9},{9,8},{10,11... | collective-permute-start | bytes 2752520 | tf_op jit(solution)/shard_map/ppermute | solution.py:300
  12.3 17.0 %collective-permute-start.8 = (bf16[16,7168]{1,0:T(8,128)(2,1)}, bf16[16,7168]{1,0:T(8,128)(2,1)S(1)}, u32[]{:S(2)}, u32[]{:S(2)}) collective-permute-start(bf16[16,7168]{1,0:T(8,128)(2,1)} %pad_maximum_fusion.3), channel_id=1, source_target_pairs={{16,0},{17,29},{12,4},{13,25},{18,2},{19,31},{14,6},{15,27}} | collective-permute-start | bytes 688136 | tf_op jit(solution)/shard_map/ppermute | solution.py:297
  25.9 17.9 %collective-permute-start.13 = (bf16[64,3584]{1,0:T(8,128)(2,1)}, bf16[64,3584]{1,0:T(8,128)(2,1)}, u32[]{:S(2)}, u32[]{:S(2)}) collective-permute-start(bf16[64,3584]{1,0:T(8,128)(2,1)} %bitcast.47), channel_id=1, source_target_pairs={{0,4},{1,5},{4,0},{5,1},{8,12},{9,13},{12,8},{13,9},{16,20},{17,21... | collective-permute-start | bytes 1376264 | tf_op jit(solution)/shard_map/ppermute | solution.py:297
  29.3 0.7 copy-start.2
  30.0 11.3 %collective-permute-start.9 = (bf16[16,7168]{1,0:T(8,128)(2,1)}, bf16[16,7168]{1,0:T(8,128)(2,1)}, u32[]{:S(2)}, u32[]{:S(2)}) collective-permute-start(bf16[16,7168]{1,0:T(8,128)(2,1)} %pad_maximum_fusion.3), channel_id=1, source_target_pairs={{24,0},{25,29},{20,4},{21,25},{26,2},{27,31},{22,6},{23,27}} | collective-permute-start | bytes 688136 | tf_op jit(solution)/shard_map/ppermute | solution.py:297
  32.4 2.9 %collective-permute-start.5 = (f32[8,16,64]{2,1,0:T(8,128)S(1)}, f32[8,16,64]{2,1,0:T(8,128)}, u32[]{:S(2)}, u32[]{:S(2)}) collective-permute-start(f32[8,16,64]{2,1,0:T(8,128)S(1)} %stashed.1), channel_id=1, source_target_pairs={{0,1},{1,0},{2,3},{3,2},{4,5},{5,4},{6,7},{7,6},{8,9},{9,8},{10,11... | collective-permute-start | bytes 98312 | tf_op jit(solution)/shard_map/ppermute | solution.py:300
  34.3 10.0 %copy-start.5 = (bf16[1,64,3584]{2,1,0:T(8,128)(2,1)S(1)}, bf16[1,64,3584]{2,1,0:T(8,128)(2,1)}, u32[]{:S(2)}) copy-start(bf16[1,64,3584]{2,1,0:T(8,128)(2,1)} %param.12) | copy-start | bytes 1376260
  36.1 10.1 %collective-permute-start.11 = (f32[4,16,64]{2,1,0:T(8,128)S(1)}, f32[4,16,64]{2,1,0:T(8,128)S(1)}, u32[]{:S(2)}, u32[]{:S(2)}) collective-permute-start(f32[4,16,64]{2,1,0:T(8,128)S(1)} %slice.6), channel_id=1, source_target_pairs={{1,5},{5,1},{9,13},{13,9},{17,21},{21,17},{25,29},{29,25},{3,7},{7... | collective-permute-start | bytes 49160 | tf_op jit(solution)/shard_map/ppermute | solution.py:297
  39.0 26.7 %collective-permute-start.1 = (bf16[64,3584]{1,0:T(8,128)(2,1)}, bf16[64,3584]{1,0:T(8,128)(2,1)S(1)}, u32[]{:S(2)}, u32[]{:S(2)}) collective-permute-start(bf16[64,3584]{1,0:T(8,128)(2,1)} %bitcast.49), channel_id=1, source_target_pairs={{0,2},{2,0},{1,3},{3,1},{4,6},{6,4},{5,7},{7,5},{8,10},{10,8},{9,1... | collective-permute-start | bytes 1376264 | tf_op jit(solution)/shard_map/ppermute | solution.py:384
  41.3 4.5 %collective-permute-start.14 = (bf16[64,3584]{1,0:T(8,128)(2,1)}, bf16[64,3584]{1,0:T(8,128)(2,1)S(1)}, u32[]{:S(2)}, u32[]{:S(2)}) collective-permute-start(bf16[64,3584]{1,0:T(8,128)(2,1)} %collective-permute-done.12), channel_id=1, source_target_pairs={{0,1},{1,0},{2,3},{3,2},{4,5},{5,4},{6,7},{7,6},{8,9},{9,8},{10,11... | collective-permute-start | bytes 1376264 | tf_op jit(solution)/shard_map/ppermute | solution.py:300
  41.3 4.4 %collective-permute-start.10 = (bf16[16,7168]{1,0:T(8,128)(2,1)}, bf16[16,7168]{1,0:T(8,128)(2,1)S(1)}, u32[]{:S(2)}, u32[]{:S(2)}) collective-permute-start(bf16[16,7168]{1,0:T(8,128)(2,1)} %pad_maximum_fusion.3), channel_id=1, source_target_pairs={{28,0},{30,2}} | collective-permute-start | bytes 688136 | tf_op jit(solution)/shard_map/ppermute | solution.py:297
  43.7 2.2 %collective-permute-start.15 = (bf16[64,3584]{1,0:T(8,128)(2,1)}, bf16[64,3584]{1,0:T(8,128)(2,1)S(1)}, u32[]{:S(2)}, u32[]{:S(2)}) collective-permute-start(bf16[64,3584]{1,0:T(8,128)(2,1)} %collective-permute-done.13), channel_id=1, source_target_pairs={{0,1},{1,0},{2,3},{3,2},{4,5},{5,4},{6,7},{7,6},{8,9},{9,8},{10,11... | collective-permute-start | bytes 1376264 | tf_op jit(solution)/shard_map/ppermute | solution.py:300
  44.3 1.4 %copy-start.7 = (bf16[16,3584]{1,0:T(8,128)(2,1)S(1)}, bf16[16,3584]{1,0:T(8,128)(2,1)}, u32[]{:S(2)}) copy-start(bf16[16,3584]{1,0:T(8,128)(2,1)} %copy-done.6) | copy-start | bytes 344068
  44.3 1.5 %copy-start.9 = (bf16[16,3584]{1,0:T(8,128)(2,1)S(1)}, bf16[16,3584]{1,0:T(8,128)(2,1)}, u32[]{:S(2)}) copy-start(bf16[16,3584]{1,0:T(8,128)(2,1)} %copy-done.8) | copy-start | bytes 344068
  46.2 4.6 %copy-start.10 = (bf16[1,1,3584,64]{2,3,1,0:T(8,128)(2,1)S(1)}, bf16[1,1,3584,64]{2,3,1,0:T(8,128)(2,1)}, u32[]{:S(2)}) copy-start(bf16[1,1,3584,64]{2,3,1,0:T(8,128)(2,1)} %param.13) | copy-start | bytes 1376260
  47.6 10.2 %collective-permute-start.17 = (bf16[2,16,3712]{2,1,0:T(8,128)(2,1)S(1)}, bf16[2,16,3712]{2,1,0:T(8,128)(2,1)S(1)}, u32[]{:S(2)}, u32[]{:S(2)}) collective-permute-start(bf16[2,16,3712]{2,1,0:T(8,128)(2,1)S(1)} %get-tuple-element.48), channel_id=1, source_target_pairs={{0,4},{5,1},{8,12},{13,9},{16,20},{21,17},{24,28},{29,25},{2,6},{7... | collective-permute-start | bytes 712712 | tf_op jit(solution)/shard_map/ppermute | solution.py:297
  48.9 8.9 %collective-permute-start.16 = (bf16[16,7680]{1,0:T(8,128)(2,1)S(1)}, bf16[16,7680]{1,0:T(8,128)(2,1)S(1)}, u32[]{:S(2)}, u32[]{:S(2)}) collective-permute-start(bf16[16,7680]{1,0:T(8,128)(2,1)S(1)} %get-tuple-element.46), channel_id=1, source_target_pairs={{0,8},{4,12},{8,16},{12,20},{16,24},{20,28},{24,29},{28,25},{9,1},... | collective-permute-start | bytes 737288 | tf_op jit(solution)/shard_map/ppermute | solution.py:297
  57.7 8.0 %copy-start.11 = (bf16[1,1,64,3584]{3,2,1,0:T(8,128)(2,1)S(1)}, bf16[1,1,64,3584]{3,2,1,0:T(8,128)(2,1)}, u32[]{:S(2)}) copy-start(bf16[1,1,64,3584]{3,2,1,0:T(8,128)(2,1)} %param.14) | copy-start | bytes 1376260
  60.8 11.7 %copy-start.3 = (bf16[16,7168]{1,0:T(8,128)(2,1)S(1)}, bf16[16,7168]{1,0:T(8,128)(2,1)}, u32[]{:S(2)}) copy-start(bf16[16,7168]{1,0:T(8,128)(2,1)} %copy-done.2) | copy-start | bytes 688132
  60.8 11.7 %collective-permute-start.19 = (bf16[2,16,3712]{2,1,0:T(8,128)(2,1)S(1)}, bf16[2,16,3712]{2,1,0:T(8,128)(2,1)S(1)}, u32[]{:S(2)}, u32[]{:S(2)}) collective-permute-start(bf16[2,16,3712]{2,1,0:T(8,128)(2,1)S(1)} %get-tuple-element.53), channel_id=1, source_target_pairs={{0,4},{1,5},{4,0},{5,1},{8,12},{9,13},{12,8},{13,9},{16,20},{17,21... | collective-permute-start | bytes 712712 | tf_op jit(solution)/shard_map/ppermute | solution.py:297
  63.8 8.7 %collective-permute-start.18 = (bf16[16,7680]{1,0:T(8,128)(2,1)S(1)}, bf16[16,7680]{1,0:T(8,128)(2,1)S(1)}, u32[]{:S(2)}, u32[]{:S(2)}) collective-permute-start(bf16[16,7680]{1,0:T(8,128)(2,1)S(1)} %get-tuple-element.51), channel_id=1, source_target_pairs={{0,8},{4,12},{8,16},{12,20},{16,24},{20,28},{24,29},{28,25},{9,1},... | collective-permute-start | bytes 737288 | tf_op jit(solution)/shard_map/ppermute | solution.py:297
  75.5 9.6 %collective-permute-start.20 = (bf16[16,7680]{1,0:T(8,128)(2,1)S(1)}, bf16[16,7680]{1,0:T(8,128)(2,1)S(1)}, u32[]{:S(2)}, u32[]{:S(2)}) collective-permute-start(bf16[16,7680]{1,0:T(8,128)(2,1)S(1)} %get-tuple-element.56), channel_id=1, source_target_pairs={{0,8},{4,12},{8,16},{12,20},{16,24},{20,28},{24,29},{28,25},{9,1},... | collective-permute-start | bytes 737288 | tf_op jit(solution)/shard_map/ppermute | solution.py:297
  77.5 7.2 %collective-permute-start.21 = (bf16[2,16,3712]{2,1,0:T(8,128)(2,1)S(1)}, bf16[2,16,3712]{2,1,0:T(8,128)(2,1)S(1)}, u32[]{:S(2)}, u32[]{:S(2)}) collective-permute-start(bf16[2,16,3712]{2,1,0:T(8,128)(2,1)S(1)} %get-tuple-element.57), channel_id=1, source_target_pairs={{0,4},{1,5},{4,0},{5,1},{8,12},{9,13},{12,8},{13,9},{16,20},{17,21... | collective-permute-start | bytes 712712 | tf_op jit(solution)/shard_map/ppermute | solution.py:297
  88.5 15.6 %collective-permute-start.23 = (bf16[2,16,7296]{2,1,0:T(8,128)(2,1)S(1)}, bf16[2,16,7296]{2,1,0:T(8,128)(2,1)S(1)}, u32[]{:S(2)}, u32[]{:S(2)}) collective-permute-start(bf16[2,16,7296]{2,1,0:T(8,128)(2,1)S(1)} %get-tuple-element.62), channel_id=1, source_target_pairs={{0,4},{1,5},{4,0},{5,1},{8,12},{9,13},{12,8},{13,9},{16,20},{17,21... | collective-permute-start | bytes 1400840 | tf_op jit(solution)/shard_map/ppermute | solution.py:297
  90.1 4.9 %collective-permute-start.25 = (bf16[16,7680]{1,0:T(8,128)(2,1)S(1)}, bf16[16,7680]{1,0:T(8,128)(2,1)S(1)}, u32[]{:S(2)}, u32[]{:S(2)}) collective-permute-start(bf16[16,7680]{1,0:T(8,128)(2,1)S(1)} %get-tuple-element.63), channel_id=1, source_target_pairs={{4,8},{12,16},{20,24},{28,29},{9,5},{17,13},{25,21},{6,10},{14,18}... | collective-permute-start | bytes 737288 | tf_op jit(solution)/shard_map/ppermute | solution.py:297
  91.4 14.3 %collective-permute-start.22 = (bf16[9,16,3712]{2,1,0:T(8,128)(2,1)S(1)}, bf16[9,16,3712]{2,1,0:T(8,128)(2,1)S(1)}, u32[]{:S(2)}, u32[]{:S(2)}) collective-permute-start(bf16[9,16,3712]{2,1,0:T(8,128)(2,1)S(1)} %get-tuple-element.61.sent), channel_id=1, source_target_pairs={{0,1},{1,0},{2,3},{3,2},{4,5},{5,4},{6,7},{7,6},{8,9},{9,8},{10,11... | collective-permute-start | bytes 3207176 | tf_op jit(solution)/shard_map/ppermute | solution.py:300
  96.3 8.9 %collective-permute-start.26 = (bf16[16,7296]{1,0:T(8,128)(2,1)S(1)}, bf16[16,7296]{1,0:T(8,128)(2,1)S(1)}, u32[]{:S(2)}, u32[]{:S(2)}) collective-permute-start(bf16[16,7296]{1,0:T(8,128)(2,1)S(1)} %get-tuple-element.65.last_other), channel_id=1, source_target_pairs={{0,1},{1,0},{2,3},{3,2},{4,5},{5,4},{6,7},{7,6},{8,9},{9,8},{10,11... | collective-permute-start | bytes 700424 | tf_op jit(solution)/shard_map/ppermute | solution.py:300
  104.2 1.6 %collective-permute-start.24 = (bf16[16,7296]{1,0:T(8,128)(2,1)S(1)}, bf16[16,7296]{1,0:T(8,128)(2,1)S(1)}, u32[]{:S(2)}, u32[]{:S(2)}) collective-permute-start(bf16[16,7296]{1,0:T(8,128)(2,1)S(1)} %slice_bitcast_fusion), channel_id=1, source_target_pairs={{0,1},{1,0},{2,3},{3,2},{4,5},{5,4},{6,7},{7,6},{8,9},{9,8},{10,11... | collective-permute-start | bytes 700424 | tf_op jit(solution)/shard_map/ppermute | solution.py:300

commit v4 on v3

--- a/solution.py
+++ b/solution.py
@@ -107,10 +107,17 @@
         partial[t] = whole[t * rows : (t + 1) * rows]
 
 
-def keep(size, keep_mine, keep_other, slot, x0, x1, ranks):
-    keep_mine[slot] = x0
-    keep_other[slot, :, : size.half] = x1
-    keep_other[slot, :, size.half :] = ranks
+def keep(size, keep_mine, keep_other, x0, x1, ranks):
+    keep_mine[0] = x0
+    keep_other[0, :, : size.half] = x1
+    keep_other[0, :, size.half :] = ranks
+
+
+def keep_passed(size, ref, x0, x1, ranks):
+    half, kept = size.half, size.kept
+    for part, x in enumerate((x0, x1)):
+        ref[part, 0, :, :half] = x
+        ref[part, 0, :, half:kept] = ranks
 
 
 def first_kernel(size, where, x_in, again_own, mine, other, out, hist_mine, hist_other, keep_mine, keep_other, sems):
@@ -119,7 +126,7 @@
     y0, y1, ranks, payload = section_step(
         size, place, place.section, 0, x0, x1, again_own[0], payload, mine, other, 0
     )
-    keep(size, keep_mine, keep_other, 0, x0, x1, ranks)
+    keep(size, keep_mine, keep_other, x0, x1, ranks)
     copies = [
         pltpu.make_async_copy(keep_mine, hist_mine.at[pl.ds(0, 1)], sems.at[0]),
         pltpu.make_async_copy(keep_other, hist_other.at[pl.ds(0, 1)], sems.at[1]),
@@ -131,31 +138,37 @@
         copy.wait()
 
 
-def second_kernel(size, where, x_in, again_peer, mine, other, out, passed):
+def second_kernel(size, where, x_in, again_peer, mine, other, out, hist_peer, keep_peer, sem):
     place = Place(where)
     x0, x1, payload = read(size, x_in)
-    y0, y1, ranks, sent = section_step(
-        size, place, place.peer, 1, x0, x1, again_peer[0], payload, mine, other, 2
-    )
-    passed[0, :, : size.half] = x0
-    passed[1, :, : size.half] = x1
-    passed[0, :, size.half :] = ranks
-    passed[1, :, size.half :] = ranks
+    again = join_words(again_peer[:, : 2 * size.rank])
+    y0, y1, ranks, sent = section_step(size, place, place.peer, 1, x0, x1, again, payload, mine, other, 2)
+    keep_passed(size, keep_peer, x0, x1, ranks)
+    copy = pltpu.make_async_copy(keep_peer, hist_peer.at[:, pl.ds(0, 1)], sem)
+    copy.start()
     aligned = place.aligned
     sent = [jnp.where(aligned, sent[j], payload[j]) for j in range(size.slots)]
     write(size, out, jnp.where(aligned, y0, x0), jnp.where(aligned, y1, x1), sent)
-
-
-def pair_kernel(size, step, where, x_in, feed, again_own, again_peer, mine, other, came, *rest):
-    _, _, out, passed, hist_mine, hist_other, keep_mine, keep_other, sems = rest
-    half, kept = size.half, size.kept
+    copy.wait()
+
+
+def pair_kernel(size, step, where, x_in, feeds, again_own, again_peer, mine, other, *rest):
+    final = step + 1 == size.steps
+    if final:
+        _, _, out, passed, hist_mine, hist_other, keep_mine, keep_other, sems = rest
+    else:
+        _, _, _, out, hist_mine, hist_other, hist_peer, keep_mine, keep_other, keep_peer, sems = rest
+        passed = keep_peer
+    half, kept, span = size.half, size.kept, 2 * size.rank
     place = Place(where)
     aligned = place.aligned
     x0, x1, payload = read(size, x_in)
+    feed = feeds.at[where[4 + step]]
     x0 = jnp.where(place.at_end, feed[:, :half], x0)
     x1 = jnp.where(place.at_end, feed[:, half:], x1)
     tick = jnp.where(aligned, 2 * step, 2 * step - 1)
-    again_peer = again_peer[jnp.where(aligned, step, step - 1)]
+    now, before = (again_peer[:, i * span : (i + 1) * span] for i in (step, step - 1))
+    again_peer = join_words(jnp.where(aligned, now, before))
     own = again_own[2 * step]
     at_peer = jnp.where(aligned, 0, 2)
     y0, y1, ranks, payload = section_step(
@@ -167,37 +180,33 @@
         jnp.where(aligned, again_peer, own), payload, mine, other, 2 - at_peer,
     )
     keep(
-        size, keep_mine, keep_other, 0,
+        size, keep_mine, keep_other,
         jnp.where(aligned, x0, y0), jnp.where(aligned, x1, y1), jnp.where(aligned, ranks, ranks_b),
     )
-    keep_mine[1] = came[0, :, :half]
-    keep_other[1] = came[1, :, :kept]
-    odd = jnp.where(aligned, 2 * step - 3 if step > 1 else size.ticks, 2 * step - 1)
+    keep_passed(
+        size, passed, jnp.where(aligned, y0, x0), jnp.where(aligned, y1, x1), jnp.where(aligned, ranks_b, ranks)
+    )
     copies = [
-        pltpu.make_async_copy(keep_mine.at[pl.ds(0, 1)], hist_mine.at[pl.ds(2 * step, 1)], sems.at[0]),
-        pltpu.make_async_copy(keep_other.at[pl.ds(0, 1)], hist_other.at[pl.ds(2 * step, 1)], sems.at[1]),
-        pltpu.make_async_copy(keep_mine.at[pl.ds(1, 1)], hist_mine.at[pl.ds(odd, 1)], sems.at[2]),
-        pltpu.make_async_copy(keep_other.at[pl.ds(1, 1)], hist_other.at[pl.ds(odd, 1)], sems.at[3]),
+        pltpu.make_async_copy(keep_mine, hist_mine.at[pl.ds(step, 1)], sems.at[0]),
+        pltpu.make_async_copy(keep_other, hist_other.at[pl.ds(step, 1)], sems.at[1]),
     ]
+    if not final:
+        copies.append(pltpu.make_async_copy(keep_peer, hist_peer.at[:, pl.ds(step, 1)], sems.at[2]))
     for copy in copies:
         copy.start()
-    ranks_peer = jnp.where(aligned, ranks_b, ranks)
-    passed[0, :, :half] = jnp.where(aligned, y0, x0)
-    passed[1, :, :half] = jnp.where(aligned, y1, x1)
-    passed[0, :, half:kept] = ranks_peer
-    passed[1, :, half:kept] = ranks_peer
-    if step + 1 == size.steps:
-        passed[0, :, kept:] = z0
-        passed[1, :, kept:] = z1
+    if final:
+        passed[0, 0, :, kept:] = z0
+        passed[1, 0, :, kept:] = z1
     write(size, out, z0, z1, payload)
     for copy in copies:
         copy.wait()
 
 
-def last_kernel(size, where, x_in, feed, again_own, mine, other, last_mine, last_other):
+def last_kernel(size, where, x_in, feeds, again_own, mine, other, last_mine, last_other):
     half, kept = size.half, size.kept
     place = Place(where)
     x0, x1, payload = read(size, x_in)
+    feed = feeds.at[where[4 + size.steps]]
     x0 = jnp.where(place.at_end, feed[:, :half], x0)
     x1 = jnp.where(place.at_end, feed[:, half:], x1)
     tick = size.ticks - 1
@@ -210,32 +219,30 @@
         ref[:, kept:] = y
 
 
-def end_kernel(size, where, mine, sent, got, late, late_got, last_mine, last_other, last_got, stash, *outs):
+def end_kernel(size, where, mine, sent, got, odd, odd_got, late, late_got, last_mine, last_other, last_got, stash, *outs):
     squeeze_grad, expand_grad, fwd, bwd = outs
-    ticks, half, kept, rank = size.ticks, size.half, size.kept, size.rank
+    ticks, half, kept, rank, steps = size.ticks, size.half, size.kept, size.rank, size.steps
     place = Place(where)
     forward = place.forward
 
     def block(role, t, cols, part=0):
-        aligned = place.side == role
         here = place.role == role
+        i = t // 2
 
         def pick(own, other):
-            return jnp.where(here, own, other)
-
-        def hist():
-            own = mine[t, :, cols] if part == 0 else sent[t, :, cols]
-            return pick(own, got[t, :, cols])
-
-        if t == ticks - 3:
-            return jnp.where(aligned, pick(late[part, :, cols], late_got[:, cols]), hist())
-        if t == ticks - 1:
-            return jnp.where(
-                aligned,
-                pick((last_mine, last_other)[part][:, cols], last_got[:, cols]),
-                pick(late[part, :, cols], late_got[:, cols]),
-            )
-        return hist()
+            return jnp.where(here, own[:, cols], other[:, cols])
+
+        if t % 2 == 0:
+            return pick((mine, sent)[part].at[i], got.at[i])
+
+        def passed(i):
+            if i + 1 < steps:
+                return pick(odd.at[part, i], odd_got.at[i])
+            if i + 1 == steps:
+                return pick(late.at[part, 0], late_got)
+            return pick((last_mine, last_other)[part], last_got)
+
+        return jnp.where(place.side == role, passed(i + 1), passed(i))
 
     lag = 2 * (place.sections - 1 - place.section) + 1
     ranks = jnp.concatenate([block(1, t, slice(half, kept), 1) for t in range(ticks)], axis=0)
@@ -256,7 +263,7 @@
 
     def carry(role):
         here = place.role == role
-        early = jnp.where(here, late[0, :, kept:], late_got[:, kept:])
+        early = jnp.where(here, late[0, 0, :, kept:], late_got[:, kept:])
         final = jnp.where(here, last_mine[:, kept:], last_got[:, kept:])
         return jnp.where(place.side == role, final, early)
 
@@ -330,73 +337,100 @@
     both = [(s, c) for s in everyone for c in (0, 1)]
 
     squeeze_peer = to_peer(squeeze, both)
-    expand_peer = to_peer(tied(expand, squeeze_peer), both)
-    own = jnp.stack([squeeze, expand])
+    own = lax.optimization_barrier(jnp.stack([squeeze, expand]))
     other = swap(own)
     squeeze_peer_other = swap(squeeze_peer)
-
     partial = call(
         stash_kernel, "stashed", shape(ticks, rows, rank, dtype=f32), [VMEM, VMEM], VMEM
     )(stash, squeeze)
     again_own = partial + swap(partial)
-    again_peer = to_peer(again_own[1::2], [(s, 1) for s in everyone])
+    words = jnp.concatenate([split_words(again_own[t]) for t in range(1, ticks, 2)], axis=1)
+    words = jnp.pad(words, ((0, 0), (0, half - words.shape[1])))
+    expand_peer = to_peer(tied(jnp.concatenate([expand, words], axis=0), squeeze_peer), both)
+    again_peer = expand_peer[rank:, : size.steps * 2 * rank]
 
     entering_full = jnp.concatenate(
         [jnp.where(forward, acts, cots), swap(jnp.where(forward, cots, acts))], axis=1
     )
     per_tick = rows // acts.shape[0]
 
-    def fed(step, *after):
+    ends = {}
+    for b in range(ticks):
+        to = b % 2 if b + 1 < ticks else 0
+        ends.setdefault((to, 0), []).append(b)
+        ends.setdefault((sections - 1 - to, 1), []).append(b)
+    turn = {}
+    trips = [[] for _ in range(ticks)]
+    for (to, core), blocks in ends.items():
+        local = [b for b in blocks if all(b * per_tick + m == to for m in range(per_tick))]
+        for n, b in enumerate(b for b in blocks if b not in local):
+            trip, swapped = n // 2, n % 2
+            turn[to, core, b] = 1 + 2 * trip + swapped
+            trips[trip].append((b, core, (to, core ^ swapped)))
+        for b in local:
+            turn[to, core, b] = 0
+
+    def fed(trip):
         pieces = []
-        entering_now = tied(entering_full, *after) if after else entering_full
         for m in range(per_tick):
-            moves = []
-            for b in (2 * step, 2 * step - 1):
-                if 0 <= b < ticks:
-                    to = b % 2 if step < size.steps else 0
-                    moves += [((b * per_tick + m, 0), (to, 0)), ((b * per_tick + m, 1), (sections - 1 - to, 1))]
-            came = send(entering_now, [(a, b) for a, b in moves if a != b])
+            moves = [((b * per_tick + m, core), to) for b, core, to in trip]
+            came = send(entering_full, [(a, b) for a, b in moves if a != b])
             for a, b in moves:
                 if a == b:
-                    here = jnp.logical_and(section == a[0], role == a[1])
-                    came = jnp.where(here, entering_full, came)
+                    came = jnp.where(jnp.logical_and(section == a[0], role == a[1]), entering_full, came)
             pieces.append(came)
         return jnp.concatenate(pieces, axis=0)
 
-    feeds = [fed(0)]
-    for step in range(1, size.steps + 1):
-        feeds.append(fed(step, *(feeds[:1] if step < 3 else feeds[step - 2 : step])))
+    feeds = [jnp.tile(entering_full, (per_tick, 1))]
+    for trip in trips:
+        if trip:
+            feeds.append(fed(trip))
+            feeds.append(swap(feeds[-1]))
+    feeds = jnp.stack(feeds)
+
+    def reads(b_of):
+        index = jnp.int32(0)
+        for (to, core), blocks in ends.items():
+            b = b_of(to, core)
+            if b in blocks:
+                here = jnp.logical_and(section == to, role == core)
+                index = jnp.where(here, jnp.int32(turn[to, core, b]), index)
+        return index
+
+    def block_at(step):
+        def b_of(to, core):
+            side_to = to if core == 0 else sections - 1 - to
+            return ticks - 1 if step == size.steps else 2 * step - side_to
+
+        return b_of
+
+    where = jnp.concatenate([where, jnp.stack([reads(block_at(step)) for step in range(size.steps + 1)])])
     first_end = section == jnp.where(forward, 0, sections - 1)
+    first_feed = lax.dynamic_index_in_dim(feeds, where[4], 0, keepdims=False)
     x = jnp.concatenate([jnp.where(forward, fwd_in, bwd_in), swap(jnp.where(forward, bwd_in, fwd_in))], axis=1)
-    x = jnp.concatenate([jnp.where(first_end, feeds[0], x), jnp.zeros((rows, size.message - size.width), bf16)], axis=1)
-
-    hist_shapes = (shape(ticks + 1, rows, half), shape(ticks + 1, rows, size.kept))
-
-    def scratch(n):
-        return (
-            pltpu.VMEM((n, rows, half), bf16),
-            pltpu.VMEM((n, rows, size.kept), bf16),
-            pltpu.SemaphoreType.DMA((2 * n,)),
-        )
-
-    def averaged(old, late):
-        if replicas == 2:
-            came = lax.ppermute(late, "dp", [(0, 1), (1, 0)])
-            total = late.astype(f32) + came.astype(f32)
-        else:
-            came = lax.psum(late, "dp")
-            total = came.astype(f32)
-        return (old.astype(f32) - STEP_RATE * total / replicas).astype(bf16), came
-
-    squeeze_new, came = averaged(squeeze, squeeze_late[0, 0].T)
-    expand_new, _ = averaged(expand, tied(expand_late[0, 0], came))
+    x = jnp.concatenate([jnp.where(first_end, first_feed, x), jnp.zeros((rows, size.message - size.width), bf16)], axis=1)
+
+    hist_shapes = (shape(size.steps, rows, half), shape(size.steps, rows, size.kept))
+    hist_peer_shape = shape(2, size.steps - 1, rows, size.kept)
+    keep_own = (pltpu.VMEM((1, rows, half), bf16), pltpu.VMEM((1, rows, size.kept), bf16))
+    keep_peer = (pltpu.VMEM((2, 1, rows, size.kept), bf16),)
+
+    def sems(n):
+        return (pltpu.SemaphoreType.DMA((n,)),)
+
+    late_own = jnp.stack([squeeze_late[0, 0].T, expand_late[0, 0]])
+    if replicas == 2:
+        total = late_own.astype(f32) + lax.ppermute(late_own, "dp", [(0, 1), (1, 0)]).astype(f32)
+    else:
+        total = lax.psum(late_own, "dp").astype(f32)
+    squeeze_new = (squeeze.astype(f32) - STEP_RATE * total[0] / replicas).astype(bf16)
+    expand_new = (expand.astype(f32) - STEP_RATE * total[1] / replicas).astype(bf16)
 
     ring = (
         [((s, 0), (s + 2, 0)) for s in range(sections - 2)]
         + [((sections - 2, 0), (sections - 1, 1)), ((sections - 1, 0), (sections - 2, 1))]
         + [((s, 1), (s - 2, 1)) for s in range(2, sections)]
     )
-    aligned = [(s, s % 2) for s in everyone]
     ring_last = (
         [((s, 0), (s + 1, 0)) for s in range(1, sections - 1, 2)]
         + [((sections - 1, 0), (sections - 1, 1))]
@@ -405,16 +439,15 @@
 
     x, hist_mine, hist_other = call(
         first_kernel, "first", (shape(rows, size.message), *hist_shapes),
-        [SMEM, VMEM, VMEM, VMEM, VMEM], (VMEM, ANY, ANY), scratch(1),
+        [SMEM, VMEM, VMEM, VMEM, VMEM], (VMEM, ANY, ANY), keep_own + sems(2),
     )(where, x, again_own, own, other)
-    expand_peer_other = swap(tied(expand_peer, x))
-    mine_all = jnp.concatenate([own, squeeze_peer[None], expand_peer[None]], axis=0)
+    expand_peer_other = swap(tied(expand_peer, x))[:rank]
+    mine_all = jnp.concatenate([own, squeeze_peer[None], expand_peer[None, :rank]], axis=0)
     other_all = jnp.concatenate([other, squeeze_peer_other[None], expand_peer_other[None]], axis=0)
-    x, passed = call(
-        second_kernel, "second", (shape(rows, size.message), shape(2, rows, size.kept)),
-        [SMEM, VMEM, VMEM, VMEM, VMEM], (VMEM, VMEM),
-    )(where, tied(x, *feeds[1:]), again_peer, mine_all, other_all)
-    came = to_peer(passed, aligned)
+    x, hist_peer = call(
+        second_kernel, "second", (shape(rows, size.message), hist_peer_shape),
+        [SMEM, VMEM, VMEM, VMEM, VMEM], (VMEM, ANY), (*keep_peer, pltpu.SemaphoreType.DMA),
+    )(where, tied(x, feeds), again_peer, mine_all, other_all)
     x = send(x, ring)
     for step in range(1, size.steps):
         final = step + 1 == size.steps
@@ -422,30 +455,36 @@
             x = tied(x, squeeze_new)
         if step == 2:
             x = tied(x, expand_new)
-        x, passed, hist_mine, hist_other = call(
-            lambda size, *refs, step=step: pair_kernel(size, step, *refs), f"pair{step}",
-            (
-                shape(rows, size.message),
-                shape(2, rows, size.kept + (half if final else 0)),
-                *hist_shapes,
-            ),
-            [SMEM, VMEM, VMEM, VMEM, VMEM, VMEM, VMEM, VMEM, ANY, ANY], (VMEM, VMEM, ANY, ANY),
-            scratch(2), {8: 2, 9: 3},
-        )(where, x, feeds[step], again_own, again_peer, mine_all, other_all, came, hist_mine, hist_other)
+        body = functools.partial(lambda step, size, *refs: pair_kernel(size, step, *refs), step)
+        ins = (where, x, feeds, again_own, again_peer, mine_all, other_all, hist_mine, hist_other)
+        if final:
+            x, passed, hist_mine, hist_other = call(
+                body, f"pair{step}",
+                (shape(rows, size.message), shape(2, 1, rows, size.kept + half), *hist_shapes),
+                [SMEM] + [VMEM] * 6 + [ANY] * 2, (VMEM, VMEM, ANY, ANY), keep_own + sems(2), {7: 2, 8: 3},
+            )(*ins)
+        else:
+            x, hist_mine, hist_other, hist_peer = call(
+                body, f"pair{step}",
+                (shape(rows, size.message), *hist_shapes, hist_peer_shape),
+                [SMEM] + [VMEM] * 6 + [ANY] * 3, (VMEM, ANY, ANY, ANY), keep_own + keep_peer + sems(3),
+                {7: 1, 8: 2, 9: 3},
+            )(*ins, hist_peer)
         x = send(x, ring_last if final else ring)
-        came = to_peer(passed, both)
+    odd = to_peer(hist_peer, both)
+    late = to_peer(passed, both)
+    odd_got, late_got = swap(odd[1]), swap(late[1, 0])
     hist_got = swap(hist_other)
-    late, late_got = came, swap(came[1])
     last_mine, last_other = call(
         last_kernel, "last", (shape(rows, size.kept + half), shape(rows, size.kept + half)),
         [SMEM, VMEM, VMEM, VMEM, VMEM, VMEM], (VMEM, VMEM),
-    )(where, x, feeds[size.steps], again_own, own, other)
+    )(where, x, feeds, again_own, own, other)
     last_got = swap(last_other)
     squeeze_grad, expand_grad, fwd_carry, bwd_carry = call(
         end_kernel, "finish",
         (shape(rank, half), shape(rank, half), shape(rows, half), shape(rows, half)),
-        [SMEM] + [VMEM] * 9, (VMEM,) * 4,
-    )(where, hist_mine, hist_other, hist_got, late, late_got, last_mine, last_other, last_got, stash)
+        [SMEM] + [VMEM] * 11, (VMEM,) * 4,
+    )(where, hist_mine, hist_other, hist_got, odd, odd_got, late, late_got, last_mine, last_other, last_got, stash)
     return (
         squeeze_new.T[None],
         expand_new[None],

time: 108 us -> 117 us (1.083)
  waiting for transfers between devices: 33.8 us -> 54.1 us
  starting transfers between devices: 44.5 us -> 34 us
  other arithmetic: 10.3 us -> 8.84 us
    ppermute x2 -> x1, waiting for transfers between devices: 0.01 us -> 13.3 us  [shards(): lax.ppermute(late_own, 'dp', [(0, 1), (1, 0)]).astype(f32)]
    ppermute x16 -> x10, starting transfers between devices: 26.1 us -> 16.3 us  [send(): lax.ppermute(x, ('pipe', 'mp'), [(a * 2 + b, c * 2 + d) for (a, b), (c, d...]
    ppermute x16 -> x10, waiting for transfers between devices: 30.5 us -> 39.6 us  [send(): lax.ppermute(x, ('pipe', 'mp'), [(a * 2 + b, c * 2 + d) for (a, b), (c, d...]
    ppermute x9 -> x12, waiting for transfers between devices: 3.3 us -> 1.12 us  [swap(): return lax.ppermute(x, 'mp', [(0, 1), (1, 0)])]
    unnamed x24 -> x31, local copies, waits for them, and re-layouts: 0.75 us -> 2.33 us
    convert_element_type x2 -> x3, other arithmetic: 2.96 us -> 1.77 us  [the longest x1 0.89 us: shards(): (squeeze.astype(f32) - STEP_RATE * total[0] / replicas).astype(bf16)]
    ppermute x9 -> x12, starting transfers between devices: 16.3 us -> 16.5 us  [swap(): return lax.ppermute(x, 'mp', [(0, 1), (1, 0)])]
  transfers between devices with their start and end apart: 27 -> 23, of which waited for: 11 -> 11; matrix products, arithmetic and copies ran while one was open for 9% -> 8% of each run, Pallas kernels for 7% -> 3%
where the time goes in v4:
time: 117 us; the launch traced here: 116 us
  waiting for transfers between devices  54.1 us (46%)
  starting transfers between devices  34 us (29%)
  Pallas kernels  15.6 us (13%)
  other arithmetic  8.84 us (8%)
  local copies, waits for them, and re-layouts  2.65 us (2%)
    ppermute x10, waiting for transfers between devices, send(): lax.ppermute(x, ('pipe', 'mp'), [(a * 2 + b, c * 2 + d) for (a, b), (c, d...  39.6 us
    ppermute x12, starting transfers between devices, swap(): return lax.ppermute(x, 'mp', [(0, 1), (1, 0)])  16.5 us
    ppermute x10, starting transfers between devices, send(): lax.ppermute(x, ('pipe', 'mp'), [(a * 2 + b, c * 2 + d) for (a, b), (c, d...  16.3 us
    ppermute x1, waiting for transfers between devices, shards(): lax.ppermute(late_own, 'dp', [(0, 1), (1, 0)]).astype(f32)  13.3 us
    pallas_call x2, Pallas kernels, shards(): call(body, f'pair{step}', (shape(rows, size.message), *hist_shapes, hist_...  5.68 us
    pallas_call x1, Pallas kernels, shards(): call(body, f'pair{step}', (shape(rows, size.message), shape(2, 1, rows, s...  2.69 us
  transfers between devices with their start and end apart: 23, of which 11 were waited for; matrix products, arithmetic and copies ran while one was open for 8% of the time, Pallas kernels for 3%

profile of v4, /device:TPU:25, one launch (start us, length us, event | category | flops | bytes accessed | tf_op | source)
XLA Modules:
  0.0 116.1 jit_solution(15608354745976483970)
XLA Ops:
  0.6 1.3 %collective-permute-start.9 = (bf16[64,3584]{1,0:T(8,128)(2,1)}, bf16[64,3584]{1,0:T(8,128)(2,1)}, u32[]{:S(2)}, u32[]{:S(2)}) collective-permute-start(bf16[64,3584]{1,0:T(8,128)(2,1)} %bitcast.95), channel_id=1, source_target_pairs={{0,4},{1,5},{4,0},{5,1},{8,12},{9,13},{12,8},{13,9},{16,20},{17,21... | collective-permute-start | bytes 1376264 | tf_op jit(solution)/shard_map/ppermute | solution.py:304
  1.9 1.1 copy-done
  3.0 1.2 %copy-done.2 = bf16[1,1,8,16,3584]{4,3,2,1,0:T(8,128)(2,1)S(1)} copy-done((bf16[1,1,8,16,3584]{4,3,2,1,0:T(8,128)(2,1)S(1)}, bf16[1,1,8,16,3584]{4,3,2,1,0:T(8,128)(2,1)}, u32[]{:S(2)}) %copy-start.2) | copy-done | bytes 917528
  4.6 1.0 collective-permute-start.7
  5.6 0.7 select_bitcast_fusion.3
  6.3 0.5 collective-permute-start.1
  6.8 0.7 select_bitcast_fusion.1
  7.6 0.5 collective-permute-start.8
  8.1 1.0 pad_maximum_fusion.2
  9.4 1.0 pad_maximum_fusion.4
  10.4 1.4 %collective-permute-start.2 = (bf16[16,7168]{1,0:T(8,128)(2,1)S(1)}, bf16[16,7168]{1,0:T(8,128)(2,1)S(1)}, u32[]{:S(2)}, u32[]{:S(2)}) collective-permute-start(bf16[16,7168]{1,0:T(8,128)(2,1)S(1)} %pad_maximum_fusion.4), channel_id=1, source_target_pairs={{8,0},{16,1},{1,29},{9,28},{12,4},{20,5},{5,25},{13,24},{10,2},{18... | collective-permute-start | bytes 688136 | tf_op jit(solution)/shard_map/ppermute | solution.py:304
  11.9 2.1 %collective-permute-start.4 = (bf16[16,7168]{1,0:T(8,128)(2,1)S(1)}, bf16[16,7168]{1,0:T(8,128)(2,1)S(1)}, u32[]{:S(2)}, u32[]{:S(2)}) collective-permute-start(bf16[16,7168]{1,0:T(8,128)(2,1)S(1)} %pad_maximum_fusion.4), channel_id=1, source_target_pairs={{24,0},{28,1},{17,29},{25,28},{21,25},{26,2},{30,3},{19,31},{27,30... | collective-permute-start | bytes 688136 | tf_op jit(solution)/shard_map/ppermute | solution.py:304
  13.9 0.9 bitcast_dynamic-update-slice_fusion.4
  14.8 5.4 %collective-permute-done.2 = bf16[16,7168]{1,0:T(8,128)(2,1)S(1)} collective-permute-done((bf16[16,7168]{1,0:T(8,128)(2,1)S(1)}, bf16[16,7168]{1,0:T(8,128)(2,1)S(1)}, u32[]{:S(2)}, u32[]{:S(2)}) %collective-permute-start.2) | collective-permute-done | bytes 229408 | tf_op jit(solution)/shard_map/ppermute | solution.py:304
  20.2 2.1 %collective-permute-start.3 = (bf16[16,7168]{1,0:T(8,128)(2,1)S(1)}, bf16[16,7168]{1,0:T(8,128)(2,1)S(1)}, u32[]{:S(2)}, u32[]{:S(2)}) collective-permute-start(bf16[16,7168]{1,0:T(8,128)(2,1)S(1)} %collective-permute-done.2), channel_id=1, source_target_pairs={{0,1},{1,0},{2,3},{3,2},{4,5},{5,4},{6,7},{7,6},{8,9},{9,8},{10,11... | collective-permute-start | bytes 688136 | tf_op jit(solution)/shard_map/ppermute | solution.py:307
  22.3 1.9 %collective-permute-done.4 = bf16[16,7168]{1,0:T(8,128)(2,1)S(1)} collective-permute-done((bf16[16,7168]{1,0:T(8,128)(2,1)S(1)}, bf16[16,7168]{1,0:T(8,128)(2,1)S(1)}, u32[]{:S(2)}, u32[]{:S(2)}) %collective-permute-start.4) | collective-permute-done | bytes 229408 | tf_op jit(solution)/shard_map/ppermute | solution.py:304
  24.2 1.2 %collective-permute-start = (bf16[2,64,3584]{2,1,0:T(8,128)(2,1)S(1)}, bf16[2,64,3584]{2,1,0:T(8,128)(2,1)S(1)}, u32[]{:S(2)}, u32[]{:S(2)}) collective-permute-start(bf16[2,64,3584]{2,1,0:T(8,128)(2,1)S(1)} %copy-done.8), channel_id=1, source_target_pairs={{0,2},{2,0},{1,3},{3,1},{4,6},{6,4},{5,7},{7,5},{8,10},{10,8},{9,1... | collective-permute-start | bytes 2752520 | tf_op jit(solution)/shard_map/ppermute | solution.py:423
  25.5 2.9 %collective-permute-start.10 = (bf16[80,3584]{1,0:T(8,128)(2,1)S(1)}, bf16[80,3584]{1,0:T(8,128)(2,1)S(1)}, u32[]{:S(2)}, u32[]{:S(2)}) collective-permute-start(bf16[80,3584]{1,0:T(8,128)(2,1)S(1)} %fusion.6), channel_id=1, source_target_pairs={{0,4},{1,5},{4,0},{5,1},{8,12},{9,13},{12,8},{13,9},{16,20},{17,21... | collective-permute-start | bytes 1720328 | tf_op jit(solution)/shard_map/ppermute | solution.py:304
  28.4 0.4 collective-permute-start.11
  28.8 1.0 maximum_select_fusion
  29.9 1.7 %first.1 = (bf16[16,7680]{1,0:T(8,128)(2,1)S(1)}, bf16[4,16,3584]{2,1,0:T(8,128)(2,1)S(1)}, bf16[4,16,3712]{2,1,0:T(8,128)(2,1)S(1)}) custom-call(s32[9]{0:T(128)S(1)} %concatenate.24.where.refs_0_, bf16[16,7680]{1,0:T(8,128)(2,1)S(1)} %concatenate.27.x_in, f32[8,16,64]{2,1,0:T(8,128)S(1)} %add.18.again_own.refs_3_, ...), custom_call_target="tpu_custom_call" | custom-call | flops 58720256 | bytes 3670016 | tf_op jit(solution)/shard_map/first/pallas_call | solution.py:440
  31.6 13.3 %collective-permute-done = bf16[2,64,3584]{2,1,0:T(8,128)(2,1)S(1)} collective-permute-done((bf16[2,64,3584]{2,1,0:T(8,128)(2,1)S(1)}, bf16[2,64,3584]{2,1,0:T(8,128)(2,1)S(1)}, u32[]{:S(2)}, u32[]{:S(2)}) %collective-permute-start) | collective-permute-done | bytes 917536 | tf_op jit(solution)/shard_map/ppermute | solution.py:423
  45.3 1.2 %pad_maximum_fusion.mine.refs_5_ = bf16[4,64,3584]{2,1,0:T(8,128)(2,1)S(1)} fusion(bf16[1,64,3584]{2,1,0:T(8,128)(2,1)S(1)} %slice_bitcast_fusion.1, bf16[1,64,3584]{2,1,0:T(8,128)(2,1)} %bitcast.35, bf16[2,64,3584]{2,1,0:T(8,128)(2,1)S(1)} %pad_maximum_fusion.3.mine), kind=kLoop, calls=%fused_computation | loop fusion | flops 1835008 | bytes 3670016 | tf_op jit(solution)/shard_map/concatenate | solution.py:445
  46.6 0.7 collective-permute-done.12
  47.5 1.6 %second.1 = (bf16[16,7680]{1,0:T(8,128)(2,1)S(1)}, bf16[2,3,16,3712]{3,2,1,0:T(8,128)(2,1)S(1)}) custom-call(s32[9]{0:T(128)S(1)} %concatenate.24.where.refs_0_, bf16[16,7680]{1,0:T(8,128)(2,1)S(1)} %get-tuple-element.34.x_in, bf16[16,512]{1,0:T(8,128)(2,1)S(1)} %slice.50.again_peer.refs_4_, bf16[4,64,3584]{2,1,0:T(8,128)(2,1)S(1)} %pad_maximum_fusion.mine.refs_5_, ...), custom_call_target="tpu_custom_call" | custom-call | flops 58720256 | bytes 3670016 | tf_op jit(solution)/shard_map/second/pallas_call | solution.py:447
  49.1 1.9 %collective-permute-start.13 = (bf16[16,7680]{1,0:T(8,128)(2,1)S(1)}, bf16[16,7680]{1,0:T(8,128)(2,1)S(1)}, u32[]{:S(2)}, u32[]{:S(2)}) collective-permute-start(bf16[16,7680]{1,0:T(8,128)(2,1)S(1)} %get-tuple-element.37), channel_id=1, source_target_pairs={{0,8},{4,12},{8,16},{12,20},{16,24},{20,28},{24,29},{28,25},{9,1},... | collective-permute-start | bytes 737288 | tf_op jit(solution)/shard_map/ppermute | solution.py:304
  51.0 0.9 fusion.5
  51.9 5.0 %collective-permute-done.13.refs_1_ = bf16[16,7680]{1,0:T(8,128)(2,1)S(1)} collective-permute-done((bf16[16,7680]{1,0:T(8,128)(2,1)S(1)}, bf16[16,7680]{1,0:T(8,128)(2,1)S(1)}, u32[]{:S(2)}, u32[]{:S(2)}) %collective-permute-start.13) | collective-permute-done | bytes 245792 | tf_op jit(solution)/shard_map/ppermute | solution.py:304
  56.9 2.8 %pair1.1 = (bf16[16,7680]{1,0:T(8,128)(2,1)S(1)}, bf16[4,16,3584]{2,1,0:T(8,128)(2,1)S(1)}, bf16[4,16,3712]{2,1,0:T(8,128)(2,1)S(1)}, bf16[2,3,16,3712]{3,2,1,0:T(8,128)(2,1)S(1)}) custom-call(s32[9]{0:T(128)S(1)} %concatenate.24.where.refs_0_, ...), custom_call_target="tpu_custom_call", output_to_operand_aliasing={{1}: (7, {}), {2}: (8, {}), {3}: (9, {})} | custom-call | flops 58720256 | bytes 3670016 | tf_op jit(solution)/shard_map/pair1/pallas_call | solution.py:467
  59.8 1.9 %collective-permute-start.14 = (bf16[16,7680]{1,0:T(8,128)(2,1)S(1)}, bf16[16,7680]{1,0:T(8,128)(2,1)S(1)}, u32[]{:S(2)}, u32[]{:S(2)}) collective-permute-start(bf16[16,7680]{1,0:T(8,128)(2,1)S(1)} %get-tuple-element.42), channel_id=1, source_target_pairs={{0,8},{4,12},{8,16},{12,20},{16,24},{20,28},{24,29},{28,25},{9,1},... | collective-permute-start | bytes 737288 | tf_op jit(solution)/shard_map/ppermute | solution.py:304
  61.7 6.2 %collective-permute-done.14.refs_1_ = bf16[16,7680]{1,0:T(8,128)(2,1)S(1)} collective-permute-done((bf16[16,7680]{1,0:T(8,128)(2,1)S(1)}, bf16[16,7680]{1,0:T(8,128)(2,1)S(1)}, u32[]{:S(2)}, u32[]{:S(2)}) %collective-permute-start.14) | collective-permute-done | bytes 245792 | tf_op jit(solution)/shard_map/ppermute | solution.py:304
  67.8 2.8 %pair2.1 = (bf16[16,7680]{1,0:T(8,128)(2,1)S(1)}, bf16[4,16,3584]{2,1,0:T(8,128)(2,1)S(1)}, bf16[4,16,3712]{2,1,0:T(8,128)(2,1)S(1)}, bf16[2,3,16,3712]{3,2,1,0:T(8,128)(2,1)S(1)}) custom-call(s32[9]{0:T(128)S(1)} %concatenate.24.where.refs_0_, ...), custom_call_target="tpu_custom_call", output_to_operand_aliasing={{1}: (7, {}), {2}: (8, {}), {3}: (9, {})} | custom-call | flops 58720256 | bytes 3670016 | tf_op jit(solution)/shard_map/pair2/pallas_call | solution.py:467
  70.7 1.9 %collective-permute-start.15 = (bf16[16,7680]{1,0:T(8,128)(2,1)S(1)}, bf16[16,7680]{1,0:T(8,128)(2,1)S(1)}, u32[]{:S(2)}, u32[]{:S(2)}) collective-permute-start(bf16[16,7680]{1,0:T(8,128)(2,1)S(1)} %get-tuple-element.46), channel_id=1, source_target_pairs={{0,8},{4,12},{8,16},{12,20},{16,24},{20,28},{24,29},{28,25},{9,1},... | collective-permute-start | bytes 737288 | tf_op jit(solution)/shard_map/ppermute | solution.py:304
  72.6 6.2 %collective-permute-done.15.refs_1_ = bf16[16,7680]{1,0:T(8,128)(2,1)S(1)} collective-permute-done((bf16[16,7680]{1,0:T(8,128)(2,1)S(1)}, bf16[16,7680]{1,0:T(8,128)(2,1)S(1)}, u32[]{:S(2)}, u32[]{:S(2)}) %collective-permute-start.15) | collective-permute-done | bytes 245792 | tf_op jit(solution)/shard_map/ppermute | solution.py:304
  78.8 2.7 %pair3.1 = (bf16[16,7680]{1,0:T(8,128)(2,1)S(1)}, bf16[2,1,16,7296]{3,2,1,0:T(8,128)(2,1)S(1)}, bf16[4,16,3584]{2,1,0:T(8,128)(2,1)S(1)}, bf16[4,16,3712]{2,1,0:T(8,128)(2,1)S(1)}) custom-call(s32[9]{0:T(128)S(1)} %concatenate.24.where.refs_0_, bf16[16,7680]{1,0:T(8,128)(2,1)S(1)} %collective-permute-done.15.refs_1_, ...), custom_call_target="tpu_custom_call", output_to_operand_aliasing={{2}: (7, {}), {3}: (8, {})} | custom-call | flops 58720256 | bytes 3670016 | tf_op jit(solution)/shard_map/pair3/pallas_call | solution.py:461
  81.5 1.2 %collective-permute-start.19 = (bf16[2,1,16,7296]{3,2,1,0:T(8,128)(2,1)S(1)}, bf16[2,1,16,7296]{3,2,1,0:T(8,128)(2,1)S(1)}, u32[]{:S(2)}, u32[]{:S(2)}) collective-permute-start(bf16[2,1,16,7296]{3,2,1,0:T(8,128)(2,1)S(1)} %get-tuple-element.52), channel_id=1, source_target_pairs={{0,4},{1,5},{4,0},{5,1},{8,12},{9,13},{12,8},{13,9},{16,20},{17,21... | collective-permute-start | bytes 1400840 | tf_op jit(solution)/shard_map/ppermute | solution.py:304
  82.7 1.3 %collective-permute-start.21 = (bf16[16,7680]{1,0:T(8,128)(2,1)S(1)}, bf16[16,7680]{1,0:T(8,128)(2,1)S(1)}, u32[]{:S(2)}, u32[]{:S(2)}) collective-permute-start(bf16[16,7680]{1,0:T(8,128)(2,1)S(1)} %get-tuple-element.53), channel_id=1, source_target_pairs={{4,8},{12,16},{20,24},{28,29},{9,5},{17,13},{25,21},{6,10},{14,18}... | collective-permute-start | bytes 737288 | tf_op jit(solution)/shard_map/ppermute | solution.py:304
  84.4 1.4 %collective-permute-start.16 = (bf16[4,16,3712]{2,1,0:T(8,128)(2,1)S(1)}, bf16[4,16,3712]{2,1,0:T(8,128)(2,1)S(1)}, u32[]{:S(2)}, u32[]{:S(2)}) collective-permute-start(bf16[4,16,3712]{2,1,0:T(8,128)(2,1)S(1)} %get-tuple-element.50.sent), channel_id=1, source_target_pairs={{0,1},{1,0},{2,3},{3,2},{4,5},{5,4},{6,7},{7,6},{8,9},{9,8},{10,11... | collective-permute-start | bytes 1425416 | tf_op jit(solution)/shard_map/ppermute | solution.py:307
  85.8 1.4 %collective-permute-done.21.x_in = bf16[16,7680]{1,0:T(8,128)(2,1)S(1)} collective-permute-done((bf16[16,7680]{1,0:T(8,128)(2,1)S(1)}, bf16[16,7680]{1,0:T(8,128)(2,1)S(1)}, u32[]{:S(2)}, u32[]{:S(2)}) %collective-permute-start.21) | collective-permute-done | bytes 245792 | tf_op jit(solution)/shard_map/ppermute | solution.py:304
  87.2 1.4 %last.1 = (bf16[16,7296]{1,0:T(8,128)(2,1)S(1)}, bf16[16,7296]{1,0:T(8,128)(2,1)S(1)}) custom-call(s32[9]{0:T(128)S(1)} %concatenate.24.where.refs_0_, bf16[16,7680]{1,0:T(8,128)(2,1)S(1)} %collective-permute-done.21.x_in, bf16[5,16,7168]{2,1,0:T(8,128)(2,1)S(1)} %bitcast_dynamic-update-slice_fusion.refs_2_.feeds, f32[8,16,64]{2,1,0:T(8,128)S(1)} %add.18.again_own.refs_3_, ...), custom_call_target="tpu_custom_call" | custom-call | flops 58720256 | bytes 3670016 | tf_op jit(solution)/shard_map/last/pallas_call | solution.py:478
  88.6 6.2 %collective-permute-start.22 = (bf16[16,7296]{1,0:T(8,128)(2,1)S(1)}, bf16[16,7296]{1,0:T(8,128)(2,1)S(1)}, u32[]{:S(2)}, u32[]{:S(2)}) collective-permute-start(bf16[16,7296]{1,0:T(8,128)(2,1)S(1)} %get-tuple-element.55.last_other), channel_id=1, source_target_pairs={{0,1},{1,0},{2,3},{3,2},{4,5},{5,4},{6,7},{7,6},{8,9},{9,8},{10,11... | collective-permute-start | bytes 700424 | tf_op jit(solution)/shard_map/ppermute | solution.py:307
  94.8 1.0 collective-permute-done.19.late
  95.8 2.7 %collective-permute-start.20 = (bf16[16,7296]{1,0:T(8,128)(2,1)S(1)}, bf16[16,7296]{1,0:T(8,128)(2,1)S(1)}, u32[]{:S(2)}, u32[]{:S(2)}) collective-permute-start(bf16[16,7296]{1,0:T(8,128)(2,1)S(1)} %slice_bitcast_fusion.3), channel_id=1, source_target_pairs={{0,1},{1,0},{2,3},{3,2},{4,5},{5,4},{6,7},{7,6},{8,9},{9,8},{10,11... | collective-permute-start | bytes 700424 | tf_op jit(solution)/shard_map/ppermute | solution.py:307
  98.5 12.6 %collective-permute-done.17.odd = bf16[2,3,16,3712]{3,2,1,0:T(8,128)(2,1)S(1)} collective-permute-done((bf16[2,3,16,3712]{3,2,1,0:T(8,128)(2,1)S(1)}, bf16[2,3,16,3712]{3,2,1,0:T(8,128)(2,1)S(1)}, u32[]{:S(2)}, u32[]{:S(2)}) %collective-permute-start.17) | collective-permute-done | bytes 712736 | tf_op jit(solution)/shard_map/ppermute | solution.py:304
  111.1 1.6 %collective-permute-start.18 = (bf16[3,16,3712]{2,1,0:T(8,128)(2,1)S(1)}, bf16[3,16,3712]{2,1,0:T(8,128)(2,1)S(1)}, u32[]{:S(2)}, u32[]{:S(2)}) collective-permute-start(bf16[3,16,3712]{2,1,0:T(8,128)(2,1)S(1)} %slice_bitcast_fusion.2), channel_id=1, source_target_pairs={{0,1},{1,0},{2,3},{3,2},{4,5},{5,4},{6,7},{7,6},{8,9},{9,8},{10,11... | collective-permute-start | bytes 1069064 | tf_op jit(solution)/shard_map/ppermute | solution.py:307
  112.7 0.9 fusion.2
  113.5 0.4 collective-permute-done.18.odd_got
  114.0 2.2 %finish.1 = (bf16[64,3584]{1,0:T(8,128)(2,1)}, bf16[64,3584]{1,0:T(8,128)(2,1)}, bf16[16,3584]{1,0:T(8,128)(2,1)}, bf16[16,3584]{1,0:T(8,128)(2,1)}) custom-call(s32[9]{0:T(128)S(1)} %concatenate.24.where.refs_0_, bf16[4,16,3584]{2,1,0:T(8,128)(2,1)S(1)} %get-tuple-element.49.mine, bf16[4,16,3712]{2,1,0:T(8,128)(2,1)S(1)} %get-tuple-element.50.sent, ...), custom_call_target="tpu_custom_call" | custom-call | flops 58720256 | bytes 3670016 | tf_op jit(solution)/shard_map/finish/pallas_call | solution.py:483
  (61 shorter events, 1.9 us)
Async XLA Ops:
  0.6 24.8 %collective-permute-start.9 = (bf16[64,3584]{1,0:T(8,128)(2,1)}, bf16[64,3584]{1,0:T(8,128)(2,1)}, u32[]{:S(2)}, u32[]{:S(2)}) collective-permute-start(bf16[64,3584]{1,0:T(8,128)(2,1)} %bitcast.95), channel_id=1, source_target_pairs={{0,4},{1,5},{4,0},{5,1},{8,12},{9,13},{12,8},{13,9},{16,20},{17,21... | collective-permute-start | bytes 1376264 | tf_op jit(solution)/shard_map/ppermute | solution.py:304
  1.9 1.1 copy-start
  3.0 1.2 %copy-start.2 = (bf16[1,1,8,16,3584]{4,3,2,1,0:T(8,128)(2,1)S(1)}, bf16[1,1,8,16,3584]{4,3,2,1,0:T(8,128)(2,1)}, u32[]{:S(2)}) copy-start(bf16[1,1,8,16,3584]{4,3,2,1,0:T(8,128)(2,1)} %param.15) | copy-start | bytes 2752516
  4.2 1.4 %copy-start.10 = (bf16[1,16,3584]{2,1,0:T(8,128)(2,1)S(1)}, bf16[1,16,3584]{2,1,0:T(8,128)(2,1)}, u32[]{:S(2)}) copy-start(bf16[1,16,3584]{2,1,0:T(8,128)(2,1)} %param.9) | copy-start | bytes 344068
  4.2 1.4 %copy-start.11 = (bf16[1,16,3584]{2,1,0:T(8,128)(2,1)S(1)}, bf16[1,16,3584]{2,1,0:T(8,128)(2,1)}, u32[]{:S(2)}) copy-start(bf16[1,16,3584]{2,1,0:T(8,128)(2,1)} %param.10) | copy-start | bytes 344068
  4.2 2.6 %copy-start.12 = (bf16[1,1,16,3584]{3,2,1,0:T(8,128)(2,1)S(1)}, bf16[1,1,16,3584]{3,2,1,0:T(8,128)(2,1)}, u32[]{:S(2)}) copy-start(bf16[1,1,16,3584]{3,2,1,0:T(8,128)(2,1)} %param.16) | copy-start | bytes 344068
  4.2 2.6 %copy-start.13 = (bf16[1,1,16,3584]{3,2,1,0:T(8,128)(2,1)S(1)}, bf16[1,1,16,3584]{3,2,1,0:T(8,128)(2,1)}, u32[]{:S(2)}) copy-start(bf16[1,1,16,3584]{3,2,1,0:T(8,128)(2,1)} %param.17) | copy-start | bytes 344068
  4.2 3.3 %copy-start.1 = (bf16[1,3584,64]{1,2,0:T(8,128)(2,1)S(1)}, bf16[1,3584,64]{1,2,0:T(8,128)(2,1)}, u32[]{:S(2)}) copy-start(bf16[1,3584,64]{1,2,0:T(8,128)(2,1)} %param.11) | copy-start | bytes 1376260
  4.2 3.3 %copy-start.4 = (bf16[1,64,3584]{2,1,0:T(8,128)(2,1)S(1)}, bf16[1,64,3584]{2,1,0:T(8,128)(2,1)}, u32[]{:S(2)}) copy-start(bf16[1,64,3584]{2,1,0:T(8,128)(2,1)} %param.12) | copy-start | bytes 1376260
  4.6 4.6 %collective-permute-start.7 = (f32[8,16,64]{2,1,0:T(8,128)S(1)}, f32[8,16,64]{2,1,0:T(8,128)S(1)}, u32[]{:S(2)}, u32[]{:S(2)}) collective-permute-start(f32[8,16,64]{2,1,0:T(8,128)S(1)} %stashed.1), channel_id=1, source_target_pairs={{0,1},{1,0},{2,3},{3,2},{4,5},{5,4},{6,7},{7,6},{8,9},{9,8},{10,11... | collective-permute-start | bytes 98312 | tf_op jit(solution)/shard_map/ppermute | solution.py:307
  6.3 1.9 %copy-start.5 = (bf16[1,1,64,3584]{3,2,1,0:T(8,128)(2,1)S(1)}, bf16[1,1,64,3584]{3,2,1,0:T(8,128)(2,1)}, u32[]{:S(2)}) copy-start(bf16[1,1,64,3584]{3,2,1,0:T(8,128)(2,1)} %param.14) | copy-start | bytes 1376260
  6.3 1.9 %copy-start.6 = (bf16[1,1,3584,64]{2,3,1,0:T(8,128)(2,1)S(1)}, bf16[1,1,3584,64]{2,3,1,0:T(8,128)(2,1)}, u32[]{:S(2)}) copy-start(bf16[1,1,3584,64]{2,3,1,0:T(8,128)(2,1)} %param.13) | copy-start | bytes 1376260
  6.3 3.1 %collective-permute-start.1 = (bf16[16,3584]{1,0:T(8,128)(2,1)}, bf16[16,3584]{1,0:T(8,128)(2,1)}, u32[]{:S(2)}, u32[]{:S(2)}) collective-permute-start(bf16[16,3584]{1,0:T(8,128)(2,1)} %get-tuple-element.69), channel_id=1, source_target_pairs={{0,1},{1,0},{2,3},{3,2},{4,5},{5,4},{6,7},{7,6},{8,9},{9,8},{10,11... | collective-permute-start | bytes 344072 | tf_op jit(solution)/shard_map/ppermute | solution.py:307
  7.5 21.4 %collective-permute-start.6 = (bf16[16,3584]{1,0:T(8,128)(2,1)}, bf16[16,3584]{1,0:T(8,128)(2,1)}, u32[]{:S(2)}, u32[]{:S(2)}) collective-permute-start(bf16[16,3584]{1,0:T(8,128)(2,1)} %get-tuple-element.71), channel_id=1, source_target_pairs={{0,1},{1,0},{2,3},{3,2},{4,5},{5,4},{6,7},{7,6},{8,9},{9,8},{10,11... | collective-permute-start | bytes 344072 | tf_op jit(solution)/shard_map/ppermute | solution.py:307
  7.6 22.3 %collective-permute-start.8 = (bf16[2,64,3584]{2,1,0:T(8,128)(2,1)S(1)}, bf16[2,64,3584]{2,1,0:T(8,128)(2,1)S(1)}, u32[]{:S(2)}, u32[]{:S(2)}) collective-permute-start(bf16[2,64,3584]{2,1,0:T(8,128)(2,1)S(1)} %pad_maximum_fusion.3.mine), channel_id=1, source_target_pairs={{0,1},{1,0},{2,3},{3,2},{4,5},{5,4},{6,7},{7,6},{8,9},{9,8},{10,11... | collective-permute-start | bytes 2752520 | tf_op jit(solution)/shard_map/ppermute | solution.py:307
  9.4 14.9 %copy-start.8 = (bf16[2,64,3584]{2,1,0:T(8,128)(2,1)S(1)}, bf16[2,64,3584]{2,1,0:T(8,128)(2,1)}, u32[]{:S(2)}) copy-start(bf16[2,64,3584]{2,1,0:T(8,128)(2,1)} %pad_maximum_fusion.2) | copy-start | bytes 2752516
  10.4 18.4 %copy-start.9 = (bf16[16,3584]{1,0:T(8,128)(2,1)S(1)}, bf16[16,3584]{1,0:T(8,128)(2,1)}, u32[]{:S(2)}) copy-start(bf16[16,3584]{1,0:T(8,128)(2,1)} %get-tuple-element.70) | copy-start | bytes 344068
  10.4 9.8 %collective-permute-start.2 = (bf16[16,7168]{1,0:T(8,128)(2,1)S(1)}, bf16[16,7168]{1,0:T(8,128)(2,1)S(1)}, u32[]{:S(2)}, u32[]{:S(2)}) collective-permute-start(bf16[16,7168]{1,0:T(8,128)(2,1)S(1)} %pad_maximum_fusion.4), channel_id=1, source_target_pairs={{8,0},{16,1},{1,29},{9,28},{12,4},{20,5},{5,25},{13,24},{10,2},{18... | collective-permute-start | bytes 688136 | tf_op jit(solution)/shard_map/ppermute | solution.py:304
  11.9 12.4 %collective-permute-start.4 = (bf16[16,7168]{1,0:T(8,128)(2,1)S(1)}, bf16[16,7168]{1,0:T(8,128)(2,1)S(1)}, u32[]{:S(2)}, u32[]{:S(2)}) collective-permute-start(bf16[16,7168]{1,0:T(8,128)(2,1)S(1)} %pad_maximum_fusion.4), channel_id=1, source_target_pairs={{24,0},{28,1},{17,29},{25,28},{21,25},{26,2},{30,3},{19,31},{27,30... | collective-permute-start | bytes 688136 | tf_op jit(solution)/shard_map/ppermute | solution.py:304
  20.2 5.2 %collective-permute-start.3 = (bf16[16,7168]{1,0:T(8,128)(2,1)S(1)}, bf16[16,7168]{1,0:T(8,128)(2,1)S(1)}, u32[]{:S(2)}, u32[]{:S(2)}) collective-permute-start(bf16[16,7168]{1,0:T(8,128)(2,1)S(1)} %collective-permute-done.2), channel_id=1, source_target_pairs={{0,1},{1,0},{2,3},{3,2},{4,5},{5,4},{6,7},{7,6},{8,9},{9,8},{10,11... | collective-permute-start | bytes 688136 | tf_op jit(solution)/shard_map/ppermute | solution.py:307
  24.2 20.7 %collective-permute-start = (bf16[2,64,3584]{2,1,0:T(8,128)(2,1)S(1)}, bf16[2,64,3584]{2,1,0:T(8,128)(2,1)S(1)}, u32[]{:S(2)}, u32[]{:S(2)}) collective-permute-start(bf16[2,64,3584]{2,1,0:T(8,128)(2,1)S(1)} %copy-done.8), channel_id=1, source_target_pairs={{0,2},{2,0},{1,3},{3,1},{4,6},{6,4},{5,7},{7,5},{8,10},{10,8},{9,1... | collective-permute-start | bytes 2752520 | tf_op jit(solution)/shard_map/ppermute | solution.py:423
  25.5 2.9 %collective-permute-start.5 = (bf16[16,7168]{1,0:T(8,128)(2,1)S(1)}, bf16[16,7168]{1,0:T(8,128)(2,1)S(1)}, u32[]{:S(2)}, u32[]{:S(2)}) collective-permute-start(bf16[16,7168]{1,0:T(8,128)(2,1)S(1)} %collective-permute-done.4), channel_id=1, source_target_pairs={{0,1},{1,0},{2,3},{3,2},{4,5},{5,4},{6,7},{7,6},{8,9},{9,8},{10,11... | collective-permute-start | bytes 688136 | tf_op jit(solution)/shard_map/ppermute | solution.py:307
  25.5 19.7 %collective-permute-start.10 = (bf16[80,3584]{1,0:T(8,128)(2,1)S(1)}, bf16[80,3584]{1,0:T(8,128)(2,1)S(1)}, u32[]{:S(2)}, u32[]{:S(2)}) collective-permute-start(bf16[80,3584]{1,0:T(8,128)(2,1)S(1)} %fusion.6), channel_id=1, source_target_pairs={{0,4},{1,5},{4,0},{5,1},{8,12},{9,13},{12,8},{13,9},{16,20},{17,21... | collective-permute-start | bytes 1720328 | tf_op jit(solution)/shard_map/ppermute | solution.py:304
  28.4 18.9 %collective-permute-start.11 = (bf16[64,3584]{1,0:T(8,128)(2,1)}, bf16[64,3584]{1,0:T(8,128)(2,1)S(1)}, u32[]{:S(2)}, u32[]{:S(2)}) collective-permute-start(bf16[64,3584]{1,0:T(8,128)(2,1)} %collective-permute-done.9), channel_id=1, source_target_pairs={{0,1},{1,0},{2,3},{3,2},{4,5},{5,4},{6,7},{7,6},{8,9},{9,8},{10,11... | collective-permute-start | bytes 1376264 | tf_op jit(solution)/shard_map/ppermute | solution.py:307
  29.8 15.1 %copy-start.7 = (bf16[1,1,3584,64]{2,3,1,0:T(8,128)(2,1)S(1)}, bf16[1,1,3584,64]{2,3,1,0:T(8,128)(2,1)}, u32[]{:S(2)}) copy-start(bf16[1,1,3584,64]{2,3,1,0:T(8,128)(2,1)} %param.13) | copy-start | bytes 1376260
  45.2 2.0 %collective-permute-start.12 = (bf16[80,3584]{1,0:T(8,128)(2,1)S(1)}, bf16[80,3584]{1,0:T(8,128)(2,1)S(1)}, u32[]{:S(2)}, u32[]{:S(2)}) collective-permute-start(bf16[80,3584]{1,0:T(8,128)(2,1)S(1)} %collective-permute-done.10), channel_id=1, source_target_pairs={{0,1},{1,0},{2,3},{3,2},{4,5},{5,4},{6,7},{7,6},{8,9},{9,8},{10,11... | collective-permute-start | bytes 1720328 | tf_op jit(solution)/shard_map/ppermute | solution.py:307
  49.1 7.8 %collective-permute-start.13 = (bf16[16,7680]{1,0:T(8,128)(2,1)S(1)}, bf16[16,7680]{1,0:T(8,128)(2,1)S(1)}, u32[]{:S(2)}, u32[]{:S(2)}) collective-permute-start(bf16[16,7680]{1,0:T(8,128)(2,1)S(1)} %get-tuple-element.37), channel_id=1, source_target_pairs={{0,8},{4,12},{8,16},{12,20},{16,24},{20,28},{24,29},{28,25},{9,1},... | collective-permute-start | bytes 737288 | tf_op jit(solution)/shard_map/ppermute | solution.py:304
  59.8 8.1 %collective-permute-start.14 = (bf16[16,7680]{1,0:T(8,128)(2,1)S(1)}, bf16[16,7680]{1,0:T(8,128)(2,1)S(1)}, u32[]{:S(2)}, u32[]{:S(2)}) collective-permute-start(bf16[16,7680]{1,0:T(8,128)(2,1)S(1)} %get-tuple-element.42), channel_id=1, source_target_pairs={{0,8},{4,12},{8,16},{12,20},{16,24},{20,28},{24,29},{28,25},{9,1},... | collective-permute-start | bytes 737288 | tf_op jit(solution)/shard_map/ppermute | solution.py:304
  70.7 8.1 %collective-permute-start.15 = (bf16[16,7680]{1,0:T(8,128)(2,1)S(1)}, bf16[16,7680]{1,0:T(8,128)(2,1)S(1)}, u32[]{:S(2)}, u32[]{:S(2)}) collective-permute-start(bf16[16,7680]{1,0:T(8,128)(2,1)S(1)} %get-tuple-element.46), channel_id=1, source_target_pairs={{0,8},{4,12},{8,16},{12,20},{16,24},{20,28},{24,29},{28,25},{9,1},... | collective-permute-start | bytes 737288 | tf_op jit(solution)/shard_map/ppermute | solution.py:304
  81.5 14.3 %collective-permute-start.19 = (bf16[2,1,16,7296]{3,2,1,0:T(8,128)(2,1)S(1)}, bf16[2,1,16,7296]{3,2,1,0:T(8,128)(2,1)S(1)}, u32[]{:S(2)}, u32[]{:S(2)}) collective-permute-start(bf16[2,1,16,7296]{3,2,1,0:T(8,128)(2,1)S(1)} %get-tuple-element.52), channel_id=1, source_target_pairs={{0,4},{1,5},{4,0},{5,1},{8,12},{9,13},{12,8},{13,9},{16,20},{17,21... | collective-permute-start | bytes 1400840 | tf_op jit(solution)/shard_map/ppermute | solution.py:304
  82.7 4.5 %collective-permute-start.21 = (bf16[16,7680]{1,0:T(8,128)(2,1)S(1)}, bf16[16,7680]{1,0:T(8,128)(2,1)S(1)}, u32[]{:S(2)}, u32[]{:S(2)}) collective-permute-start(bf16[16,7680]{1,0:T(8,128)(2,1)S(1)} %get-tuple-element.53), channel_id=1, source_target_pairs={{4,8},{12,16},{20,24},{28,29},{9,5},{17,13},{25,21},{6,10},{14,18}... | collective-permute-start | bytes 737288 | tf_op jit(solution)/shard_map/ppermute | solution.py:304
  84.0 27.0 %collective-permute-start.17 = (bf16[2,3,16,3712]{3,2,1,0:T(8,128)(2,1)S(1)}, bf16[2,3,16,3712]{3,2,1,0:T(8,128)(2,1)S(1)}, u32[]{:S(2)}, u32[]{:S(2)}) collective-permute-start(bf16[2,3,16,3712]{3,2,1,0:T(8,128)(2,1)S(1)} %get-tuple-element.51), channel_id=1, source_target_pairs={{0,4},{1,5},{4,0},{5,1},{8,12},{9,13},{12,8},{13,9},{16,20},{17,21... | collective-permute-start | bytes 2138120 | tf_op jit(solution)/shard_map/ppermute | solution.py:304
  84.4 29.2 %collective-permute-start.16 = (bf16[4,16,3712]{2,1,0:T(8,128)(2,1)S(1)}, bf16[4,16,3712]{2,1,0:T(8,128)(2,1)S(1)}, u32[]{:S(2)}, u32[]{:S(2)}) collective-permute-start(bf16[4,16,3712]{2,1,0:T(8,128)(2,1)S(1)} %get-tuple-element.50.sent), channel_id=1, source_target_pairs={{0,1},{1,0},{2,3},{3,2},{4,5},{5,4},{6,7},{7,6},{8,9},{9,8},{10,11... | collective-permute-start | bytes 1425416 | tf_op jit(solution)/shard_map/ppermute | solution.py:307
  88.6 25.0 %collective-permute-start.22 = (bf16[16,7296]{1,0:T(8,128)(2,1)S(1)}, bf16[16,7296]{1,0:T(8,128)(2,1)S(1)}, u32[]{:S(2)}, u32[]{:S(2)}) collective-permute-start(bf16[16,7296]{1,0:T(8,128)(2,1)S(1)} %get-tuple-element.55.last_other), channel_id=1, source_target_pairs={{0,1},{1,0},{2,3},{3,2},{4,5},{5,4},{6,7},{7,6},{8,9},{9,8},{10,11... | collective-permute-start | bytes 700424 | tf_op jit(solution)/shard_map/ppermute | solution.py:307
  95.8 18.2 %copy-start.3 = (bf16[1,1,8,16,3584]{4,3,2,1,0:T(8,128)(2,1)S(1)}, bf16[1,1,8,16,3584]{4,3,2,1,0:T(8,128)(2,1)}, u32[]{:S(2)}) copy-start(bf16[1,1,8,16,3584]{4,3,2,1,0:T(8,128)(2,1)} %param.15) | copy-start | bytes 2752516
  95.8 17.7 %collective-permute-start.20 = (bf16[16,7296]{1,0:T(8,128)(2,1)S(1)}, bf16[16,7296]{1,0:T(8,128)(2,1)S(1)}, u32[]{:S(2)}, u32[]{:S(2)}) collective-permute-start(bf16[16,7296]{1,0:T(8,128)(2,1)S(1)} %slice_bitcast_fusion.3), channel_id=1, source_target_pairs={{0,1},{1,0},{2,3},{3,2},{4,5},{5,4},{6,7},{7,6},{8,9},{9,8},{10,11... | collective-permute-start | bytes 700424 | tf_op jit(solution)/shard_map/ppermute | solution.py:307
  111.1 2.9 %collective-permute-start.18 = (bf16[3,16,3712]{2,1,0:T(8,128)(2,1)S(1)}, bf16[3,16,3712]{2,1,0:T(8,128)(2,1)S(1)}, u32[]{:S(2)}, u32[]{:S(2)}) collective-permute-start(bf16[3,16,3712]{2,1,0:T(8,128)(2,1)S(1)} %slice_bitcast_fusion.2), channel_id=1, source_target_pairs={{0,1},{1,0},{2,3},{3,2},{4,5},{5,4},{6,7},{7,6},{8,9},{9,8},{10,11... | collective-permute-start | bytes 1069064 | tf_op jit(solution)/shard_map/ppermute | solution.py:307

commit v5 on v4

--- a/solution.py
+++ b/solution.py
@@ -116,8 +116,17 @@
 def keep_passed(size, ref, x0, x1, ranks):
     half, kept = size.half, size.kept
     for part, x in enumerate((x0, x1)):
-        ref[part, 0, :, :half] = x
-        ref[part, 0, :, half:kept] = ranks
+        ref[part, :, :half] = x
+        ref[part, :, half:kept] = ranks
+
+
+def entering(place, size, step, x0, x1, where, feeds, at_end):
+    index = where[4 + step]
+    for n, ref in feeds.items():
+        here = jnp.logical_and(at_end, index == n)
+        x0 = jnp.where(here, ref[:, : size.half], x0)
+        x1 = jnp.where(here, ref[:, size.half :], x1)
+    return x0, x1
 
 
 def first_kernel(size, where, x_in, again_own, mine, other, out, hist_mine, hist_other, keep_mine, keep_other, sems):
@@ -138,77 +147,75 @@
         copy.wait()
 
 
-def second_kernel(size, where, x_in, again_peer, mine, other, out, hist_peer, keep_peer, sem):
+def second_kernel(size, where, x_in, again_peer, mine, other, out, held):
     place = Place(where)
     x0, x1, payload = read(size, x_in)
-    again = join_words(again_peer[:, : 2 * size.rank])
-    y0, y1, ranks, sent = section_step(size, place, place.peer, 1, x0, x1, again, payload, mine, other, 2)
-    keep_passed(size, keep_peer, x0, x1, ranks)
-    copy = pltpu.make_async_copy(keep_peer, hist_peer.at[:, pl.ds(0, 1)], sem)
-    copy.start()
+    y0, y1, ranks, sent = section_step(
+        size, place, place.peer, 1, x0, x1, again_peer[0], payload, mine, other, 2
+    )
+    keep_passed(size, held, x0, x1, ranks)
     aligned = place.aligned
     sent = [jnp.where(aligned, sent[j], payload[j]) for j in range(size.slots)]
     write(size, out, jnp.where(aligned, y0, x0), jnp.where(aligned, y1, x1), sent)
-    copy.wait()
-
-
-def pair_kernel(size, step, where, x_in, feeds, again_own, again_peer, mine, other, *rest):
-    final = step + 1 == size.steps
-    if final:
-        _, _, out, passed, hist_mine, hist_other, keep_mine, keep_other, sems = rest
-    else:
-        _, _, _, out, hist_mine, hist_other, hist_peer, keep_mine, keep_other, keep_peer, sems = rest
-        passed = keep_peer
-    half, kept, span = size.half, size.kept, 2 * size.rank
+
+
+def pair_kernel(size, step, turns, where, x_in, held, passed, again_own, again_peer, mine, other, *rest):
+    feeds = dict(zip(turns, rest))
+    _, _, out, held_out, passed_out, hist_mine, hist_other, keep_mine, keep_other, sems = rest[len(turns) :]
+    half, kept = size.half, size.kept
     place = Place(where)
     aligned = place.aligned
     x0, x1, payload = read(size, x_in)
-    feed = feeds.at[where[4 + step]]
-    x0 = jnp.where(place.at_end, feed[:, :half], x0)
-    x1 = jnp.where(place.at_end, feed[:, half:], x1)
+    x0, x1 = entering(place, size, step, x0, x1, where, feeds, place.at_end)
     tick = jnp.where(aligned, 2 * step, 2 * step - 1)
-    now, before = (again_peer[:, i * span : (i + 1) * span] for i in (step, step - 1))
-    again_peer = join_words(jnp.where(aligned, now, before))
+    again_peer = again_peer[jnp.where(aligned, step, step - 1)]
     own = again_own[2 * step]
     at_peer = jnp.where(aligned, 0, 2)
     y0, y1, ranks, payload = section_step(
         size, place, jnp.where(aligned, place.section, place.peer), tick, x0, x1,
         jnp.where(aligned, own, again_peer), payload, mine, other, at_peer,
     )
-    z0, z1, ranks_b, payload = section_step(
+    z0, z1, ranks_b, sent = section_step(
         size, place, jnp.where(aligned, place.peer, place.section), tick + 1, y0, y1,
         jnp.where(aligned, again_peer, own), payload, mine, other, 2 - at_peer,
     )
     keep(
         size, keep_mine, keep_other,
         jnp.where(aligned, x0, y0), jnp.where(aligned, x1, y1), jnp.where(aligned, ranks, ranks_b),
-    )
-    keep_passed(
-        size, passed, jnp.where(aligned, y0, x0), jnp.where(aligned, y1, x1), jnp.where(aligned, ranks_b, ranks)
     )
     copies = [
         pltpu.make_async_copy(keep_mine, hist_mine.at[pl.ds(step, 1)], sems.at[0]),
         pltpu.make_async_copy(keep_other, hist_other.at[pl.ds(step, 1)], sems.at[1]),
     ]
-    if not final:
-        copies.append(pltpu.make_async_copy(keep_peer, hist_peer.at[:, pl.ds(step, 1)], sems.at[2]))
     for copy in copies:
         copy.start()
+    final = step + 1 == size.steps
+    for part, (first, second) in enumerate(((x0, y0), (x1, y1))):
+        if not final:
+            held_out[part, :, :half] = second
+            held_out[part, :, half:] = ranks_b
+        if step == 2:
+            passed_out[0, part] = passed[0, part]
+        at = passed_out.at[step - 1 if not final else 0, part]
+        at[:, :half] = jnp.where(aligned, held[part, :, :half], first)
+        at[:, half:] = jnp.where(aligned, held[part, :, half:], ranks)
     if final:
-        passed[0, 0, :, kept:] = z0
-        passed[1, 0, :, kept:] = z1
-    write(size, out, z0, z1, payload)
+        held_out[...] = jnp.zeros(held_out.shape, held_out.dtype)
+        sent = [jnp.where(aligned, payload[j], sent[j]) for j in range(size.slots)]
+        z0, z1 = jnp.where(aligned, y0, z0), jnp.where(aligned, y1, z1)
+    write(size, out, z0, z1, sent)
     for copy in copies:
         copy.wait()
 
 
-def last_kernel(size, where, x_in, feeds, again_own, mine, other, last_mine, last_other):
+def last_kernel(size, turns, where, x_in, again_own, mine, other, *rest):
+    feeds = dict(zip(turns, rest))
+    last_mine, last_other = rest[len(turns) :]
     half, kept = size.half, size.kept
     place = Place(where)
     x0, x1, payload = read(size, x_in)
-    feed = feeds.at[where[4 + size.steps]]
-    x0 = jnp.where(place.at_end, feed[:, :half], x0)
-    x1 = jnp.where(place.at_end, feed[:, half:], x1)
+    at_end = jnp.where(place.forward, place.section, place.sections - 1 - place.section) == 0
+    x0, x1 = entering(place, size, size.steps, x0, x1, where, feeds, at_end)
     tick = size.ticks - 1
     y0, y1, ranks, _ = section_step(
         size, place, place.section, tick, x0, x1, again_own[tick], payload, mine, other, 0
@@ -221,9 +228,8 @@
 
 def end_kernel(size, where, mine, sent, got, odd, odd_got, late, late_got, last_mine, last_other, last_got, stash, *outs):
     squeeze_grad, expand_grad, fwd, bwd = outs
-    ticks, half, kept, rank, steps = size.ticks, size.half, size.kept, size.rank, size.steps
+    ticks, half, kept, rank = size.ticks, size.half, size.kept, size.rank
     place = Place(where)
-    forward = place.forward
 
     def block(role, t, cols, part=0):
         here = place.role == role
@@ -234,15 +240,11 @@
 
         if t % 2 == 0:
             return pick((mine, sent)[part].at[i], got.at[i])
-
-        def passed(i):
-            if i + 1 < steps:
-                return pick(odd.at[part, i], odd_got.at[i])
-            if i + 1 == steps:
-                return pick(late.at[part, 0], late_got)
+        if t + 1 == ticks:
             return pick((last_mine, last_other)[part], last_got)
-
-        return jnp.where(place.side == role, passed(i + 1), passed(i))
+        if t + 3 == ticks:
+            return pick(late.at[part], late_got)
+        return pick(odd.at[i, part], odd_got.at[i])
 
     lag = 2 * (place.sections - 1 - place.section) + 1
     ranks = jnp.concatenate([block(1, t, slice(half, kept), 1) for t in range(ticks)], axis=0)
@@ -262,10 +264,7 @@
         expand_grad[:, cols] = (dot(regated, g, TN) * size.out_scale).astype(jnp.bfloat16)
 
     def carry(role):
-        here = place.role == role
-        early = jnp.where(here, late[0, 0, :, kept:], late_got[:, kept:])
-        final = jnp.where(here, last_mine[:, kept:], last_got[:, kept:])
-        return jnp.where(place.side == role, final, early)
+        return jnp.where(place.role == role, last_mine[:, kept:], last_got[:, kept:])
 
     fwd[...] = carry(0)
     bwd[...] = carry(1)
@@ -336,18 +335,15 @@
     acts, cots = activations[0], cotangent[0]
     both = [(s, c) for s in everyone for c in (0, 1)]
 
-    squeeze_peer = to_peer(squeeze, both)
     own = lax.optimization_barrier(jnp.stack([squeeze, expand]))
+    peer = to_peer(own, both)
     other = swap(own)
-    squeeze_peer_other = swap(squeeze_peer)
+
     partial = call(
         stash_kernel, "stashed", shape(ticks, rows, rank, dtype=f32), [VMEM, VMEM], VMEM
     )(stash, squeeze)
     again_own = partial + swap(partial)
-    words = jnp.concatenate([split_words(again_own[t]) for t in range(1, ticks, 2)], axis=1)
-    words = jnp.pad(words, ((0, 0), (0, half - words.shape[1])))
-    expand_peer = to_peer(tied(jnp.concatenate([expand, words], axis=0), squeeze_peer), both)
-    again_peer = expand_peer[rank:, : size.steps * 2 * rank]
+    again_peer = to_peer(again_own[1::2], [(s, 1) for s in everyone])
 
     entering_full = jnp.concatenate(
         [jnp.where(forward, acts, cots), swap(jnp.where(forward, cots, acts))], axis=1
@@ -386,7 +382,6 @@
         if trip:
             feeds.append(fed(trip))
             feeds.append(swap(feeds[-1]))
-    feeds = jnp.stack(feeds)
 
     def reads(b_of):
         index = jnp.int32(0)
@@ -397,6 +392,10 @@
                 index = jnp.where(here, jnp.int32(turn[to, core, b]), index)
         return index
 
+    def used(b_of):
+        turns = {turn[to, core, b_of(to, core)] for (to, core), blocks in ends.items() if b_of(to, core) in blocks}
+        return tuple(sorted(turns))
+
     def block_at(step):
         def b_of(to, core):
             side_to = to if core == 0 else sections - 1 - to
@@ -406,25 +405,31 @@
 
     where = jnp.concatenate([where, jnp.stack([reads(block_at(step)) for step in range(size.steps + 1)])])
     first_end = section == jnp.where(forward, 0, sections - 1)
-    first_feed = lax.dynamic_index_in_dim(feeds, where[4], 0, keepdims=False)
+    first_feed = feeds[0]
+    for n in used(block_at(0)):
+        first_feed = jnp.where(where[4] == n, feeds[n], first_feed)
     x = jnp.concatenate([jnp.where(forward, fwd_in, bwd_in), swap(jnp.where(forward, bwd_in, fwd_in))], axis=1)
     x = jnp.concatenate([jnp.where(first_end, first_feed, x), jnp.zeros((rows, size.message - size.width), bf16)], axis=1)
 
     hist_shapes = (shape(size.steps, rows, half), shape(size.steps, rows, size.kept))
-    hist_peer_shape = shape(2, size.steps - 1, rows, size.kept)
-    keep_own = (pltpu.VMEM((1, rows, half), bf16), pltpu.VMEM((1, rows, size.kept), bf16))
-    keep_peer = (pltpu.VMEM((2, 1, rows, size.kept), bf16),)
-
-    def sems(n):
-        return (pltpu.SemaphoreType.DMA((n,)),)
-
-    late_own = jnp.stack([squeeze_late[0, 0].T, expand_late[0, 0]])
-    if replicas == 2:
-        total = late_own.astype(f32) + lax.ppermute(late_own, "dp", [(0, 1), (1, 0)]).astype(f32)
-    else:
-        total = lax.psum(late_own, "dp").astype(f32)
-    squeeze_new = (squeeze.astype(f32) - STEP_RATE * total[0] / replicas).astype(bf16)
-    expand_new = (expand.astype(f32) - STEP_RATE * total[1] / replicas).astype(bf16)
+    odd_shape = (2, rows, size.kept)
+    keep_own = (
+        pltpu.VMEM((1, rows, half), bf16),
+        pltpu.VMEM((1, rows, size.kept), bf16),
+        pltpu.SemaphoreType.DMA((2,)),
+    )
+
+    def averaged(old, late):
+        if replicas == 2:
+            came = lax.ppermute(late, "dp", [(0, 1), (1, 0)])
+            total = late.astype(f32) + came.astype(f32)
+        else:
+            came = lax.psum(late, "dp")
+            total = came.astype(f32)
+        return (old.astype(f32) - STEP_RATE * total / replicas).astype(bf16), came
+
+    squeeze_new, came = averaged(squeeze, squeeze_late[0, 0].T)
+    expand_new, _ = averaged(expand, tied(expand_late[0, 0], came))
 
     ring = (
         [((s, 0), (s + 2, 0)) for s in range(sections - 2)]
@@ -432,53 +437,58 @@
         + [((s, 1), (s - 2, 1)) for s in range(2, sections)]
     )
     ring_last = (
-        [((s, 0), (s + 1, 0)) for s in range(1, sections - 1, 2)]
+        [((s, 0), (s + 1, 0)) for s in range(sections - 1)]
         + [((sections - 1, 0), (sections - 1, 1))]
-        + [((s, 1), (s - 1, 1)) for s in range(2, sections, 2)]
-    )
-
+        + [((s, 1), (s - 1, 1)) for s in range(1, sections)]
+    )
+    passing = [(s, c) for s, c in both if c == 1 or (s ^ 1) >= sections - size.slots]
     x, hist_mine, hist_other = call(
         first_kernel, "first", (shape(rows, size.message), *hist_shapes),
-        [SMEM, VMEM, VMEM, VMEM, VMEM], (VMEM, ANY, ANY), keep_own + sems(2),
+        [SMEM, VMEM, VMEM, VMEM, VMEM], (VMEM, ANY, ANY), keep_own,
     )(where, x, again_own, own, other)
-    expand_peer_other = swap(tied(expand_peer, x))[:rank]
-    mine_all = jnp.concatenate([own, squeeze_peer[None], expand_peer[None, :rank]], axis=0)
-    other_all = jnp.concatenate([other, squeeze_peer_other[None], expand_peer_other[None]], axis=0)
-    x, hist_peer = call(
-        second_kernel, "second", (shape(rows, size.message), hist_peer_shape),
-        [SMEM, VMEM, VMEM, VMEM, VMEM], (VMEM, ANY), (*keep_peer, pltpu.SemaphoreType.DMA),
-    )(where, tied(x, feeds), again_peer, mine_all, other_all)
+    peer_other = swap(peer)
+    mine_all = jnp.concatenate([own, tied(peer, x)], axis=0)
+    other_all = jnp.concatenate([other, peer_other], axis=0)
+    x, held = call(
+        second_kernel, "second", (shape(rows, size.message), shape(*odd_shape)),
+        [SMEM, VMEM, VMEM, VMEM, VMEM], (VMEM, VMEM),
+    )(where, tied(x, *feeds[1::2]), again_peer, mine_all, other_all)
     x = send(x, ring)
+    passed = jnp.zeros((1, *odd_shape), bf16)
     for step in range(1, size.steps):
         final = step + 1 == size.steps
-        if step == 1:
+        if step == 2:
             x = tied(x, squeeze_new)
-        if step == 2:
+        if step == 3:
             x = tied(x, expand_new)
-        body = functools.partial(lambda step, size, *refs: pair_kernel(size, step, *refs), step)
-        ins = (where, x, feeds, again_own, again_peer, mine_all, other_all, hist_mine, hist_other)
+        turns = used(block_at(step))
+        body = functools.partial(lambda step, turns, size, *refs: pair_kernel(size, step, turns, *refs), step, turns)
+        x, held, passed_now, hist_mine, hist_other = call(
+            body, f"pair{step}",
+            (
+                shape(rows, size.message),
+                shape(*((8, 128) if final else odd_shape)),
+                shape(1 if final else step, *odd_shape),
+                *hist_shapes,
+            ),
+            [SMEM] + [VMEM] * (7 + len(turns)) + [ANY] * 2, (VMEM, VMEM, VMEM, ANY, ANY), keep_own,
+            {8 + len(turns): 3, 9 + len(turns): 4},
+        )(
+            where, x, held, passed, again_own, again_peer, mine_all, other_all, *(feeds[n] for n in turns),
+            hist_mine, hist_other,
+        )
+        x = send(x, ring_last if final else ring)
         if final:
-            x, passed, hist_mine, hist_other = call(
-                body, f"pair{step}",
-                (shape(rows, size.message), shape(2, 1, rows, size.kept + half), *hist_shapes),
-                [SMEM] + [VMEM] * 6 + [ANY] * 2, (VMEM, VMEM, ANY, ANY), keep_own + sems(2), {7: 2, 8: 3},
-            )(*ins)
-        else:
-            x, hist_mine, hist_other, hist_peer = call(
-                body, f"pair{step}",
-                (shape(rows, size.message), *hist_shapes, hist_peer_shape),
-                [SMEM] + [VMEM] * 6 + [ANY] * 3, (VMEM, ANY, ANY, ANY), keep_own + keep_peer + sems(3),
-                {7: 1, 8: 2, 9: 3},
-            )(*ins, hist_peer)
-        x = send(x, ring_last if final else ring)
-    odd = to_peer(hist_peer, both)
-    late = to_peer(passed, both)
-    odd_got, late_got = swap(odd[1]), swap(late[1, 0])
+            odd, late = to_peer(passed, passing), to_peer(passed_now[0], passing)
+        passed = passed_now
+    odd_got, late_got = swap(odd[:, 1]), swap(late[1])
     hist_got = swap(hist_other)
+    turns = used(block_at(size.steps))
     last_mine, last_other = call(
-        last_kernel, "last", (shape(rows, size.kept + half), shape(rows, size.kept + half)),
-        [SMEM, VMEM, VMEM, VMEM, VMEM, VMEM], (VMEM, VMEM),
-    )(where, x, feeds, again_own, own, other)
+        functools.partial(lambda turns, size, *refs: last_kernel(size, turns, *refs), turns), "last",
+        (shape(rows, size.kept + half), shape(rows, size.kept + half)),
+        [SMEM] + [VMEM] * (4 + len(turns)), (VMEM, VMEM),
+    )(where, tied(x, odd), again_own, own, other, *(feeds[n] for n in turns))
     last_got = swap(last_other)
     squeeze_grad, expand_grad, fwd_carry, bwd_carry = call(
         end_kernel, "finish",

time: 117 us -> 99.1 us (0.85)
  waiting for transfers between devices: 54.1 us -> 36.5 us
    ppermute x1 -> x2, waiting for transfers between devices: 13.3 us -> 0.01 us  [averaged(): came = lax.ppermute(late, 'dp', [(0, 1), (1, 0)])]
    ppermute x12 -> x11, starting transfers between devices: 16.5 us -> 8.18 us  [swap(): return lax.ppermute(x, 'mp', [(0, 1), (1, 0)])]
    ppermute x10, starting transfers between devices: 16.3 us -> 24.3 us  [send(): lax.ppermute(x, ('pipe', 'mp'), [(a * 2 + b, c * 2 + d) for (a, b), (c, d...]
    ppermute x10, waiting for transfers between devices: 39.6 us -> 33.9 us  [send(): lax.ppermute(x, ('pipe', 'mp'), [(a * 2 + b, c * 2 + d) for (a, b), (c, d...]
    ppermute x12 -> x11, waiting for transfers between devices: 1.12 us -> 2.57 us  [swap(): return lax.ppermute(x, 'mp', [(0, 1), (1, 0)])]
    ppermute x1 -> x2, starting transfers between devices: 1.21 us -> 2.48 us  [averaged(): came = lax.ppermute(late, 'dp', [(0, 1), (1, 0)])]
  transfers between devices with their start and end apart: 23 -> 23, of which waited for: 11 -> 10; matrix products, arithmetic and copies ran while one was open for 8% -> 7% of each run, Pallas kernels for 3% -> 14%
where the time goes in v5:
time: 99.1 us; the launch traced here: 98.6 us
  waiting for transfers between devices  36.5 us (37%)
  starting transfers between devices  34.9 us (35%)
  Pallas kernels  15.7 us (16%)
  other arithmetic  7.97 us (8%)
  local copies, waits for them, and re-layouts  2.56 us (3%)
    ppermute x10, waiting for transfers between devices, send(): lax.ppermute(x, ('pipe', 'mp'), [(a * 2 + b, c * 2 + d) for (a, b), (c, d...  33.9 us
    ppermute x10, starting transfers between devices, send(): lax.ppermute(x, ('pipe', 'mp'), [(a * 2 + b, c * 2 + d) for (a, b), (c, d...  24.3 us
    pallas_call x3, Pallas kernels, shards(): call(body, f'pair{step}', (shape(rows, size.message), shape(*((8, 128) if...  8.74 us
    ppermute x11, starting transfers between devices, swap(): return lax.ppermute(x, 'mp', [(0, 1), (1, 0)])  8.18 us
    ppermute x11, waiting for transfers between devices, swap(): return lax.ppermute(x, 'mp', [(0, 1), (1, 0)])  2.57 us
    ppermute x2, starting transfers between devices, averaged(): came = lax.ppermute(late, 'dp', [(0, 1), (1, 0)])  2.48 us
    unnamed x15, local copies, waits for them, and re-layouts  2.28 us
    pallas_call x1, Pallas kernels, shards(): call(end_kernel, 'finish', (shape(rank, half), shape(rank, half), shape(r...  2.07 us
  transfers between devices with their start and end apart: 23, of which 10 were waited for; matrix products, arithmetic and copies ran while one was open for 7% of the time, Pallas kernels for 14%

profile of v5, /device:TPU:25, one launch (start us, length us, event | category | flops | bytes accessed | tf_op | source)
XLA Modules:
  0.0 98.6 jit_solution(12130271308077304484)
XLA Ops:
  0.6 1.0 %select_bitcast_fusion.3 = (bf16[16,3584]{1,0:T(8,128)(2,1)S(1)}, bf16[16,3584]{1,0:T(8,128)(2,1)S(1)}) fusion(bf16[1,16,3584]{2,1,0:T(8,128)(2,1)} %param.9, bf16[1,16,3584]{2,1,0:T(8,128)(2,1)} %param.10, pred[]{:T(512)S(6)} %eq.22), kind=kLoop, calls=%fused_computation.12 | loop fusion | flops 114688 | bytes 458753 | tf_op jit(solution)/shard_map/jit(_where)/select_n | solution.py:349
  1.7 0.7 collective-permute-start.2
  2.4 1.7 %select_bitcast_fusion.1 = (bf16[16,3584]{1,0:T(8,128)(2,1)}, bf16[16,3584]{1,0:T(8,128)(2,1)}) fusion(bf16[1,1,16,3584]{3,2,1,0:T(8,128)(2,1)} %param.16, bf16[1,1,16,3584]{3,2,1,0:T(8,128)(2,1)} %param.17, pred[]{:T(512)S(6)} %eq.22), kind=kLoop, calls=%fused_computation.10 | loop fusion | flops 114688 | bytes 458753 | tf_op jit(solution)/shard_map/jit(_where)/select_n | solution.py:411
  4.1 1.0 %copy-done = bf16[1,3584,64]{1,2,0:T(8,128)(2,1)S(1)} copy-done((bf16[1,3584,64]{1,2,0:T(8,128)(2,1)S(1)}, bf16[1,3584,64]{1,2,0:T(8,128)(2,1)}, u32[]{:S(2)}) %copy-start) | copy-done | bytes 458776
  5.1 1.2 %copy-done.2 = bf16[1,1,8,16,3584]{4,3,2,1,0:T(8,128)(2,1)S(1)} copy-done((bf16[1,1,8,16,3584]{4,3,2,1,0:T(8,128)(2,1)S(1)}, bf16[1,1,8,16,3584]{4,3,2,1,0:T(8,128)(2,1)}, u32[]{:S(2)}) %copy-start.2) | copy-done | bytes 917528
  6.3 0.4 stashed.1
  6.7 0.6 collective-permute-start.5
  7.3 1.3 %collective-permute-start.3 = (bf16[16,7168]{1,0:T(8,128)(2,1)S(1)}, bf16[16,7168]{1,0:T(8,128)(2,1)S(1)}, u32[]{:S(2)}, u32[]{:S(2)}) collective-permute-start(bf16[16,7168]{1,0:T(8,128)(2,1)S(1)} %pad_maximum_fusion.2.refs_8_.refs_5_), channel_id=1, source_target_pairs={{8,0},{16,1},{1,29},{9,28},{12,4},{20,5},{5,25},{13,24},{10,2},{18... | collective-permute-start | bytes 688136 | tf_op jit(solution)/shard_map/ppermute | solution.py:303
  8.6 0.1 pad_maximum_fusion.1.mine.refs_3_
  8.7 0.1 collective-permute-start.6
  8.8 1.3 %collective-permute-start.9 = (bf16[2,64,3584]{2,1,0:T(8,128)(2,1)S(1)}, bf16[2,64,3584]{2,1,0:T(8,128)(2,1)}, u32[]{:S(2)}, u32[]{:S(2)}) collective-permute-start(bf16[2,64,3584]{2,1,0:T(8,128)(2,1)S(1)} %pad_maximum_fusion.1.mine.refs_3_), channel_id=1, source_target_pairs={{0,4},{1,5},{4,0},{5,1},{8,12},{9,13},{12,8},{13,9},{16,20},{17,21... | collective-permute-start | bytes 2752520 | tf_op jit(solution)/shard_map/ppermute | solution.py:303
  10.1 0.1 concatenate.18.where.refs_0_
  10.2 1.3 %collective-permute-start = (bf16[64,3584]{1,0:T(8,128)(2,1)S(1)}, bf16[64,3584]{1,0:T(8,128)(2,1)S(1)}, u32[]{:S(2)}, u32[]{:S(2)}) collective-permute-start(bf16[64,3584]{1,0:T(8,128)(2,1)S(1)} %bitcast.51), channel_id=1, source_target_pairs={{0,2},{2,0},{1,3},{3,1},{4,6},{6,4},{5,7},{7,5},{8,10},{10,8},{9,1... | collective-permute-start | bytes 1376264 | tf_op jit(solution)/shard_map/ppermute | solution.py:424
  11.4 0.8 add.18.again_own.refs_4_.refs_2_
  12.3 2.1 %collective-permute-start.8 = (f32[4,16,64]{2,1,0:T(8,128)S(1)}, f32[4,16,64]{2,1,0:T(8,128)S(1)}, u32[]{:S(2)}, u32[]{:S(2)}) collective-permute-start(f32[4,16,64]{2,1,0:T(8,128)S(1)} %slice.9), channel_id=1, source_target_pairs={{1,5},{5,1},{9,13},{13,9},{17,21},{21,17},{25,29},{29,25},{3,7},{7... | collective-permute-start | bytes 49160 | tf_op jit(solution)/shard_map/ppermute | solution.py:303
  14.4 2.5 %collective-permute-done.3.refs_9_.refs_8_ = bf16[16,7168]{1,0:T(8,128)(2,1)S(1)} collective-permute-done((bf16[16,7168]{1,0:T(8,128)(2,1)S(1)}, bf16[16,7168]{1,0:T(8,128)(2,1)S(1)}, u32[]{:S(2)}, u32[]{:S(2)}) %collective-permute-start.3) | collective-permute-done | bytes 229408 | tf_op jit(solution)/shard_map/ppermute | solution.py:303
  16.9 5.1 %collective-permute-start.7 = (bf16[16,7168]{1,0:T(8,128)(2,1)S(1)}, bf16[16,7168]{1,0:T(8,128)(2,1)S(1)}, u32[]{:S(2)}, u32[]{:S(2)}) collective-permute-start(bf16[16,7168]{1,0:T(8,128)(2,1)S(1)} %pad_maximum_fusion.2.refs_8_.refs_5_), channel_id=1, source_target_pairs={{24,0},{28,1},{17,29},{25,28},{21,25},{26,2},{30,3},{19,31},{27,30... | collective-permute-start | bytes 688136 | tf_op jit(solution)/shard_map/ppermute | solution.py:303
  22.0 1.1 %maximum_select_fusion = bf16[16,7168]{1,0:T(8,128)(2,1)S(1)} fusion(bf16[16,3584]{1,0:T(8,128)(2,1)} %collective-permute-done.4, bf16[16,3584]{1,0:T(8,128)(2,1)} %get-tuple-element.70, bf16[16,7168]{1,0:T(8,128)(2,1)S(1)} %collective-permute-done.3.refs_9_.refs_8_, pred[]{:T(512)S(6)} %eq.25, pred[]{:T(512)S(6)} %eq.24, ...), kind=kLoop, calls=%fused_computation.7 | loop fusion | flops 1146880 | bytes 917506 | tf_op jit(solution)/shard_map/jit(_where)/select_n | solution.py:412
  23.1 1.7 %first.1 = (bf16[16,7680]{1,0:T(8,128)(2,1)S(1)}, bf16[4,16,3584]{2,1,0:T(8,128)(2,1)S(1)}, bf16[4,16,3712]{2,1,0:T(8,128)(2,1)S(1)}) custom-call(s32[9]{0:T(128)S(1)} %concatenate.18.where.refs_0_, bf16[16,7680]{1,0:T(8,128)(2,1)S(1)} %concatenate.21.x_in, f32[8,16,64]{2,1,0:T(8,128)S(1)} %add.18.again_own.refs_4_.refs_2_, ...), custom_call_target="tpu_custom_call" | custom-call | flops 58720256 | bytes 3670016 | tf_op jit(solution)/shard_map/first/pallas_call | solution.py:445
  24.8 12.9 %collective-permute-done.9 = bf16[2,64,3584]{2,1,0:T(8,128)(2,1)} collective-permute-done((bf16[2,64,3584]{2,1,0:T(8,128)(2,1)S(1)}, bf16[2,64,3584]{2,1,0:T(8,128)(2,1)}, u32[]{:S(2)}, u32[]{:S(2)}) %collective-permute-start.9) | collective-permute-done | bytes 917536 | tf_op jit(solution)/shard_map/ppermute | solution.py:303
  37.8 2.6 %collective-permute-done.7.refs_10_.refs_9_ = bf16[16,7168]{1,0:T(8,128)(2,1)S(1)} collective-permute-done((bf16[16,7168]{1,0:T(8,128)(2,1)S(1)}, bf16[16,7168]{1,0:T(8,128)(2,1)S(1)}, u32[]{:S(2)}, u32[]{:S(2)}) %collective-permute-start.7) | collective-permute-done | bytes 229408 | tf_op jit(solution)/shard_map/ppermute | solution.py:303
  40.5 1.3 %pad_maximum_fusion.mine.refs_6_ = bf16[4,64,3584]{2,1,0:T(8,128)(2,1)S(1)} fusion(bf16[2,64,3584]{2,1,0:T(8,128)(2,1)} %collective-permute-done.9, bf16[2,64,3584]{2,1,0:T(8,128)(2,1)S(1)} %pad_maximum_fusion.1.mine.refs_3_), kind=kLoop, calls=%fused_computation | loop fusion | flops 917504 | bytes 3670016 | tf_op jit(solution)/shard_map/concatenate | solution.py:450
  41.8 1.3 %collective-permute-done.10 = bf16[2,64,3584]{2,1,0:T(8,128)(2,1)S(1)} collective-permute-done((bf16[2,64,3584]{2,1,0:T(8,128)(2,1)}, bf16[2,64,3584]{2,1,0:T(8,128)(2,1)S(1)}, u32[]{:S(2)}, u32[]{:S(2)}) %collective-permute-start.10) | collective-permute-done | bytes 917536 | tf_op jit(solution)/shard_map/ppermute | solution.py:306
  43.2 1.4 %second.1 = (bf16[16,7680]{1,0:T(8,128)(2,1)S(1)}, bf16[2,16,3712]{2,1,0:T(8,128)(2,1)S(1)}) custom-call(s32[9]{0:T(128)S(1)} %concatenate.18.where.refs_0_, bf16[16,7680]{1,0:T(8,128)(2,1)S(1)} %get-tuple-element.39.x_in, f32[4,16,64]{2,1,0:T(8,128)S(1)} %collective-permute-done.8.again_peer.refs_5_, bf16[4,64,3584]{2,1,0:T(8,128)(2,1)S(1)} %pad_maximum_fusion.mine.refs_6_, ...), custom_call_target="tpu_custom_call" | custom-call | flops 58720256 | bytes 3670016 | tf_op jit(solution)/shard_map/second/pallas_call | solution.py:452
  44.6 1.9 %collective-permute-start.11 = (bf16[16,7680]{1,0:T(8,128)(2,1)S(1)}, bf16[16,7680]{1,0:T(8,128)(2,1)S(1)}, u32[]{:S(2)}, u32[]{:S(2)}) collective-permute-start(bf16[16,7680]{1,0:T(8,128)(2,1)S(1)} %get-tuple-element.41), channel_id=1, source_target_pairs={{0,8},{4,12},{8,16},{12,20},{16,24},{20,28},{24,29},{28,25},{9,1},... | collective-permute-start | bytes 737288 | tf_op jit(solution)/shard_map/ppermute | solution.py:303
  46.5 2.7 %collective-permute-start.12 = (bf16[16,7168]{1,0:T(8,128)(2,1)S(1)}, bf16[16,7168]{1,0:T(8,128)(2,1)S(1)}, u32[]{:S(2)}, u32[]{:S(2)}) collective-permute-start(bf16[16,7168]{1,0:T(8,128)(2,1)S(1)} %collective-permute-done.3.refs_9_.refs_8_), channel_id=1, source_target_pairs={{0,1},{1,0},{2,3},{3,2},{4,5},{5,4},{6,7},{7,6},{8,9},{9,8},{10,11... | collective-permute-start | bytes 688136 | tf_op jit(solution)/shard_map/ppermute | solution.py:306
  49.2 0.1 collective-permute-start.15
  49.2 1.2 %collective-permute-start.1 = (bf16[64,3584]{1,0:T(8,128)(2,1)S(1)}, bf16[64,3584]{1,0:T(8,128)(2,1)S(1)}, u32[]{:S(2)}, u32[]{:S(2)}) collective-permute-start(bf16[64,3584]{1,0:T(8,128)(2,1)S(1)} %bitcast.52), channel_id=1, source_target_pairs={{0,2},{2,0},{1,3},{3,1},{4,6},{6,4},{5,7},{7,5},{8,10},{10,8},{9,1... | collective-permute-start | bytes 1376264 | tf_op jit(solution)/shard_map/ppermute | solution.py:424
  50.5 2.7 %collective-permute-done.11.refs_1_ = bf16[16,7680]{1,0:T(8,128)(2,1)S(1)} collective-permute-done((bf16[16,7680]{1,0:T(8,128)(2,1)S(1)}, bf16[16,7680]{1,0:T(8,128)(2,1)S(1)}, u32[]{:S(2)}, u32[]{:S(2)}) %collective-permute-start.11) | collective-permute-done | bytes 245792 | tf_op jit(solution)/shard_map/ppermute | solution.py:303
  53.2 2.7 %pair1.1 = (bf16[16,7680]{1,0:T(8,128)(2,1)S(1)}, bf16[2,16,3712]{2,1,0:T(8,128)(2,1)S(1)}, bf16[1,2,16,3712]{3,2,1,0:T(8,128)(2,1)S(1)}, bf16[4,16,3584]{2,1,0:T(8,128)(2,1)S(1)}, bf16[4,16,3712]{2,1,0:T(8,128)(2,1)S(1)}) custom-call(s32[9]{0:T(128)S(1)} %concatenate.18.where.refs_0_, ...), custom_call_target="tpu_custom_call", output_to_operand_aliasing={{3}: (11, {}), {4}: (12, {})} | custom-call | flops 58720256 | bytes 3670016 | tf_op jit(solution)/shard_map/pair1/pallas_call | solution.py:466
  55.9 1.9 %collective-permute-start.13 = (bf16[16,7680]{1,0:T(8,128)(2,1)S(1)}, bf16[16,7680]{1,0:T(8,128)(2,1)S(1)}, u32[]{:S(2)}, u32[]{:S(2)}) collective-permute-start(bf16[16,7680]{1,0:T(8,128)(2,1)S(1)} %get-tuple-element.45), channel_id=1, source_target_pairs={{0,8},{4,12},{8,16},{12,20},{16,24},{20,28},{24,29},{28,25},{9,1},... | collective-permute-start | bytes 737288 | tf_op jit(solution)/shard_map/ppermute | solution.py:303
  57.8 1.0 subtract_convert_fusion
  58.8 4.9 %collective-permute-done.13.refs_1_ = bf16[16,7680]{1,0:T(8,128)(2,1)S(1)} collective-permute-done((bf16[16,7680]{1,0:T(8,128)(2,1)S(1)}, bf16[16,7680]{1,0:T(8,128)(2,1)S(1)}, u32[]{:S(2)}, u32[]{:S(2)}) %collective-permute-start.13) | collective-permute-done | bytes 245792 | tf_op jit(solution)/shard_map/ppermute | solution.py:303
  63.7 2.7 %pair2.1 = (bf16[16,7680]{1,0:T(8,128)(2,1)S(1)}, bf16[2,16,3712]{2,1,0:T(8,128)(2,1)S(1)}, bf16[2,2,16,3712]{3,2,1,0:T(8,128)(2,1)S(1)}, bf16[4,16,3584]{2,1,0:T(8,128)(2,1)S(1)}, bf16[4,16,3712]{2,1,0:T(8,128)(2,1)S(1)}) custom-call(s32[9]{0:T(128)S(1)} %concatenate.18.where.refs_0_, ...), custom_call_target="tpu_custom_call", output_to_operand_aliasing={{3}: (11, {}), {4}: (12, {})} | custom-call | flops 58720256 | bytes 3670016 | tf_op jit(solution)/shard_map/pair2/pallas_call | solution.py:466
  66.4 1.9 %collective-permute-start.14 = (bf16[16,7680]{1,0:T(8,128)(2,1)S(1)}, bf16[16,7680]{1,0:T(8,128)(2,1)S(1)}, u32[]{:S(2)}, u32[]{:S(2)}) collective-permute-start(bf16[16,7680]{1,0:T(8,128)(2,1)S(1)} %get-tuple-element.51), channel_id=1, source_target_pairs={{0,8},{4,12},{8,16},{12,20},{16,24},{20,28},{24,29},{28,25},{9,1},... | collective-permute-start | bytes 737288 | tf_op jit(solution)/shard_map/ppermute | solution.py:303
  68.4 3.4 %collective-permute-start.17 = (bf16[2,2,16,3712]{3,2,0,1:T(8,128)(2,1)S(1)}, bf16[2,2,16,3712]{3,2,0,1:T(8,128)(2,1)S(1)}, u32[]{:S(2)}, u32[]{:S(2)}) collective-permute-start(bf16[2,2,16,3712]{3,2,0,1:T(8,128)(2,1)S(1)} %copy.21), channel_id=1, source_target_pairs={{1,5},{5,1},{9,13},{13,9},{16,20},{17,21},{20,16},{21,17},{24,28},... | collective-permute-start | bytes 1425416 | tf_op jit(solution)/shard_map/ppermute | solution.py:303
  71.8 1.0 fusion
  72.8 3.5 %collective-permute-done.14.refs_1_ = bf16[16,7680]{1,0:T(8,128)(2,1)S(1)} collective-permute-done((bf16[16,7680]{1,0:T(8,128)(2,1)S(1)}, bf16[16,7680]{1,0:T(8,128)(2,1)S(1)}, u32[]{:S(2)}, u32[]{:S(2)}) %collective-permute-start.14) | collective-permute-done | bytes 245792 | tf_op jit(solution)/shard_map/ppermute | solution.py:303
  76.3 3.3 %pair3.1 = (bf16[16,7680]{1,0:T(8,128)(2,1)S(1)}, bf16[8,128]{1,0:T(8,128)(2,1)}, bf16[1,2,16,3712]{3,2,1,0:T(8,128)(2,1)S(1)}, bf16[4,16,3584]{2,1,0:T(8,128)(2,1)S(1)}, bf16[4,16,3712]{2,1,0:T(8,128)(2,1)S(1)}) custom-call(s32[9]{0:T(128)S(1)} %concatenate.18.where.refs_0_, ...), custom_call_target="tpu_custom_call", output_to_operand_aliasing={{3}: (11, {}), {4}: (12, {})} | custom-call | flops 58720256 | bytes 3670016 | tf_op jit(solution)/shard_map/pair3/pallas_call | solution.py:466
  79.6 1.9 %collective-permute-start.21 = (bf16[16,7680]{1,0:T(8,128)(2,1)S(1)}, bf16[16,7680]{1,0:T(8,128)(2,1)S(1)}, u32[]{:S(2)}, u32[]{:S(2)}) collective-permute-start(bf16[16,7680]{1,0:T(8,128)(2,1)S(1)} %get-tuple-element.60), channel_id=1, source_target_pairs={{0,4},{4,8},{8,12},{12,16},{16,20},{20,24},{24,28},{28,29},{5,1},{... | collective-permute-start | bytes 737288 | tf_op jit(solution)/shard_map/ppermute | solution.py:303
  81.5 3.4 %collective-permute-start.19 = (bf16[2,16,3712]{2,1,0:T(8,128)(2,1)S(1)}, bf16[2,16,3712]{2,1,0:T(8,128)(2,1)S(1)}, u32[]{:S(2)}, u32[]{:S(2)}) collective-permute-start(bf16[2,16,3712]{2,1,0:T(8,128)(2,1)S(1)} %bitcast.50), channel_id=1, source_target_pairs={{1,5},{5,1},{9,13},{13,9},{16,20},{17,21},{20,16},{21,17},{24,28},... | collective-permute-start | bytes 712712 | tf_op jit(solution)/shard_map/ppermute | solution.py:303
  84.9 0.1 collective-permute-start.16
  85.0 3.8 %collective-permute-start.18 = (bf16[2,16,3712]{2,1,0:T(8,128)(2,1)S(1)}, bf16[2,16,3712]{2,1,0:T(8,128)(2,1)S(1)}, u32[]{:S(2)}, u32[]{:S(2)}) collective-permute-start(bf16[2,16,3712]{2,1,0:T(8,128)(2,1)S(1)} %slice_bitcast_fusion), channel_id=1, source_target_pairs={{0,1},{1,0},{2,3},{3,2},{4,5},{5,4},{6,7},{7,6},{8,9},{9,8},{10,11... | collective-permute-start | bytes 712712 | tf_op jit(solution)/shard_map/ppermute | solution.py:306
  88.8 3.3 %collective-permute-done.21.refs_1_ = bf16[16,7680]{1,0:T(8,128)(2,1)S(1)} collective-permute-done((bf16[16,7680]{1,0:T(8,128)(2,1)S(1)}, bf16[16,7680]{1,0:T(8,128)(2,1)S(1)}, u32[]{:S(2)}, u32[]{:S(2)}) %collective-permute-start.21) | collective-permute-done | bytes 245792 | tf_op jit(solution)/shard_map/ppermute | solution.py:303
  92.2 1.4 %last.1 = (bf16[16,7296]{1,0:T(8,128)(2,1)S(1)}, bf16[16,7296]{1,0:T(8,128)(2,1)S(1)}) custom-call(s32[9]{0:T(128)S(1)} %concatenate.18.where.refs_0_, bf16[16,7680]{1,0:T(8,128)(2,1)S(1)} %collective-permute-done.21.refs_1_, f32[8,16,64]{2,1,0:T(8,128)S(1)} %add.18.again_own.refs_4_.refs_2_, bf16[2,64,3584]{2,1,0:T(8,128)(2,1)S(1)} %pad_maximum_fusion.1.mine.refs_3_, ...), custom_call_target="tpu_custom_call" | custom-call | flops 58720256 | bytes 3670016 | tf_op jit(solution)/shard_map/last/pallas_call | solution.py:487
  93.6 1.4 %collective-permute-done.19.late = bf16[2,16,3712]{2,1,0:T(8,128)(2,1)S(1)} collective-permute-done((bf16[2,16,3712]{2,1,0:T(8,128)(2,1)S(1)}, bf16[2,16,3712]{2,1,0:T(8,128)(2,1)S(1)}, u32[]{:S(2)}, u32[]{:S(2)}) %collective-permute-start.19) | collective-permute-done | bytes 237600 | tf_op jit(solution)/shard_map/ppermute | solution.py:303
  95.2 1.3 %collective-permute-done.20.late_got = bf16[16,3712]{1,0:T(8,128)(2,1)S(1)} collective-permute-done((bf16[16,3712]{1,0:T(8,128)(2,1)S(1)}, bf16[16,3712]{1,0:T(8,128)(2,1)S(1)}, u32[]{:S(2)}, u32[]{:S(2)}) %collective-permute-start.20) | collective-permute-done | bytes 118816 | tf_op jit(solution)/shard_map/ppermute | solution.py:306
  96.5 2.1 %finish.1 = (bf16[64,3584]{1,0:T(8,128)(2,1)}, bf16[64,3584]{1,0:T(8,128)(2,1)}, bf16[16,3584]{1,0:T(8,128)(2,1)}, bf16[16,3584]{1,0:T(8,128)(2,1)}) custom-call(s32[9]{0:T(128)S(1)} %concatenate.18.where.refs_0_, bf16[4,16,3584]{2,1,0:T(8,128)(2,1)S(1)} %get-tuple-element.57.mine, bf16[4,16,3712]{2,1,0:T(8,128)(2,1)S(1)} %get-tuple-element.58.sent, ...), custom_call_target="tpu_custom_call" | custom-call | flops 58720256 | bytes 3670016 | tf_op jit(solution)/shard_map/finish/pallas_call | solution.py:493
  (39 shorter events, 0.5 us)
Async XLA Ops:
  0.6 7.9 %copy-start.4 = (bf16[1,64,3584]{2,1,0:T(8,128)(2,1)S(1)}, bf16[1,64,3584]{2,1,0:T(8,128)(2,1)}, u32[]{:S(2)}) copy-start(bf16[1,64,3584]{2,1,0:T(8,128)(2,1)} %param.12) | copy-start | bytes 1376260
  1.7 5.6 %collective-permute-start.2 = (bf16[16,3584]{1,0:T(8,128)(2,1)S(1)}, bf16[16,3584]{1,0:T(8,128)(2,1)S(1)}, u32[]{:S(2)}, u32[]{:S(2)}) collective-permute-start(bf16[16,3584]{1,0:T(8,128)(2,1)S(1)} %get-tuple-element.69), channel_id=1, source_target_pairs={{0,1},{1,0},{2,3},{3,2},{4,5},{5,4},{6,7},{7,6},{8,9},{9,8},{10,11... | collective-permute-start | bytes 344072 | tf_op jit(solution)/shard_map/ppermute | solution.py:306
  4.1 8.2 %collective-permute-start.4 = (bf16[16,3584]{1,0:T(8,128)(2,1)}, bf16[16,3584]{1,0:T(8,128)(2,1)}, u32[]{:S(2)}, u32[]{:S(2)}) collective-permute-start(bf16[16,3584]{1,0:T(8,128)(2,1)} %get-tuple-element.71), channel_id=1, source_target_pairs={{0,1},{1,0},{2,3},{3,2},{4,5},{5,4},{6,7},{7,6},{8,9},{9,8},{10,11... | collective-permute-start | bytes 344072 | tf_op jit(solution)/shard_map/ppermute | solution.py:306
  4.1 1.0 %copy-start = (bf16[1,3584,64]{1,2,0:T(8,128)(2,1)S(1)}, bf16[1,3584,64]{1,2,0:T(8,128)(2,1)}, u32[]{:S(2)}) copy-start(bf16[1,3584,64]{1,2,0:T(8,128)(2,1)} %param.11) | copy-start | bytes 1376260
  5.1 1.2 %copy-start.2 = (bf16[1,1,8,16,3584]{4,3,2,1,0:T(8,128)(2,1)S(1)}, bf16[1,1,8,16,3584]{4,3,2,1,0:T(8,128)(2,1)}, u32[]{:S(2)}) copy-start(bf16[1,1,8,16,3584]{4,3,2,1,0:T(8,128)(2,1)} %param.15) | copy-start | bytes 2752516
  6.3 3.9 %copy-start.5 = (bf16[1,1,3584,64]{2,3,1,0:T(8,128)(2,1)S(1)}, bf16[1,1,3584,64]{2,3,1,0:T(8,128)(2,1)}, u32[]{:S(2)}) copy-start(bf16[1,1,3584,64]{2,3,1,0:T(8,128)(2,1)} %param.13) | copy-start | bytes 1376260
  6.7 3.5 %collective-permute-start.5 = (f32[8,16,64]{2,1,0:T(8,128)S(1)}, f32[8,16,64]{2,1,0:T(8,128)}, u32[]{:S(2)}, u32[]{:S(2)}) collective-permute-start(f32[8,16,64]{2,1,0:T(8,128)S(1)} %stashed.1), channel_id=1, source_target_pairs={{0,1},{1,0},{2,3},{3,2},{4,5},{5,4},{6,7},{7,6},{8,9},{9,8},{10,11... | collective-permute-start | bytes 98312 | tf_op jit(solution)/shard_map/ppermute | solution.py:306
  7.3 9.7 %collective-permute-start.3 = (bf16[16,7168]{1,0:T(8,128)(2,1)S(1)}, bf16[16,7168]{1,0:T(8,128)(2,1)S(1)}, u32[]{:S(2)}, u32[]{:S(2)}) collective-permute-start(bf16[16,7168]{1,0:T(8,128)(2,1)S(1)} %pad_maximum_fusion.2.refs_8_.refs_5_), channel_id=1, source_target_pairs={{8,0},{16,1},{1,29},{9,28},{12,4},{20,5},{5,25},{13,24},{10,2},{18... | collective-permute-start | bytes 688136 | tf_op jit(solution)/shard_map/ppermute | solution.py:303
  8.7 14.4 %collective-permute-start.6 = (bf16[2,64,3584]{2,1,0:T(8,128)(2,1)S(1)}, bf16[2,64,3584]{2,1,0:T(8,128)(2,1)S(1)}, u32[]{:S(2)}, u32[]{:S(2)}) collective-permute-start(bf16[2,64,3584]{2,1,0:T(8,128)(2,1)S(1)} %pad_maximum_fusion.1.mine.refs_3_), channel_id=1, source_target_pairs={{0,1},{1,0},{2,3},{3,2},{4,5},{5,4},{6,7},{7,6},{8,9},{9,8},{10,11... | collective-permute-start | bytes 2752520 | tf_op jit(solution)/shard_map/ppermute | solution.py:306
  8.8 29.0 %collective-permute-start.9 = (bf16[2,64,3584]{2,1,0:T(8,128)(2,1)S(1)}, bf16[2,64,3584]{2,1,0:T(8,128)(2,1)}, u32[]{:S(2)}, u32[]{:S(2)}) collective-permute-start(bf16[2,64,3584]{2,1,0:T(8,128)(2,1)S(1)} %pad_maximum_fusion.1.mine.refs_3_), channel_id=1, source_target_pairs={{0,4},{1,5},{4,0},{5,1},{8,12},{9,13},{12,8},{13,9},{16,20},{17,21... | collective-permute-start | bytes 2752520 | tf_op jit(solution)/shard_map/ppermute | solution.py:303
  10.2 39.1 %collective-permute-start = (bf16[64,3584]{1,0:T(8,128)(2,1)S(1)}, bf16[64,3584]{1,0:T(8,128)(2,1)S(1)}, u32[]{:S(2)}, u32[]{:S(2)}) collective-permute-start(bf16[64,3584]{1,0:T(8,128)(2,1)S(1)} %bitcast.51), channel_id=1, source_target_pairs={{0,2},{2,0},{1,3},{3,1},{4,6},{6,4},{5,7},{7,5},{8,10},{10,8},{9,1... | collective-permute-start | bytes 1376264 | tf_op jit(solution)/shard_map/ppermute | solution.py:424
  12.3 30.9 %collective-permute-start.8 = (f32[4,16,64]{2,1,0:T(8,128)S(1)}, f32[4,16,64]{2,1,0:T(8,128)S(1)}, u32[]{:S(2)}, u32[]{:S(2)}) collective-permute-start(f32[4,16,64]{2,1,0:T(8,128)S(1)} %slice.9), channel_id=1, source_target_pairs={{1,5},{5,1},{9,13},{13,9},{17,21},{21,17},{25,29},{29,25},{3,7},{7... | collective-permute-start | bytes 49160 | tf_op jit(solution)/shard_map/ppermute | solution.py:303
  16.9 23.5 %collective-permute-start.7 = (bf16[16,7168]{1,0:T(8,128)(2,1)S(1)}, bf16[16,7168]{1,0:T(8,128)(2,1)S(1)}, u32[]{:S(2)}, u32[]{:S(2)}) collective-permute-start(bf16[16,7168]{1,0:T(8,128)(2,1)S(1)} %pad_maximum_fusion.2.refs_8_.refs_5_), channel_id=1, source_target_pairs={{24,0},{28,1},{17,29},{25,28},{21,25},{26,2},{30,3},{19,31},{27,30... | collective-permute-start | bytes 688136 | tf_op jit(solution)/shard_map/ppermute | solution.py:303
  40.4 2.7 %collective-permute-start.10 = (bf16[2,64,3584]{2,1,0:T(8,128)(2,1)}, bf16[2,64,3584]{2,1,0:T(8,128)(2,1)S(1)}, u32[]{:S(2)}, u32[]{:S(2)}) collective-permute-start(bf16[2,64,3584]{2,1,0:T(8,128)(2,1)} %collective-permute-done.9), channel_id=1, source_target_pairs={{0,1},{1,0},{2,3},{3,2},{4,5},{5,4},{6,7},{7,6},{8,9},{9,8},{10,11... | collective-permute-start | bytes 2752520 | tf_op jit(solution)/shard_map/ppermute | solution.py:306
  43.2 6.1 %copy-start.6 = (bf16[1,1,64,3584]{3,2,1,0:T(8,128)(2,1)S(1)}, bf16[1,1,64,3584]{3,2,1,0:T(8,128)(2,1)}, u32[]{:S(2)}) copy-start(bf16[1,1,64,3584]{3,2,1,0:T(8,128)(2,1)} %param.14) | copy-start | bytes 1376260
  44.6 8.6 %collective-permute-start.11 = (bf16[16,7680]{1,0:T(8,128)(2,1)S(1)}, bf16[16,7680]{1,0:T(8,128)(2,1)S(1)}, u32[]{:S(2)}, u32[]{:S(2)}) collective-permute-start(bf16[16,7680]{1,0:T(8,128)(2,1)S(1)} %get-tuple-element.41), channel_id=1, source_target_pairs={{0,8},{4,12},{8,16},{12,20},{16,24},{20,28},{24,29},{28,25},{9,1},... | collective-permute-start | bytes 737288 | tf_op jit(solution)/shard_map/ppermute | solution.py:303
  46.5 4.0 %collective-permute-start.12 = (bf16[16,7168]{1,0:T(8,128)(2,1)S(1)}, bf16[16,7168]{1,0:T(8,128)(2,1)S(1)}, u32[]{:S(2)}, u32[]{:S(2)}) collective-permute-start(bf16[16,7168]{1,0:T(8,128)(2,1)S(1)} %collective-permute-done.3.refs_9_.refs_8_), channel_id=1, source_target_pairs={{0,1},{1,0},{2,3},{3,2},{4,5},{5,4},{6,7},{7,6},{8,9},{9,8},{10,11... | collective-permute-start | bytes 688136 | tf_op jit(solution)/shard_map/ppermute | solution.py:306
  49.2 27.1 %collective-permute-start.15 = (bf16[16,7168]{1,0:T(8,128)(2,1)S(1)}, bf16[16,7168]{1,0:T(8,128)(2,1)S(1)}, u32[]{:S(2)}, u32[]{:S(2)}) collective-permute-start(bf16[16,7168]{1,0:T(8,128)(2,1)S(1)} %collective-permute-done.7.refs_10_.refs_9_), channel_id=1, source_target_pairs={{0,1},{1,0},{2,3},{3,2},{4,5},{5,4},{6,7},{7,6},{8,9},{9,8},{10,11... | collective-permute-start | bytes 688136 | tf_op jit(solution)/shard_map/ppermute | solution.py:306
  49.2 22.6 %collective-permute-start.1 = (bf16[64,3584]{1,0:T(8,128)(2,1)S(1)}, bf16[64,3584]{1,0:T(8,128)(2,1)S(1)}, u32[]{:S(2)}, u32[]{:S(2)}) collective-permute-start(bf16[64,3584]{1,0:T(8,128)(2,1)S(1)} %bitcast.52), channel_id=1, source_target_pairs={{0,2},{2,0},{1,3},{3,1},{4,6},{6,4},{5,7},{7,5},{8,10},{10,8},{9,1... | collective-permute-start | bytes 1376264 | tf_op jit(solution)/shard_map/ppermute | solution.py:424
  53.1 4.7 %copy-start.1 = (bf16[1,3584,64]{1,2,0:T(8,128)(2,1)S(1)}, bf16[1,3584,64]{1,2,0:T(8,128)(2,1)}, u32[]{:S(2)}) copy-start(bf16[1,3584,64]{1,2,0:T(8,128)(2,1)} %param.11) | copy-start | bytes 1376260
  55.9 7.8 %collective-permute-start.13 = (bf16[16,7680]{1,0:T(8,128)(2,1)S(1)}, bf16[16,7680]{1,0:T(8,128)(2,1)S(1)}, u32[]{:S(2)}, u32[]{:S(2)}) collective-permute-start(bf16[16,7680]{1,0:T(8,128)(2,1)S(1)} %get-tuple-element.45), channel_id=1, source_target_pairs={{0,8},{4,12},{8,16},{12,20},{16,24},{20,28},{24,29},{28,25},{9,1},... | collective-permute-start | bytes 737288 | tf_op jit(solution)/shard_map/ppermute | solution.py:303
  66.4 9.9 %collective-permute-start.14 = (bf16[16,7680]{1,0:T(8,128)(2,1)S(1)}, bf16[16,7680]{1,0:T(8,128)(2,1)S(1)}, u32[]{:S(2)}, u32[]{:S(2)}) collective-permute-start(bf16[16,7680]{1,0:T(8,128)(2,1)S(1)} %get-tuple-element.51), channel_id=1, source_target_pairs={{0,8},{4,12},{8,16},{12,20},{16,24},{20,28},{24,29},{28,25},{9,1},... | collective-permute-start | bytes 737288 | tf_op jit(solution)/shard_map/ppermute | solution.py:303
  68.4 16.6 %collective-permute-start.17 = (bf16[2,2,16,3712]{3,2,0,1:T(8,128)(2,1)S(1)}, bf16[2,2,16,3712]{3,2,0,1:T(8,128)(2,1)S(1)}, u32[]{:S(2)}, u32[]{:S(2)}) collective-permute-start(bf16[2,2,16,3712]{3,2,0,1:T(8,128)(2,1)S(1)} %copy.21), channel_id=1, source_target_pairs={{1,5},{5,1},{9,13},{13,9},{16,20},{17,21},{20,16},{21,17},{24,28},... | collective-permute-start | bytes 1425416 | tf_op jit(solution)/shard_map/ppermute | solution.py:303
  79.6 12.6 %collective-permute-start.21 = (bf16[16,7680]{1,0:T(8,128)(2,1)S(1)}, bf16[16,7680]{1,0:T(8,128)(2,1)S(1)}, u32[]{:S(2)}, u32[]{:S(2)}) collective-permute-start(bf16[16,7680]{1,0:T(8,128)(2,1)S(1)} %get-tuple-element.60), channel_id=1, source_target_pairs={{0,4},{4,8},{8,12},{12,16},{16,20},{20,24},{24,28},{28,29},{5,1},{... | collective-permute-start | bytes 737288 | tf_op jit(solution)/shard_map/ppermute | solution.py:303
  81.5 13.5 %collective-permute-start.19 = (bf16[2,16,3712]{2,1,0:T(8,128)(2,1)S(1)}, bf16[2,16,3712]{2,1,0:T(8,128)(2,1)S(1)}, u32[]{:S(2)}, u32[]{:S(2)}) collective-permute-start(bf16[2,16,3712]{2,1,0:T(8,128)(2,1)S(1)} %bitcast.50), channel_id=1, source_target_pairs={{1,5},{5,1},{9,13},{13,9},{16,20},{17,21},{20,16},{21,17},{24,28},... | collective-permute-start | bytes 712712 | tf_op jit(solution)/shard_map/ppermute | solution.py:303
  84.9 11.6 %collective-permute-start.16 = (bf16[4,16,3712]{2,1,0:T(8,128)(2,1)S(1)}, bf16[4,16,3712]{2,1,0:T(8,128)(2,1)S(1)}, u32[]{:S(2)}, u32[]{:S(2)}) collective-permute-start(bf16[4,16,3712]{2,1,0:T(8,128)(2,1)S(1)} %get-tuple-element.58.sent), channel_id=1, source_target_pairs={{0,1},{1,0},{2,3},{3,2},{4,5},{5,4},{6,7},{7,6},{8,9},{9,8},{10,11... | collective-permute-start | bytes 1425416 | tf_op jit(solution)/shard_map/ppermute | solution.py:306
  85.0 11.5 %copy-start.3 = (bf16[1,1,8,16,3584]{4,3,2,1,0:T(8,128)(2,1)S(1)}, bf16[1,1,8,16,3584]{4,3,2,1,0:T(8,128)(2,1)}, u32[]{:S(2)}) copy-start(bf16[1,1,8,16,3584]{4,3,2,1,0:T(8,128)(2,1)} %param.15) | copy-start | bytes 2752516
  85.0 11.4 %collective-permute-start.18 = (bf16[2,16,3712]{2,1,0:T(8,128)(2,1)S(1)}, bf16[2,16,3712]{2,1,0:T(8,128)(2,1)S(1)}, u32[]{:S(2)}, u32[]{:S(2)}) collective-permute-start(bf16[2,16,3712]{2,1,0:T(8,128)(2,1)S(1)} %slice_bitcast_fusion), channel_id=1, source_target_pairs={{0,1},{1,0},{2,3},{3,2},{4,5},{5,4},{6,7},{7,6},{8,9},{9,8},{10,11... | collective-permute-start | bytes 712712 | tf_op jit(solution)/shard_map/ppermute | solution.py:306
  93.6 2.9 %collective-permute-start.22 = (bf16[16,7296]{1,0:T(8,128)(2,1)S(1)}, bf16[16,7296]{1,0:T(8,128)(2,1)S(1)}, u32[]{:S(2)}, u32[]{:S(2)}) collective-permute-start(bf16[16,7296]{1,0:T(8,128)(2,1)S(1)} %get-tuple-element.63.last_other), channel_id=1, source_target_pairs={{0,1},{1,0},{2,3},{3,2},{4,5},{5,4},{6,7},{7,6},{8,9},{9,8},{10,11... | collective-permute-start | bytes 700424 | tf_op jit(solution)/shard_map/ppermute | solution.py:306
  95.1 1.4 %collective-permute-start.20 = (bf16[16,3712]{1,0:T(8,128)(2,1)S(1)}, bf16[16,3712]{1,0:T(8,128)(2,1)S(1)}, u32[]{:S(2)}, u32[]{:S(2)}) collective-permute-start(bf16[16,3712]{1,0:T(8,128)(2,1)S(1)} %slice_bitcast_fusion.1), channel_id=1, source_target_pairs={{0,1},{1,0},{2,3},{3,2},{4,5},{5,4},{6,7},{7,6},{8,9},{9,8},{10,11... | collective-permute-start | bytes 356360 | tf_op jit(solution)/shard_map/ppermute | solution.py:306

commit v6 on v5

--- a/solution.py
+++ b/solution.py
@@ -65,11 +65,23 @@
         self.out_scale = BRANCH_SCALE / math.sqrt(rank)
 
 
-def section_step(size, place, section, tick, x0, x1, again, payload, mine, other, at):
+def stacked(place, mine, other, at=0):
+    into, out = at + place.role, at + 1 - place.role
+    return (lambda: mine[into]), (lambda: other[into]), (lambda: mine[out]), (lambda: other[out])
+
+
+def separate(place, squeeze0, squeeze1, expand0, expand1):
+    def either(a, b):
+        return lambda: jnp.where(place.forward, a[...], b[...])
+
+    return either(squeeze0, expand0), either(squeeze1, expand1), either(expand0, squeeze0), either(expand1, squeeze1)
+
+
+def section_step(size, place, section, tick, x0, x1, again, payload, weights):
     forward = place.forward
     back = place.sections - 1 - section
-    first, second = at + place.role, at + 1 - place.role
-    h = (dot(x0, mine[first], NT) + dot(x1, other[first], NT)) * jnp.where(
+    into0, into1, from0, from1 = weights
+    h = (dot(x0, into0(), NT) + dot(x1, into1(), NT)) * jnp.where(
         forward, size.in_scale, size.out_scale
     )
     for j in range(size.slots):
@@ -79,8 +91,8 @@
     z = jnp.where(forward, value, h * slope).astype(jnp.bfloat16)
     ranks = jnp.concatenate([value.astype(jnp.bfloat16), z], axis=1)
     scale = jnp.where(forward, size.out_scale, size.in_scale)
-    y0 = (x0.astype(jnp.float32) + dot(z, mine[second]) * scale).astype(jnp.bfloat16)
-    y1 = (x1.astype(jnp.float32) + dot(z, other[second]) * scale).astype(jnp.bfloat16)
+    y0 = (x0.astype(jnp.float32) + dot(z, from0()) * scale).astype(jnp.bfloat16)
+    y1 = (x1.astype(jnp.float32) + dot(z, from1()) * scale).astype(jnp.bfloat16)
     words = split_words(h)
     payload = [jnp.where(jnp.logical_and(forward, back == j), words, payload[j]) for j in range(size.slots)]
     return y0, y1, ranks, payload
@@ -133,7 +145,7 @@
     place = Place(where)
     x0, x1, payload = read(size, x_in)
     y0, y1, ranks, payload = section_step(
-        size, place, place.section, 0, x0, x1, again_own[0], payload, mine, other, 0
+        size, place, place.section, 0, x0, x1, again_own[0], payload, stacked(place, mine, other)
     )
     keep(size, keep_mine, keep_other, x0, x1, ranks)
     copies = [
@@ -147,11 +159,12 @@
         copy.wait()
 
 
-def second_kernel(size, where, x_in, again_peer, mine, other, out, held):
+def second_kernel(size, where, x_in, again_peer, squeeze0, squeeze1, expand0, expand1, out, held):
     place = Place(where)
     x0, x1, payload = read(size, x_in)
     y0, y1, ranks, sent = section_step(
-        size, place, place.peer, 1, x0, x1, again_peer[0], payload, mine, other, 2
+        size, place, place.peer, 1, x0, x1, again_peer[0], payload,
+        separate(place, squeeze0, squeeze1, expand0, expand1),
     )
     keep_passed(size, held, x0, x1, ranks)
     aligned = place.aligned
@@ -173,11 +186,11 @@
     at_peer = jnp.where(aligned, 0, 2)
     y0, y1, ranks, payload = section_step(
         size, place, jnp.where(aligned, place.section, place.peer), tick, x0, x1,
-        jnp.where(aligned, own, again_peer), payload, mine, other, at_peer,
+        jnp.where(aligned, own, again_peer), payload, stacked(place, mine, other, at_peer),
     )
     z0, z1, ranks_b, sent = section_step(
         size, place, jnp.where(aligned, place.peer, place.section), tick + 1, y0, y1,
-        jnp.where(aligned, again_peer, own), payload, mine, other, 2 - at_peer,
+        jnp.where(aligned, again_peer, own), payload, stacked(place, mine, other, 2 - at_peer),
     )
     keep(
         size, keep_mine, keep_other,
@@ -218,7 +231,7 @@
     x0, x1 = entering(place, size, size.steps, x0, x1, where, feeds, at_end)
     tick = size.ticks - 1
     y0, y1, ranks, _ = section_step(
-        size, place, place.section, tick, x0, x1, again_own[tick], payload, mine, other, 0
+        size, place, place.section, tick, x0, x1, again_own[tick], payload, stacked(place, mine, other)
     )
     for ref, x, y in ((last_mine, x0, y0), (last_other, x1, y1)):
         ref[:, :half] = x
@@ -335,9 +348,11 @@
     acts, cots = activations[0], cotangent[0]
     both = [(s, c) for s in everyone for c in (0, 1)]
 
+    squeeze_peer = to_peer(squeeze, both)
+    expand_peer = to_peer(tied(expand, squeeze_peer), both)
     own = lax.optimization_barrier(jnp.stack([squeeze, expand]))
-    peer = to_peer(own, both)
     other = swap(own)
+    squeeze_peer_other, expand_peer_other = swap(squeeze_peer), swap(expand_peer)
 
     partial = call(
         stash_kernel, "stashed", shape(ticks, rows, rank, dtype=f32), [VMEM, VMEM], VMEM
@@ -345,9 +360,10 @@
     again_own = partial + swap(partial)
     again_peer = to_peer(again_own[1::2], [(s, 1) for s in everyone])
 
-    entering_full = jnp.concatenate(
-        [jnp.where(forward, acts, cots), swap(jnp.where(forward, cots, acts))], axis=1
-    )
+    cots_crossed = to_peer(cots, both)
+    entering = jnp.concatenate([jnp.where(forward, acts, cots), swap(jnp.where(forward, cots, acts))], axis=1)
+    crossed = jnp.concatenate([cots_crossed, swap(cots_crossed)], axis=1)
+    crossed = jnp.where(forward, entering, crossed)
     per_tick = rows // acts.shape[0]
 
     ends = {}
@@ -358,30 +374,47 @@
     turn = {}
     trips = [[] for _ in range(ticks)]
     for (to, core), blocks in ends.items():
-        local = [b for b in blocks if all(b * per_tick + m == to for m in range(per_tick))]
-        for n, b in enumerate(b for b in blocks if b not in local):
-            trip, swapped = n // 2, n % 2
-            turn[to, core, b] = 1 + 2 * trip + swapped
-            trips[trip].append((b, core, (to, core ^ swapped)))
-        for b in local:
-            turn[to, core, b] = 0
-
-    def fed(trip):
+        seen = {0: 0, 1: 0}
+        for b in blocks:
+            at = [b * per_tick + m for m in range(per_tick)]
+            crosses = int(core == 1 and b > 1 and not all(i == to for i in at))
+            at = [i ^ crosses for i in at]
+            if all(i == to for i in at):
+                turn[to, core, b] = 1 - crosses
+                continue
+            n = seen[crosses]
+            seen[crosses] += 1
+            trip, swapped = crosses + n // 2, n % 2
+            turn[to, core, b] = 2 + 2 * trip + swapped
+            trips[trip].append((at, core, (to, core ^ swapped)))
+
+    def fed(trip, rows_of):
         pieces = []
         for m in range(per_tick):
-            moves = [((b * per_tick + m, core), to) for b, core, to in trip]
-            came = send(entering_full, [(a, b) for a, b in moves if a != b])
+            moves = [((at[m], core), to) for at, core, to in trip]
+            came = send(rows_of, [(a, b) for a, b in moves if a != b])
             for a, b in moves:
                 if a == b:
-                    came = jnp.where(jnp.logical_and(section == a[0], role == a[1]), entering_full, came)
+                    came = jnp.where(jnp.logical_and(section == a[0], role == a[1]), rows_of, came)
             pieces.append(came)
         return jnp.concatenate(pieces, axis=0)
 
-    feeds = [jnp.tile(entering_full, (per_tick, 1))]
-    for trip in trips:
+    feeds = [jnp.tile(crossed, (per_tick, 1)), jnp.tile(entering, (per_tick, 1))]
+    for n, trip in enumerate(trips):
         if trip:
-            feeds.append(fed(trip))
+            feeds.append(fed(trip, crossed if n else entering))
             feeds.append(swap(feeds[-1]))
+
+    def used(b_of):
+        turns = {turn[to, core, b_of(to, core)] for (to, core), blocks in ends.items() if b_of(to, core) in blocks}
+        return tuple(sorted(turns))
+
+    def block_at(step):
+        def b_of(to, core):
+            side_to = to if core == 0 else sections - 1 - to
+            return ticks - 1 if step == size.steps else 2 * step - side_to
+
+        return b_of
 
     def reads(b_of):
         index = jnp.int32(0)
@@ -392,20 +425,9 @@
                 index = jnp.where(here, jnp.int32(turn[to, core, b]), index)
         return index
 
-    def used(b_of):
-        turns = {turn[to, core, b_of(to, core)] for (to, core), blocks in ends.items() if b_of(to, core) in blocks}
-        return tuple(sorted(turns))
-
-    def block_at(step):
-        def b_of(to, core):
-            side_to = to if core == 0 else sections - 1 - to
-            return ticks - 1 if step == size.steps else 2 * step - side_to
-
-        return b_of
-
     where = jnp.concatenate([where, jnp.stack([reads(block_at(step)) for step in range(size.steps + 1)])])
     first_end = section == jnp.where(forward, 0, sections - 1)
-    first_feed = feeds[0]
+    first_feed = feeds[1]
     for n in used(block_at(0)):
         first_feed = jnp.where(where[4] == n, feeds[n], first_feed)
     x = jnp.concatenate([jnp.where(forward, fwd_in, bwd_in), swap(jnp.where(forward, bwd_in, fwd_in))], axis=1)
@@ -421,15 +443,13 @@
 
     def averaged(old, late):
         if replicas == 2:
-            came = lax.ppermute(late, "dp", [(0, 1), (1, 0)])
-            total = late.astype(f32) + came.astype(f32)
+            total = late.astype(f32) + lax.ppermute(late, "dp", [(0, 1), (1, 0)]).astype(f32)
         else:
-            came = lax.psum(late, "dp")
-            total = came.astype(f32)
-        return (old.astype(f32) - STEP_RATE * total / replicas).astype(bf16), came
-
-    squeeze_new, came = averaged(squeeze, squeeze_late[0, 0].T)
-    expand_new, _ = averaged(expand, tied(expand_late[0, 0], came))
+            total = lax.psum(late, "dp").astype(f32)
+        return (old.astype(f32) - STEP_RATE * total / replicas).astype(bf16)
+
+    squeeze_new = averaged(squeeze, squeeze_late[0, 0].T)
+    expand_new = averaged(expand, expand_late[0, 0])
 
     ring = (
         [((s, 0), (s + 2, 0)) for s in range(sections - 2)]
@@ -441,18 +461,19 @@
         + [((sections - 1, 0), (sections - 1, 1))]
         + [((s, 1), (s - 1, 1)) for s in range(1, sections)]
     )
-    passing = [(s, c) for s, c in both if c == 1 or (s ^ 1) >= sections - size.slots]
+    def passing(slot):
+        return [(s, c) for s, c in both if c == 1 or sections - 1 - (s ^ 1) + slot < size.slots - 1]
+
     x, hist_mine, hist_other = call(
         first_kernel, "first", (shape(rows, size.message), *hist_shapes),
         [SMEM, VMEM, VMEM, VMEM, VMEM], (VMEM, ANY, ANY), keep_own,
     )(where, x, again_own, own, other)
-    peer_other = swap(peer)
-    mine_all = jnp.concatenate([own, tied(peer, x)], axis=0)
-    other_all = jnp.concatenate([other, peer_other], axis=0)
     x, held = call(
         second_kernel, "second", (shape(rows, size.message), shape(*odd_shape)),
-        [SMEM, VMEM, VMEM, VMEM, VMEM], (VMEM, VMEM),
-    )(where, tied(x, *feeds[1::2]), again_peer, mine_all, other_all)
+        [SMEM] + [VMEM] * 6, (VMEM, VMEM),
+    )(where, tied(x, *feeds[2::2]), again_peer, squeeze_peer, squeeze_peer_other, expand_peer, expand_peer_other)
+    mine_all = jnp.concatenate([own, squeeze_peer[None], expand_peer[None]], axis=0)
+    other_all = jnp.concatenate([other, squeeze_peer_other[None], expand_peer_other[None]], axis=0)
     x = send(x, ring)
     passed = jnp.zeros((1, *odd_shape), bf16)
     for step in range(1, size.steps):
@@ -479,7 +500,7 @@
         )
         x = send(x, ring_last if final else ring)
         if final:
-            odd, late = to_peer(passed, passing), to_peer(passed_now[0], passing)
+            odd, late = to_peer(passed, passing(0)), to_peer(passed_now[0], passing(size.steps - 2))
         passed = passed_now
     odd_got, late_got = swap(odd[:, 1]), swap(late[1])
     hist_got = swap(hist_other)

time: 99.1 us -> 92.9 us (0.937)
  other arithmetic: 7.97 us -> 4.6 us
  starting transfers between devices: 34.9 us -> 32 us
    ppermute x10 -> x12, starting transfers between devices: 24.3 us -> 21.6 us  [send(): lax.ppermute(x, ('pipe', 'mp'), [(a * 2 + b, c * 2 + d) for (a, b), (c, d...]
    ppermute x11 -> x13, waiting for transfers between devices: 2.57 us -> 1.31 us  [swap(): return lax.ppermute(x, 'mp', [(0, 1), (1, 0)])]
    unnamed x15 -> x14, local copies, waits for them, and re-layouts: 2.28 us -> 3.04 us
    ppermute x11 -> x13, starting transfers between devices: 8.18 us -> 8.9 us  [swap(): return lax.ppermute(x, 'mp', [(0, 1), (1, 0)])]
    ppermute x10 -> x12, waiting for transfers between devices: 33.9 us -> 34.3 us  [send(): lax.ppermute(x, ('pipe', 'mp'), [(a * 2 + b, c * 2 + d) for (a, b), (c, d...]
  transfers between devices with their start and end apart: 23 -> 27, of which waited for: 10 -> 8; matrix products, arithmetic and copies ran while one was open for 7% -> 4% of each run, Pallas kernels for 14% -> 15%
where the time goes in v6:
time: 92.9 us; the launch traced here: 92.5 us
  waiting for transfers between devices  35.6 us (38%)
  starting transfers between devices  32 us (34%)
  Pallas kernels  15.9 us (17%)
  other arithmetic  4.6 us (5%)
  local copies, waits for them, and re-layouts  3.26 us (4%)
  between operations  1.07 us (1%)
    ppermute x12, waiting for transfers between devices, send(): lax.ppermute(x, ('pipe', 'mp'), [(a * 2 + b, c * 2 + d) for (a, b), (c, d...  34.3 us
    ppermute x12, starting transfers between devices, send(): lax.ppermute(x, ('pipe', 'mp'), [(a * 2 + b, c * 2 + d) for (a, b), (c, d...  21.6 us
    pallas_call x3, Pallas kernels, shards(): call(body, f'pair{step}', (shape(rows, size.message), shape(*((8, 128) if...  8.9 us
    ppermute x13, starting transfers between devices, swap(): return lax.ppermute(x, 'mp', [(0, 1), (1, 0)])  8.9 us
    unnamed x14, local copies, waits for them, and re-layouts  3.04 us
    pallas_call x1, Pallas kernels, shards(): call(end_kernel, 'finish', (shape(rank, half), shape(rank, half), shape(r...  2.11 us
    convert_element_type x2, other arithmetic, averaged(): return (old.astype(f32) - STEP_RATE * total / replicas).astype(bf16)  1.95 us
  transfers between devices with their start and end apart: 27, of which 8 were waited for; matrix products, arithmetic and copies ran while one was open for 4% of the time, Pallas kernels for 15%

profile of v6, /device:TPU:25, one launch (start us, length us, event | category | flops | bytes accessed | tf_op | source)
XLA Modules:
  0.0 92.5 jit_solution(1085611035724541611)
XLA Ops:
  0.6 1.0 %bitcast_select_fusion.1 = (bf16[16,3584]{1,0:T(8,128)(2,1)S(1)}, bf16[16,3584]{1,0:T(8,128)(2,1)S(1)}) fusion(bf16[1,16,3584]{2,1,0:T(8,128)(2,1)} %param.9, pred[]{:T(512)S(6)} %eq.21, bf16[1,16,3584]{2,1,0:T(8,128)(2,1)} %param.10), kind=kLoop, calls=%fused_computation.11 | loop fusion | flops 114688 | bytes 458753 | tf_op jit(solution)/shard_map/jit(_where)/select_n | solution.py:364
  1.7 0.7 collective-permute-start.2
  2.4 1.0 %select_bitcast_fusion.1 = (bf16[16,3584]{1,0:T(8,128)(2,1)S(1)}, bf16[16,3584]{1,0:T(8,128)(2,1)S(1)}) fusion(bf16[1,1,16,3584]{3,2,1,0:T(8,128)(2,1)} %param.16, bf16[1,1,16,3584]{3,2,1,0:T(8,128)(2,1)} %param.17, pred[]{:T(512)S(6)} %eq.21), kind=kLoop, calls=%fused_computation.13 | loop fusion | flops 114688 | bytes 458753 | tf_op jit(solution)/shard_map/jit(_where)/select_n | solution.py:433
  3.5 1.3 %collective-permute-start.7 = (bf16[16,3584]{1,0:T(8,128)(2,1)}, bf16[16,3584]{1,0:T(8,128)(2,1)S(1)}, u32[]{:S(2)}, u32[]{:S(2)}) collective-permute-start(bf16[16,3584]{1,0:T(8,128)(2,1)} %bitcast.67), channel_id=1, source_target_pairs={{0,4},{1,5},{4,0},{5,1},{8,12},{9,13},{12,8},{13,9},{16,20},{17,21... | collective-permute-start | bytes 344072 | tf_op jit(solution)/shard_map/ppermute | solution.py:316
  4.8 0.2 collective-permute-start.11
  5.0 1.1 %copy-done = bf16[1,3584,64]{1,2,0:T(8,128)(2,1)S(1)} copy-done((bf16[1,3584,64]{1,2,0:T(8,128)(2,1)S(1)}, bf16[1,3584,64]{1,2,0:T(8,128)(2,1)}, u32[]{:S(2)}) %copy-start) | copy-done | bytes 458776
  6.1 1.2 %copy-done.2 = bf16[1,1,8,16,3584]{4,3,2,1,0:T(8,128)(2,1)S(1)} copy-done((bf16[1,1,8,16,3584]{4,3,2,1,0:T(8,128)(2,1)S(1)}, bf16[1,1,8,16,3584]{4,3,2,1,0:T(8,128)(2,1)}, u32[]{:S(2)}) %copy-start.2) | copy-done | bytes 917528
  7.2 0.4 stashed.1
  7.6 1.1 %collective-permute-start.5 = (f32[8,16,64]{2,1,0:T(8,128)S(1)}, f32[8,16,64]{2,1,0:T(8,128)S(1)}, u32[]{:S(2)}, u32[]{:S(2)}) collective-permute-start(f32[8,16,64]{2,1,0:T(8,128)S(1)} %stashed.1), channel_id=1, source_target_pairs={{0,1},{1,0},{2,3},{3,2},{4,5},{5,4},{6,7},{7,6},{8,9},{9,8},{10,11... | collective-permute-start | bytes 98312 | tf_op jit(solution)/shard_map/ppermute | solution.py:319
  8.7 1.3 %collective-permute-start.3 = (bf16[16,7168]{1,0:T(8,128)(2,1)S(1)}, bf16[16,7168]{1,0:T(8,128)(2,1)S(1)}, u32[]{:S(2)}, u32[]{:S(2)}) collective-permute-start(bf16[16,7168]{1,0:T(8,128)(2,1)S(1)} %pad_maximum_fusion.3.refs_8_.refs_5_), channel_id=1, source_target_pairs={{8,0},{16,1},{1,29},{12,4},{20,5},{5,25},{10,2},{18,3},{3,31},{14,... | collective-permute-start | bytes 688136 | tf_op jit(solution)/shard_map/ppermute | solution.py:316
  10.0 0.2 collective-permute-start.8
  10.3 0.1 concatenate.21.where.refs_0_
  10.4 0.5 collective-permute-start.6
  10.9 9.4 %collective-permute-done.11.squeeze0 = bf16[64,3584]{1,0:T(8,128)(2,1)S(1)} collective-permute-done((bf16[64,3584]{1,0:T(8,128)(2,1)}, bf16[64,3584]{1,0:T(8,128)(2,1)S(1)}, u32[]{:S(2)}, u32[]{:S(2)}) %collective-permute-start.11) | collective-permute-done | bytes 458784 | tf_op jit(solution)/shard_map/ppermute | solution.py:316
  20.3 3.1 %collective-permute-start.10 = (f32[4,16,64]{2,1,0:T(8,128)S(1)}, f32[4,16,64]{2,1,0:T(8,128)S(1)}, u32[]{:S(2)}, u32[]{:S(2)}) collective-permute-start(f32[4,16,64]{2,1,0:T(8,128)S(1)} %slice.9), channel_id=1, source_target_pairs={{1,5},{5,1},{9,13},{13,9},{17,21},{21,17},{25,29},{29,25},{3,7},{7... | collective-permute-start | bytes 49160 | tf_op jit(solution)/shard_map/ppermute | solution.py:316
  23.5 0.3 collective-permute-start.13
  23.8 0.1 maximum_select_fusion.1
  23.9 1.3 %collective-permute-start.9 = (bf16[16,7168]{1,0:T(8,128)(2,1)S(1)}, bf16[16,7168]{1,0:T(8,128)(2,1)S(1)}, u32[]{:S(2)}, u32[]{:S(2)}) collective-permute-start(bf16[16,7168]{1,0:T(8,128)(2,1)S(1)} %get-tuple-element.66.refs_8_), channel_id=1, source_target_pairs={{24,0},{28,1},{13,29},{21,28},{9,25},{17,24},{26,2},{30,3},{15,31}... | collective-permute-start | bytes 688136 | tf_op jit(solution)/shard_map/ppermute | solution.py:316
  25.2 0.8 collective-permute-start.12
  26.0 9.0 %collective-permute-done.13.expand0 = bf16[64,3584]{1,0:T(8,128)(2,1)S(1)} collective-permute-done((bf16[64,3584]{1,0:T(8,128)(2,1)S(1)}, bf16[64,3584]{1,0:T(8,128)(2,1)S(1)}, u32[]{:S(2)}, u32[]{:S(2)}) %collective-permute-start.13) | collective-permute-done | bytes 458784 | tf_op jit(solution)/shard_map/ppermute | solution.py:316
  35.0 0.2 pad_maximum_fusion.refs_6_
  35.3 0.8 copy-done.5
  36.1 1.2 %collective-permute-start = (bf16[64,3584]{1,0:T(8,128)(2,1)S(1)}, bf16[64,3584]{1,0:T(8,128)(2,1)S(1)}, u32[]{:S(2)}, u32[]{:S(2)}) collective-permute-start(bf16[64,3584]{1,0:T(8,128)(2,1)S(1)} %bitcast.63), channel_id=1, source_target_pairs={{0,2},{2,0},{1,3},{3,1},{4,6},{6,4},{5,7},{7,5},{8,10},{10,8},{9,1... | collective-permute-start | bytes 1376264 | tf_op jit(solution)/shard_map/ppermute | solution.py:446
  37.3 1.7 %first.1 = (bf16[16,7680]{1,0:T(8,128)(2,1)S(1)}, bf16[4,16,3584]{2,1,0:T(8,128)(2,1)S(1)}, bf16[4,16,3712]{2,1,0:T(8,128)(2,1)S(1)}) custom-call(s32[9]{0:T(128)S(1)} %concatenate.21.where.refs_0_, bf16[16,7680]{1,0:T(8,128)(2,1)S(1)} %concatenate.24.x_in, f32[8,16,64]{2,1,0:T(8,128)S(1)} %add.18.again_own.refs_4_.refs_2_, ...), custom_call_target="tpu_custom_call" | custom-call | flops 58720256 | bytes 3670016 | tf_op jit(solution)/shard_map/first/pallas_call | solution.py:467
  39.0 0.3 collective-permute-start.1
  39.3 1.1 %collective-permute-start.17 = (bf16[16,7168]{1,0:T(8,128)(2,1)S(1)}, bf16[16,7168]{1,0:T(8,128)(2,1)S(1)}, u32[]{:S(2)}, u32[]{:S(2)}) collective-permute-start(bf16[16,7168]{1,0:T(8,128)(2,1)S(1)} %collective-permute-done.3.refs_9_.refs_8_), channel_id=1, source_target_pairs={{0,1},{1,0},{2,3},{3,2},{4,5},{5,4},{6,7},{7,6},{8,9},{9,8},{10,11... | collective-permute-start | bytes 688136 | tf_op jit(solution)/shard_map/ppermute | solution.py:319
  40.5 1.4 %second.1 = (bf16[16,7680]{1,0:T(8,128)(2,1)S(1)}, bf16[2,16,3712]{2,1,0:T(8,128)(2,1)S(1)}) custom-call(s32[9]{0:T(128)S(1)} %concatenate.21.where.refs_0_, bf16[16,7680]{1,0:T(8,128)(2,1)S(1)} %get-tuple-element.37.x_in, f32[4,16,64]{2,1,0:T(8,128)S(1)} %collective-permute-done.10.again_peer.refs_5_, ...), custom_call_target="tpu_custom_call" | custom-call | flops 58720256 | bytes 3670016 | tf_op jit(solution)/shard_map/second/pallas_call | solution.py:471
  41.9 1.9 %collective-permute-start.15 = (bf16[16,7680]{1,0:T(8,128)(2,1)S(1)}, bf16[16,7680]{1,0:T(8,128)(2,1)S(1)}, u32[]{:S(2)}, u32[]{:S(2)}) collective-permute-start(bf16[16,7680]{1,0:T(8,128)(2,1)S(1)} %get-tuple-element.39), channel_id=1, source_target_pairs={{0,8},{4,12},{8,16},{12,20},{16,24},{20,28},{24,29},{28,25},{9,1},... | collective-permute-start | bytes 737288 | tf_op jit(solution)/shard_map/ppermute | solution.py:316
  43.8 0.2 pad_maximum_fusion.1.refs_7_
  44.0 5.7 %collective-permute-done.15.refs_1_ = bf16[16,7680]{1,0:T(8,128)(2,1)S(1)} collective-permute-done((bf16[16,7680]{1,0:T(8,128)(2,1)S(1)}, bf16[16,7680]{1,0:T(8,128)(2,1)S(1)}, u32[]{:S(2)}, u32[]{:S(2)}) %collective-permute-start.15) | collective-permute-done | bytes 245792 | tf_op jit(solution)/shard_map/ppermute | solution.py:316
  49.7 2.7 %pair1.1 = (bf16[16,7680]{1,0:T(8,128)(2,1)S(1)}, bf16[2,16,3712]{2,1,0:T(8,128)(2,1)S(1)}, bf16[1,2,16,3712]{3,2,1,0:T(8,128)(2,1)S(1)}, bf16[4,16,3584]{2,1,0:T(8,128)(2,1)S(1)}, bf16[4,16,3712]{2,1,0:T(8,128)(2,1)S(1)}) custom-call(s32[9]{0:T(128)S(1)} %concatenate.21.where.refs_0_, ...), custom_call_target="tpu_custom_call", output_to_operand_aliasing={{3}: (11, {}), {4}: (12, {})} | custom-call | flops 58720256 | bytes 3670016 | tf_op jit(solution)/shard_map/pair1/pallas_call | solution.py:487
  52.5 1.9 %collective-permute-start.16 = (bf16[16,7680]{1,0:T(8,128)(2,1)S(1)}, bf16[16,7680]{1,0:T(8,128)(2,1)S(1)}, u32[]{:S(2)}, u32[]{:S(2)}) collective-permute-start(bf16[16,7680]{1,0:T(8,128)(2,1)S(1)} %get-tuple-element.43), channel_id=1, source_target_pairs={{0,8},{4,12},{8,16},{12,20},{16,24},{20,28},{24,29},{28,25},{9,1},... | collective-permute-start | bytes 737288 | tf_op jit(solution)/shard_map/ppermute | solution.py:316
  54.4 1.0 %subtract_convert_fusion.1 = bf16[64,3584]{1,0:T(8,128)(2,1)} fusion(bf16[64,3584]{1,0:T(8,128)(2,1)S(1)} %collective-permute-done, bf16[1,3584,64]{1,2,0:T(8,128)(2,1)S(1)} %copy-done.1, bf16[1,1,3584,64]{2,3,1,0:T(8,128)(2,1)S(1)} %copy-done.5), kind=kLoop, calls=%fused_computation.4 | loop fusion | flops 1605632 | bytes 1835008 | tf_op jit(solution)/shard_map/convert_element_type | solution.py:449
  55.4 4.9 %collective-permute-done.16.refs_1_ = bf16[16,7680]{1,0:T(8,128)(2,1)S(1)} collective-permute-done((bf16[16,7680]{1,0:T(8,128)(2,1)S(1)}, bf16[16,7680]{1,0:T(8,128)(2,1)S(1)}, u32[]{:S(2)}, u32[]{:S(2)}) %collective-permute-start.16) | collective-permute-done | bytes 245792 | tf_op jit(solution)/shard_map/ppermute | solution.py:316
  60.3 2.8 %pair2.1 = (bf16[16,7680]{1,0:T(8,128)(2,1)S(1)}, bf16[2,16,3712]{2,1,0:T(8,128)(2,1)S(1)}, bf16[2,2,16,3712]{3,2,1,0:T(8,128)(2,1)S(1)}, bf16[4,16,3584]{2,1,0:T(8,128)(2,1)S(1)}, bf16[4,16,3712]{2,1,0:T(8,128)(2,1)S(1)}) custom-call(s32[9]{0:T(128)S(1)} %concatenate.21.where.refs_0_, ...), custom_call_target="tpu_custom_call", output_to_operand_aliasing={{3}: (12, {}), {4}: (13, {})} | custom-call | flops 58720256 | bytes 3670016 | tf_op jit(solution)/shard_map/pair2/pallas_call | solution.py:487
  63.1 1.9 %collective-permute-start.19 = (bf16[16,7680]{1,0:T(8,128)(2,1)S(1)}, bf16[16,7680]{1,0:T(8,128)(2,1)S(1)}, u32[]{:S(2)}, u32[]{:S(2)}) collective-permute-start(bf16[16,7680]{1,0:T(8,128)(2,1)S(1)} %get-tuple-element.49), channel_id=1, source_target_pairs={{0,8},{4,12},{8,16},{12,20},{16,24},{20,28},{24,29},{28,25},{9,1},... | collective-permute-start | bytes 737288 | tf_op jit(solution)/shard_map/ppermute | solution.py:316
  65.1 3.0 %collective-permute-start.21 = (bf16[2,2,16,3712]{3,2,0,1:T(8,128)(2,1)S(1)}, bf16[2,2,16,3712]{3,2,0,1:T(8,128)(2,1)S(1)}, u32[]{:S(2)}, u32[]{:S(2)}) collective-permute-start(bf16[2,2,16,3712]{3,2,0,1:T(8,128)(2,1)S(1)} %copy.21), channel_id=1, source_target_pairs={{1,5},{5,1},{9,13},{13,9},{16,20},{17,21},{21,17},{24,28},{25,29},... | collective-permute-start | bytes 1425416 | tf_op jit(solution)/shard_map/ppermute | solution.py:316
  68.2 1.0 %subtract_convert_fusion = bf16[64,3584]{1,0:T(8,128)(2,1)} fusion(bf16[64,3584]{1,0:T(8,128)(2,1)S(1)} %collective-permute-done.1, bf16[1,1,64,3584]{3,2,1,0:T(8,128)(2,1)S(1)} %copy-done.6, bf16[1,64,3584]{2,1,0:T(8,128)(2,1)S(1)} %copy-done.4), kind=kLoop, calls=%fused_computation.3 | loop fusion | flops 1605632 | bytes 1835008 | tf_op jit(solution)/shard_map/convert_element_type | solution.py:449
  69.1 3.3 %collective-permute-done.19.refs_1_ = bf16[16,7680]{1,0:T(8,128)(2,1)S(1)} collective-permute-done((bf16[16,7680]{1,0:T(8,128)(2,1)S(1)}, bf16[16,7680]{1,0:T(8,128)(2,1)S(1)}, u32[]{:S(2)}, u32[]{:S(2)}) %collective-permute-start.19) | collective-permute-done | bytes 245792 | tf_op jit(solution)/shard_map/ppermute | solution.py:316
  72.4 3.4 %pair3.1 = (bf16[16,7680]{1,0:T(8,128)(2,1)S(1)}, bf16[8,128]{1,0:T(8,128)(2,1)}, bf16[1,2,16,3712]{3,2,1,0:T(8,128)(2,1)S(1)}, bf16[4,16,3584]{2,1,0:T(8,128)(2,1)S(1)}, bf16[4,16,3712]{2,1,0:T(8,128)(2,1)S(1)}) custom-call(s32[9]{0:T(128)S(1)} %concatenate.21.where.refs_0_, ...), custom_call_target="tpu_custom_call", output_to_operand_aliasing={{3}: (12, {}), {4}: (13, {})} | custom-call | flops 58720256 | bytes 3670016 | tf_op jit(solution)/shard_map/pair3/pallas_call | solution.py:487
  75.8 1.9 %collective-permute-start.25 = (bf16[16,7680]{1,0:T(8,128)(2,1)S(1)}, bf16[16,7680]{1,0:T(8,128)(2,1)S(1)}, u32[]{:S(2)}, u32[]{:S(2)}) collective-permute-start(bf16[16,7680]{1,0:T(8,128)(2,1)S(1)} %get-tuple-element.58), channel_id=1, source_target_pairs={{0,4},{4,8},{8,12},{12,16},{16,20},{20,24},{24,28},{28,29},{5,1},{... | collective-permute-start | bytes 737288 | tf_op jit(solution)/shard_map/ppermute | solution.py:316
  77.7 3.4 %collective-permute-start.23 = (bf16[2,16,3712]{2,1,0:T(8,128)(2,1)S(1)}, bf16[2,16,3712]{2,1,0:T(8,128)(2,1)S(1)}, u32[]{:S(2)}, u32[]{:S(2)}) collective-permute-start(bf16[2,16,3712]{2,1,0:T(8,128)(2,1)S(1)} %bitcast.61), channel_id=1, source_target_pairs={{1,5},{5,1},{9,13},{13,9},{17,21},{21,17},{24,28},{25,29},{29,25},... | collective-permute-start | bytes 712712 | tf_op jit(solution)/shard_map/ppermute | solution.py:316
  81.2 4.2 %collective-permute-start.22 = (bf16[2,16,3712]{2,1,0:T(8,128)(2,1)S(1)}, bf16[2,16,3712]{2,1,0:T(8,128)(2,1)S(1)}, u32[]{:S(2)}, u32[]{:S(2)}) collective-permute-start(bf16[2,16,3712]{2,1,0:T(8,128)(2,1)S(1)} %slice_bitcast_fusion), channel_id=1, source_target_pairs={{0,1},{1,0},{2,3},{3,2},{4,5},{5,4},{6,7},{7,6},{8,9},{9,8},{10,11... | collective-permute-start | bytes 712712 | tf_op jit(solution)/shard_map/ppermute | solution.py:319
  85.5 0.9 collective-permute-done.25.refs_1_
  86.4 1.4 %last.1 = (bf16[16,7296]{1,0:T(8,128)(2,1)S(1)}, bf16[16,7296]{1,0:T(8,128)(2,1)S(1)}) custom-call(s32[9]{0:T(128)S(1)} %concatenate.21.where.refs_0_, bf16[16,7680]{1,0:T(8,128)(2,1)S(1)} %collective-permute-done.25.refs_1_, f32[8,16,64]{2,1,0:T(8,128)S(1)} %add.18.again_own.refs_4_.refs_2_, bf16[2,64,3584]{2,1,0:T(8,128)(2,1)S(1)} %pad_maximum_fusion.2.mine.refs_3_, ...), custom_call_target="tpu_custom_call" | custom-call | flops 58720256 | bytes 3670016 | tf_op jit(solution)/shard_map/last/pallas_call | solution.py:508
  87.9 1.1 %collective-permute-done.23.late = bf16[2,16,3712]{2,1,0:T(8,128)(2,1)S(1)} collective-permute-done((bf16[2,16,3712]{2,1,0:T(8,128)(2,1)S(1)}, bf16[2,16,3712]{2,1,0:T(8,128)(2,1)S(1)}, u32[]{:S(2)}, u32[]{:S(2)}) %collective-permute-start.23) | collective-permute-done | bytes 237600 | tf_op jit(solution)/shard_map/ppermute | solution.py:316
  89.1 1.3 %collective-permute-done.24.late_got = bf16[16,3712]{1,0:T(8,128)(2,1)S(1)} collective-permute-done((bf16[16,3712]{1,0:T(8,128)(2,1)S(1)}, bf16[16,3712]{1,0:T(8,128)(2,1)S(1)}, u32[]{:S(2)}, u32[]{:S(2)}) %collective-permute-start.24) | collective-permute-done | bytes 118816 | tf_op jit(solution)/shard_map/ppermute | solution.py:319
  90.4 2.1 %finish.1 = (bf16[64,3584]{1,0:T(8,128)(2,1)}, bf16[64,3584]{1,0:T(8,128)(2,1)}, bf16[16,3584]{1,0:T(8,128)(2,1)}, bf16[16,3584]{1,0:T(8,128)(2,1)}) custom-call(s32[9]{0:T(128)S(1)} %concatenate.21.where.refs_0_, bf16[4,16,3584]{2,1,0:T(8,128)(2,1)S(1)} %get-tuple-element.55.mine, bf16[4,16,3712]{2,1,0:T(8,128)(2,1)S(1)} %get-tuple-element.56.sent, ...), custom_call_target="tpu_custom_call" | custom-call | flops 58720256 | bytes 3670016 | tf_op jit(solution)/shard_map/finish/pallas_call | solution.py:514
  (46 shorter events, 0.7 us)
Async XLA Ops:
  0.6 9.6 %copy-start.4 = (bf16[1,64,3584]{2,1,0:T(8,128)(2,1)S(1)}, bf16[1,64,3584]{2,1,0:T(8,128)(2,1)}, u32[]{:S(2)}) copy-start(bf16[1,64,3584]{2,1,0:T(8,128)(2,1)} %param.12) | copy-start | bytes 1376260
  1.7 7.0 %collective-permute-start.2 = (bf16[16,3584]{1,0:T(8,128)(2,1)S(1)}, bf16[16,3584]{1,0:T(8,128)(2,1)S(1)}, u32[]{:S(2)}, u32[]{:S(2)}) collective-permute-start(bf16[16,3584]{1,0:T(8,128)(2,1)S(1)} %get-tuple-element.69), channel_id=1, source_target_pairs={{0,1},{1,0},{2,3},{3,2},{4,5},{5,4},{6,7},{7,6},{8,9},{9,8},{10,11... | collective-permute-start | bytes 344072 | tf_op jit(solution)/shard_map/ppermute | solution.py:319
  3.4 20.1 %collective-permute-start.4 = (bf16[16,3584]{1,0:T(8,128)(2,1)S(1)}, bf16[16,3584]{1,0:T(8,128)(2,1)S(1)}, u32[]{:S(2)}, u32[]{:S(2)}) collective-permute-start(bf16[16,3584]{1,0:T(8,128)(2,1)S(1)} %get-tuple-element.71), channel_id=1, source_target_pairs={{0,1},{1,0},{2,3},{3,2},{4,5},{5,4},{6,7},{7,6},{8,9},{9,8},{10,11... | collective-permute-start | bytes 344072 | tf_op jit(solution)/shard_map/ppermute | solution.py:319
  3.5 6.5 %collective-permute-start.7 = (bf16[16,3584]{1,0:T(8,128)(2,1)}, bf16[16,3584]{1,0:T(8,128)(2,1)S(1)}, u32[]{:S(2)}, u32[]{:S(2)}) collective-permute-start(bf16[16,3584]{1,0:T(8,128)(2,1)} %bitcast.67), channel_id=1, source_target_pairs={{0,4},{1,5},{4,0},{5,1},{8,12},{9,13},{12,8},{13,9},{16,20},{17,21... | collective-permute-start | bytes 344072 | tf_op jit(solution)/shard_map/ppermute | solution.py:316
  4.8 15.5 %collective-permute-start.11 = (bf16[64,3584]{1,0:T(8,128)(2,1)}, bf16[64,3584]{1,0:T(8,128)(2,1)S(1)}, u32[]{:S(2)}, u32[]{:S(2)}) collective-permute-start(bf16[64,3584]{1,0:T(8,128)(2,1)} %bitcast.52), channel_id=1, source_target_pairs={{0,4},{1,5},{4,0},{5,1},{8,12},{9,13},{12,8},{13,9},{16,20},{17,21... | collective-permute-start | bytes 1376264 | tf_op jit(solution)/shard_map/ppermute | solution.py:316
  5.0 1.1 %copy-start = (bf16[1,3584,64]{1,2,0:T(8,128)(2,1)S(1)}, bf16[1,3584,64]{1,2,0:T(8,128)(2,1)}, u32[]{:S(2)}) copy-start(bf16[1,3584,64]{1,2,0:T(8,128)(2,1)} %param.11) | copy-start | bytes 1376260
  6.1 1.2 %copy-start.2 = (bf16[1,1,8,16,3584]{4,3,2,1,0:T(8,128)(2,1)S(1)}, bf16[1,1,8,16,3584]{4,3,2,1,0:T(8,128)(2,1)}, u32[]{:S(2)}) copy-start(bf16[1,1,8,16,3584]{4,3,2,1,0:T(8,128)(2,1)} %param.15) | copy-start | bytes 2752516
  7.6 2.8 %collective-permute-start.5 = (f32[8,16,64]{2,1,0:T(8,128)S(1)}, f32[8,16,64]{2,1,0:T(8,128)S(1)}, u32[]{:S(2)}, u32[]{:S(2)}) collective-permute-start(f32[8,16,64]{2,1,0:T(8,128)S(1)} %stashed.1), channel_id=1, source_target_pairs={{0,1},{1,0},{2,3},{3,2},{4,5},{5,4},{6,7},{7,6},{8,9},{9,8},{10,11... | collective-permute-start | bytes 98312 | tf_op jit(solution)/shard_map/ppermute | solution.py:319
  8.7 15.1 %collective-permute-start.3 = (bf16[16,7168]{1,0:T(8,128)(2,1)S(1)}, bf16[16,7168]{1,0:T(8,128)(2,1)S(1)}, u32[]{:S(2)}, u32[]{:S(2)}) collective-permute-start(bf16[16,7168]{1,0:T(8,128)(2,1)S(1)} %pad_maximum_fusion.3.refs_8_.refs_5_), channel_id=1, source_target_pairs={{8,0},{16,1},{1,29},{12,4},{20,5},{5,25},{10,2},{18,3},{3,31},{14,... | collective-permute-start | bytes 688136 | tf_op jit(solution)/shard_map/ppermute | solution.py:316
  10.0 13.8 %collective-permute-start.8 = (bf16[16,3584]{1,0:T(8,128)(2,1)S(1)}, bf16[16,3584]{1,0:T(8,128)(2,1)S(1)}, u32[]{:S(2)}, u32[]{:S(2)}) collective-permute-start(bf16[16,3584]{1,0:T(8,128)(2,1)S(1)} %collective-permute-done.7), channel_id=1, source_target_pairs={{0,1},{1,0},{2,3},{3,2},{4,5},{5,4},{6,7},{7,6},{8,9},{9,8},{10,11... | collective-permute-start | bytes 344072 | tf_op jit(solution)/shard_map/ppermute | solution.py:319
  10.4 24.8 %collective-permute-start.6 = (bf16[2,64,3584]{2,1,0:T(8,128)(2,1)S(1)}, bf16[2,64,3584]{2,1,0:T(8,128)(2,1)S(1)}, u32[]{:S(2)}, u32[]{:S(2)}) collective-permute-start(bf16[2,64,3584]{2,1,0:T(8,128)(2,1)S(1)} %pad_maximum_fusion.2.mine.refs_3_), channel_id=1, source_target_pairs={{0,1},{1,0},{2,3},{3,2},{4,5},{5,4},{6,7},{7,6},{8,9},{9,8},{10,11... | collective-permute-start | bytes 2752520 | tf_op jit(solution)/shard_map/ppermute | solution.py:319
  20.3 19.0 %collective-permute-start.10 = (f32[4,16,64]{2,1,0:T(8,128)S(1)}, f32[4,16,64]{2,1,0:T(8,128)S(1)}, u32[]{:S(2)}, u32[]{:S(2)}) collective-permute-start(f32[4,16,64]{2,1,0:T(8,128)S(1)} %slice.9), channel_id=1, source_target_pairs={{1,5},{5,1},{9,13},{13,9},{17,21},{21,17},{25,29},{29,25},{3,7},{7... | collective-permute-start | bytes 49160 | tf_op jit(solution)/shard_map/ppermute | solution.py:316
  23.5 11.6 %collective-permute-start.13 = (bf16[64,3584]{1,0:T(8,128)(2,1)S(1)}, bf16[64,3584]{1,0:T(8,128)(2,1)S(1)}, u32[]{:S(2)}, u32[]{:S(2)}) collective-permute-start(bf16[64,3584]{1,0:T(8,128)(2,1)S(1)} %bitcast.62), channel_id=1, source_target_pairs={{0,4},{1,5},{4,0},{5,1},{8,12},{9,13},{12,8},{13,9},{16,20},{17,21... | collective-permute-start | bytes 1376264 | tf_op jit(solution)/shard_map/ppermute | solution.py:316
  23.9 15.1 %collective-permute-start.9 = (bf16[16,7168]{1,0:T(8,128)(2,1)S(1)}, bf16[16,7168]{1,0:T(8,128)(2,1)S(1)}, u32[]{:S(2)}, u32[]{:S(2)}) collective-permute-start(bf16[16,7168]{1,0:T(8,128)(2,1)S(1)} %get-tuple-element.66.refs_8_), channel_id=1, source_target_pairs={{24,0},{28,1},{13,29},{21,28},{9,25},{17,24},{26,2},{30,3},{15,31}... | collective-permute-start | bytes 688136 | tf_op jit(solution)/shard_map/ppermute | solution.py:316
  25.2 15.2 %collective-permute-start.12 = (bf16[64,3584]{1,0:T(8,128)(2,1)S(1)}, bf16[64,3584]{1,0:T(8,128)(2,1)S(1)}, u32[]{:S(2)}, u32[]{:S(2)}) collective-permute-start(bf16[64,3584]{1,0:T(8,128)(2,1)S(1)} %collective-permute-done.11.squeeze0), channel_id=1, source_target_pairs={{0,1},{1,0},{2,3},{3,2},{4,5},{5,4},{6,7},{7,6},{8,9},{9,8},{10,11... | collective-permute-start | bytes 1376264 | tf_op jit(solution)/shard_map/ppermute | solution.py:319
  35.0 5.4 %collective-permute-start.14 = (bf16[64,3584]{1,0:T(8,128)(2,1)S(1)}, bf16[64,3584]{1,0:T(8,128)(2,1)S(1)}, u32[]{:S(2)}, u32[]{:S(2)}) collective-permute-start(bf16[64,3584]{1,0:T(8,128)(2,1)S(1)} %collective-permute-done.13.expand0), channel_id=1, source_target_pairs={{0,1},{1,0},{2,3},{3,2},{4,5},{5,4},{6,7},{7,6},{8,9},{9,8},{10,11... | collective-permute-start | bytes 1376264 | tf_op jit(solution)/shard_map/ppermute | solution.py:319
  35.0 1.0 %copy-start.5 = (bf16[1,1,3584,64]{2,3,1,0:T(8,128)(2,1)S(1)}, bf16[1,1,3584,64]{2,3,1,0:T(8,128)(2,1)}, u32[]{:S(2)}) copy-start(bf16[1,1,3584,64]{2,3,1,0:T(8,128)(2,1)} %param.13) | copy-start | bytes 1376260
  35.3 3.7 %copy-start.6 = (bf16[1,1,64,3584]{3,2,1,0:T(8,128)(2,1)S(1)}, bf16[1,1,64,3584]{3,2,1,0:T(8,128)(2,1)}, u32[]{:S(2)}) copy-start(bf16[1,1,64,3584]{3,2,1,0:T(8,128)(2,1)} %param.14) | copy-start | bytes 1376260
  36.1 18.3 %collective-permute-start = (bf16[64,3584]{1,0:T(8,128)(2,1)S(1)}, bf16[64,3584]{1,0:T(8,128)(2,1)S(1)}, u32[]{:S(2)}, u32[]{:S(2)}) collective-permute-start(bf16[64,3584]{1,0:T(8,128)(2,1)S(1)} %bitcast.63), channel_id=1, source_target_pairs={{0,2},{2,0},{1,3},{3,1},{4,6},{6,4},{5,7},{7,5},{8,10},{10,8},{9,1... | collective-permute-start | bytes 1376264 | tf_op jit(solution)/shard_map/ppermute | solution.py:446
  39.0 29.2 %collective-permute-start.1 = (bf16[64,3584]{1,0:T(8,128)(2,1)S(1)}, bf16[64,3584]{1,0:T(8,128)(2,1)S(1)}, u32[]{:S(2)}, u32[]{:S(2)}) collective-permute-start(bf16[64,3584]{1,0:T(8,128)(2,1)S(1)} %bitcast.64), channel_id=1, source_target_pairs={{0,2},{2,0},{1,3},{3,1},{4,6},{6,4},{5,7},{7,5},{8,10},{10,8},{9,1... | collective-permute-start | bytes 1376264 | tf_op jit(solution)/shard_map/ppermute | solution.py:446
  39.3 21.0 %collective-permute-start.17 = (bf16[16,7168]{1,0:T(8,128)(2,1)S(1)}, bf16[16,7168]{1,0:T(8,128)(2,1)S(1)}, u32[]{:S(2)}, u32[]{:S(2)}) collective-permute-start(bf16[16,7168]{1,0:T(8,128)(2,1)S(1)} %collective-permute-done.3.refs_9_.refs_8_), channel_id=1, source_target_pairs={{0,1},{1,0},{2,3},{3,2},{4,5},{5,4},{6,7},{7,6},{8,9},{9,8},{10,11... | collective-permute-start | bytes 688136 | tf_op jit(solution)/shard_map/ppermute | solution.py:319
  40.4 19.9 %collective-permute-start.18 = (bf16[16,7168]{1,0:T(8,128)(2,1)S(1)}, bf16[16,7168]{1,0:T(8,128)(2,1)S(1)}, u32[]{:S(2)}, u32[]{:S(2)}) collective-permute-start(bf16[16,7168]{1,0:T(8,128)(2,1)S(1)} %collective-permute-done.9.refs_10_), channel_id=1, source_target_pairs={{0,1},{1,0},{2,3},{3,2},{4,5},{5,4},{6,7},{7,6},{8,9},{9,8},{10,11... | collective-permute-start | bytes 688136 | tf_op jit(solution)/shard_map/ppermute | solution.py:319
  41.9 7.8 %collective-permute-start.15 = (bf16[16,7680]{1,0:T(8,128)(2,1)S(1)}, bf16[16,7680]{1,0:T(8,128)(2,1)S(1)}, u32[]{:S(2)}, u32[]{:S(2)}) collective-permute-start(bf16[16,7680]{1,0:T(8,128)(2,1)S(1)} %get-tuple-element.39), channel_id=1, source_target_pairs={{0,8},{4,12},{8,16},{12,20},{16,24},{20,28},{24,29},{28,25},{9,1},... | collective-permute-start | bytes 737288 | tf_op jit(solution)/shard_map/ppermute | solution.py:316
  49.7 4.7 %copy-start.1 = (bf16[1,3584,64]{1,2,0:T(8,128)(2,1)S(1)}, bf16[1,3584,64]{1,2,0:T(8,128)(2,1)}, u32[]{:S(2)}) copy-start(bf16[1,3584,64]{1,2,0:T(8,128)(2,1)} %param.11) | copy-start | bytes 1376260
  52.5 7.9 %collective-permute-start.16 = (bf16[16,7680]{1,0:T(8,128)(2,1)S(1)}, bf16[16,7680]{1,0:T(8,128)(2,1)S(1)}, u32[]{:S(2)}, u32[]{:S(2)}) collective-permute-start(bf16[16,7680]{1,0:T(8,128)(2,1)S(1)} %get-tuple-element.43), channel_id=1, source_target_pairs={{0,8},{4,12},{8,16},{12,20},{16,24},{20,28},{24,29},{28,25},{9,1},... | collective-permute-start | bytes 737288 | tf_op jit(solution)/shard_map/ppermute | solution.py:316
  63.1 9.3 %collective-permute-start.19 = (bf16[16,7680]{1,0:T(8,128)(2,1)S(1)}, bf16[16,7680]{1,0:T(8,128)(2,1)S(1)}, u32[]{:S(2)}, u32[]{:S(2)}) collective-permute-start(bf16[16,7680]{1,0:T(8,128)(2,1)S(1)} %get-tuple-element.49), channel_id=1, source_target_pairs={{0,8},{4,12},{8,16},{12,20},{16,24},{20,28},{24,29},{28,25},{9,1},... | collective-permute-start | bytes 737288 | tf_op jit(solution)/shard_map/ppermute | solution.py:316
  65.1 16.1 %collective-permute-start.21 = (bf16[2,2,16,3712]{3,2,0,1:T(8,128)(2,1)S(1)}, bf16[2,2,16,3712]{3,2,0,1:T(8,128)(2,1)S(1)}, u32[]{:S(2)}, u32[]{:S(2)}) collective-permute-start(bf16[2,2,16,3712]{3,2,0,1:T(8,128)(2,1)S(1)} %copy.21), channel_id=1, source_target_pairs={{1,5},{5,1},{9,13},{13,9},{16,20},{17,21},{21,17},{24,28},{25,29},... | collective-permute-start | bytes 1425416 | tf_op jit(solution)/shard_map/ppermute | solution.py:316
  75.8 10.6 %collective-permute-start.25 = (bf16[16,7680]{1,0:T(8,128)(2,1)S(1)}, bf16[16,7680]{1,0:T(8,128)(2,1)S(1)}, u32[]{:S(2)}, u32[]{:S(2)}) collective-permute-start(bf16[16,7680]{1,0:T(8,128)(2,1)S(1)} %get-tuple-element.58), channel_id=1, source_target_pairs={{0,4},{4,8},{8,12},{12,16},{16,20},{20,24},{24,28},{28,29},{5,1},{... | collective-permute-start | bytes 737288 | tf_op jit(solution)/shard_map/ppermute | solution.py:316
  77.7 11.2 %collective-permute-start.23 = (bf16[2,16,3712]{2,1,0:T(8,128)(2,1)S(1)}, bf16[2,16,3712]{2,1,0:T(8,128)(2,1)S(1)}, u32[]{:S(2)}, u32[]{:S(2)}) collective-permute-start(bf16[2,16,3712]{2,1,0:T(8,128)(2,1)S(1)} %bitcast.61), channel_id=1, source_target_pairs={{1,5},{5,1},{9,13},{13,9},{17,21},{21,17},{24,28},{25,29},{29,25},... | collective-permute-start | bytes 712712 | tf_op jit(solution)/shard_map/ppermute | solution.py:316
  81.1 9.2 %collective-permute-start.20 = (bf16[4,16,3712]{2,1,0:T(8,128)(2,1)S(1)}, bf16[4,16,3712]{2,1,0:T(8,128)(2,1)S(1)}, u32[]{:S(2)}, u32[]{:S(2)}) collective-permute-start(bf16[4,16,3712]{2,1,0:T(8,128)(2,1)S(1)} %get-tuple-element.56.sent), channel_id=1, source_target_pairs={{0,1},{1,0},{2,3},{3,2},{4,5},{5,4},{6,7},{7,6},{8,9},{9,8},{10,11... | collective-permute-start | bytes 1425416 | tf_op jit(solution)/shard_map/ppermute | solution.py:319
  81.2 9.1 %copy-start.3 = (bf16[1,1,8,16,3584]{4,3,2,1,0:T(8,128)(2,1)S(1)}, bf16[1,1,8,16,3584]{4,3,2,1,0:T(8,128)(2,1)}, u32[]{:S(2)}) copy-start(bf16[1,1,8,16,3584]{4,3,2,1,0:T(8,128)(2,1)} %param.15) | copy-start | bytes 2752516
  81.2 9.1 %collective-permute-start.22 = (bf16[2,16,3712]{2,1,0:T(8,128)(2,1)S(1)}, bf16[2,16,3712]{2,1,0:T(8,128)(2,1)S(1)}, u32[]{:S(2)}, u32[]{:S(2)}) collective-permute-start(bf16[2,16,3712]{2,1,0:T(8,128)(2,1)S(1)} %slice_bitcast_fusion), channel_id=1, source_target_pairs={{0,1},{1,0},{2,3},{3,2},{4,5},{5,4},{6,7},{7,6},{8,9},{9,8},{10,11... | collective-permute-start | bytes 712712 | tf_op jit(solution)/shard_map/ppermute | solution.py:319
  87.8 2.6 %collective-permute-start.26 = (bf16[16,7296]{1,0:T(8,128)(2,1)S(1)}, bf16[16,7296]{1,0:T(8,128)(2,1)S(1)}, u32[]{:S(2)}, u32[]{:S(2)}) collective-permute-start(bf16[16,7296]{1,0:T(8,128)(2,1)S(1)} %get-tuple-element.61.last_other), channel_id=1, source_target_pairs={{0,1},{1,0},{2,3},{3,2},{4,5},{5,4},{6,7},{7,6},{8,9},{9,8},{10,11... | collective-permute-start | bytes 700424 | tf_op jit(solution)/shard_map/ppermute | solution.py:319
  89.0 1.4 %collective-permute-start.24 = (bf16[16,3712]{1,0:T(8,128)(2,1)S(1)}, bf16[16,3712]{1,0:T(8,128)(2,1)S(1)}, u32[]{:S(2)}, u32[]{:S(2)}) collective-permute-start(bf16[16,3712]{1,0:T(8,128)(2,1)S(1)} %slice_bitcast_fusion.1), channel_id=1, source_target_pairs={{0,1},{1,0},{2,3},{3,2},{4,5},{5,4},{6,7},{7,6},{8,9},{9,8},{10,11... | collective-permute-start | bytes 356360 | tf_op jit(solution)/shard_map/ppermute | solution.py:319

commit v7 on v6

--- a/solution.py
+++ b/solution.py
@@ -348,17 +348,29 @@
     acts, cots = activations[0], cotangent[0]
     both = [(s, c) for s in everyone for c in (0, 1)]
 
+    def averaged(old, late, came):
+        total = late.astype(f32) + came.astype(f32) if replicas == 2 else came.astype(f32)
+        return (old.astype(f32) - STEP_RATE * total / replicas).astype(bf16)
+
+    def across(late):
+        return lax.ppermute(late, "dp", [(0, 1), (1, 0)]) if replicas == 2 else lax.psum(late, "dp")
+
+    squeeze_late, expand_late = squeeze_late[0, 0].T, expand_late[0, 0]
     squeeze_peer = to_peer(squeeze, both)
     expand_peer = to_peer(tied(expand, squeeze_peer), both)
+    squeeze_peer_other = swap(squeeze_peer)
+    squeeze_came = across(tied(squeeze_late, squeeze_peer_other))
+    expand_came = across(tied(expand_late, squeeze_peer_other))
+    squeeze_new = averaged(squeeze, squeeze_late, squeeze_came)
+    expand_new = averaged(expand, expand_late, expand_came)
     own = lax.optimization_barrier(jnp.stack([squeeze, expand]))
     other = swap(own)
-    squeeze_peer_other, expand_peer_other = swap(squeeze_peer), swap(expand_peer)
 
     partial = call(
         stash_kernel, "stashed", shape(ticks, rows, rank, dtype=f32), [VMEM, VMEM], VMEM
     )(stash, squeeze)
     again_own = partial + swap(partial)
-    again_peer = to_peer(again_own[1::2], [(s, 1) for s in everyone])
+    again_peer = to_peer(tied(again_own[1::2], squeeze_peer_other), [(s, 1) for s in everyone])
 
     cots_crossed = to_peer(cots, both)
     entering = jnp.concatenate([jnp.where(forward, acts, cots), swap(jnp.where(forward, cots, acts))], axis=1)
@@ -402,7 +414,7 @@
     feeds = [jnp.tile(crossed, (per_tick, 1)), jnp.tile(entering, (per_tick, 1))]
     for n, trip in enumerate(trips):
         if trip:
-            feeds.append(fed(trip, crossed if n else entering))
+            feeds.append(fed(trip, crossed if n else tied(entering, squeeze_peer)))
             feeds.append(swap(feeds[-1]))
 
     def used(b_of):
@@ -441,16 +453,6 @@
         pltpu.SemaphoreType.DMA((2,)),
     )
 
-    def averaged(old, late):
-        if replicas == 2:
-            total = late.astype(f32) + lax.ppermute(late, "dp", [(0, 1), (1, 0)]).astype(f32)
-        else:
-            total = lax.psum(late, "dp").astype(f32)
-        return (old.astype(f32) - STEP_RATE * total / replicas).astype(bf16)
-
-    squeeze_new = averaged(squeeze, squeeze_late[0, 0].T)
-    expand_new = averaged(expand, expand_late[0, 0])
-
     ring = (
         [((s, 0), (s + 2, 0)) for s in range(sections - 2)]
         + [((sections - 2, 0), (sections - 1, 1)), ((sections - 1, 0), (sections - 2, 1))]
@@ -468,6 +470,7 @@
         first_kernel, "first", (shape(rows, size.message), *hist_shapes),
         [SMEM, VMEM, VMEM, VMEM, VMEM], (VMEM, ANY, ANY), keep_own,
     )(where, x, again_own, own, other)
+    expand_peer_other = swap(tied(expand_peer, x))
     x, held = call(
         second_kernel, "second", (shape(rows, size.message), shape(*odd_shape)),
         [SMEM] + [VMEM] * 6, (VMEM, VMEM),

time: 92.9 us -> 91.7 us (0.987)
  waiting for transfers between devices: 35.6 us -> 32.6 us
  other arithmetic: 4.6 us -> 6.26 us
    ppermute x12, waiting for transfers between devices: 34.3 us -> 31.5 us  [send(): lax.ppermute(x, ('pipe', 'mp'), [(a * 2 + b, c * 2 + d) for (a, b), (c, d...]
    select_n x1, other arithmetic: 0.12 us -> 1.19 us  [shards(): crossed = jnp.where(forward, entering, crossed)]
    unnamed x14 -> x20, local copies, waits for them, and re-layouts: 3.04 us -> 3.04 us
  transfers between devices with their start and end apart: 27 -> 27, of which waited for: 8 -> 7; matrix products, arithmetic and copies ran while one was open for 4% -> 7% of each run, Pallas kernels for 15% -> 15%
where the time goes in v7:
time: 91.7 us; the launch traced here: 91 us
  waiting for transfers between devices  32.6 us (36%)
  starting transfers between devices  32.1 us (35%)
  Pallas kernels  15.8 us (17%)
  other arithmetic  6.26 us (7%)
  local copies, waits for them, and re-layouts  3.26 us (4%)
  between operations  1.07 us (1%)
    ppermute x12, waiting for transfers between devices, send(): lax.ppermute(x, ('pipe', 'mp'), [(a * 2 + b, c * 2 + d) for (a, b), (c, d...  31.5 us
    ppermute x12, starting transfers between devices, send(): lax.ppermute(x, ('pipe', 'mp'), [(a * 2 + b, c * 2 + d) for (a, b), (c, d...  21.2 us
    ppermute x13, starting transfers between devices, swap(): return lax.ppermute(x, 'mp', [(0, 1), (1, 0)])  8.98 us
    pallas_call x3, Pallas kernels, shards(): call(body, f'pair{step}', (shape(rows, size.message), shape(*((8, 128) if...  8.87 us
    unnamed x20, local copies, waits for them, and re-layouts  3.04 us
    pallas_call x1, Pallas kernels, shards(): call(end_kernel, 'finish', (shape(rank, half), shape(rank, half), shape(r...  2.08 us
    convert_element_type x2, other arithmetic, averaged(): return (old.astype(f32) - STEP_RATE * total / replicas).astype(bf16)  1.94 us
    ppermute x2, starting transfers between devices, across(): lax.ppermute(late, 'dp', [(0, 1), (1, 0)])  1.86 us
  transfers between devices with their start and end apart: 27, of which 7 were waited for; matrix products, arithmetic and copies ran while one was open for 7% of the time, Pallas kernels for 15%

profile of v7, /device:TPU:25, one launch (start us, length us, event | category | flops | bytes accessed | tf_op | source)
XLA Modules:
  0.0 91.0 jit_solution(17859166883845052881)
XLA Ops:
  0.6 1.3 %collective-permute-start = (bf16[64,3584]{1,0:T(8,128)(2,1)}, bf16[64,3584]{1,0:T(8,128)(2,1)S(1)}, u32[]{:S(2)}, u32[]{:S(2)}) collective-permute-start(bf16[64,3584]{1,0:T(8,128)(2,1)} %bitcast.52), channel_id=1, source_target_pairs={{0,4},{1,5},{4,0},{5,1},{8,12},{9,13},{12,8},{13,9},{16,20},{17,21... | collective-permute-start | bytes 1376264 | tf_op jit(solution)/shard_map/ppermute | solution.py:316
  1.9 1.1 %copy-done = bf16[1,3584,64]{1,2,0:T(8,128)(2,1)S(1)} copy-done((bf16[1,3584,64]{1,2,0:T(8,128)(2,1)S(1)}, bf16[1,3584,64]{1,2,0:T(8,128)(2,1)}, u32[]{:S(2)}) %copy-start) | copy-done | bytes 458776
  3.0 1.2 %copy-done.2 = bf16[1,1,8,16,3584]{4,3,2,1,0:T(8,128)(2,1)S(1)} copy-done((bf16[1,1,8,16,3584]{4,3,2,1,0:T(8,128)(2,1)S(1)}, bf16[1,1,8,16,3584]{4,3,2,1,0:T(8,128)(2,1)}, u32[]{:S(2)}) %copy-start.2) | copy-done | bytes 917528
  4.2 0.4 stashed.1
  4.6 1.0 %collective-permute-start.7 = (f32[8,16,64]{2,1,0:T(8,128)S(1)}, f32[8,16,64]{2,1,0:T(8,128)}, u32[]{:S(2)}, u32[]{:S(2)}) collective-permute-start(f32[8,16,64]{2,1,0:T(8,128)S(1)} %stashed.1), channel_id=1, source_target_pairs={{0,1},{1,0},{2,3},{3,2},{4,5},{5,4},{6,7},{7,6},{8,9},{9,8},{10,11... | collective-permute-start | bytes 98312 | tf_op jit(solution)/shard_map/ppermute | solution.py:319
  5.6 0.2 collective-permute-start.9
  5.8 1.0 %bitcast_select_fusion.1 = (bf16[16,3584]{1,0:T(8,128)(2,1)S(1)}, bf16[16,3584]{1,0:T(8,128)(2,1)S(1)}) fusion(bf16[1,16,3584]{2,1,0:T(8,128)(2,1)} %param.9, pred[]{:T(512)S(6)} %eq.21, bf16[1,16,3584]{2,1,0:T(8,128)(2,1)} %param.10), kind=kLoop, calls=%fused_computation.11 | loop fusion | flops 114688 | bytes 458753 | tf_op jit(solution)/shard_map/jit(_where)/select_n | solution.py:376
  6.8 0.4 collective-permute-start.4
  7.2 0.7 select_bitcast_fusion.1
  8.1 6.7 %collective-permute-done.9 = bf16[16,3584]{1,0:T(8,128)(2,1)} collective-permute-done((bf16[16,3584]{1,0:T(8,128)(2,1)}, bf16[16,3584]{1,0:T(8,128)(2,1)}, u32[]{:S(2)}, u32[]{:S(2)}) %collective-permute-start.9) | collective-permute-done | bytes 114720 | tf_op jit(solution)/shard_map/ppermute | solution.py:316
  14.9 1.5 %collective-permute-start.10 = (bf16[16,3584]{1,0:T(8,128)(2,1)}, bf16[16,3584]{1,0:T(8,128)(2,1)}, u32[]{:S(2)}, u32[]{:S(2)}) collective-permute-start(bf16[16,3584]{1,0:T(8,128)(2,1)} %collective-permute-done.9), channel_id=1, source_target_pairs={{0,1},{1,0},{2,3},{3,2},{4,5},{5,4},{6,7},{7,6},{8,9},{9,8},{10,11... | collective-permute-start | bytes 344072 | tf_op jit(solution)/shard_map/ppermute | solution.py:319
  16.4 1.3 %collective-permute-start.5 = (bf16[16,7168]{1,0:T(8,128)(2,1)S(1)}, bf16[16,7168]{1,0:T(8,128)(2,1)S(1)}, u32[]{:S(2)}, u32[]{:S(2)}) collective-permute-start(bf16[16,7168]{1,0:T(8,128)(2,1)S(1)} %pad_maximum_fusion.3.refs_8_.refs_5_), channel_id=1, source_target_pairs={{8,0},{16,1},{1,29},{12,4},{20,5},{5,25},{10,2},{18,3},{3,31},{14,... | collective-permute-start | bytes 688136 | tf_op jit(solution)/shard_map/ppermute | solution.py:316
  18.1 0.9 add.18.again_own.refs_4_.refs_2_
  19.0 1.3 %collective-permute-start.13 = (bf16[64,3584]{1,0:T(8,128)(2,1)}, bf16[64,3584]{1,0:T(8,128)(2,1)S(1)}, u32[]{:S(2)}, u32[]{:S(2)}) collective-permute-start(bf16[64,3584]{1,0:T(8,128)(2,1)} %bitcast.62), channel_id=1, source_target_pairs={{0,4},{1,5},{4,0},{5,1},{8,12},{9,13},{12,8},{13,9},{16,20},{17,21... | collective-permute-start | bytes 1376264 | tf_op jit(solution)/shard_map/ppermute | solution.py:316
  20.3 0.7 collective-permute-start.1
  21.0 5.0 %collective-permute-done.5.refs_9_.refs_8_ = bf16[16,7168]{1,0:T(8,128)(2,1)S(1)} collective-permute-done((bf16[16,7168]{1,0:T(8,128)(2,1)S(1)}, bf16[16,7168]{1,0:T(8,128)(2,1)S(1)}, u32[]{:S(2)}, u32[]{:S(2)}) %collective-permute-start.5) | collective-permute-done | bytes 229408 | tf_op jit(solution)/shard_map/ppermute | solution.py:316
  26.0 1.2 %maximum_select_fusion.1 = (bf16[16,7168]{1,0:T(8,128)(2,1)S(1)}, bf16[16,7168]{1,0:T(8,128)(2,1)S(1)}) fusion(bf16[16,3584]{1,0:T(8,128)(2,1)} %collective-permute-done.10, bf16[16,3584]{1,0:T(8,128)(2,1)} %collective-permute-done.9, pred[]{:T(512)S(6)} %eq.21, bf16[16,3584]{1,0:T(8,128)(2,1)S(1)} %collective-permute-done.4, ...), kind=kLoop, calls=%fused_computation.8 | loop fusion | flops 1720320 | bytes 1376259 | tf_op jit(solution)/shard_map/jit(_where)/select_n | solution.py:378
  27.2 1.3 %collective-permute-start.11 = (bf16[16,7168]{1,0:T(8,128)(2,1)S(1)}, bf16[16,7168]{1,0:T(8,128)(2,1)S(1)}, u32[]{:S(2)}, u32[]{:S(2)}) collective-permute-start(bf16[16,7168]{1,0:T(8,128)(2,1)S(1)} %get-tuple-element.76.refs_8_), channel_id=1, source_target_pairs={{24,0},{28,1},{13,29},{21,28},{9,25},{17,24},{26,2},{30,3},{15,31}... | collective-permute-start | bytes 688136 | tf_op jit(solution)/shard_map/ppermute | solution.py:316
  28.5 1.5 %collective-permute-start.17 = (bf16[16,7168]{1,0:T(8,128)(2,1)S(1)}, bf16[16,7168]{1,0:T(8,128)(2,1)S(1)}, u32[]{:S(2)}, u32[]{:S(2)}) collective-permute-start(bf16[16,7168]{1,0:T(8,128)(2,1)S(1)} %collective-permute-done.5.refs_9_.refs_8_), channel_id=1, source_target_pairs={{0,1},{1,0},{2,3},{3,2},{4,5},{5,4},{6,7},{7,6},{8,9},{9,8},{10,11... | collective-permute-start | bytes 688136 | tf_op jit(solution)/shard_map/ppermute | solution.py:319
  30.0 2.2 %collective-permute-start.12 = (f32[4,16,64]{2,1,0:T(8,128)S(1)}, f32[4,16,64]{2,1,0:T(8,128)S(1)}, u32[]{:S(2)}, u32[]{:S(2)}) collective-permute-start(f32[4,16,64]{2,1,0:T(8,128)S(1)} %slice.9), channel_id=1, source_target_pairs={{1,5},{5,1},{9,13},{13,9},{17,21},{21,17},{25,29},{29,25},{3,7},{7... | collective-permute-start | bytes 49160 | tf_op jit(solution)/shard_map/ppermute | solution.py:316
  32.2 1.3 %collective-permute-start.2 = (bf16[64,3584]{1,0:T(8,128)(2,1)S(1)}, bf16[64,3584]{1,0:T(8,128)(2,1)S(1)}, u32[]{:S(2)}, u32[]{:S(2)}) collective-permute-start(bf16[64,3584]{1,0:T(8,128)(2,1)S(1)} %bitcast.63), channel_id=1, source_target_pairs={{0,2},{2,0},{1,3},{3,1},{4,6},{6,4},{5,7},{7,5},{8,10},{10,8},{9,1... | collective-permute-start | bytes 1376264 | tf_op jit(solution)/shard_map/ppermute | solution.py:356
  33.5 1.7 %first.1 = (bf16[16,7680]{1,0:T(8,128)(2,1)S(1)}, bf16[4,16,3584]{2,1,0:T(8,128)(2,1)S(1)}, bf16[4,16,3712]{2,1,0:T(8,128)(2,1)S(1)}) custom-call(s32[9]{0:T(128)S(1)} %concatenate.21.where.refs_0_, bf16[16,7680]{1,0:T(8,128)(2,1)S(1)} %concatenate.24.x_in, f32[8,16,64]{2,1,0:T(8,128)S(1)} %add.18.again_own.refs_4_.refs_2_, ...), custom_call_target="tpu_custom_call" | custom-call | flops 58720256 | bytes 3670016 | tf_op jit(solution)/shard_map/first/pallas_call | solution.py:469
  35.3 0.2 pad_maximum_fusion.refs_6_
  35.6 0.8 copy-done.7
  36.3 0.6 collective-permute-start.3
  36.9 0.4 collective-permute-start.18
  37.4 1.4 %second.1 = (bf16[16,7680]{1,0:T(8,128)(2,1)S(1)}, bf16[2,16,3712]{2,1,0:T(8,128)(2,1)S(1)}) custom-call(s32[9]{0:T(128)S(1)} %concatenate.21.where.refs_0_, bf16[16,7680]{1,0:T(8,128)(2,1)S(1)} %get-tuple-element.45.x_in, f32[4,16,64]{2,1,0:T(8,128)S(1)} %collective-permute-done.12.again_peer.refs_5_, bf16[64,3584]{1,0:T(8,128)(2,1)S(1)} %collective-permute-done.squeeze0, ...), custom_call_target="tpu_custom_call" | custom-call | flops 58720256 | bytes 3670016 | tf_op jit(solution)/shard_map/second/pallas_call | solution.py:474
  38.8 1.9 %collective-permute-start.15 = (bf16[16,7680]{1,0:T(8,128)(2,1)S(1)}, bf16[16,7680]{1,0:T(8,128)(2,1)S(1)}, u32[]{:S(2)}, u32[]{:S(2)}) collective-permute-start(bf16[16,7680]{1,0:T(8,128)(2,1)S(1)} %get-tuple-element.49), channel_id=1, source_target_pairs={{0,8},{4,12},{8,16},{12,20},{16,24},{20,28},{24,29},{28,25},{9,1},... | collective-permute-start | bytes 737288 | tf_op jit(solution)/shard_map/ppermute | solution.py:316
  40.9 5.7 %collective-permute-done.15.refs_1_ = bf16[16,7680]{1,0:T(8,128)(2,1)S(1)} collective-permute-done((bf16[16,7680]{1,0:T(8,128)(2,1)S(1)}, bf16[16,7680]{1,0:T(8,128)(2,1)S(1)}, u32[]{:S(2)}, u32[]{:S(2)}) %collective-permute-start.15) | collective-permute-done | bytes 245792 | tf_op jit(solution)/shard_map/ppermute | solution.py:316
  46.6 2.7 %pair1.1 = (bf16[16,7680]{1,0:T(8,128)(2,1)S(1)}, bf16[2,16,3712]{2,1,0:T(8,128)(2,1)S(1)}, bf16[1,2,16,3712]{3,2,1,0:T(8,128)(2,1)S(1)}, bf16[4,16,3584]{2,1,0:T(8,128)(2,1)S(1)}, bf16[4,16,3712]{2,1,0:T(8,128)(2,1)S(1)}) custom-call(s32[9]{0:T(128)S(1)} %concatenate.21.where.refs_0_, ...), custom_call_target="tpu_custom_call", output_to_operand_aliasing={{3}: (11, {}), {4}: (12, {})} | custom-call | flops 58720256 | bytes 3670016 | tf_op jit(solution)/shard_map/pair1/pallas_call | solution.py:490
  49.3 2.0 %collective-permute-start.16 = (bf16[16,7680]{1,0:T(8,128)(2,1)S(1)}, bf16[16,7680]{1,0:T(8,128)(2,1)S(1)}, u32[]{:S(2)}, u32[]{:S(2)}) collective-permute-start(bf16[16,7680]{1,0:T(8,128)(2,1)S(1)} %get-tuple-element.53), channel_id=1, source_target_pairs={{0,8},{4,12},{8,16},{12,20},{16,24},{20,28},{24,29},{28,25},{9,1},... | collective-permute-start | bytes 737288 | tf_op jit(solution)/shard_map/ppermute | solution.py:316
  51.3 1.0 %subtract_convert_fusion.1 = bf16[64,3584]{1,0:T(8,128)(2,1)} fusion(bf16[64,3584]{1,0:T(8,128)(2,1)S(1)} %collective-permute-done.2, bf16[1,3584,64]{1,2,0:T(8,128)(2,1)S(1)} %copy-done.1, bf16[1,1,3584,64]{2,3,1,0:T(8,128)(2,1)S(1)} %copy-done.6), kind=kLoop, calls=%fused_computation.4 | loop fusion | flops 1605632 | bytes 1835008 | tf_op jit(solution)/shard_map/convert_element_type | solution.py:353
  52.3 4.9 %collective-permute-done.16.refs_1_ = bf16[16,7680]{1,0:T(8,128)(2,1)S(1)} collective-permute-done((bf16[16,7680]{1,0:T(8,128)(2,1)S(1)}, bf16[16,7680]{1,0:T(8,128)(2,1)S(1)}, u32[]{:S(2)}, u32[]{:S(2)}) %collective-permute-start.16) | collective-permute-done | bytes 245792 | tf_op jit(solution)/shard_map/ppermute | solution.py:316
  57.2 2.8 %pair2.1 = (bf16[16,7680]{1,0:T(8,128)(2,1)S(1)}, bf16[2,16,3712]{2,1,0:T(8,128)(2,1)S(1)}, bf16[2,2,16,3712]{3,2,1,0:T(8,128)(2,1)S(1)}, bf16[4,16,3584]{2,1,0:T(8,128)(2,1)S(1)}, bf16[4,16,3712]{2,1,0:T(8,128)(2,1)S(1)}) custom-call(s32[9]{0:T(128)S(1)} %concatenate.21.where.refs_0_, ...), custom_call_target="tpu_custom_call", output_to_operand_aliasing={{3}: (12, {}), {4}: (13, {})} | custom-call | flops 58720256 | bytes 3670016 | tf_op jit(solution)/shard_map/pair2/pallas_call | solution.py:490
  60.0 1.9 %collective-permute-start.19 = (bf16[16,7680]{1,0:T(8,128)(2,1)S(1)}, bf16[16,7680]{1,0:T(8,128)(2,1)S(1)}, u32[]{:S(2)}, u32[]{:S(2)}) collective-permute-start(bf16[16,7680]{1,0:T(8,128)(2,1)S(1)} %get-tuple-element.59), channel_id=1, source_target_pairs={{0,8},{4,12},{8,16},{12,20},{16,24},{20,28},{24,29},{28,25},{9,1},... | collective-permute-start | bytes 737288 | tf_op jit(solution)/shard_map/ppermute | solution.py:316
  62.0 3.3 %collective-permute-start.21 = (bf16[2,2,16,3712]{3,2,0,1:T(8,128)(2,1)S(1)}, bf16[2,2,16,3712]{3,2,0,1:T(8,128)(2,1)S(1)}, u32[]{:S(2)}, u32[]{:S(2)}) collective-permute-start(bf16[2,2,16,3712]{3,2,0,1:T(8,128)(2,1)S(1)} %copy.21), channel_id=1, source_target_pairs={{1,5},{5,1},{9,13},{13,9},{16,20},{17,21},{21,17},{24,28},{25,29},... | collective-permute-start | bytes 1425416 | tf_op jit(solution)/shard_map/ppermute | solution.py:316
  65.3 1.0 %subtract_convert_fusion = bf16[64,3584]{1,0:T(8,128)(2,1)} fusion(bf16[64,3584]{1,0:T(8,128)(2,1)S(1)} %collective-permute-done.3, bf16[1,1,64,3584]{3,2,1,0:T(8,128)(2,1)S(1)} %copy-done.7, bf16[1,64,3584]{2,1,0:T(8,128)(2,1)S(1)} %copy-done.5), kind=kLoop, calls=%fused_computation.3 | loop fusion | flops 1605632 | bytes 1835008 | tf_op jit(solution)/shard_map/convert_element_type | solution.py:353
  66.3 3.1 %collective-permute-done.19.refs_1_ = bf16[16,7680]{1,0:T(8,128)(2,1)S(1)} collective-permute-done((bf16[16,7680]{1,0:T(8,128)(2,1)S(1)}, bf16[16,7680]{1,0:T(8,128)(2,1)S(1)}, u32[]{:S(2)}, u32[]{:S(2)}) %collective-permute-start.19) | collective-permute-done | bytes 245792 | tf_op jit(solution)/shard_map/ppermute | solution.py:316
  69.3 3.3 %pair3.1 = (bf16[16,7680]{1,0:T(8,128)(2,1)S(1)}, bf16[8,128]{1,0:T(8,128)(2,1)}, bf16[1,2,16,3712]{3,2,1,0:T(8,128)(2,1)S(1)}, bf16[4,16,3584]{2,1,0:T(8,128)(2,1)S(1)}, bf16[4,16,3712]{2,1,0:T(8,128)(2,1)S(1)}) custom-call(s32[9]{0:T(128)S(1)} %concatenate.21.where.refs_0_, ...), custom_call_target="tpu_custom_call", output_to_operand_aliasing={{3}: (12, {}), {4}: (13, {})} | custom-call | flops 58720256 | bytes 3670016 | tf_op jit(solution)/shard_map/pair3/pallas_call | solution.py:490
  72.7 2.7 %collective-permute-start.23 = (bf16[2,16,3712]{2,1,0:T(8,128)(2,1)S(1)}, bf16[2,16,3712]{2,1,0:T(8,128)(2,1)S(1)}, u32[]{:S(2)}, u32[]{:S(2)}) collective-permute-start(bf16[2,16,3712]{2,1,0:T(8,128)(2,1)S(1)} %bitcast.61), channel_id=1, source_target_pairs={{1,5},{5,1},{9,13},{13,9},{17,21},{21,17},{24,28},{25,29},{29,25},... | collective-permute-start | bytes 712712 | tf_op jit(solution)/shard_map/ppermute | solution.py:316
  75.3 1.9 %collective-permute-start.25 = (bf16[16,7680]{1,0:T(8,128)(2,1)S(1)}, bf16[16,7680]{1,0:T(8,128)(2,1)S(1)}, u32[]{:S(2)}, u32[]{:S(2)}) collective-permute-start(bf16[16,7680]{1,0:T(8,128)(2,1)S(1)} %get-tuple-element.68), channel_id=1, source_target_pairs={{0,4},{4,8},{8,12},{12,16},{16,20},{20,24},{24,28},{28,29},{5,1},{... | collective-permute-start | bytes 737288 | tf_op jit(solution)/shard_map/ppermute | solution.py:316
  77.3 0.5 collective-permute-start.20
  77.9 1.9 %collective-permute-start.22 = (bf16[2,16,3712]{2,1,0:T(8,128)(2,1)S(1)}, bf16[2,16,3712]{2,1,0:T(8,128)(2,1)S(1)}, u32[]{:S(2)}, u32[]{:S(2)}) collective-permute-start(bf16[2,16,3712]{2,1,0:T(8,128)(2,1)S(1)} %slice_bitcast_fusion), channel_id=1, source_target_pairs={{0,1},{1,0},{2,3},{3,2},{4,5},{5,4},{6,7},{7,6},{8,9},{9,8},{10,11... | collective-permute-start | bytes 712712 | tf_op jit(solution)/shard_map/ppermute | solution.py:319
  79.8 6.1 %collective-permute-done.25.refs_1_ = bf16[16,7680]{1,0:T(8,128)(2,1)S(1)} collective-permute-done((bf16[16,7680]{1,0:T(8,128)(2,1)S(1)}, bf16[16,7680]{1,0:T(8,128)(2,1)S(1)}, u32[]{:S(2)}, u32[]{:S(2)}) %collective-permute-start.25) | collective-permute-done | bytes 245792 | tf_op jit(solution)/shard_map/ppermute | solution.py:316
  85.8 1.4 %last.1 = (bf16[16,7296]{1,0:T(8,128)(2,1)S(1)}, bf16[16,7296]{1,0:T(8,128)(2,1)S(1)}) custom-call(s32[9]{0:T(128)S(1)} %concatenate.21.where.refs_0_, bf16[16,7680]{1,0:T(8,128)(2,1)S(1)} %collective-permute-done.25.refs_1_, f32[8,16,64]{2,1,0:T(8,128)S(1)} %add.18.again_own.refs_4_.refs_2_, bf16[2,64,3584]{2,1,0:T(8,128)(2,1)S(1)} %pad_maximum_fusion.2.mine.refs_3_, ...), custom_call_target="tpu_custom_call" | custom-call | flops 58720256 | bytes 3670016 | tf_op jit(solution)/shard_map/last/pallas_call | solution.py:511
  87.3 0.6 collective-permute-start.24
  87.9 1.0 %collective-permute-done.24.late_got = bf16[16,3712]{1,0:T(8,128)(2,1)S(1)} collective-permute-done((bf16[16,3712]{1,0:T(8,128)(2,1)S(1)}, bf16[16,3712]{1,0:T(8,128)(2,1)S(1)}, u32[]{:S(2)}, u32[]{:S(2)}) %collective-permute-start.24) | collective-permute-done | bytes 118816 | tf_op jit(solution)/shard_map/ppermute | solution.py:319
  89.0 2.1 %finish.1 = (bf16[64,3584]{1,0:T(8,128)(2,1)}, bf16[64,3584]{1,0:T(8,128)(2,1)}, bf16[16,3584]{1,0:T(8,128)(2,1)}, bf16[16,3584]{1,0:T(8,128)(2,1)}) custom-call(s32[9]{0:T(128)S(1)} %concatenate.21.where.refs_0_, bf16[4,16,3584]{2,1,0:T(8,128)(2,1)S(1)} %get-tuple-element.65.mine, bf16[4,16,3712]{2,1,0:T(8,128)(2,1)S(1)} %get-tuple-element.66.sent, ...), custom_call_target="tpu_custom_call" | custom-call | flops 58720256 | bytes 3670016 | tf_op jit(solution)/shard_map/finish/pallas_call | solution.py:517
  (52 shorter events, 1.0 us)
Async XLA Ops:
  0.6 15.8 %collective-permute-start = (bf16[64,3584]{1,0:T(8,128)(2,1)}, bf16[64,3584]{1,0:T(8,128)(2,1)S(1)}, u32[]{:S(2)}, u32[]{:S(2)}) collective-permute-start(bf16[64,3584]{1,0:T(8,128)(2,1)} %bitcast.52), channel_id=1, source_target_pairs={{0,4},{1,5},{4,0},{5,1},{8,12},{9,13},{12,8},{13,9},{16,20},{17,21... | collective-permute-start | bytes 1376264 | tf_op jit(solution)/shard_map/ppermute | solution.py:316
  1.9 1.1 %copy-start = (bf16[1,3584,64]{1,2,0:T(8,128)(2,1)S(1)}, bf16[1,3584,64]{1,2,0:T(8,128)(2,1)}, u32[]{:S(2)}) copy-start(bf16[1,3584,64]{1,2,0:T(8,128)(2,1)} %param.11) | copy-start | bytes 1376260
  3.0 1.2 %copy-start.2 = (bf16[1,1,8,16,3584]{4,3,2,1,0:T(8,128)(2,1)S(1)}, bf16[1,1,8,16,3584]{4,3,2,1,0:T(8,128)(2,1)}, u32[]{:S(2)}) copy-start(bf16[1,1,8,16,3584]{4,3,2,1,0:T(8,128)(2,1)} %param.15) | copy-start | bytes 2752516
  4.2 3.1 %copy-start.8 = (bf16[1,1,16,3584]{3,2,1,0:T(8,128)(2,1)S(1)}, bf16[1,1,16,3584]{3,2,1,0:T(8,128)(2,1)}, u32[]{:S(2)}) copy-start(bf16[1,1,16,3584]{3,2,1,0:T(8,128)(2,1)} %param.16) | copy-start | bytes 344068
  4.2 3.1 %copy-start.9 = (bf16[1,1,16,3584]{3,2,1,0:T(8,128)(2,1)S(1)}, bf16[1,1,16,3584]{3,2,1,0:T(8,128)(2,1)}, u32[]{:S(2)}) copy-start(bf16[1,1,16,3584]{3,2,1,0:T(8,128)(2,1)} %param.17) | copy-start | bytes 344068
  4.2 13.6 %copy-start.1 = (bf16[1,3584,64]{1,2,0:T(8,128)(2,1)S(1)}, bf16[1,3584,64]{1,2,0:T(8,128)(2,1)}, u32[]{:S(2)}) copy-start(bf16[1,3584,64]{1,2,0:T(8,128)(2,1)} %param.11) | copy-start | bytes 1376260
  4.2 13.6 %copy-start.4 = (bf16[1,64,3584]{2,1,0:T(8,128)(2,1)S(1)}, bf16[1,64,3584]{2,1,0:T(8,128)(2,1)}, u32[]{:S(2)}) copy-start(bf16[1,64,3584]{2,1,0:T(8,128)(2,1)} %param.12) | copy-start | bytes 1376260
  4.6 13.5 %collective-permute-start.7 = (f32[8,16,64]{2,1,0:T(8,128)S(1)}, f32[8,16,64]{2,1,0:T(8,128)}, u32[]{:S(2)}, u32[]{:S(2)}) collective-permute-start(f32[8,16,64]{2,1,0:T(8,128)S(1)} %stashed.1), channel_id=1, source_target_pairs={{0,1},{1,0},{2,3},{3,2},{4,5},{5,4},{6,7},{7,6},{8,9},{9,8},{10,11... | collective-permute-start | bytes 98312 | tf_op jit(solution)/shard_map/ppermute | solution.py:319
  5.6 9.3 %collective-permute-start.9 = (bf16[16,3584]{1,0:T(8,128)(2,1)}, bf16[16,3584]{1,0:T(8,128)(2,1)}, u32[]{:S(2)}, u32[]{:S(2)}) collective-permute-start(bf16[16,3584]{1,0:T(8,128)(2,1)} %bitcast.67), channel_id=1, source_target_pairs={{0,4},{1,5},{4,0},{5,1},{8,12},{9,13},{12,8},{13,9},{16,20},{17,21... | collective-permute-start | bytes 344072 | tf_op jit(solution)/shard_map/ppermute | solution.py:316
  6.8 9.6 %collective-permute-start.4 = (bf16[16,3584]{1,0:T(8,128)(2,1)S(1)}, bf16[16,3584]{1,0:T(8,128)(2,1)S(1)}, u32[]{:S(2)}, u32[]{:S(2)}) collective-permute-start(bf16[16,3584]{1,0:T(8,128)(2,1)S(1)} %get-tuple-element.79), channel_id=1, source_target_pairs={{0,1},{1,0},{2,3},{3,2},{4,5},{5,4},{6,7},{7,6},{8,9},{9,8},{10,11... | collective-permute-start | bytes 344072 | tf_op jit(solution)/shard_map/ppermute | solution.py:319
  7.9 12.4 %collective-permute-start.6 = (bf16[16,3584]{1,0:T(8,128)(2,1)}, bf16[16,3584]{1,0:T(8,128)(2,1)}, u32[]{:S(2)}, u32[]{:S(2)}) collective-permute-start(bf16[16,3584]{1,0:T(8,128)(2,1)} %get-tuple-element.81), channel_id=1, source_target_pairs={{0,1},{1,0},{2,3},{3,2},{4,5},{5,4},{6,7},{7,6},{8,9},{9,8},{10,11... | collective-permute-start | bytes 344072 | tf_op jit(solution)/shard_map/ppermute | solution.py:319
  14.9 6.2 %collective-permute-start.10 = (bf16[16,3584]{1,0:T(8,128)(2,1)}, bf16[16,3584]{1,0:T(8,128)(2,1)}, u32[]{:S(2)}, u32[]{:S(2)}) collective-permute-start(bf16[16,3584]{1,0:T(8,128)(2,1)} %collective-permute-done.9), channel_id=1, source_target_pairs={{0,1},{1,0},{2,3},{3,2},{4,5},{5,4},{6,7},{7,6},{8,9},{9,8},{10,11... | collective-permute-start | bytes 344072 | tf_op jit(solution)/shard_map/ppermute | solution.py:319
  16.4 9.6 %collective-permute-start.5 = (bf16[16,7168]{1,0:T(8,128)(2,1)S(1)}, bf16[16,7168]{1,0:T(8,128)(2,1)S(1)}, u32[]{:S(2)}, u32[]{:S(2)}) collective-permute-start(bf16[16,7168]{1,0:T(8,128)(2,1)S(1)} %pad_maximum_fusion.3.refs_8_.refs_5_), channel_id=1, source_target_pairs={{8,0},{16,1},{1,29},{12,4},{20,5},{5,25},{10,2},{18,3},{3,31},{14,... | collective-permute-start | bytes 688136 | tf_op jit(solution)/shard_map/ppermute | solution.py:316
  17.9 14.4 %collective-permute-start.8 = (bf16[2,64,3584]{2,1,0:T(8,128)(2,1)S(1)}, bf16[2,64,3584]{2,1,0:T(8,128)(2,1)S(1)}, u32[]{:S(2)}, u32[]{:S(2)}) collective-permute-start(bf16[2,64,3584]{2,1,0:T(8,128)(2,1)S(1)} %pad_maximum_fusion.2.mine.refs_3_), channel_id=1, source_target_pairs={{0,1},{1,0},{2,3},{3,2},{4,5},{5,4},{6,7},{7,6},{8,9},{9,8},{10,11... | collective-permute-start | bytes 2752520 | tf_op jit(solution)/shard_map/ppermute | solution.py:319
  18.1 14.1 %copy-start.6 = (bf16[1,1,3584,64]{2,3,1,0:T(8,128)(2,1)S(1)}, bf16[1,1,3584,64]{2,3,1,0:T(8,128)(2,1)}, u32[]{:S(2)}) copy-start(bf16[1,1,3584,64]{2,3,1,0:T(8,128)(2,1)} %param.13) | copy-start | bytes 1376260
  19.0 16.2 %collective-permute-start.13 = (bf16[64,3584]{1,0:T(8,128)(2,1)}, bf16[64,3584]{1,0:T(8,128)(2,1)S(1)}, u32[]{:S(2)}, u32[]{:S(2)}) collective-permute-start(bf16[64,3584]{1,0:T(8,128)(2,1)} %bitcast.62), channel_id=1, source_target_pairs={{0,4},{1,5},{4,0},{5,1},{8,12},{9,13},{12,8},{13,9},{16,20},{17,21... | collective-permute-start | bytes 1376264 | tf_op jit(solution)/shard_map/ppermute | solution.py:316
  20.3 9.7 %collective-permute-start.1 = (bf16[64,3584]{1,0:T(8,128)(2,1)S(1)}, bf16[64,3584]{1,0:T(8,128)(2,1)S(1)}, u32[]{:S(2)}, u32[]{:S(2)}) collective-permute-start(bf16[64,3584]{1,0:T(8,128)(2,1)S(1)} %collective-permute-done.squeeze0), channel_id=1, source_target_pairs={{0,1},{1,0},{2,3},{3,2},{4,5},{5,4},{6,7},{7,6},{8,9},{9,8},{10,11... | collective-permute-start | bytes 1376264 | tf_op jit(solution)/shard_map/ppermute | solution.py:319
  27.2 8.3 %collective-permute-start.11 = (bf16[16,7168]{1,0:T(8,128)(2,1)S(1)}, bf16[16,7168]{1,0:T(8,128)(2,1)S(1)}, u32[]{:S(2)}, u32[]{:S(2)}) collective-permute-start(bf16[16,7168]{1,0:T(8,128)(2,1)S(1)} %get-tuple-element.76.refs_8_), channel_id=1, source_target_pairs={{24,0},{28,1},{13,29},{21,28},{9,25},{17,24},{26,2},{30,3},{15,31}... | collective-permute-start | bytes 688136 | tf_op jit(solution)/shard_map/ppermute | solution.py:316
  28.5 28.7 %collective-permute-start.17 = (bf16[16,7168]{1,0:T(8,128)(2,1)S(1)}, bf16[16,7168]{1,0:T(8,128)(2,1)S(1)}, u32[]{:S(2)}, u32[]{:S(2)}) collective-permute-start(bf16[16,7168]{1,0:T(8,128)(2,1)S(1)} %collective-permute-done.5.refs_9_.refs_8_), channel_id=1, source_target_pairs={{0,1},{1,0},{2,3},{3,2},{4,5},{5,4},{6,7},{7,6},{8,9},{9,8},{10,11... | collective-permute-start | bytes 688136 | tf_op jit(solution)/shard_map/ppermute | solution.py:319
  30.0 6.9 %collective-permute-start.12 = (f32[4,16,64]{2,1,0:T(8,128)S(1)}, f32[4,16,64]{2,1,0:T(8,128)S(1)}, u32[]{:S(2)}, u32[]{:S(2)}) collective-permute-start(f32[4,16,64]{2,1,0:T(8,128)S(1)} %slice.9), channel_id=1, source_target_pairs={{1,5},{5,1},{9,13},{13,9},{17,21},{21,17},{25,29},{29,25},{3,7},{7... | collective-permute-start | bytes 49160 | tf_op jit(solution)/shard_map/ppermute | solution.py:316
  32.2 19.1 %collective-permute-start.2 = (bf16[64,3584]{1,0:T(8,128)(2,1)S(1)}, bf16[64,3584]{1,0:T(8,128)(2,1)S(1)}, u32[]{:S(2)}, u32[]{:S(2)}) collective-permute-start(bf16[64,3584]{1,0:T(8,128)(2,1)S(1)} %bitcast.63), channel_id=1, source_target_pairs={{0,2},{2,0},{1,3},{3,1},{4,6},{6,4},{5,7},{7,5},{8,10},{10,8},{9,1... | collective-permute-start | bytes 1376264 | tf_op jit(solution)/shard_map/ppermute | solution.py:356
  35.2 2.1 %collective-permute-start.14 = (bf16[64,3584]{1,0:T(8,128)(2,1)S(1)}, bf16[64,3584]{1,0:T(8,128)(2,1)S(1)}, u32[]{:S(2)}, u32[]{:S(2)}) collective-permute-start(bf16[64,3584]{1,0:T(8,128)(2,1)S(1)} %collective-permute-done.13.expand0), channel_id=1, source_target_pairs={{0,1},{1,0},{2,3},{3,2},{4,5},{5,4},{6,7},{7,6},{8,9},{9,8},{10,11... | collective-permute-start | bytes 1376264 | tf_op jit(solution)/shard_map/ppermute | solution.py:319
  35.3 1.0 %copy-start.7 = (bf16[1,1,64,3584]{3,2,1,0:T(8,128)(2,1)S(1)}, bf16[1,1,64,3584]{3,2,1,0:T(8,128)(2,1)}, u32[]{:S(2)}) copy-start(bf16[1,1,64,3584]{3,2,1,0:T(8,128)(2,1)} %param.14) | copy-start | bytes 1376260
  36.3 28.9 %collective-permute-start.3 = (bf16[64,3584]{1,0:T(8,128)(2,1)S(1)}, bf16[64,3584]{1,0:T(8,128)(2,1)S(1)}, u32[]{:S(2)}, u32[]{:S(2)}) collective-permute-start(bf16[64,3584]{1,0:T(8,128)(2,1)S(1)} %bitcast.64), channel_id=1, source_target_pairs={{0,2},{2,0},{1,3},{3,1},{4,6},{6,4},{5,7},{7,5},{8,10},{10,8},{9,1... | collective-permute-start | bytes 1376264 | tf_op jit(solution)/shard_map/ppermute | solution.py:356
  36.9 20.3 %collective-permute-start.18 = (bf16[16,7168]{1,0:T(8,128)(2,1)S(1)}, bf16[16,7168]{1,0:T(8,128)(2,1)S(1)}, u32[]{:S(2)}, u32[]{:S(2)}) collective-permute-start(bf16[16,7168]{1,0:T(8,128)(2,1)S(1)} %collective-permute-done.11.refs_10_), channel_id=1, source_target_pairs={{0,1},{1,0},{2,3},{3,2},{4,5},{5,4},{6,7},{7,6},{8,9},{9,8},{10,11... | collective-permute-start | bytes 688136 | tf_op jit(solution)/shard_map/ppermute | solution.py:319
  38.8 7.8 %collective-permute-start.15 = (bf16[16,7680]{1,0:T(8,128)(2,1)S(1)}, bf16[16,7680]{1,0:T(8,128)(2,1)S(1)}, u32[]{:S(2)}, u32[]{:S(2)}) collective-permute-start(bf16[16,7680]{1,0:T(8,128)(2,1)S(1)} %get-tuple-element.49), channel_id=1, source_target_pairs={{0,8},{4,12},{8,16},{12,20},{16,24},{20,28},{24,29},{28,25},{9,1},... | collective-permute-start | bytes 737288 | tf_op jit(solution)/shard_map/ppermute | solution.py:316
  49.3 7.9 %collective-permute-start.16 = (bf16[16,7680]{1,0:T(8,128)(2,1)S(1)}, bf16[16,7680]{1,0:T(8,128)(2,1)S(1)}, u32[]{:S(2)}, u32[]{:S(2)}) collective-permute-start(bf16[16,7680]{1,0:T(8,128)(2,1)S(1)} %get-tuple-element.53), channel_id=1, source_target_pairs={{0,8},{4,12},{8,16},{12,20},{16,24},{20,28},{24,29},{28,25},{9,1},... | collective-permute-start | bytes 737288 | tf_op jit(solution)/shard_map/ppermute | solution.py:316
  57.2 8.1 %copy-start.5 = (bf16[1,64,3584]{2,1,0:T(8,128)(2,1)S(1)}, bf16[1,64,3584]{2,1,0:T(8,128)(2,1)}, u32[]{:S(2)}) copy-start(bf16[1,64,3584]{2,1,0:T(8,128)(2,1)} %param.12) | copy-start | bytes 1376260
  60.0 9.3 %collective-permute-start.19 = (bf16[16,7680]{1,0:T(8,128)(2,1)S(1)}, bf16[16,7680]{1,0:T(8,128)(2,1)S(1)}, u32[]{:S(2)}, u32[]{:S(2)}) collective-permute-start(bf16[16,7680]{1,0:T(8,128)(2,1)S(1)} %get-tuple-element.59), channel_id=1, source_target_pairs={{0,8},{4,12},{8,16},{12,20},{16,24},{20,28},{24,29},{28,25},{9,1},... | collective-permute-start | bytes 737288 | tf_op jit(solution)/shard_map/ppermute | solution.py:316
  62.0 15.8 %collective-permute-start.21 = (bf16[2,2,16,3712]{3,2,0,1:T(8,128)(2,1)S(1)}, bf16[2,2,16,3712]{3,2,0,1:T(8,128)(2,1)S(1)}, u32[]{:S(2)}, u32[]{:S(2)}) collective-permute-start(bf16[2,2,16,3712]{3,2,0,1:T(8,128)(2,1)S(1)} %copy.21), channel_id=1, source_target_pairs={{1,5},{5,1},{9,13},{13,9},{16,20},{17,21},{21,17},{24,28},{25,29},... | collective-permute-start | bytes 1425416 | tf_op jit(solution)/shard_map/ppermute | solution.py:316
  72.7 14.6 %collective-permute-start.23 = (bf16[2,16,3712]{2,1,0:T(8,128)(2,1)S(1)}, bf16[2,16,3712]{2,1,0:T(8,128)(2,1)S(1)}, u32[]{:S(2)}, u32[]{:S(2)}) collective-permute-start(bf16[2,16,3712]{2,1,0:T(8,128)(2,1)S(1)} %bitcast.61), channel_id=1, source_target_pairs={{1,5},{5,1},{9,13},{13,9},{17,21},{21,17},{24,28},{25,29},{29,25},... | collective-permute-start | bytes 712712 | tf_op jit(solution)/shard_map/ppermute | solution.py:316
  75.3 10.5 %collective-permute-start.25 = (bf16[16,7680]{1,0:T(8,128)(2,1)S(1)}, bf16[16,7680]{1,0:T(8,128)(2,1)S(1)}, u32[]{:S(2)}, u32[]{:S(2)}) collective-permute-start(bf16[16,7680]{1,0:T(8,128)(2,1)S(1)} %get-tuple-element.68), channel_id=1, source_target_pairs={{0,4},{4,8},{8,12},{12,16},{16,20},{20,24},{24,28},{28,29},{5,1},{... | collective-permute-start | bytes 737288 | tf_op jit(solution)/shard_map/ppermute | solution.py:316
  77.3 11.7 %collective-permute-start.20 = (bf16[4,16,3712]{2,1,0:T(8,128)(2,1)S(1)}, bf16[4,16,3712]{2,1,0:T(8,128)(2,1)S(1)}, u32[]{:S(2)}, u32[]{:S(2)}) collective-permute-start(bf16[4,16,3712]{2,1,0:T(8,128)(2,1)S(1)} %get-tuple-element.66.sent), channel_id=1, source_target_pairs={{0,1},{1,0},{2,3},{3,2},{4,5},{5,4},{6,7},{7,6},{8,9},{9,8},{10,11... | collective-permute-start | bytes 1425416 | tf_op jit(solution)/shard_map/ppermute | solution.py:319
  77.8 11.1 %copy-start.3 = (bf16[1,1,8,16,3584]{4,3,2,1,0:T(8,128)(2,1)S(1)}, bf16[1,1,8,16,3584]{4,3,2,1,0:T(8,128)(2,1)}, u32[]{:S(2)}) copy-start(bf16[1,1,8,16,3584]{4,3,2,1,0:T(8,128)(2,1)} %param.15) | copy-start | bytes 2752516
  77.9 11.1 %collective-permute-start.22 = (bf16[2,16,3712]{2,1,0:T(8,128)(2,1)S(1)}, bf16[2,16,3712]{2,1,0:T(8,128)(2,1)S(1)}, u32[]{:S(2)}, u32[]{:S(2)}) collective-permute-start(bf16[2,16,3712]{2,1,0:T(8,128)(2,1)S(1)} %slice_bitcast_fusion), channel_id=1, source_target_pairs={{0,1},{1,0},{2,3},{3,2},{4,5},{5,4},{6,7},{7,6},{8,9},{9,8},{10,11... | collective-permute-start | bytes 712712 | tf_op jit(solution)/shard_map/ppermute | solution.py:319
  87.2 1.7 %collective-permute-start.26 = (bf16[16,7296]{1,0:T(8,128)(2,1)S(1)}, bf16[16,7296]{1,0:T(8,128)(2,1)S(1)}, u32[]{:S(2)}, u32[]{:S(2)}) collective-permute-start(bf16[16,7296]{1,0:T(8,128)(2,1)S(1)} %get-tuple-element.71.last_other), channel_id=1, source_target_pairs={{0,1},{1,0},{2,3},{3,2},{4,5},{5,4},{6,7},{7,6},{8,9},{9,8},{10,11... | collective-permute-start | bytes 700424 | tf_op jit(solution)/shard_map/ppermute | solution.py:319
  87.3 1.6 %collective-permute-start.24 = (bf16[16,3712]{1,0:T(8,128)(2,1)S(1)}, bf16[16,3712]{1,0:T(8,128)(2,1)S(1)}, u32[]{:S(2)}, u32[]{:S(2)}) collective-permute-start(bf16[16,3712]{1,0:T(8,128)(2,1)S(1)} %slice_bitcast_fusion.1), channel_id=1, source_target_pairs={{0,1},{1,0},{2,3},{3,2},{4,5},{5,4},{6,7},{7,6},{8,9},{9,8},{10,11... | collective-permute-start | bytes 356360 | tf_op jit(solution)/shard_map/ppermute | solution.py:319

commit v8 on v7

--- a/solution.py
+++ b/solution.py
@@ -359,8 +359,8 @@
     squeeze_peer = to_peer(squeeze, both)
     expand_peer = to_peer(tied(expand, squeeze_peer), both)
     squeeze_peer_other = swap(squeeze_peer)
-    squeeze_came = across(tied(squeeze_late, squeeze_peer_other))
-    expand_came = across(tied(expand_late, squeeze_peer_other))
+    squeeze_came = across(tied(squeeze_late, squeeze_peer))
+    expand_came = across(tied(expand_late, squeeze_peer))
     squeeze_new = averaged(squeeze, squeeze_late, squeeze_came)
     expand_new = averaged(expand, expand_late, expand_came)
     own = lax.optimization_barrier(jnp.stack([squeeze, expand]))
@@ -370,7 +370,7 @@
         stash_kernel, "stashed", shape(ticks, rows, rank, dtype=f32), [VMEM, VMEM], VMEM
     )(stash, squeeze)
     again_own = partial + swap(partial)
-    again_peer = to_peer(tied(again_own[1::2], squeeze_peer_other), [(s, 1) for s in everyone])
+    again_peer = to_peer(tied(again_own[1::2], squeeze_peer), [(s, 1) for s in everyone])
 
     cots_crossed = to_peer(cots, both)
     entering = jnp.concatenate([jnp.where(forward, acts, cots), swap(jnp.where(forward, cots, acts))], axis=1)
@@ -482,9 +482,9 @@
     for step in range(1, size.steps):
         final = step + 1 == size.steps
         if step == 2:
+            x = tied(x, squeeze_came, expand_came)
+        if step == 3:
             x = tied(x, squeeze_new)
-        if step == 3:
-            x = tied(x, expand_new)
         turns = used(block_at(step))
         body = functools.partial(lambda step, turns, size, *refs: pair_kernel(size, step, turns, *refs), step, turns)
         x, held, passed_now, hist_mine, hist_other = call(
@@ -512,7 +512,7 @@
         functools.partial(lambda turns, size, *refs: last_kernel(size, turns, *refs), turns), "last",
         (shape(rows, size.kept + half), shape(rows, size.kept + half)),
         [SMEM] + [VMEM] * (4 + len(turns)), (VMEM, VMEM),
-    )(where, tied(x, odd), again_own, own, other, *(feeds[n] for n in turns))
+    )(where, tied(x, odd, expand_new), again_own, own, other, *(feeds[n] for n in turns))
     last_got = swap(last_other)
     squeeze_grad, expand_grad, fwd_carry, bwd_carry = call(
         end_kernel, "finish",

time: 91.7 us -> 93.4 us (1.019)
  starting transfers between devices: 32.1 us -> 34.6 us
  waiting for transfers between devices: 32.6 us -> 31 us
  other arithmetic: 6.26 us -> 7.2 us
    ppermute x12, waiting for transfers between devices: 31.5 us -> 29.6 us  [send(): lax.ppermute(x, ('pipe', 'mp'), [(a * 2 + b, c * 2 + d) for (a, b), (c, d...]
    ppermute x13, starting transfers between devices: 8.98 us -> 10.6 us  [swap(): return lax.ppermute(x, 'mp', [(0, 1), (1, 0)])]
    select_n x1, other arithmetic: 0.7 us -> 1.66 us  [shards(): jnp.where(forward, fwd_in, bwd_in)]
    unnamed x20 -> x14, local copies, waits for them, and re-layouts: 3.04 us -> 2.98 us
  transfers between devices with their start and end apart: 27 -> 27, of which waited for: 7 -> 9; matrix products, arithmetic and copies ran while one was open for 7% -> 7% of each run, Pallas kernels for 15% -> 12%
where the time goes in v8:
time: 93.4 us; the launch traced here: 92.9 us
  starting transfers between devices  34.6 us (37%)
  waiting for transfers between devices  31 us (33%)
  Pallas kernels  15.8 us (17%)
  other arithmetic  7.2 us (8%)
  local copies, waits for them, and re-layouts  3.2 us (3%)
  between operations  1.08 us (1%)
    ppermute x12, waiting for transfers between devices, send(): lax.ppermute(x, ('pipe', 'mp'), [(a * 2 + b, c * 2 + d) for (a, b), (c, d...  29.6 us
    ppermute x12, starting transfers between devices, send(): lax.ppermute(x, ('pipe', 'mp'), [(a * 2 + b, c * 2 + d) for (a, b), (c, d...  21.6 us
    ppermute x13, starting transfers between devices, swap(): return lax.ppermute(x, 'mp', [(0, 1), (1, 0)])  10.6 us
    pallas_call x3, Pallas kernels, shards(): call(body, f'pair{step}', (shape(rows, size.message), shape(*((8, 128) if...  8.86 us
    unnamed x14, local copies, waits for them, and re-layouts  2.98 us
    ppermute x2, starting transfers between devices, across(): lax.ppermute(late, 'dp', [(0, 1), (1, 0)])  2.49 us
    pallas_call x1, Pallas kernels, shards(): call(end_kernel, 'finish', (shape(rank, half), shape(rank, half), shape(r...  2.07 us
    convert_element_type x2, other arithmetic, averaged(): return (old.astype(f32) - STEP_RATE * total / replicas).astype(bf16)  1.94 us
  transfers between devices with their start and end apart: 27, of which 9 were waited for; matrix products, arithmetic and copies ran while one was open for 7% of the time, Pallas kernels for 12%

profile of v8, /device:TPU:25, one launch (start us, length us, event | category | flops | bytes accessed | tf_op | source)
XLA Modules:
  0.0 92.9 jit_solution(12018105357626611079)
XLA Ops:
  0.6 1.0 %bitcast_select_fusion.1 = (bf16[16,3584]{1,0:T(8,128)(2,1)S(1)}, bf16[16,3584]{1,0:T(8,128)(2,1)S(1)}) fusion(bf16[1,16,3584]{2,1,0:T(8,128)(2,1)} %param.9, pred[]{:T(512)S(6)} %eq.21, bf16[1,16,3584]{2,1,0:T(8,128)(2,1)} %param.10), kind=kLoop, calls=%fused_computation.11 | loop fusion | flops 114688 | bytes 458753 | tf_op jit(solution)/shard_map/jit(_where)/select_n | solution.py:376
  1.7 0.7 collective-permute-start.3
  2.4 1.3 %collective-permute-start = (bf16[64,3584]{1,0:T(8,128)(2,1)}, bf16[64,3584]{1,0:T(8,128)(2,1)S(1)}, u32[]{:S(2)}, u32[]{:S(2)}) collective-permute-start(bf16[64,3584]{1,0:T(8,128)(2,1)} %bitcast.52), channel_id=1, source_target_pairs={{0,4},{1,5},{4,0},{5,1},{8,12},{9,13},{12,8},{13,9},{16,20},{17,21... | collective-permute-start | bytes 1376264 | tf_op jit(solution)/shard_map/ppermute | solution.py:316
  3.7 0.2 collective-permute-start.8
  3.9 1.7 %select_bitcast_fusion.1 = (bf16[16,3584]{1,0:T(8,128)(2,1)}, bf16[16,3584]{1,0:T(8,128)(2,1)}) fusion(bf16[1,1,16,3584]{3,2,1,0:T(8,128)(2,1)} %param.16, bf16[1,1,16,3584]{3,2,1,0:T(8,128)(2,1)} %param.17, pred[]{:T(512)S(6)} %eq.21), kind=kLoop, calls=%fused_computation.13 | loop fusion | flops 114688 | bytes 458753 | tf_op jit(solution)/shard_map/jit(_where)/select_n | solution.py:445
  5.6 0.6 collective-permute-start.5
  6.2 1.0 %copy-done = bf16[1,3584,64]{1,2,0:T(8,128)(2,1)S(1)} copy-done((bf16[1,3584,64]{1,2,0:T(8,128)(2,1)S(1)}, bf16[1,3584,64]{1,2,0:T(8,128)(2,1)}, u32[]{:S(2)}) %copy-start) | copy-done | bytes 458776
  7.2 1.2 %copy-done.2 = bf16[1,1,8,16,3584]{4,3,2,1,0:T(8,128)(2,1)S(1)} copy-done((bf16[1,1,8,16,3584]{4,3,2,1,0:T(8,128)(2,1)S(1)}, bf16[1,1,8,16,3584]{4,3,2,1,0:T(8,128)(2,1)}, u32[]{:S(2)}) %copy-start.2) | copy-done | bytes 917528
  8.4 0.4 stashed.1
  8.8 8.4 %collective-permute-done.8 = bf16[16,3584]{1,0:T(8,128)(2,1)} collective-permute-done((bf16[16,3584]{1,0:T(8,128)(2,1)}, bf16[16,3584]{1,0:T(8,128)(2,1)}, u32[]{:S(2)}, u32[]{:S(2)}) %collective-permute-start.8) | collective-permute-done | bytes 114720 | tf_op jit(solution)/shard_map/ppermute | solution.py:316
  17.3 0.8 collective-permute-start.9
  18.2 1.3 %collective-permute-start.4 = (bf16[16,7168]{1,0:T(8,128)(2,1)S(1)}, bf16[16,7168]{1,0:T(8,128)(2,1)S(1)}, u32[]{:S(2)}, u32[]{:S(2)}) collective-permute-start(bf16[16,7168]{1,0:T(8,128)(2,1)S(1)} %pad_maximum_fusion.3.refs_8_.refs_5_), channel_id=1, source_target_pairs={{8,0},{16,1},{1,29},{12,4},{20,5},{5,25},{10,2},{18,3},{3,31},{14,... | collective-permute-start | bytes 688136 | tf_op jit(solution)/shard_map/ppermute | solution.py:316
  19.8 0.9 add.18.again_own.refs_4_.refs_2_
  20.7 1.3 %collective-permute-start.13 = (bf16[64,3584]{1,0:T(8,128)(2,1)S(1)}, bf16[64,3584]{1,0:T(8,128)(2,1)S(1)}, u32[]{:S(2)}, u32[]{:S(2)}) collective-permute-start(bf16[64,3584]{1,0:T(8,128)(2,1)S(1)} %bitcast.62), channel_id=1, source_target_pairs={{0,4},{1,5},{4,0},{5,1},{8,12},{9,13},{12,8},{13,9},{16,20},{17,21... | collective-permute-start | bytes 1376264 | tf_op jit(solution)/shard_map/ppermute | solution.py:316
  22.0 2.1 %collective-permute-start.11 = (f32[4,16,64]{2,1,0:T(8,128)S(1)}, f32[4,16,64]{2,1,0:T(8,128)S(1)}, u32[]{:S(2)}, u32[]{:S(2)}) collective-permute-start(f32[4,16,64]{2,1,0:T(8,128)S(1)} %slice.9), channel_id=1, source_target_pairs={{1,5},{5,1},{9,13},{13,9},{17,21},{21,17},{25,29},{29,25},{3,7},{7... | collective-permute-start | bytes 49160 | tf_op jit(solution)/shard_map/ppermute | solution.py:316
  24.1 1.3 %collective-permute-start.1 = (bf16[64,3584]{1,0:T(8,128)(2,1)}, bf16[64,3584]{1,0:T(8,128)(2,1)S(1)}, u32[]{:S(2)}, u32[]{:S(2)}) collective-permute-start(bf16[64,3584]{1,0:T(8,128)(2,1)} %bitcast.63), channel_id=1, source_target_pairs={{0,2},{2,0},{1,3},{3,1},{4,6},{6,4},{5,7},{7,5},{8,10},{10,8},{9,1... | collective-permute-start | bytes 1376264 | tf_op jit(solution)/shard_map/ppermute | solution.py:356
  25.4 2.3 %collective-permute-done.4.refs_9_.refs_8_ = bf16[16,7168]{1,0:T(8,128)(2,1)S(1)} collective-permute-done((bf16[16,7168]{1,0:T(8,128)(2,1)S(1)}, bf16[16,7168]{1,0:T(8,128)(2,1)S(1)}, u32[]{:S(2)}, u32[]{:S(2)}) %collective-permute-start.4) | collective-permute-done | bytes 229408 | tf_op jit(solution)/shard_map/ppermute | solution.py:316
  27.8 1.2 %maximum_select_fusion.1 = (bf16[16,7168]{1,0:T(8,128)(2,1)S(1)}, bf16[16,7168]{1,0:T(8,128)(2,1)S(1)}) fusion(bf16[16,3584]{1,0:T(8,128)(2,1)} %collective-permute-done.9, bf16[16,3584]{1,0:T(8,128)(2,1)} %collective-permute-done.8, pred[]{:T(512)S(6)} %eq.21, bf16[16,3584]{1,0:T(8,128)(2,1)S(1)} %collective-permute-done.3, ...), kind=kLoop, calls=%fused_computation.8 | loop fusion | flops 1720320 | bytes 1376259 | tf_op jit(solution)/shard_map/jit(_where)/select_n | solution.py:378
  29.0 1.3 %collective-permute-start.10 = (bf16[16,7168]{1,0:T(8,128)(2,1)S(1)}, bf16[16,7168]{1,0:T(8,128)(2,1)S(1)}, u32[]{:S(2)}, u32[]{:S(2)}) collective-permute-start(bf16[16,7168]{1,0:T(8,128)(2,1)S(1)} %get-tuple-element.76.refs_8_), channel_id=1, source_target_pairs={{24,0},{28,1},{13,29},{21,28},{9,25},{17,24},{26,2},{30,3},{15,31}... | collective-permute-start | bytes 688136 | tf_op jit(solution)/shard_map/ppermute | solution.py:316
  30.3 1.7 %first.1 = (bf16[16,7680]{1,0:T(8,128)(2,1)S(1)}, bf16[4,16,3584]{2,1,0:T(8,128)(2,1)S(1)}, bf16[4,16,3712]{2,1,0:T(8,128)(2,1)S(1)}) custom-call(s32[9]{0:T(128)S(1)} %concatenate.21.where.refs_0_, bf16[16,7680]{1,0:T(8,128)(2,1)S(1)} %concatenate.24.x_in, f32[8,16,64]{2,1,0:T(8,128)S(1)} %add.18.again_own.refs_4_.refs_2_, ...), custom_call_target="tpu_custom_call" | custom-call | flops 58720256 | bytes 3670016 | tf_op jit(solution)/shard_map/first/pallas_call | solution.py:469
  32.0 2.9 %collective-permute-done.13.expand0 = bf16[64,3584]{1,0:T(8,128)(2,1)S(1)} collective-permute-done((bf16[64,3584]{1,0:T(8,128)(2,1)S(1)}, bf16[64,3584]{1,0:T(8,128)(2,1)S(1)}, u32[]{:S(2)}, u32[]{:S(2)}) %collective-permute-start.13) | collective-permute-done | bytes 458784 | tf_op jit(solution)/shard_map/ppermute | solution.py:316
  34.9 1.6 %collective-permute-start.14 = (bf16[64,3584]{1,0:T(8,128)(2,1)S(1)}, bf16[64,3584]{1,0:T(8,128)(2,1)S(1)}, u32[]{:S(2)}, u32[]{:S(2)}) collective-permute-start(bf16[64,3584]{1,0:T(8,128)(2,1)S(1)} %collective-permute-done.13.expand0), channel_id=1, source_target_pairs={{0,1},{1,0},{2,3},{3,2},{4,5},{5,4},{6,7},{7,6},{8,9},{9,8},{10,11... | collective-permute-start | bytes 1376264 | tf_op jit(solution)/shard_map/ppermute | solution.py:319
  36.5 0.2 pad_maximum_fusion.refs_6_
  36.8 0.8 copy-done.6
  37.5 1.2 %collective-permute-start.2 = (bf16[64,3584]{1,0:T(8,128)(2,1)S(1)}, bf16[64,3584]{1,0:T(8,128)(2,1)S(1)}, u32[]{:S(2)}, u32[]{:S(2)}) collective-permute-start(bf16[64,3584]{1,0:T(8,128)(2,1)S(1)} %bitcast.64), channel_id=1, source_target_pairs={{0,2},{2,0},{1,3},{3,1},{4,6},{6,4},{5,7},{7,5},{8,10},{10,8},{9,1... | collective-permute-start | bytes 1376264 | tf_op jit(solution)/shard_map/ppermute | solution.py:356
  38.7 2.1 %collective-permute-start.17 = (bf16[16,7168]{1,0:T(8,128)(2,1)S(1)}, bf16[16,7168]{1,0:T(8,128)(2,1)S(1)}, u32[]{:S(2)}, u32[]{:S(2)}) collective-permute-start(bf16[16,7168]{1,0:T(8,128)(2,1)S(1)} %collective-permute-done.4.refs_9_.refs_8_), channel_id=1, source_target_pairs={{0,1},{1,0},{2,3},{3,2},{4,5},{5,4},{6,7},{7,6},{8,9},{9,8},{10,11... | collective-permute-start | bytes 688136 | tf_op jit(solution)/shard_map/ppermute | solution.py:319
  40.9 1.4 %second.1 = (bf16[16,7680]{1,0:T(8,128)(2,1)S(1)}, bf16[2,16,3712]{2,1,0:T(8,128)(2,1)S(1)}) custom-call(s32[9]{0:T(128)S(1)} %concatenate.21.where.refs_0_, bf16[16,7680]{1,0:T(8,128)(2,1)S(1)} %get-tuple-element.45.x_in, f32[4,16,64]{2,1,0:T(8,128)S(1)} %collective-permute-done.11.again_peer.refs_5_, bf16[64,3584]{1,0:T(8,128)(2,1)S(1)} %collective-permute-done.squeeze0, ...), custom_call_target="tpu_custom_call" | custom-call | flops 58720256 | bytes 3670016 | tf_op jit(solution)/shard_map/second/pallas_call | solution.py:474
  42.3 1.9 %collective-permute-start.15 = (bf16[16,7680]{1,0:T(8,128)(2,1)S(1)}, bf16[16,7680]{1,0:T(8,128)(2,1)S(1)}, u32[]{:S(2)}, u32[]{:S(2)}) collective-permute-start(bf16[16,7680]{1,0:T(8,128)(2,1)S(1)} %get-tuple-element.49), channel_id=1, source_target_pairs={{0,8},{4,12},{8,16},{12,20},{16,24},{20,28},{24,29},{28,25},{9,1},... | collective-permute-start | bytes 737288 | tf_op jit(solution)/shard_map/ppermute | solution.py:316
  44.2 0.2 pad_maximum_fusion.1.refs_7_
  44.4 5.7 %collective-permute-done.15.refs_1_ = bf16[16,7680]{1,0:T(8,128)(2,1)S(1)} collective-permute-done((bf16[16,7680]{1,0:T(8,128)(2,1)S(1)}, bf16[16,7680]{1,0:T(8,128)(2,1)S(1)}, u32[]{:S(2)}, u32[]{:S(2)}) %collective-permute-start.15) | collective-permute-done | bytes 245792 | tf_op jit(solution)/shard_map/ppermute | solution.py:316
  50.1 2.7 %pair1.1 = (bf16[16,7680]{1,0:T(8,128)(2,1)S(1)}, bf16[2,16,3712]{2,1,0:T(8,128)(2,1)S(1)}, bf16[1,2,16,3712]{3,2,1,0:T(8,128)(2,1)S(1)}, bf16[4,16,3584]{2,1,0:T(8,128)(2,1)S(1)}, bf16[4,16,3712]{2,1,0:T(8,128)(2,1)S(1)}) custom-call(s32[9]{0:T(128)S(1)} %concatenate.21.where.refs_0_, ...), custom_call_target="tpu_custom_call", output_to_operand_aliasing={{3}: (11, {}), {4}: (12, {})} | custom-call | flops 58720256 | bytes 3670016 | tf_op jit(solution)/shard_map/pair1/pallas_call | solution.py:490
  52.8 1.9 %collective-permute-start.16 = (bf16[16,7680]{1,0:T(8,128)(2,1)S(1)}, bf16[16,7680]{1,0:T(8,128)(2,1)S(1)}, u32[]{:S(2)}, u32[]{:S(2)}) collective-permute-start(bf16[16,7680]{1,0:T(8,128)(2,1)S(1)} %get-tuple-element.53), channel_id=1, source_target_pairs={{0,8},{4,12},{8,16},{12,20},{16,24},{20,28},{24,29},{28,25},{9,1},... | collective-permute-start | bytes 737288 | tf_op jit(solution)/shard_map/ppermute | solution.py:316
  54.8 1.0 %subtract_convert_fusion.1 = bf16[64,3584]{1,0:T(8,128)(2,1)} fusion(bf16[64,3584]{1,0:T(8,128)(2,1)S(1)} %collective-permute-done.1, bf16[1,3584,64]{1,2,0:T(8,128)(2,1)S(1)} %copy-done.1, bf16[1,1,3584,64]{2,3,1,0:T(8,128)(2,1)S(1)} %copy-done.5), kind=kLoop, calls=%fused_computation.4 | loop fusion | flops 1605632 | bytes 1835008 | tf_op jit(solution)/shard_map/convert_element_type | solution.py:353
  55.8 5.0 %collective-permute-done.16.refs_1_ = bf16[16,7680]{1,0:T(8,128)(2,1)S(1)} collective-permute-done((bf16[16,7680]{1,0:T(8,128)(2,1)S(1)}, bf16[16,7680]{1,0:T(8,128)(2,1)S(1)}, u32[]{:S(2)}, u32[]{:S(2)}) %collective-permute-start.16) | collective-permute-done | bytes 245792 | tf_op jit(solution)/shard_map/ppermute | solution.py:316
  60.8 2.8 %pair2.1 = (bf16[16,7680]{1,0:T(8,128)(2,1)S(1)}, bf16[2,16,3712]{2,1,0:T(8,128)(2,1)S(1)}, bf16[2,2,16,3712]{3,2,1,0:T(8,128)(2,1)S(1)}, bf16[4,16,3584]{2,1,0:T(8,128)(2,1)S(1)}, bf16[4,16,3712]{2,1,0:T(8,128)(2,1)S(1)}) custom-call(s32[9]{0:T(128)S(1)} %concatenate.21.where.refs_0_, ...), custom_call_target="tpu_custom_call", output_to_operand_aliasing={{3}: (12, {}), {4}: (13, {})} | custom-call | flops 58720256 | bytes 3670016 | tf_op jit(solution)/shard_map/pair2/pallas_call | solution.py:490
  63.6 1.9 %collective-permute-start.19 = (bf16[16,7680]{1,0:T(8,128)(2,1)S(1)}, bf16[16,7680]{1,0:T(8,128)(2,1)S(1)}, u32[]{:S(2)}, u32[]{:S(2)}) collective-permute-start(bf16[16,7680]{1,0:T(8,128)(2,1)S(1)} %get-tuple-element.59), channel_id=1, source_target_pairs={{0,8},{4,12},{8,16},{12,20},{16,24},{20,28},{24,29},{28,25},{9,1},... | collective-permute-start | bytes 737288 | tf_op jit(solution)/shard_map/ppermute | solution.py:316
  65.5 3.0 %collective-permute-start.21 = (bf16[2,2,16,3712]{3,2,0,1:T(8,128)(2,1)S(1)}, bf16[2,2,16,3712]{3,2,0,1:T(8,128)(2,1)S(1)}, u32[]{:S(2)}, u32[]{:S(2)}) collective-permute-start(bf16[2,2,16,3712]{3,2,0,1:T(8,128)(2,1)S(1)} %copy.21), channel_id=1, source_target_pairs={{1,5},{5,1},{9,13},{13,9},{16,20},{17,21},{21,17},{24,28},{25,29},... | collective-permute-start | bytes 1425416 | tf_op jit(solution)/shard_map/ppermute | solution.py:316
  68.6 1.0 %subtract_convert_fusion = bf16[64,3584]{1,0:T(8,128)(2,1)} fusion(bf16[64,3584]{1,0:T(8,128)(2,1)S(1)} %collective-permute-done.2, bf16[1,1,64,3584]{3,2,1,0:T(8,128)(2,1)S(1)} %copy-done.6, bf16[1,64,3584]{2,1,0:T(8,128)(2,1)S(1)} %copy-done.4), kind=kLoop, calls=%fused_computation.3 | loop fusion | flops 1605632 | bytes 1835008 | tf_op jit(solution)/shard_map/convert_element_type | solution.py:353
  69.6 3.3 %collective-permute-done.19.refs_1_ = bf16[16,7680]{1,0:T(8,128)(2,1)S(1)} collective-permute-done((bf16[16,7680]{1,0:T(8,128)(2,1)S(1)}, bf16[16,7680]{1,0:T(8,128)(2,1)S(1)}, u32[]{:S(2)}, u32[]{:S(2)}) %collective-permute-start.19) | collective-permute-done | bytes 245792 | tf_op jit(solution)/shard_map/ppermute | solution.py:316
  72.9 3.4 %pair3.1 = (bf16[16,7680]{1,0:T(8,128)(2,1)S(1)}, bf16[8,128]{1,0:T(8,128)(2,1)}, bf16[1,2,16,3712]{3,2,1,0:T(8,128)(2,1)S(1)}, bf16[4,16,3584]{2,1,0:T(8,128)(2,1)S(1)}, bf16[4,16,3712]{2,1,0:T(8,128)(2,1)S(1)}) custom-call(s32[9]{0:T(128)S(1)} %concatenate.21.where.refs_0_, ...), custom_call_target="tpu_custom_call", output_to_operand_aliasing={{3}: (12, {}), {4}: (13, {})} | custom-call | flops 58720256 | bytes 3670016 | tf_op jit(solution)/shard_map/pair3/pallas_call | solution.py:490
  76.2 1.9 %collective-permute-start.25 = (bf16[16,7680]{1,0:T(8,128)(2,1)S(1)}, bf16[16,7680]{1,0:T(8,128)(2,1)S(1)}, u32[]{:S(2)}, u32[]{:S(2)}) collective-permute-start(bf16[16,7680]{1,0:T(8,128)(2,1)S(1)} %get-tuple-element.68), channel_id=1, source_target_pairs={{0,4},{4,8},{8,12},{12,16},{16,20},{20,24},{24,28},{28,29},{5,1},{... | collective-permute-start | bytes 737288 | tf_op jit(solution)/shard_map/ppermute | solution.py:316
  78.1 3.4 %collective-permute-start.23 = (bf16[2,16,3712]{2,1,0:T(8,128)(2,1)S(1)}, bf16[2,16,3712]{2,1,0:T(8,128)(2,1)S(1)}, u32[]{:S(2)}, u32[]{:S(2)}) collective-permute-start(bf16[2,16,3712]{2,1,0:T(8,128)(2,1)S(1)} %bitcast.61), channel_id=1, source_target_pairs={{1,5},{5,1},{9,13},{13,9},{17,21},{21,17},{24,28},{25,29},{29,25},... | collective-permute-start | bytes 712712 | tf_op jit(solution)/shard_map/ppermute | solution.py:316
  81.6 4.3 %collective-permute-start.22 = (bf16[2,16,3712]{2,1,0:T(8,128)(2,1)S(1)}, bf16[2,16,3712]{2,1,0:T(8,128)(2,1)S(1)}, u32[]{:S(2)}, u32[]{:S(2)}) collective-permute-start(bf16[2,16,3712]{2,1,0:T(8,128)(2,1)S(1)} %slice_bitcast_fusion), channel_id=1, source_target_pairs={{0,1},{1,0},{2,3},{3,2},{4,5},{5,4},{6,7},{7,6},{8,9},{9,8},{10,11... | collective-permute-start | bytes 712712 | tf_op jit(solution)/shard_map/ppermute | solution.py:319
  85.9 0.9 collective-permute-done.25.refs_1_
  86.8 1.4 %last.1 = (bf16[16,7296]{1,0:T(8,128)(2,1)S(1)}, bf16[16,7296]{1,0:T(8,128)(2,1)S(1)}) custom-call(s32[9]{0:T(128)S(1)} %concatenate.21.where.refs_0_, bf16[16,7680]{1,0:T(8,128)(2,1)S(1)} %collective-permute-done.25.refs_1_, f32[8,16,64]{2,1,0:T(8,128)S(1)} %add.18.again_own.refs_4_.refs_2_, bf16[2,64,3584]{2,1,0:T(8,128)(2,1)S(1)} %pad_maximum_fusion.2.mine.refs_3_, ...), custom_call_target="tpu_custom_call" | custom-call | flops 58720256 | bytes 3670016 | tf_op jit(solution)/shard_map/last/pallas_call | solution.py:511
  88.3 1.1 %collective-permute-done.23.late = bf16[2,16,3712]{2,1,0:T(8,128)(2,1)S(1)} collective-permute-done((bf16[2,16,3712]{2,1,0:T(8,128)(2,1)S(1)}, bf16[2,16,3712]{2,1,0:T(8,128)(2,1)S(1)}, u32[]{:S(2)}, u32[]{:S(2)}) %collective-permute-start.23) | collective-permute-done | bytes 237600 | tf_op jit(solution)/shard_map/ppermute | solution.py:316
  89.5 1.3 %collective-permute-done.24.late_got = bf16[16,3712]{1,0:T(8,128)(2,1)S(1)} collective-permute-done((bf16[16,3712]{1,0:T(8,128)(2,1)S(1)}, bf16[16,3712]{1,0:T(8,128)(2,1)S(1)}, u32[]{:S(2)}, u32[]{:S(2)}) %collective-permute-start.24) | collective-permute-done | bytes 118816 | tf_op jit(solution)/shard_map/ppermute | solution.py:319
  90.8 2.1 %finish.1 = (bf16[64,3584]{1,0:T(8,128)(2,1)}, bf16[64,3584]{1,0:T(8,128)(2,1)}, bf16[16,3584]{1,0:T(8,128)(2,1)}, bf16[16,3584]{1,0:T(8,128)(2,1)}) custom-call(s32[9]{0:T(128)S(1)} %concatenate.21.where.refs_0_, bf16[4,16,3584]{2,1,0:T(8,128)(2,1)S(1)} %get-tuple-element.65.mine, bf16[4,16,3712]{2,1,0:T(8,128)(2,1)S(1)} %get-tuple-element.66.sent, ...), custom_call_target="tpu_custom_call" | custom-call | flops 58720256 | bytes 3670016 | tf_op jit(solution)/shard_map/finish/pallas_call | solution.py:517
  (46 shorter events, 0.9 us)
Async XLA Ops:
  0.6 18.8 %copy-start.4 = (bf16[1,64,3584]{2,1,0:T(8,128)(2,1)S(1)}, bf16[1,64,3584]{2,1,0:T(8,128)(2,1)}, u32[]{:S(2)}) copy-start(bf16[1,64,3584]{2,1,0:T(8,128)(2,1)} %param.12) | copy-start | bytes 1376260
  1.7 16.5 %collective-permute-start.3 = (bf16[16,3584]{1,0:T(8,128)(2,1)S(1)}, bf16[16,3584]{1,0:T(8,128)(2,1)S(1)}, u32[]{:S(2)}, u32[]{:S(2)}) collective-permute-start(bf16[16,3584]{1,0:T(8,128)(2,1)S(1)} %get-tuple-element.79), channel_id=1, source_target_pairs={{0,1},{1,0},{2,3},{3,2},{4,5},{5,4},{6,7},{7,6},{8,9},{9,8},{10,11... | collective-permute-start | bytes 344072 | tf_op jit(solution)/shard_map/ppermute | solution.py:319
  2.4 15.7 %collective-permute-start = (bf16[64,3584]{1,0:T(8,128)(2,1)}, bf16[64,3584]{1,0:T(8,128)(2,1)S(1)}, u32[]{:S(2)}, u32[]{:S(2)}) collective-permute-start(bf16[64,3584]{1,0:T(8,128)(2,1)} %bitcast.52), channel_id=1, source_target_pairs={{0,4},{1,5},{4,0},{5,1},{8,12},{9,13},{12,8},{13,9},{16,20},{17,21... | collective-permute-start | bytes 1376264 | tf_op jit(solution)/shard_map/ppermute | solution.py:316
  3.7 13.6 %collective-permute-start.8 = (bf16[16,3584]{1,0:T(8,128)(2,1)}, bf16[16,3584]{1,0:T(8,128)(2,1)}, u32[]{:S(2)}, u32[]{:S(2)}) collective-permute-start(bf16[16,3584]{1,0:T(8,128)(2,1)} %bitcast.67), channel_id=1, source_target_pairs={{0,4},{1,5},{4,0},{5,1},{8,12},{9,13},{12,8},{13,9},{16,20},{17,21... | collective-permute-start | bytes 344072 | tf_op jit(solution)/shard_map/ppermute | solution.py:316
  5.6 16.4 %collective-permute-start.5 = (bf16[16,3584]{1,0:T(8,128)(2,1)}, bf16[16,3584]{1,0:T(8,128)(2,1)}, u32[]{:S(2)}, u32[]{:S(2)}) collective-permute-start(bf16[16,3584]{1,0:T(8,128)(2,1)} %get-tuple-element.81), channel_id=1, source_target_pairs={{0,1},{1,0},{2,3},{3,2},{4,5},{5,4},{6,7},{7,6},{8,9},{9,8},{10,11... | collective-permute-start | bytes 344072 | tf_op jit(solution)/shard_map/ppermute | solution.py:319
  6.2 1.0 %copy-start = (bf16[1,3584,64]{1,2,0:T(8,128)(2,1)S(1)}, bf16[1,3584,64]{1,2,0:T(8,128)(2,1)}, u32[]{:S(2)}) copy-start(bf16[1,3584,64]{1,2,0:T(8,128)(2,1)} %param.11) | copy-start | bytes 1376260
  7.2 1.2 %copy-start.2 = (bf16[1,1,8,16,3584]{4,3,2,1,0:T(8,128)(2,1)S(1)}, bf16[1,1,8,16,3584]{4,3,2,1,0:T(8,128)(2,1)}, u32[]{:S(2)}) copy-start(bf16[1,1,8,16,3584]{4,3,2,1,0:T(8,128)(2,1)} %param.15) | copy-start | bytes 2752516
  8.8 11.1 %collective-permute-start.6 = (f32[8,16,64]{2,1,0:T(8,128)S(1)}, f32[8,16,64]{2,1,0:T(8,128)}, u32[]{:S(2)}, u32[]{:S(2)}) collective-permute-start(f32[8,16,64]{2,1,0:T(8,128)S(1)} %stashed.1), channel_id=1, source_target_pairs={{0,1},{1,0},{2,3},{3,2},{4,5},{5,4},{6,7},{7,6},{8,9},{9,8},{10,11... | collective-permute-start | bytes 98312 | tf_op jit(solution)/shard_map/ppermute | solution.py:319
  17.3 6.8 %collective-permute-start.9 = (bf16[16,3584]{1,0:T(8,128)(2,1)}, bf16[16,3584]{1,0:T(8,128)(2,1)}, u32[]{:S(2)}, u32[]{:S(2)}) collective-permute-start(bf16[16,3584]{1,0:T(8,128)(2,1)} %collective-permute-done.8), channel_id=1, source_target_pairs={{0,1},{1,0},{2,3},{3,2},{4,5},{5,4},{6,7},{7,6},{8,9},{9,8},{10,11... | collective-permute-start | bytes 344072 | tf_op jit(solution)/shard_map/ppermute | solution.py:319
  18.2 9.6 %collective-permute-start.4 = (bf16[16,7168]{1,0:T(8,128)(2,1)S(1)}, bf16[16,7168]{1,0:T(8,128)(2,1)S(1)}, u32[]{:S(2)}, u32[]{:S(2)}) collective-permute-start(bf16[16,7168]{1,0:T(8,128)(2,1)S(1)} %pad_maximum_fusion.3.refs_8_.refs_5_), channel_id=1, source_target_pairs={{8,0},{16,1},{1,29},{12,4},{20,5},{5,25},{10,2},{18,3},{3,31},{14,... | collective-permute-start | bytes 688136 | tf_op jit(solution)/shard_map/ppermute | solution.py:316
  19.6 9.4 %collective-permute-start.7 = (bf16[2,64,3584]{2,1,0:T(8,128)(2,1)S(1)}, bf16[2,64,3584]{2,1,0:T(8,128)(2,1)S(1)}, u32[]{:S(2)}, u32[]{:S(2)}) collective-permute-start(bf16[2,64,3584]{2,1,0:T(8,128)(2,1)S(1)} %pad_maximum_fusion.2.mine.refs_3_), channel_id=1, source_target_pairs={{0,1},{1,0},{2,3},{3,2},{4,5},{5,4},{6,7},{7,6},{8,9},{9,8},{10,11... | collective-permute-start | bytes 2752520 | tf_op jit(solution)/shard_map/ppermute | solution.py:319
  20.7 14.2 %collective-permute-start.13 = (bf16[64,3584]{1,0:T(8,128)(2,1)S(1)}, bf16[64,3584]{1,0:T(8,128)(2,1)S(1)}, u32[]{:S(2)}, u32[]{:S(2)}) collective-permute-start(bf16[64,3584]{1,0:T(8,128)(2,1)S(1)} %bitcast.62), channel_id=1, source_target_pairs={{0,4},{1,5},{4,0},{5,1},{8,12},{9,13},{12,8},{13,9},{16,20},{17,21... | collective-permute-start | bytes 1376264 | tf_op jit(solution)/shard_map/ppermute | solution.py:316
  22.0 16.7 %collective-permute-start.11 = (f32[4,16,64]{2,1,0:T(8,128)S(1)}, f32[4,16,64]{2,1,0:T(8,128)S(1)}, u32[]{:S(2)}, u32[]{:S(2)}) collective-permute-start(f32[4,16,64]{2,1,0:T(8,128)S(1)} %slice.9), channel_id=1, source_target_pairs={{1,5},{5,1},{9,13},{13,9},{17,21},{21,17},{25,29},{29,25},{3,7},{7... | collective-permute-start | bytes 49160 | tf_op jit(solution)/shard_map/ppermute | solution.py:316
  24.1 30.6 %collective-permute-start.1 = (bf16[64,3584]{1,0:T(8,128)(2,1)}, bf16[64,3584]{1,0:T(8,128)(2,1)S(1)}, u32[]{:S(2)}, u32[]{:S(2)}) collective-permute-start(bf16[64,3584]{1,0:T(8,128)(2,1)} %bitcast.63), channel_id=1, source_target_pairs={{0,2},{2,0},{1,3},{3,1},{4,6},{6,4},{5,7},{7,5},{8,10},{10,8},{9,1... | collective-permute-start | bytes 1376264 | tf_op jit(solution)/shard_map/ppermute | solution.py:356
  27.7 13.0 %collective-permute-start.12 = (bf16[64,3584]{1,0:T(8,128)(2,1)S(1)}, bf16[64,3584]{1,0:T(8,128)(2,1)S(1)}, u32[]{:S(2)}, u32[]{:S(2)}) collective-permute-start(bf16[64,3584]{1,0:T(8,128)(2,1)S(1)} %collective-permute-done.squeeze0), channel_id=1, source_target_pairs={{0,1},{1,0},{2,3},{3,2},{4,5},{5,4},{6,7},{7,6},{8,9},{9,8},{10,11... | collective-permute-start | bytes 1376264 | tf_op jit(solution)/shard_map/ppermute | solution.py:319
  29.0 7.8 %collective-permute-start.10 = (bf16[16,7168]{1,0:T(8,128)(2,1)S(1)}, bf16[16,7168]{1,0:T(8,128)(2,1)S(1)}, u32[]{:S(2)}, u32[]{:S(2)}) collective-permute-start(bf16[16,7168]{1,0:T(8,128)(2,1)S(1)} %get-tuple-element.76.refs_8_), channel_id=1, source_target_pairs={{24,0},{28,1},{13,29},{21,28},{9,25},{17,24},{26,2},{30,3},{15,31}... | collective-permute-start | bytes 688136 | tf_op jit(solution)/shard_map/ppermute | solution.py:316
  34.9 6.0 %collective-permute-start.14 = (bf16[64,3584]{1,0:T(8,128)(2,1)S(1)}, bf16[64,3584]{1,0:T(8,128)(2,1)S(1)}, u32[]{:S(2)}, u32[]{:S(2)}) collective-permute-start(bf16[64,3584]{1,0:T(8,128)(2,1)S(1)} %collective-permute-done.13.expand0), channel_id=1, source_target_pairs={{0,1},{1,0},{2,3},{3,2},{4,5},{5,4},{6,7},{7,6},{8,9},{9,8},{10,11... | collective-permute-start | bytes 1376264 | tf_op jit(solution)/shard_map/ppermute | solution.py:319
  36.5 1.0 %copy-start.6 = (bf16[1,1,64,3584]{3,2,1,0:T(8,128)(2,1)S(1)}, bf16[1,1,64,3584]{3,2,1,0:T(8,128)(2,1)}, u32[]{:S(2)}) copy-start(bf16[1,1,64,3584]{3,2,1,0:T(8,128)(2,1)} %param.14) | copy-start | bytes 1376260
  37.5 18.3 %collective-permute-start.2 = (bf16[64,3584]{1,0:T(8,128)(2,1)S(1)}, bf16[64,3584]{1,0:T(8,128)(2,1)S(1)}, u32[]{:S(2)}, u32[]{:S(2)}) collective-permute-start(bf16[64,3584]{1,0:T(8,128)(2,1)S(1)} %bitcast.64), channel_id=1, source_target_pairs={{0,2},{2,0},{1,3},{3,1},{4,6},{6,4},{5,7},{7,5},{8,10},{10,8},{9,1... | collective-permute-start | bytes 1376264 | tf_op jit(solution)/shard_map/ppermute | solution.py:356
  38.7 22.0 %collective-permute-start.17 = (bf16[16,7168]{1,0:T(8,128)(2,1)S(1)}, bf16[16,7168]{1,0:T(8,128)(2,1)S(1)}, u32[]{:S(2)}, u32[]{:S(2)}) collective-permute-start(bf16[16,7168]{1,0:T(8,128)(2,1)S(1)} %collective-permute-done.4.refs_9_.refs_8_), channel_id=1, source_target_pairs={{0,1},{1,0},{2,3},{3,2},{4,5},{5,4},{6,7},{7,6},{8,9},{9,8},{10,11... | collective-permute-start | bytes 688136 | tf_op jit(solution)/shard_map/ppermute | solution.py:319
  40.8 20.0 %collective-permute-start.18 = (bf16[16,7168]{1,0:T(8,128)(2,1)S(1)}, bf16[16,7168]{1,0:T(8,128)(2,1)S(1)}, u32[]{:S(2)}, u32[]{:S(2)}) collective-permute-start(bf16[16,7168]{1,0:T(8,128)(2,1)S(1)} %collective-permute-done.10.refs_10_), channel_id=1, source_target_pairs={{0,1},{1,0},{2,3},{3,2},{4,5},{5,4},{6,7},{7,6},{8,9},{9,8},{10,11... | collective-permute-start | bytes 688136 | tf_op jit(solution)/shard_map/ppermute | solution.py:319
  42.3 7.8 %collective-permute-start.15 = (bf16[16,7680]{1,0:T(8,128)(2,1)S(1)}, bf16[16,7680]{1,0:T(8,128)(2,1)S(1)}, u32[]{:S(2)}, u32[]{:S(2)}) collective-permute-start(bf16[16,7680]{1,0:T(8,128)(2,1)S(1)} %get-tuple-element.49), channel_id=1, source_target_pairs={{0,8},{4,12},{8,16},{12,20},{16,24},{20,28},{24,29},{28,25},{9,1},... | collective-permute-start | bytes 737288 | tf_op jit(solution)/shard_map/ppermute | solution.py:316
  50.1 4.7 %copy-start.1 = (bf16[1,3584,64]{1,2,0:T(8,128)(2,1)S(1)}, bf16[1,3584,64]{1,2,0:T(8,128)(2,1)}, u32[]{:S(2)}) copy-start(bf16[1,3584,64]{1,2,0:T(8,128)(2,1)} %param.11) | copy-start | bytes 1376260
  50.1 4.7 %copy-start.5 = (bf16[1,1,3584,64]{2,3,1,0:T(8,128)(2,1)S(1)}, bf16[1,1,3584,64]{2,3,1,0:T(8,128)(2,1)}, u32[]{:S(2)}) copy-start(bf16[1,1,3584,64]{2,3,1,0:T(8,128)(2,1)} %param.13) | copy-start | bytes 1376260
  52.8 7.9 %collective-permute-start.16 = (bf16[16,7680]{1,0:T(8,128)(2,1)S(1)}, bf16[16,7680]{1,0:T(8,128)(2,1)S(1)}, u32[]{:S(2)}, u32[]{:S(2)}) collective-permute-start(bf16[16,7680]{1,0:T(8,128)(2,1)S(1)} %get-tuple-element.53), channel_id=1, source_target_pairs={{0,8},{4,12},{8,16},{12,20},{16,24},{20,28},{24,29},{28,25},{9,1},... | collective-permute-start | bytes 737288 | tf_op jit(solution)/shard_map/ppermute | solution.py:316
  63.6 9.3 %collective-permute-start.19 = (bf16[16,7680]{1,0:T(8,128)(2,1)S(1)}, bf16[16,7680]{1,0:T(8,128)(2,1)S(1)}, u32[]{:S(2)}, u32[]{:S(2)}) collective-permute-start(bf16[16,7680]{1,0:T(8,128)(2,1)S(1)} %get-tuple-element.59), channel_id=1, source_target_pairs={{0,8},{4,12},{8,16},{12,20},{16,24},{20,28},{24,29},{28,25},{9,1},... | collective-permute-start | bytes 737288 | tf_op jit(solution)/shard_map/ppermute | solution.py:316
  65.5 16.1 %collective-permute-start.21 = (bf16[2,2,16,3712]{3,2,0,1:T(8,128)(2,1)S(1)}, bf16[2,2,16,3712]{3,2,0,1:T(8,128)(2,1)S(1)}, u32[]{:S(2)}, u32[]{:S(2)}) collective-permute-start(bf16[2,2,16,3712]{3,2,0,1:T(8,128)(2,1)S(1)} %copy.21), channel_id=1, source_target_pairs={{1,5},{5,1},{9,13},{13,9},{16,20},{17,21},{21,17},{24,28},{25,29},... | collective-permute-start | bytes 1425416 | tf_op jit(solution)/shard_map/ppermute | solution.py:316
  76.2 10.6 %collective-permute-start.25 = (bf16[16,7680]{1,0:T(8,128)(2,1)S(1)}, bf16[16,7680]{1,0:T(8,128)(2,1)S(1)}, u32[]{:S(2)}, u32[]{:S(2)}) collective-permute-start(bf16[16,7680]{1,0:T(8,128)(2,1)S(1)} %get-tuple-element.68), channel_id=1, source_target_pairs={{0,4},{4,8},{8,12},{12,16},{16,20},{20,24},{24,28},{28,29},{5,1},{... | collective-permute-start | bytes 737288 | tf_op jit(solution)/shard_map/ppermute | solution.py:316
  78.1 11.2 %collective-permute-start.23 = (bf16[2,16,3712]{2,1,0:T(8,128)(2,1)S(1)}, bf16[2,16,3712]{2,1,0:T(8,128)(2,1)S(1)}, u32[]{:S(2)}, u32[]{:S(2)}) collective-permute-start(bf16[2,16,3712]{2,1,0:T(8,128)(2,1)S(1)} %bitcast.61), channel_id=1, source_target_pairs={{1,5},{5,1},{9,13},{13,9},{17,21},{21,17},{24,28},{25,29},{29,25},... | collective-permute-start | bytes 712712 | tf_op jit(solution)/shard_map/ppermute | solution.py:316
  81.5 9.3 %collective-permute-start.20 = (bf16[4,16,3712]{2,1,0:T(8,128)(2,1)S(1)}, bf16[4,16,3712]{2,1,0:T(8,128)(2,1)S(1)}, u32[]{:S(2)}, u32[]{:S(2)}) collective-permute-start(bf16[4,16,3712]{2,1,0:T(8,128)(2,1)S(1)} %get-tuple-element.66.sent), channel_id=1, source_target_pairs={{0,1},{1,0},{2,3},{3,2},{4,5},{5,4},{6,7},{7,6},{8,9},{9,8},{10,11... | collective-permute-start | bytes 1425416 | tf_op jit(solution)/shard_map/ppermute | solution.py:319
  81.6 9.1 %copy-start.3 = (bf16[1,1,8,16,3584]{4,3,2,1,0:T(8,128)(2,1)S(1)}, bf16[1,1,8,16,3584]{4,3,2,1,0:T(8,128)(2,1)}, u32[]{:S(2)}) copy-start(bf16[1,1,8,16,3584]{4,3,2,1,0:T(8,128)(2,1)} %param.15) | copy-start | bytes 2752516
  81.6 9.1 %collective-permute-start.22 = (bf16[2,16,3712]{2,1,0:T(8,128)(2,1)S(1)}, bf16[2,16,3712]{2,1,0:T(8,128)(2,1)S(1)}, u32[]{:S(2)}, u32[]{:S(2)}) collective-permute-start(bf16[2,16,3712]{2,1,0:T(8,128)(2,1)S(1)} %slice_bitcast_fusion), channel_id=1, source_target_pairs={{0,1},{1,0},{2,3},{3,2},{4,5},{5,4},{6,7},{7,6},{8,9},{9,8},{10,11... | collective-permute-start | bytes 712712 | tf_op jit(solution)/shard_map/ppermute | solution.py:319
  88.2 2.6 %collective-permute-start.26 = (bf16[16,7296]{1,0:T(8,128)(2,1)S(1)}, bf16[16,7296]{1,0:T(8,128)(2,1)S(1)}, u32[]{:S(2)}, u32[]{:S(2)}) collective-permute-start(bf16[16,7296]{1,0:T(8,128)(2,1)S(1)} %get-tuple-element.71.last_other), channel_id=1, source_target_pairs={{0,1},{1,0},{2,3},{3,2},{4,5},{5,4},{6,7},{7,6},{8,9},{9,8},{10,11... | collective-permute-start | bytes 700424 | tf_op jit(solution)/shard_map/ppermute | solution.py:319
  89.4 1.4 %collective-permute-start.24 = (bf16[16,3712]{1,0:T(8,128)(2,1)S(1)}, bf16[16,3712]{1,0:T(8,128)(2,1)S(1)}, u32[]{:S(2)}, u32[]{:S(2)}) collective-permute-start(bf16[16,3712]{1,0:T(8,128)(2,1)S(1)} %slice_bitcast_fusion.1), channel_id=1, source_target_pairs={{0,1},{1,0},{2,3},{3,2},{4,5},{5,4},{6,7},{7,6},{8,9},{9,8},{10,11... | collective-permute-start | bytes 356360 | tf_op jit(solution)/shard_map/ppermute | solution.py:319
